TPU v7x, 32 devices: a whole 2x2x4 slice. The times are simulated.
32 devices in a mesh: row: 8 (over z, core), col: 4 (over y, x).
Axes of the slice: x: 2, y: 2, z: 4, core: 2. Of those that a mesh axis runs over, the one named last changes fastest.
Arguments:
- tokens: bfloat16 [8192, 2048], P('row', 'col'), may hold values from -6 to 6
- attn_gain: float32 [2048], P('col'), may hold values from 0.5 to 1.5
- qkv_weight: bfloat16 [3, 2048, 2048], P(None, 'col', 'row'), may hold values from -0.125 to 0.125
- query_gain: float32 [128], replicated, may hold values from 0.5 to 1.5
- key_gain: float32 [128], replicated, may hold values from 0.5 to 1.5
- out_weight: bfloat16 [2048, 2048], P('row', 'col'), may hold values from -1.5 to 1.5
- moe_gain: float32 [2048], P('col'), may hold values from 0.5 to 1.5
- gate_up_weight: bfloat16 [64, 2048, 2048], P('row', 'col'), may hold values from -0.125 to 0.125
- down_weight: bfloat16 [64, 1024, 2048], P('row', None, 'col'), may hold values from -0.75 to 0.75
- segments: int32 [8, 1024], P('col'), may hold values from 0 to 3, never falling along the last dimension, each value on 1 to 800 neighbouring positions
- routes: int32 [8192, 8], replicated, may hold values from 0 to 63, all different within a row; in each aligned block of 8192 rows (0 to 8191, 8192 to 16383, ...) at most 2048 rows name the same one
- route_gates: float32 [8192, 8], replicated, may hold values from 0.06 to 0.19
- cotangent: bfloat16 [8192, 2048], P('row', 'col'), may hold values from -6 to 6
Outputs:
- output: bfloat16 [8192, 2048], P('row', 'col')
- grad_tokens: bfloat16 [8192, 2048], P('row', 'col')
- grad_attn_gain: float32 [2048], P('col')
- grad_qkv: float32 [3, 2048, 2048], P(None, 'col', 'row')
- grad_query_gain: float32 [128], replicated
- grad_key_gain: float32 [128], replicated
- grad_out_weight: float32 [2048, 2048], P('row', 'col')
- grad_moe_gain: float32 [2048], P('col')
- grad_gate_up: float32 [64, 2048, 2048], P('row', 'col')
- grad_down: float32 [64, 1024, 2048], P('row', None, 'col')
Inputs may be any that keep to these rules, and one draw needn't show every extreme that they name: `routes`: each row names 8 different experts; each expert is named by at most 2048 rows in all, a bound that some block reaches. `segments`: in each sequence the numbers never fall and each of 0 to 3 appears; a document has at most 800 tokens, and some document has exactly 800.
All inputs are finite; a program needn't handle non-finite values.
Results may differ from a plain program's by a relative error of at most 0.028.
Values may be sent and summed in bfloat16 or wider, within the bound.
No kernel may reach another device: no remote copies, remote signals or barrier semaphores. Data moves between devices by JAX's collectives and lax.ppermute only.
A program may use at most 448 MiB of HBM per device.

v0:
```python
from functools import partial

import jax
import jax.numpy as jnp
from jax import lax
from jax.sharding import PartitionSpec as P

DOCS = 4


epsilon = 1e-06
rope_base = 10000.0
neg_large = -1e30


def rotate(values, cosine, sine):
    half_size = values.shape[-1] // 2
    turned = jnp.concatenate([-values[..., half_size:], values[..., :half_size]], axis=-1)
    return values * cosine + turned * sine


def rotate_back(grads, cosine, sine):
    half_size = grads.shape[-1] // 2
    moved = grads * sine
    turned = jnp.concatenate([moved[..., half_size:], -moved[..., :half_size]], axis=-1)
    return grads * cosine + turned


def rope_tables(segments, head_size):
    onehot = (segments[..., None] == jnp.arange(DOCS, dtype=jnp.int32)).astype(jnp.int32)
    counts = jnp.sum(onehot, axis=1)
    starts = jnp.cumsum(counts, axis=-1) - counts
    first_index = jnp.sum(onehot * starts[:, None, :], axis=-1)
    places = (jnp.arange(segments.shape[1], dtype=jnp.int32)[None, :] - first_index).astype(
        jnp.float32
    )
    rates = rope_base ** (-jnp.arange(0, head_size, 2, dtype=jnp.float32) / head_size)
    angles = places[..., None] * rates
    angles = jnp.concatenate([angles, angles], axis=-1)
    return (jnp.cos(angles), jnp.sin(angles))


def width_total(values):
    return lax.psum(values, "col")


def token_rows(values):
    return lax.all_gather(values, "row", axis=0, tiled=True)


def token_sums(values):
    return lax.psum_scatter(
        values.astype(jnp.bfloat16), "row", scatter_dimension=0, tiled=True
    ).astype(jnp.float32)


def norm_back(grad_normed, stream, rate, gain, model_width):
    scaled_grad = grad_normed * gain
    across = width_total(jnp.sum(scaled_grad * stream, axis=-1))[:, None]
    return rate * scaled_grad - stream * rate * rate * rate * across / model_width


def head_norm_back(grad_rot, normed, rate, gain, cosine, sine):
    grad_normed = rotate_back(grad_rot, cosine, sine)
    gain_grad = jnp.sum(grad_normed * normed, axis=(0, 1, 2))
    scaled_grad = grad_normed * gain
    grad_raw = rate * (
        scaled_grad - normed * jnp.mean(scaled_grad * normed, axis=-1, keepdims=True)
    )
    return (grad_raw, gain_grad)


def to_items(values):
    seq_count, seq_len, head_count, head_size = values.shape
    return values.transpose(2, 0, 1, 3).reshape(head_count * seq_count, seq_len, head_size)


def from_items(values, seq_count, seq_len, head_count):
    return (
        values.reshape(head_count, seq_count, seq_len, -1)
        .transpose(1, 2, 0, 3)
        .reshape(seq_count * seq_len, -1)
    )


def attend_forward(factor, packed):
    query, key, value, seg_row = packed
    same = seg_row[:, None] == seg_row[None, :]
    scores = jnp.einsum("qd,kd->qk", query, key, preferred_element_type=jnp.float32) * factor
    scores = jnp.where(same, scores, neg_large)
    top_score = jnp.max(scores, axis=-1, keepdims=True)
    totals = jnp.sum(jnp.exp(scores - top_score), axis=-1, keepdims=True)
    log_total = top_score + jnp.log(totals)
    probs = jnp.exp(scores - log_total)
    result = jnp.einsum(
        "qk,kd->qd", probs.astype(jnp.bfloat16), value, preferred_element_type=jnp.float32
    )
    return (result.astype(jnp.bfloat16), log_total[:, 0])


def attend_backward(factor, packed):
    query, key, value, grad_out, log_total, seg_row = packed
    same = seg_row[:, None] == seg_row[None, :]
    scores = jnp.einsum("qd,kd->qk", query, key, preferred_element_type=jnp.float32) * factor
    scores = jnp.where(same, scores, neg_large)
    probs = jnp.exp(scores - log_total[:, None])
    grad_probs = jnp.einsum("qd,kd->qk", grad_out, value, preferred_element_type=jnp.float32)
    center = jnp.sum(probs * grad_probs, axis=-1, keepdims=True)
    grad_scores = (probs * (grad_probs - center)).astype(jnp.bfloat16)
    grad_query = (
        jnp.einsum("qk,kd->qd", grad_scores, key, preferred_element_type=jnp.float32) * factor
    )
    grad_key = (
        jnp.einsum("qk,qd->kd", grad_scores, query, preferred_element_type=jnp.float32) * factor
    )
    grad_value = jnp.einsum(
        "qk,qd->kd", probs.astype(jnp.bfloat16), grad_out, preferred_element_type=jnp.float32
    )
    return (grad_query, grad_key, grad_value.astype(jnp.bfloat16))


def combine_slots(slot_values, token_slots, slot_weight, tok_total):
    width = slot_values.shape[-1]
    flat_values = slot_values.reshape(-1, width) * slot_weight.reshape(-1)[:, None]
    total = jnp.zeros((tok_total, width), jnp.float32)
    return total.at[token_slots.reshape(-1)].add(flat_values)


def local(
    tokens,
    attn_gain,
    qkv_weight,
    query_gain,
    key_gain,
    out_weight,
    moe_gain,
    gate_up_weight,
    down_weight,
    segments,
    routes,
    route_gates,
    cotangent,
):
    col_count = lax.axis_size("col")
    row_count = lax.axis_size("row")
    col_index = lax.axis_index("col")
    tok_rows, col_width = tokens.shape
    model_width = col_width * col_count
    head_size = query_gain.shape[0]
    head_width = qkv_weight.shape[2]
    head_count = head_width // head_size
    seq_count, seq_len = segments.shape
    tok_share = seq_count * seq_len
    cosine, sine = rope_tables(segments, head_size)
    cosine = cosine[:, :, None, :]
    sine = sine[:, :, None, :]
    factor = head_size ** (-0.5)
    stream = tokens.astype(jnp.float32)
    rate_one = lax.rsqrt(width_total(jnp.sum(stream * stream, axis=-1)) / model_width + epsilon)[
        :, None
    ]
    normed = (stream * rate_one * attn_gain).astype(jnp.bfloat16)
    normed_all = token_rows(normed)
    tok_total = normed_all.shape[0]
    qkv = lax.psum_scatter(
        jnp.einsum("td,adk->tak", normed_all, qkv_weight, preferred_element_type=jnp.float32),
        "col",
        scatter_dimension=0,
        tiled=True,
    )

    def head_split(values):
        return values.reshape(seq_count, seq_len, head_count, head_size)

    query_raw = head_split(qkv[:, 0])
    key_raw = head_split(qkv[:, 1])
    query_rate = lax.rsqrt(jnp.mean(query_raw * query_raw, axis=-1, keepdims=True) + epsilon)
    key_rate = lax.rsqrt(jnp.mean(key_raw * key_raw, axis=-1, keepdims=True) + epsilon)
    query_normed = query_raw * query_rate
    key_normed = key_raw * key_rate
    query_low = rotate(query_normed * query_gain, cosine, sine).astype(jnp.bfloat16)
    key_low = rotate(key_normed * key_gain, cosine, sine).astype(jnp.bfloat16)
    value_low = head_split(qkv[:, 2]).astype(jnp.bfloat16)
    seg_items = jnp.tile(segments, (head_count, 1))
    query_items = to_items(query_low)
    key_items = to_items(key_low)
    value_items = to_items(value_low)
    attended, log_totals = lax.map(
        partial(attend_forward, factor), (query_items, key_items, value_items, seg_items)
    )
    heads_low = from_items(attended, seq_count, seq_len, head_count)
    heads_all = lax.all_gather(heads_low, "col", axis=0, tiled=True)
    attn_result = token_sums(jnp.dot(heads_all, out_weight, preferred_element_type=jnp.float32))
    hidden_one = stream + attn_result
    rate_two = lax.rsqrt(
        width_total(jnp.sum(hidden_one * hidden_one, axis=-1)) / model_width + epsilon
    )[:, None]
    moe_in = (hidden_one * rate_two * moe_gain).astype(jnp.bfloat16)
    moe_all = token_rows(moe_in)
    experts_here = gate_up_weight.shape[0]
    top_count = routes.shape[1]
    pair_total = tok_total * top_count
    capacity = 2 * tok_total * top_count // (experts_here * row_count)
    first_expert = lax.axis_index("row") * experts_here
    expert_ids = first_expert + jnp.arange(experts_here, dtype=jnp.int32)
    flat_routes = routes.reshape(-1)
    flat_gates = route_gates.reshape(-1)
    hits = (flat_routes[None, :] == expert_ids[:, None]).astype(jnp.int32)
    running = jnp.cumsum(hits, axis=1)
    pair_place = jnp.sum(hits * (running - 1), axis=0)
    pair_local = flat_routes - first_expert
    pair_mine = (pair_local >= 0) & (pair_local < experts_here)
    pair_expert = jnp.where(pair_mine, pair_local, experts_here)
    pair_token = jnp.arange(pair_total, dtype=jnp.int32) // top_count
    slot_token = (
        jnp.zeros((experts_here, capacity), jnp.int32)
        .at[pair_expert, pair_place]
        .set(pair_token, mode="drop")
    )
    slot_gate = (
        jnp.zeros((experts_here, capacity), jnp.float32)
        .at[pair_expert, pair_place]
        .set(flat_gates, mode="drop")
    )
    slot_live = (
        jnp.zeros((experts_here, capacity), jnp.float32)
        .at[pair_expert, pair_place]
        .set(1.0, mode="drop")
    )
    token_slots = slot_token.T
    gate_slots = slot_gate.T
    live_slots = slot_live.T
    slot_inputs = moe_all[slot_token]
    hidden_units = down_weight.shape[1]
    part = slot_inputs
    inner = lax.psum_scatter(
        jnp.einsum("ecd,edf->cef", part, gate_up_weight, preferred_element_type=jnp.float32).astype(
            jnp.bfloat16
        ),
        "col",
        scatter_dimension=0,
        tiled=True,
    ).astype(jnp.float32)
    gate_pre = inner[..., :hidden_units]
    up_pre = inner[..., hidden_units:]
    sigmoid_gate = jax.nn.sigmoid(gate_pre)
    activated = gate_pre * sigmoid_gate
    hidden = (activated * up_pre).astype(jnp.bfloat16)
    expert_out = jnp.einsum(
        "cef,efd->ced",
        lax.all_gather(hidden, "col", axis=0, tiled=True),
        down_weight,
        preferred_element_type=jnp.float32,
    )
    moe_part = combine_slots(expert_out, token_slots, gate_slots, tok_total)
    moe_result = token_sums(moe_part)
    output = (hidden_one + moe_result).astype(jnp.bfloat16)
    grad_result = cotangent.astype(jnp.float32)
    cot_all = token_rows(cotangent)
    grad_slot = (gate_slots[..., None] * cot_all[token_slots].astype(jnp.float32)).astype(
        jnp.bfloat16
    )
    part = grad_slot
    grad_hidden = lax.psum_scatter(
        jnp.einsum("ced,efd->cef", part, down_weight, preferred_element_type=jnp.float32).astype(
            jnp.bfloat16
        ),
        "col",
        scatter_dimension=0,
        tiled=True,
    ).astype(jnp.float32)
    grad_gate_pre = (
        grad_hidden * up_pre * sigmoid_gate * (1.0 + gate_pre * (1.0 - sigmoid_gate))
    ).astype(jnp.bfloat16)
    grad_up_pre = (grad_hidden * activated).astype(jnp.bfloat16)
    grad_inner = jnp.concatenate([grad_gate_pre, grad_up_pre], axis=-1)
    hidden_piece = lax.all_gather(hidden, "col", axis=0, tiled=True)
    inner_piece = lax.all_gather(grad_inner, "col", axis=0, tiled=True)
    acc_down = jnp.einsum(
        "cef,ced->efd", hidden_piece, grad_slot, preferred_element_type=jnp.float32
    )
    acc_inner = jnp.einsum(
        "ecd,cef->edf", slot_inputs, inner_piece, preferred_element_type=jnp.float32
    )
    rows_grad = jnp.einsum(
        "cef,edf->ced", inner_piece, gate_up_weight, preferred_element_type=jnp.float32
    )
    acc_rows = rows_grad
    grad_moe_part = combine_slots(acc_rows, token_slots, live_slots, tok_total)
    grad_moe_in = token_sums(grad_moe_part)
    gain_two = jnp.sum(grad_moe_in * hidden_one * rate_two, axis=0)
    grad_hidden_one = grad_result + norm_back(
        grad_moe_in, hidden_one, rate_two, moe_gain, model_width
    )
    grad_branch = grad_hidden_one.astype(jnp.bfloat16)
    branch_all = token_rows(grad_branch)
    part = branch_all
    grad_heads = lax.psum_scatter(
        jnp.einsum("td,kd->tk", part, out_weight, preferred_element_type=jnp.float32).astype(
            jnp.bfloat16
        ),
        "col",
        scatter_dimension=0,
        tiled=True,
    )
    grad_out_weight = jnp.einsum(
        "tk,td->kd", heads_all, branch_all, preferred_element_type=jnp.float32
    )
    grad_att_items = to_items(head_split(grad_heads))
    grad_query_items, grad_key_items, grad_value_items = lax.map(
        partial(attend_backward, factor),
        (query_items, key_items, value_items, grad_att_items, log_totals, seg_items),
    )
    grad_query_rot = head_split(from_items(grad_query_items, seq_count, seq_len, head_count))
    grad_key_rot = head_split(from_items(grad_key_items, seq_count, seq_len, head_count))
    grad_query_raw, gain_query = head_norm_back(
        grad_query_rot, query_normed, query_rate, query_gain, cosine, sine
    )
    grad_key_raw, gain_key = head_norm_back(
        grad_key_rot, key_normed, key_rate, key_gain, cosine, sine
    )
    grad_value = from_items(grad_value_items, seq_count, seq_len, head_count)
    grad_projected = jnp.stack(
        [
            grad_query_raw.reshape(tok_share, head_width).astype(jnp.bfloat16),
            grad_key_raw.reshape(tok_share, head_width).astype(jnp.bfloat16),
            grad_value,
        ],
        axis=1,
    )
    piece = lax.all_gather(grad_projected, "col", axis=0, tiled=True)
    part_grad = jnp.einsum("tak,adk->td", piece, qkv_weight, preferred_element_type=jnp.float32)
    rows_grad = part_grad
    acc_weight = jnp.einsum("td,tak->adk", normed_all, piece, preferred_element_type=jnp.float32)
    grad_normed = token_sums(rows_grad)
    gain_one = jnp.sum(grad_normed * stream * rate_one, axis=0)
    grad_tokens = (
        grad_hidden_one + norm_back(grad_normed, stream, rate_one, attn_gain, model_width)
    ).astype(jnp.bfloat16)
    offset = col_index * col_width
    full_one = lax.dynamic_update_slice_in_dim(
        jnp.zeros((model_width,), jnp.float32), gain_one, offset, 0
    )
    full_two = lax.dynamic_update_slice_in_dim(
        jnp.zeros((model_width,), jnp.float32), gain_two, offset, 0
    )
    summed_one, summed_two, grad_query_gain, grad_key_gain = lax.psum(
        (full_one, full_two, gain_query, gain_key), ("row", "col")
    )
    grad_attn_gain = lax.dynamic_slice_in_dim(summed_one, offset, col_width, 0)
    grad_moe_gain = lax.dynamic_slice_in_dim(summed_two, offset, col_width, 0)
    return (
        output,
        grad_tokens,
        grad_attn_gain,
        acc_weight,
        grad_query_gain,
        grad_key_gain,
        grad_out_weight,
        grad_moe_gain,
        acc_inner,
        acc_down,
    )


def solution(mesh):
    return jax.shard_map(
        local,
        mesh=mesh,
        in_specs=(
            P("row", "col"),
            P("col"),
            P(None, "col", "row"),
            P(),
            P(),
            P("row", "col"),
            P("col"),
            P("row", "col", None),
            P("row", None, "col"),
            P("col", None),
            P(),
            P(),
            P("row", "col"),
        ),
        out_specs=(
            P("row", "col"),
            P("row", "col"),
            P("col"),
            P(None, "col", "row"),
            P(),
            P(),
            P("row", "col"),
            P("col"),
            P("row", "col", None),
            P("row", None, "col"),
        ),
        check_vma=False,
    )
```

profile of v0, /device:TPU:3, one launch (start us, length us, event | category | flops | bytes accessed | tf_op | source)
XLA Modules:
  0.0 3779.7 jit_solution(5712849504971932263)
XLA Ops:
  18.2 85.7 %all-gather.9.cloned.1.call-done = bf16[8192,512]{1,0:T(8,128)(2,1)} async-done(((bf16[1024,512]{1,0:T(8,128)(2,1)}), bf16[8192,512]{1,0:T(8,128)(2,1)}) %all-gather.9.cloned.1.call-update) | async-done | bytes 8388624 | tf_op jit(solution)/shard_map/all_gather | solution.py:48
  125.6 213.1 %reduce-scatter.9.cloned.1.call-done = f32[2048,3,256]{2,0,1:T(8,128)} async-done(((f32[8192,3,256]{2,0,1:T(8,128)}), f32[2048,3,256]{2,0,1:T(8,128)}) %reduce-scatter.9.cloned.1.call-update) | async-done | bytes 6291472 | tf_op jit(solution)/shard_map/reduce_scatter | solution.py:165
  391.6 24.8 while.26
  420.7 53.0 %all-gather.11.cloned.1.call-done = bf16[8192,256]{1,0:T(8,128)(2,1)} async-done(((bf16[2048,256]{1,0:T(8,128)(2,1)}), bf16[8192,256]{1,0:T(8,128)(2,1)}) %all-gather.11.cloned.1.call-update) | async-done | bytes 4194320 | tf_op jit(solution)/shard_map/all_gather | solution.py:192
  481.7 87.5 %reduce-scatter.11.cloned.1.call-done = bf16[1024,512]{1,0:T(8,128)(2,1)} async-done(((bf16[8192,512]{1,0:T(8,128)(2,1)}), bf16[1024,512]{1,0:T(8,128)(2,1)}) %reduce-scatter.11.cloned.1.call-update) | async-done | bytes 1048592 | tf_op jit(solution)/shard_map/reduce_scatter | solution.py:52
  602.0 239.5 %scatter_custom_fusion.2 = s32[16384]{0:T(1024)S(1)} fusion(s32[65536]{0:T(1024)S(1)} %broadcast_select_fusion, s32[65536]{0:T(1024)S(1)} %add_select_fusion, s32[]{:T(128)} %constant.113.clone.1), kind=kCustom, calls=%fused_computation.204 | custom fusion | bytes 65540
  841.7 71.5 %gather_fusion = bf16[16384,512]{1,0:T(8,128)(2,1)} fusion(bf16[8192,512]{1,0:T(8,128)(2,1)} %all-gather.13.cloned.1.call-done, s32[16384]{0:T(1024)S(1)} %broadcast_clamp_fusion.1), kind=kCustom, calls=%fused_computation | custom fusion | bytes 33619968 | tf_op jit(solution)/shard_map/gather | solution.py:233
  913.2 46.1 %convert_bitcast_fusion = bf16[2048,8,2048]{2,0,1:T(8,128)(2,1)} fusion(bf16[8,2048,512]{2,1,0:T(8,128)(2,1)} %bitcast.203, bf16[8,512,2048]{2,1,0:T(8,128)(2,1)} %param.24), kind=kOutput, calls=%fused_computation.65 | convolution fusion | flops 34393292800 | bytes 100663296 | tf_op jit(solution)/shard_map/ecd,edf->cef/dot_general | solution.py:237
  966.5 239.9 %scatter_custom_fusion.3 = f32[16384]{0:T(1024)S(1)} fusion(s32[65536]{0:T(1024)} %copy-done.36, f32[65536]{0:T(1024)S(1)} %reshape.411, f32[]{:T(128)} %constant.115.clone.1), kind=kCustom, calls=%fused_computation.202 | custom fusion | bytes 66048
  1207.4 71.6 %gather_fusion.1 = bf16[16384,512]{1,0:T(8,128)(2,1)} fusion(bf16[8192,512]{1,0:T(8,128)(2,1)} %all-gather.17.cloned.1.call-done, s32[16384]{0:T(1024)S(1)} %broadcast_clamp_fusion), kind=kCustom, calls=%fused_computation.1 | custom fusion | bytes 33619968 | tf_op jit(solution)/shard_map/gather | solution.py:260
  1279.0 19.2 bitcast_convert_fusion
  1298.2 46.0 %convert_bitcast_fusion.1 = bf16[2048,8,1024]{2,0,1:T(8,128)(2,1)} fusion(bf16[8,1024,512]{2,1,0:T(8,128)(2,1)} %param.25, f32[2048,8,512]{2,1,0:T(8,128)} %bitcast_convert_fusion, f32[2048,8]{0,1:T(8,128)S(1)} %bitcast.212), kind=kOutput, calls=%fused_computation.74 | convolution fusion | flops 17213423616 | bytes 75563008 | tf_op jit(solution)/shard_map/ced,efd->cef/dot_general | solution.py:265
  1344.3 176.0 %reduce-scatter.13.cloned.1.call-done = bf16[512,8,2048]{2,0,1:T(8,128)(2,1)} async-done(((bf16[2048,8,2048]{2,0,1:T(8,128)(2,1)}), bf16[512,8,2048]{2,0,1:T(8,128)(2,1)}) %reduce-scatter.13.cloned.1.call-update) | async-done | bytes 16777232 | tf_op jit(solution)/shard_map/reduce_scatter | solution.py:236
  1520.3 18.8 convert_element_type.159
  1539.1 273.2 %reduce-scatter.17.cloned.1.call-done = bf16[512,8,1024]{2,0,1:T(8,128)(2,1)} async-done(((bf16[2048,8,1024]{2,0,1:T(8,128)(2,1)}), bf16[512,8,1024]{2,0,1:T(8,128)(2,1)}) %reduce-scatter.17.cloned.1.call-update) | async-done | bytes 8388624 | tf_op jit(solution)/shard_map/reduce_scatter | solution.py:264
  1812.4 19.5 fusion.59
  1838.5 240.3 %scatter_custom_fusion.4 = f32[16384]{0:T(1024)S(1)} fusion(s32[65536]{0:T(1024)} %copy-done.36, f32[65536]{0:T(1024)S(1)} %broadcast.310, f32[]{:T(128)} %constant.115.clone.1), kind=kCustom, calls=%fused_computation.200 | custom fusion | bytes 66048
  2080.6 334.9 %all-gather.19.cloned.1.call-done = bf16[2048,8,2048]{2,0,1:T(8,128)(2,1)} async-done(((bf16[512,8,2048]{2,0,1:T(8,128)(2,1)}), bf16[2048,8,2048]{2,0,1:T(8,128)(2,1)}) %all-gather.19.cloned.1.call-update) | async-done | bytes 67108880 | tf_op jit(solution)/shard_map/all_gather | solution.py:278
  2415.5 49.1 %convolution_bitcast_fusion = f32[2048,8,512]{2,0,1:T(8,128)} fusion(bf16[2048,8,2048]{2,0,1:T(8,128)(2,1)} %all-gather.19.cloned.1.call-done, bf16[8,512,2048]{2,1,0:T(8,128)(2,1)} %param.24), kind=kOutput, calls=%fused_computation.77 | convolution fusion | flops 34359738368 | bytes 117440512 | tf_op jit(solution)/shard_map/cef,edf->ced/dot_general | solution.py:285
  2464.6 140.2 %scatter_custom_fusion.1 = f32[8192,512]{1,0:T(8,128)} fusion(s32[16384]{0:T(1024)S(1)} %bitcast.233, f32[2048,8,512]{2,0,1:T(8,128)} %convolution_bitcast_fusion, f32[16384]{0:T(1024)S(1)} %mul.459, f32[]{:T(128)} %constant.115.clone.1), kind=kCustom, calls=%fused_computation.67 | custom fusion | flops 16777216 | bytes 50397188 | tf_op jit(solution)/shard_map/scatter-add | solution.py:126
  2614.0 91.1 %reduce-scatter.19.cloned.1.call-done = bf16[1024,512]{1,0:T(8,128)(2,1)} async-done(((bf16[8192,512]{1,0:T(8,128)(2,1)}), bf16[1024,512]{1,0:T(8,128)(2,1)}) %reduce-scatter.19.cloned.1.call-update) | async-done | bytes 1048592 | tf_op jit(solution)/shard_map/reduce_scatter | solution.py:52
  2717.5 85.1 %all-gather.21.cloned.1.call-done = bf16[8192,512]{1,0:T(8,128)(2,1)} async-done(((bf16[1024,512]{1,0:T(8,128)(2,1)}), bf16[8192,512]{1,0:T(8,128)(2,1)}) %all-gather.21.cloned.1.call-update) | async-done | bytes 8388624 | tf_op jit(solution)/shard_map/all_gather | solution.py:48
  2810.5 50.8 %reduce-scatter.21.cloned.1.call-done = bf16[2048,256]{1,0:T(8,128)(2,1)} async-done(((bf16[8192,256]{1,0:T(8,128)(2,1)}), bf16[2048,256]{1,0:T(8,128)(2,1)}) %reduce-scatter.21.cloned.1.call-update) | async-done | bytes 1048592 | tf_op jit(solution)/shard_map/reduce_scatter | solution.py:298
  2866.0 40.8 %while.27 = (s32[]{:T(128)}, f32[4,1024,128]{2,1,0:T(8,128)}, f32[4,1024,128]{2,1,0:T(8,128)}, bf16[4,1024,128]{2,1,0:T(8,128)(2,1)}, s32[4,1024]{1,0:T(4,128)},...) while((s32[]{:T(128)}, f32[4,1024,128]{2,1,0:T(8,128)}, ...), condition=%wide.region_33.34_spmd, body=%wide.region_31.33_spmd.sunk | while | flops 1353055232 | bytes 38839448 | solution.py:310
  2925.7 22.7 multiply_reduce_fusion.2
  2979.4 122.1 %all-gather.23.cloned.1.call-done = bf16[8192,3,256]{2,0,1:T(8,128)(2,1)} async-done(((bf16[2048,3,256]{2,0,1:T(8,128)(2,1)}), bf16[8192,3,256]{2,0,1:T(8,128)(2,1)}) %all-gather.23.cloned.1.call-update) | async-done | bytes 12582928 | tf_op jit(solution)/shard_map/all_gather | solution.py:331
  3117.9 282.7 %all-gather.15.cloned.1.call-done = bf16[2048,8,1024]{2,0,1:T(8,128)(2,1)} async-done(((bf16[512,8,1024]{2,0,1:T(8,128)(2,1)}), bf16[2048,8,1024]{2,0,1:T(8,128)(2,1)}) %all-gather.15.cloned.1.call-update) | async-done | bytes 33554448 | tf_op jit(solution)/shard_map/all_gather | solution.py:251
  3400.6 33.9 convolution_bitcast_fusion.1
  3434.5 140.2 %scatter_custom_fusion = f32[8192,512]{1,0:T(8,128)} fusion(s32[16384]{0:T(1024)S(1)} %bitcast.234, f32[2048,8,512]{2,0,1:T(8,128)} %convolution_bitcast_fusion.1, f32[16384]{0:T(1024)S(1)} %mul.449, f32[]{:T(128)} %constant.115.clone.1), kind=kCustom, calls=%fused_computation.69 | custom fusion | flops 16777216 | bytes 50397188 | tf_op jit(solution)/shard_map/scatter-add | solution.py:126
  3584.1 58.1 %fusion.70 = f32[8,1024,512]{2,1,0:T(8,128)} fusion(bf16[2048,8,1024]{2,0,1:T(8,128)(2,1)} %all-gather.15.cloned.1.call-done, f32[2048,8,512]{2,1,0:T(8,128)} %bitcast_convert_fusion, f32[2048,8]{0,1:T(8,128)S(1)} %bitcast.214), kind=kOutput, calls=%fused_computation.99 | convolution fusion | flops 17196646400 | bytes 83951616 | tf_op jit(solution)/shard_map/cef,ced->efd/dot_general | solution.py:279
  3642.2 49.8 %fusion.124 = f32[8,512,2048]{2,1,0:T(8,128)} fusion(bf16[8,2048,512]{2,1,0:T(8,128)(2,1)} %bitcast.204, bf16[2048,8,2048]{2,0,1:T(8,128)(2,1)} %all-gather.19.cloned.1.call-done), kind=kOutput, calls=%fused_computation.223 | convolution fusion | flops 34359738368 | bytes 117440512 | tf_op jit(solution)/shard_map/ecd,cef->edf/dot_general | solution.py:282
  3716.6 44.5 %all-reduce.1 = (f32[2048]{0:T(1024)S(1)}, f32[128]{0:T(128)}, f32[128]{0:T(128)}, f32[2048]{0:T(1024)S(1)}) all-reduce(f32[2048]{0:T(1024)S(1)} %dynamic_update_slice.24, f32[128]{0:T(128)S(1)} %copy-done.55, f32[128]{0:T(128)S(1)} %copy-done.56, f32[2048]{0:T(1024)S(1)} %dynamic_update_slice.25), channel_id=1, replica_groups=mesh['row'=8,'col'=4] {'row','col'}, use_global_device_ids=true, to_apply=%region_40.41 | all-reduce | flops 4352 | bytes 34816 | tf_op jit(solution)/shard_map/psum | solution.py:347
  (339 shorter events, 358.4 us)
Async XLA Ops:
  7.2 96.7 %copy-start = (bf16[3,512,256]{2,1,0:T(8,128)(2,1)S(1)}, bf16[3,512,256]{2,1,0:T(8,128)(2,1)}, u32[]{:S(2)}) copy-start(bf16[3,512,256]{2,1,0:T(8,128)(2,1)} %param.19) | copy-start | bytes 2359300
  7.2 96.7 %all-gather.9.cloned.1.call-start = ((), (), s32[]{:S(2)}) async-start(), calls=%async_computation.8 | async-start | bytes 9437184 | tf_op jit(solution)/shard_map/all_gather | solution.py:48
  18.2 320.5 %reduce-scatter.9.cloned.1.call-start = ((), (), s32[]{:S(2)}) async-start(), calls=%async_computation.9 | async-start | bytes 31457280 | tf_op jit(solution)/shard_map/reduce_scatter | solution.py:165
  118.8 354.9 %all-gather.11.cloned.1.call-start = ((), (), s32[]{:S(2)}) async-start(), calls=%async_computation.10 | async-start | bytes 5242880 | tf_op jit(solution)/shard_map/all_gather | solution.py:192
  419.5 54.2 %copy-start.33 = (bf16[256,512]{1,0:T(8,128)(2,1)S(1)}, bf16[256,512]{1,0:T(8,128)(2,1)}, u32[]{:S(2)}) copy-start(bf16[256,512]{1,0:T(8,128)(2,1)} %param.22) | copy-start | bytes 786436
  420.6 148.6 %reduce-scatter.11.cloned.1.call-start = ((), (), s32[]{:S(2)}) async-start(), calls=%async_computation.11 | async-start | bytes 9437184 | tf_op jit(solution)/shard_map/reduce_scatter | solution.py:52
  481.6 87.6 %copy-start.5 = (bf16[1024,512]{1,0:T(8,128)(2,1)S(1)}, bf16[1024,512]{1,0:T(8,128)(2,1)}, u32[]{:S(2)}) copy-start(bf16[1024,512]{1,0:T(8,128)(2,1)} %param.17) | copy-start | bytes 3145732
  481.6 96.0 %copy-start.46 = (f32[512]{0:T(512)S(1)}, f32[512]{0:T(512)}, u32[]{:S(2)}) copy-start(f32[512]{0:T(512)} %param.23) | copy-start | bytes 6148
  481.6 360.0 %all-gather.13.cloned.1.call-start = ((), (), s32[]{:S(2)}) async-start(), calls=%async_computation.12 | async-start | bytes 9437184 | tf_op jit(solution)/shard_map/all_gather | solution.py:48
  579.0 628.4 %all-gather.17.cloned.1.call-start = ((), (), s32[]{:S(2)}) async-start(), calls=%async_computation.16 | async-start | bytes 9437184 | tf_op jit(solution)/shard_map/all_gather | solution.py:48
  579.6 940.8 %reduce-scatter.13.cloned.1.call-start = ((), (), s32[]{:S(2)}) async-start(), calls=%async_computation.13 | async-start | bytes 83886080 | tf_op jit(solution)/shard_map/reduce_scatter | solution.py:236
  841.6 71.6 %copy-start.31 = (s32[8,2048]{1,0:T(8,128)}, s32[8,2048]{1,0:T(8,128)S(1)}, u32[]{:S(2)}) copy-start(s32[8,2048]{1,0:T(8,128)S(1)} %reshape.362) | copy-start | bytes 196612
  959.3 853.1 %reduce-scatter.17.cloned.1.call-start = ((), (), s32[]{:S(2)}) async-start(), calls=%async_computation.17 | async-start | bytes 41943040 | tf_op jit(solution)/shard_map/reduce_scatter | solution.py:264
  962.8 243.6 %copy-start.32 = (s32[8,2048]{1,0:T(8,128)S(1)}, s32[8,2048]{1,0:T(8,128)}, u32[]{:S(2)}) copy-start(s32[8,2048]{1,0:T(8,128)} %copy-done.31) | copy-start | bytes 196612
  1206.5 91.7 %copy-start.26 = (f32[8,2048]{1,0:T(8,128)}, f32[8,2048]{1,0:T(8,128)S(1)}, u32[]{:S(2)}) copy-start(f32[8,2048]{1,0:T(8,128)S(1)} %reshape.366) | copy-start | bytes 196612
  1344.3 1071.2 %all-gather.19.cloned.1.call-start = ((), (), s32[]{:S(2)}) async-start(), calls=%async_computation.18 | async-start | bytes 83886080 | tf_op jit(solution)/shard_map/all_gather | solution.py:278
  1838.4 866.7 %reduce-scatter.19.cloned.1.call-start = ((), (), s32[]{:S(2)}) async-start(), calls=%async_computation.19 | async-start | bytes 9437184 | tf_op jit(solution)/shard_map/reduce_scatter | solution.py:52
  2613.7 91.4 %copy-start.6 = (bf16[1024,512]{1,0:T(8,128)(2,1)S(1)}, bf16[1024,512]{1,0:T(8,128)(2,1)}, u32[]{:S(2)}) copy-start(bf16[1024,512]{1,0:T(8,128)(2,1)} %param.17) | copy-start | bytes 3145732
  2613.7 91.4 %copy-start.9 = (bf16[1024,512]{1,0:T(8,128)(2,1)S(1)}, bf16[1024,512]{1,0:T(8,128)(2,1)}, u32[]{:S(2)}) copy-start(bf16[1024,512]{1,0:T(8,128)(2,1)} %reduce-scatter.11.cloned.1.call-done) | copy-start | bytes 3145732
  2613.7 91.4 %copy-start.39 = (f32[1024]{0:T(1024)S(1)}, f32[1024]{0:T(1024)}, u32[]{:S(2)}) copy-start(f32[1024]{0:T(1024)} %copy-done.38) | copy-start | bytes 12292
  2613.7 91.4 %copy-start.47 = (f32[512]{0:T(512)S(1)}, f32[512]{0:T(512)}, u32[]{:S(2)}) copy-start(f32[512]{0:T(512)} %param.23) | copy-start | bytes 6148
  2613.7 188.9 %all-gather.21.cloned.1.call-start = ((), (), s32[]{:S(2)}) async-start(), calls=%async_computation.20 | async-start | bytes 9437184 | tf_op jit(solution)/shard_map/all_gather | solution.py:48
  2713.9 88.8 %copy-start.34 = (bf16[256,512]{1,0:T(8,128)(2,1)S(1)}, bf16[256,512]{1,0:T(8,128)(2,1)}, u32[]{:S(2)}) copy-start(bf16[256,512]{1,0:T(8,128)(2,1)} %param.22) | copy-start | bytes 786436
  2717.5 143.8 %reduce-scatter.21.cloned.1.call-start = ((), (), s32[]{:S(2)}) async-start(), calls=%async_computation.21 | async-start | bytes 5242880 | tf_op jit(solution)/shard_map/reduce_scatter | solution.py:298
  2810.5 291.1 %all-gather.23.cloned.1.call-start = ((), (), s32[]{:S(2)}) async-start(), calls=%async_computation.22 | async-start | bytes 15728640 | tf_op jit(solution)/shard_map/all_gather | solution.py:331
  2978.8 421.9 %all-gather.15.cloned.1.call-start = ((), (), s32[]{:S(2)}) async-start(), calls=%async_computation.14 | async-start | bytes 41943040 | tf_op jit(solution)/shard_map/all_gather | solution.py:251
  2979.3 734.7 %reduce-scatter.23.cloned.1.call-start = ((), (), s32[]{:S(2)}) async-start(), calls=%async_computation.23 | async-start | bytes 9437184 | tf_op jit(solution)/shard_map/reduce_scatter | solution.py:52
  3116.3 652.1 %reduce-scatter.15.cloned.1.call-start = ((), (), s32[]{:S(2)}) async-start(), calls=%async_computation.15 | async-start | bytes 9437184 | tf_op jit(solution)/shard_map/reduce_scatter | solution.py:52
  3710.9 57.5 %copy-start.10 = (bf16[1024,512]{1,0:T(8,128)(2,1)S(1)}, bf16[1024,512]{1,0:T(8,128)(2,1)}, u32[]{:S(2)}) copy-start(bf16[1024,512]{1,0:T(8,128)(2,1)} %reduce-scatter.11.cloned.1.call-done) | copy-start | bytes 3145732
  3710.9 57.5 %copy-start.40 = (f32[1024]{0:T(1024)S(1)}, f32[1024]{0:T(1024)}, u32[]{:S(2)}) copy-start(f32[1024]{0:T(1024)} %copy-done.38) | copy-start | bytes 12292
  3710.9 57.5 %copy-start.45 = (f32[1024]{0:T(1024)S(1)}, f32[1024]{0:T(1024)}, u32[]{:S(2)}) copy-start(f32[1024]{0:T(1024)} %copy-done.44) | copy-start | bytes 12292
  3710.9 57.5 %copy-start.48 = (f32[512]{0:T(512)S(1)}, f32[512]{0:T(512)}, u32[]{:S(2)}) copy-start(f32[512]{0:T(512)} %param.23) | copy-start | bytes 6148
  (48 other events, 258.8 us)
Sparse Core Ops, SparseCore 0:
  18.3 85.5 all-gather.8
  118.9 219.7 reduce-scatter.8
  420.8 52.8 all-gather.10
  481.7 87.4 reduce-scatter.10
  579.1 85.0 all-gather.12
  665.7 80.5 all-gather.16
  959.4 560.8 reduce-scatter.12
  1523.7 288.6 reduce-scatter.16
  1838.5 576.9 all-gather.18
  2613.9 91.1 reduce-scatter.18
  2717.6 85.0 all-gather.20
  2810.6 50.6 reduce-scatter.20
  2978.9 122.5 all-gather.22
  3103.4 297.2 all-gather.14
  3402.9 87.4 reduce-scatter.22
  3584.2 91.2 reduce-scatter.14
where the time goes:
time: 3790 us; the launch traced here: 3780 us
  waiting for transfers between devices  1860 us (49%)
  local copies, waits for them, and re-layouts  949 us (25%)
  other arithmetic  500 us (13%)
  matrix products  389 us (10%)
  blocking collectives  68.7 us (2%)
    unnamed x129, local copies, waits for them, and re-layouts  738 us
    all_gather x1, waiting for transfers between devices, local(): inner_piece = lax.all_gather(grad_inner, 'col', axis=0, tiled=True)  335 us
    all_gather x1, waiting for transfers between devices, local(): lax.all_gather(hidden, 'col', axis=0, tiled=True)  283 us
    scatter-add x2, other arithmetic, combine_slots(): return total.at[token_slots.reshape(-1)].add(flat_values)  280 us
    reduce_scatter x1, waiting for transfers between devices, local(): lax.psum_scatter(jnp.einsum('ced,efd->cef', part, down_weight, preferred_...  273 us
    reduce_scatter x1, waiting for transfers between devices, local(): lax.psum_scatter(jnp.einsum('td,adk->tak', normed_all, qkv_weight, prefer...  213 us
    reduce_scatter x4, waiting for transfers between devices, token_sums(): lax.psum_scatter(values.astype(jnp.bfloat16), 'row', scatter_dimension=0,...  179 us
    reduce_scatter x1, waiting for transfers between devices, local(): lax.psum_scatter(jnp.einsum('ecd,edf->cef', part, gate_up_weight, preferr...  176 us
  transfers between devices with their start and end apart: 16, of which 12 were waited for; matrix products, arithmetic and copies ran while one was open for 36% of the time, Pallas kernels for 0%

commit v1 on v0

v1 whole, which is shorter than its diff:
```python
from functools import partial

import jax
import jax.numpy as jnp
from jax import lax
from jax.experimental import pallas as pl
from jax.experimental.pallas import tpu as pltpu
from jax.sharding import Mesh, PartitionSpec as P

DOCS = 4
epsilon = 1e-06
rope_base = 10000.0
neg_large = -1e30

ROW = ("chip", "core")
ALL = ("chip", "core", "col")
TILE = 256
BLOCK = 512
VMEM_BYTES = 58 * 1024 * 1024
F32 = jnp.float32
BF16 = jnp.bfloat16


def rotate(values, cosine, sine):
    half_size = values.shape[-1] // 2
    turned = jnp.concatenate([-values[..., half_size:], values[..., :half_size]], axis=-1)
    return values * cosine + turned * sine


def rotate_back(grads, cosine, sine):
    half_size = grads.shape[-1] // 2
    moved = grads * sine
    turned = jnp.concatenate([moved[..., half_size:], -moved[..., :half_size]], axis=-1)
    return grads * cosine + turned


def rope_tables(seg_row, head_size):
    docs = jnp.arange(DOCS, dtype=jnp.int32)
    starts = jnp.sum((seg_row[:, None] < docs[None, :]).astype(jnp.int32), axis=0)
    first_index = jnp.sum(
        jnp.where(seg_row[:, None] == docs[None, :], starts[None, :], 0), axis=-1
    )
    places = (jnp.arange(seg_row.shape[0], dtype=jnp.int32) - first_index).astype(F32)
    rates = rope_base ** (-jnp.arange(0, head_size, 2, dtype=F32) / head_size)
    angles = places[..., None] * rates
    angles = jnp.concatenate([angles, angles], axis=-1)
    return (jnp.cos(angles), jnp.sin(angles))


def width_total(values):
    return lax.psum(values, "col")


def norm_back(grad_normed, stream, rate, gain, model_width):
    scaled_grad = grad_normed * gain
    across = width_total(jnp.sum(scaled_grad * stream, axis=-1))[:, None]
    return rate * scaled_grad - stream * rate * rate * rate * across / model_width


def head_norm_back(grad_rot, normed, rate, gain, cosine, sine):
    grad_normed = rotate_back(grad_rot, cosine, sine)
    gain_grad = jnp.sum(grad_normed * normed, axis=(0, 1))
    scaled_grad = grad_normed * gain
    grad_raw = rate * (
        scaled_grad - normed * jnp.mean(scaled_grad * normed, axis=-1, keepdims=True)
    )
    return (grad_raw, gain_grad)


def attend_forward(factor, seg_row, packed):
    query, key, value = packed
    same = seg_row[:, None] == seg_row[None, :]
    scores = jnp.einsum("qd,kd->qk", query, key, preferred_element_type=F32) * factor
    scores = jnp.where(same, scores, neg_large)
    top_score = jnp.max(scores, axis=-1, keepdims=True)
    totals = jnp.sum(jnp.exp(scores - top_score), axis=-1, keepdims=True)
    log_total = top_score + jnp.log(totals)
    probs = jnp.exp(scores - log_total)
    result = jnp.einsum("qk,kd->qd", probs.astype(BF16), value, preferred_element_type=F32)
    return (result.astype(BF16), log_total[:, 0])


def attend_backward(factor, seg_row, packed):
    query, key, value, grad_out, log_total = packed
    same = seg_row[:, None] == seg_row[None, :]
    scores = jnp.einsum("qd,kd->qk", query, key, preferred_element_type=F32) * factor
    scores = jnp.where(same, scores, neg_large)
    probs = jnp.exp(scores - log_total[:, None])
    grad_probs = jnp.einsum("qd,kd->qk", grad_out, value, preferred_element_type=F32)
    center = jnp.sum(probs * grad_probs, axis=-1, keepdims=True)
    grad_scores = (probs * (grad_probs - center)).astype(BF16)
    grad_query = jnp.einsum("qk,kd->qd", grad_scores, key, preferred_element_type=F32) * factor
    grad_key = jnp.einsum("qk,qd->kd", grad_scores, query, preferred_element_type=F32) * factor
    grad_value = jnp.einsum("qk,qd->kd", probs.astype(BF16), grad_out, preferred_element_type=F32)
    return (grad_query, grad_key, grad_value.astype(BF16))


def slot_places(routes, route_gates, expert_ids):
    chosen = routes[None] == expert_ids[:, None, None]
    hit = jnp.any(chosen, axis=-1)
    gate = jnp.sum(jnp.where(chosen, route_gates[None], 0.0), axis=-1)
    count, tok_total = hit.shape
    grouped = hit.astype(BF16).reshape(count, tok_total // 128, 128)
    lane = jnp.arange(128)
    before = (lane[:, None] < lane[None, :]).astype(BF16)
    inside = jnp.einsum("egt,tu->egu", grouped, before, preferred_element_type=F32)
    totals = jnp.sum(grouped.astype(F32), axis=-1).astype(BF16)
    group = jnp.arange(tok_total // 128)
    earlier = (group[:, None] < group[None, :]).astype(BF16)
    offset = jnp.einsum("eg,gh->eh", totals, earlier, preferred_element_type=F32)
    place = (inside + offset[..., None]).reshape(count, tok_total).astype(jnp.int32)
    per_block = jnp.sum(hit.astype(jnp.int32).reshape(count, tok_total // BLOCK, BLOCK), axis=-1)
    begin = place.reshape(count, tok_total // BLOCK, BLOCK)[:, :, 0]
    end = begin + per_block
    low = begin // TILE
    high = jnp.where(end > begin, (end + TILE - 1) // TILE, low)
    return (jnp.where(hit, place, -1), gate, low, high)


def gather_kernel(scaled, low_ref, high_ref, rows_ref, place_ref, gate_ref, slots_ref):
    step = pl.program_id(0)
    experts = slots_ref.shape[0]
    parts, width = rows_ref.shape[1], rows_ref.shape[3]

    @pl.when(step == 0)
    def _():
        slots_ref[...] = jnp.zeros_like(slots_ref)

    for e in range(experts):
        place = place_ref[e, 0]
        gate = gate_ref[e, 0]

        def body(i, carry):
            base = pl.multiple_of(i * TILE, TILE)
            wanted = lax.broadcasted_iota(jnp.int32, (TILE, BLOCK), 0) + base
            mask = place == wanted
            onehot = mask.astype(F32).astype(BF16)
            if scaled:
                factor = jnp.sum(jnp.where(mask, gate, 0.0), axis=1, keepdims=True)
            for c in range(parts):
                picked = jnp.dot(onehot, rows_ref[0, c], preferred_element_type=F32)
                if scaled:
                    picked = picked * factor
                where = (e, pl.ds(base, TILE), slice(c * width, (c + 1) * width))
                slots_ref[where] = slots_ref[where] + picked.astype(BF16)
            return carry

        lax.fori_loop(low_ref[e, step], high_ref[e, step], body, 0)


def gather_slots(rows, place, gate, low, high, capacity, scaled):
    row_count, parts, per_row, width = rows.shape
    experts = place.shape[0]
    blocks = row_count * per_row // BLOCK
    each = per_row // BLOCK
    return pl.pallas_call(
        partial(gather_kernel, scaled),
        grid_spec=pltpu.PrefetchScalarGridSpec(
            num_scalar_prefetch=2,
            grid=(blocks,),
            in_specs=[
                pl.BlockSpec((1, parts, BLOCK, width), lambda b, *_: (b // each, 0, b % each, 0)),
                pl.BlockSpec((experts, 1, 1, BLOCK), lambda b, *_: (0, b, 0, 0)),
                pl.BlockSpec((experts, 1, 1, BLOCK), lambda b, *_: (0, b, 0, 0)),
            ],
            out_specs=pl.BlockSpec((experts, capacity, parts * width), lambda b, *_: (0, 0, 0)),
        ),
        out_shape=jax.ShapeDtypeStruct((experts, capacity, parts * width), BF16),
        compiler_params=pltpu.CompilerParams(vmem_limit_bytes=VMEM_BYTES),
        cost_estimate=pl.CostEstimate(
            flops=2 * 24 * experts * TILE * BLOCK * parts * width,
            bytes_accessed=rows.size * 2 + experts * capacity * parts * width * 2,
            transcendentals=0,
        ),
        name="gather_slots",
    )(
        low,
        high,
        rows,
        place.reshape(experts, blocks, 1, BLOCK),
        gate.reshape(experts, blocks, 1, BLOCK),
    )


def combine_kernel(scaled, each, low_ref, high_ref, core_ref, slots_ref, place_ref, gate_ref, out_ref, total_ref):
    chip, piece = pl.program_id(0), pl.program_id(1)
    block = (2 * chip + core_ref[0]) * each + piece
    experts = slots_ref.shape[0]
    parts, width = out_ref.shape[0], out_ref.shape[3]
    total_ref[...] = jnp.zeros_like(total_ref)
    for e in range(experts):
        place = jnp.broadcast_to(place_ref[e, 0].astype(F32), (8, BLOCK)).T[:, :1]
        if scaled:
            gate = jnp.broadcast_to(gate_ref[e, 0], (8, BLOCK)).T[:, :1]

        def body(i, carry):
            base = pl.multiple_of(i * TILE, TILE)
            wanted = lax.broadcasted_iota(jnp.int32, (BLOCK, TILE), 1) + base
            onehot = (place == wanted.astype(F32)).astype(F32).astype(BF16)
            for c in range(parts):
                columns = slice(c * width, (c + 1) * width)
                picked = jnp.dot(
                    onehot, slots_ref[e, pl.ds(base, TILE), columns], preferred_element_type=F32
                )
                if scaled:
                    picked = picked * gate
                total_ref[:, columns] = total_ref[:, columns] + picked
            return carry

        lax.fori_loop(low_ref[e, block], high_ref[e, block], body, 0)
    for c in range(parts):
        out_ref[c, 0] = total_ref[:, c * width : (c + 1) * width].astype(BF16)


def combine_slots(slots, place, gate, low, high, core, chips, per_row, parts, scaled):
    experts, capacity, model_width = slots.shape
    width = model_width // parts
    each = per_row // BLOCK
    blocks = place.shape[1] // BLOCK

    def token_block(z, j, low_ref, high_ref, core_ref):
        return (0, (2 * z + core_ref[0]) * each + j, 0, 0)

    return pl.pallas_call(
        partial(combine_kernel, scaled, each),
        grid_spec=pltpu.PrefetchScalarGridSpec(
            num_scalar_prefetch=3,
            grid=(chips, each),
            in_specs=[
                pl.BlockSpec(
                    (experts, capacity, model_width),
                    lambda *_: (0, 0, 0),
                    pipeline_mode=pl.Buffered(1),
                ),
                pl.BlockSpec((experts, 1, 1, BLOCK), token_block),
                pl.BlockSpec((experts, 1, 1, BLOCK), token_block),
            ],
            out_specs=pl.BlockSpec((parts, 1, BLOCK, width), lambda z, j, *_: (0, z, j, 0)),
            scratch_shapes=[pltpu.VMEM((BLOCK, model_width), F32)],
        ),
        out_shape=jax.ShapeDtypeStruct((parts, chips, per_row, width), BF16),
        compiler_params=pltpu.CompilerParams(vmem_limit_bytes=VMEM_BYTES),
        cost_estimate=pl.CostEstimate(
            flops=24 * experts * TILE * BLOCK * model_width,
            bytes_accessed=slots.size * 2 + parts * chips * per_row * width * 2,
            transcendentals=0,
        ),
        name="combine_slots",
    )(
        low,
        high,
        core,
        slots,
        place.reshape(experts, blocks, 1, BLOCK),
        gate.reshape(experts, blocks, 1, BLOCK),
    )


def swap_cores(values):
    return lax.ppermute(values, "core", [(0, 1), (1, 0)])


def swap_cols(values, mask):
    count = lax.axis_size("col")
    return lax.ppermute(values, "col", [(i, i ^ mask) for i in range(count)])


def spread_parts(parts, axis_out):
    count = lax.axis_size("col")
    me = lax.axis_index("col")
    size = parts.shape[1:][axis_out]
    shape = list(parts.shape[1:])
    shape[axis_out] = size * count
    result = jnp.zeros(shape, parts.dtype)
    for mask in range(count):
        there = me ^ mask
        piece = lax.dynamic_index_in_dim(parts, there, 0, keepdims=False)
        if mask:
            piece = swap_cols(piece, mask)
        result = lax.dynamic_update_slice_in_dim(result, piece, there * size, axis_out)
    return result


def sum_over_devices(other, mine):
    total = mine + swap_cores(other)
    total = lax.psum_scatter(total, "col", scatter_dimension=0, tiled=True)[0]
    return lax.psum_scatter(total, "chip", scatter_dimension=0, tiled=True)[0].astype(F32)


def heads_in(weight, ratio):
    chips, cols = lax.axis_size("chip"), lax.axis_size("col")
    rows = 2 * chips
    row = 2 * lax.axis_index("chip") + lax.axis_index("core")
    kinds, features, width = weight.shape
    block = features // ratio
    halves = weight.reshape(kinds, ratio, block, width).transpose(1, 2, 0, 3)
    joined = jnp.zeros((block, kinds, ratio, width), weight.dtype)
    for k in range(ratio):
        pairs = []
        for r in range(rows):
            for c in range(cols):
                h = (k + r) % ratio
                pairs.append((r * cols + c, (ratio * c + h) * cols + r // ratio))
        piece = lax.dynamic_index_in_dim(halves, (k + row) % ratio, 0, keepdims=False)
        piece = lax.ppermute(piece, ALL, pairs)
        place = (row % ratio - k) % ratio
        joined = lax.dynamic_update_slice_in_dim(joined, piece[:, :, None], place, 2)
    joined = joined.reshape(block, kinds * ratio * width)
    return lax.all_gather(joined, ROW, axis=0, tiled=True)


def heads_out(grad, kinds, ratio):
    chips, cols = lax.axis_size("chip"), lax.axis_size("col")
    rows = 2 * chips
    row = 2 * lax.axis_index("chip") + lax.axis_index("core")
    block = grad.shape[0] // rows
    mine = lax.psum_scatter(grad, ROW, scatter_dimension=0, tiled=True)
    width = grad.shape[1] // (kinds * ratio)
    mine = mine.reshape(block, kinds, ratio, width)
    result = jnp.zeros((kinds, ratio, block, width), grad.dtype)
    for k in range(ratio):
        pairs = []
        for r in range(rows):
            for c in range(cols):
                s = (r % ratio - k) % ratio
                pairs.append((r * cols + c, (ratio * c + s) * cols + r // ratio))
        piece = lax.dynamic_index_in_dim(mine, (row % ratio - k) % ratio, 2, keepdims=False)
        piece = lax.ppermute(piece, ALL, pairs).transpose(1, 0, 2)
        result = lax.dynamic_update_slice_in_dim(result, piece[:, None], (k + row) % ratio, 1)
    return result.reshape(kinds, ratio * block, width).astype(F32)


def local(
    tokens,
    attn_gain,
    qkv_weight,
    query_gain,
    key_gain,
    out_weight,
    moe_gain,
    gate_up_weight,
    down_weight,
    segments,
    routes,
    route_gates,
    cotangent,
):
    cols = lax.axis_size("col")
    chips = lax.axis_size("chip")
    rows = 2 * chips
    col = lax.axis_index("col")
    core = lax.axis_index("core")
    row = 2 * lax.axis_index("chip") + core
    per_row, col_width = tokens.shape
    model_width = col_width * cols
    head_size = query_gain.shape[0]
    ratio = rows // cols
    head_width = model_width // cols
    head_count = head_width // head_size
    factor = head_size ** (-0.5)

    experts_here, _, double_units = gate_up_weight.shape
    units = double_units // 2
    split = max(1, cols // experts_here)
    mine_count = experts_here * split // cols
    part_units = units // split
    capacity = 2 * rows * per_row * routes.shape[1] // (experts_here * rows)

    gate_up_parts = (
        gate_up_weight.reshape(experts_here, col_width, 2, split, part_units)
        .transpose(0, 3, 1, 2, 4)
        .reshape(cols, mine_count, col_width, 2 * part_units)
    )
    down_parts = down_weight.reshape(cols, mine_count, part_units, col_width)

    tokens_all = lax.all_gather(tokens, "col", axis=0)
    qkv_all = heads_in(qkv_weight, ratio)
    out_all = lax.all_gather(out_weight, ROW, axis=0, tiled=True)
    segs = lax.all_gather(segments, "col", axis=0, tiled=True)
    seg_row = lax.dynamic_index_in_dim(segs, row, 0, keepdims=False)
    gain_all = lax.all_gather(attn_gain, "col", axis=0)
    gate_up = spread_parts(gate_up_parts, 1)
    down = spread_parts(down_parts, 2)
    cot_all = lax.all_gather(cotangent, ALL, axis=0).reshape(rows, cols, per_row, col_width)

    cosine, sine = rope_tables(seg_row, head_size)
    cosine = cosine[:, None, :]
    sine = sine[:, None, :]
    stream_all = tokens_all.astype(F32)
    rate_one = lax.rsqrt(jnp.sum(stream_all * stream_all, axis=(0, 2)) / model_width + epsilon)
    normed_all = (stream_all * rate_one[None, :, None] * gain_all[:, None, :]).astype(BF16)
    normed_all = normed_all.transpose(1, 0, 2).reshape(per_row, model_width)
    rate_one = rate_one[:, None]
    qkv = jnp.dot(normed_all, qkv_all, preferred_element_type=F32)
    qkv = qkv.reshape(per_row, 3, head_count, head_size)
    query_raw, key_raw, value_raw = qkv[:, 0], qkv[:, 1], qkv[:, 2]
    query_rate = lax.rsqrt(jnp.mean(query_raw * query_raw, axis=-1, keepdims=True) + epsilon)
    key_rate = lax.rsqrt(jnp.mean(key_raw * key_raw, axis=-1, keepdims=True) + epsilon)
    query_normed = query_raw * query_rate
    key_normed = key_raw * key_rate
    query_items = rotate(query_normed * query_gain, cosine, sine).astype(BF16).transpose(1, 0, 2)
    key_items = rotate(key_normed * key_gain, cosine, sine).astype(BF16).transpose(1, 0, 2)
    value_items = value_raw.astype(BF16).transpose(1, 0, 2)
    attended, log_totals = lax.map(
        partial(attend_forward, factor, seg_row), (query_items, key_items, value_items)
    )
    heads_low = attended.transpose(1, 0, 2).reshape(per_row, head_width)
    heads_all = lax.all_gather(heads_low, "col", axis=0)
    out_split = out_all.reshape(cols, head_width, col_width)
    stream = tokens.astype(F32)
    hidden_one = stream + jnp.einsum("ctk,ckd->td", heads_all, out_split, preferred_element_type=F32)
    rate_two = lax.rsqrt(
        width_total(jnp.sum(hidden_one * hidden_one, axis=-1)) / model_width + epsilon
    )[:, None]
    moe_in = (hidden_one * rate_two * moe_gain).astype(BF16)

    moe_all = lax.all_gather(moe_in, ALL, axis=0).reshape(rows, cols, per_row, col_width)
    first = lax.axis_index("chip") * 2 * experts_here + core * experts_here
    expert_ids = first + (col * mine_count + jnp.arange(mine_count, dtype=jnp.int32)) // split
    place, gate, low, high = slot_places(routes, route_gates, expert_ids)
    grad_slot = gather_slots(cot_all, place, gate, low, high, capacity, True)
    slot_inputs = gather_slots(moe_all, place, gate, low, high, capacity, False)

    gate_weight = gate_up[..., :part_units]
    up_weight = gate_up[..., part_units:]
    gate_pre = jnp.einsum(
        "ecd,edf->ecf", slot_inputs, gate_weight, preferred_element_type=F32
    ).astype(BF16)
    up_pre = jnp.einsum(
        "ecd,edf->ecf", slot_inputs, up_weight, preferred_element_type=F32
    ).astype(BF16)
    grad_hidden = jnp.einsum("ecd,efd->ecf", grad_slot, down, preferred_element_type=F32)
    gate_wide = gate_pre.astype(F32)
    up_wide = up_pre.astype(F32)
    sigmoid_gate = jax.nn.sigmoid(gate_wide)
    activated = gate_wide * sigmoid_gate
    hidden = (activated * up_wide).astype(BF16)
    grad_gate_pre = (
        grad_hidden * up_wide * sigmoid_gate * (1.0 + gate_wide * (1.0 - sigmoid_gate))
    ).astype(BF16)
    grad_up_pre = (grad_hidden * activated).astype(BF16)
    grad_inner = jnp.concatenate([grad_gate_pre, grad_up_pre], axis=-1)
    grad_slot_in = jnp.einsum(
        "ecf,edf->ecd", grad_inner, gate_up, preferred_element_type=F32
    ).astype(BF16)
    mine = jnp.reshape(core, (1,))
    others = 1 - mine

    def give_back(slots, scaled):
        gather = partial(
            combine_slots, slots, place, gate, low, high,
            chips=chips, per_row=per_row, parts=cols, scaled=scaled,
        )
        return sum_over_devices(gather(core=others), gather(core=mine))

    grad_moe_in = give_back(grad_slot_in, False)
    expert_out = jnp.einsum("ecf,efd->ecd", hidden, down, preferred_element_type=F32).astype(BF16)
    moe_result = give_back(expert_out, True)
    output = (hidden_one + moe_result).astype(BF16)
    grad_down_parts = jnp.einsum(
        "ecf,ecd->efd", hidden, grad_slot, preferred_element_type=F32
    ).astype(BF16)
    grad_gate_up_parts = jnp.einsum(
        "ecd,ecf->edf", slot_inputs, grad_inner, preferred_element_type=F32
    ).astype(BF16)

    def collect(parts):
        result = spread_parts(parts[:, None], 0)
        return result

    grad_gate_up = collect(
        grad_gate_up_parts.reshape(mine_count, cols, col_width, 2 * part_units).transpose(1, 0, 2, 3)
    )
    grad_gate_up = (
        grad_gate_up.reshape(experts_here, split, col_width, 2, part_units)
        .transpose(0, 2, 3, 1, 4)
        .reshape(experts_here, col_width, double_units)
        .astype(F32)
    )
    grad_down = collect(
        grad_down_parts.reshape(mine_count, part_units, cols, col_width).transpose(2, 0, 1, 3)
    )
    grad_down = grad_down.reshape(experts_here, units, col_width).astype(F32)

    gain_two = jnp.sum(grad_moe_in * hidden_one * rate_two, axis=0)
    grad_hidden_one = cotangent.astype(F32) + norm_back(
        grad_moe_in, hidden_one, rate_two, moe_gain, model_width
    )
    grad_branch = grad_hidden_one.astype(BF16)
    grad_heads = lax.psum_scatter(
        jnp.einsum("td,ckd->ctk", grad_branch, out_split, preferred_element_type=F32).astype(BF16),
        "col",
        scatter_dimension=0,
        tiled=True,
    )[0]
    grad_out_weight = lax.psum_scatter(
        jnp.einsum("ctk,td->ckd", heads_all, grad_branch, preferred_element_type=F32)
        .astype(BF16)
        .reshape(model_width, col_width),
        ROW,
        scatter_dimension=0,
        tiled=True,
    ).astype(F32)
    grad_att_items = grad_heads.reshape(per_row, head_count, head_size).transpose(1, 0, 2)
    grad_query_items, grad_key_items, grad_value_items = lax.map(
        partial(attend_backward, factor, seg_row),
        (query_items, key_items, value_items, grad_att_items, log_totals),
    )
    grad_query_raw, gain_query = head_norm_back(
        grad_query_items.transpose(1, 0, 2), query_normed, query_rate, query_gain, cosine, sine
    )
    grad_key_raw, gain_key = head_norm_back(
        grad_key_items.transpose(1, 0, 2), key_normed, key_rate, key_gain, cosine, sine
    )
    grad_projected = jnp.concatenate(
        [
            grad_query_raw.astype(BF16),
            grad_key_raw.astype(BF16),
            grad_value_items.transpose(1, 0, 2),
        ],
        axis=1,
    ).reshape(per_row, 3 * head_width)
    grad_normed = lax.psum_scatter(
        jnp.einsum(
            "tk,cfk->ctf",
            grad_projected,
            qkv_all.reshape(cols, col_width, 3 * head_width),
            preferred_element_type=F32,
        ).astype(BF16),
        "col",
        scatter_dimension=0,
        tiled=True,
    )[0].astype(F32)
    grad_qkv = heads_out(
        jnp.einsum("td,tk->dk", normed_all, grad_projected, preferred_element_type=F32).astype(BF16),
        3,
        ratio,
    )
    gain_one = jnp.sum(grad_normed * stream * rate_one, axis=0)
    grad_tokens = (
        grad_hidden_one + norm_back(grad_normed, stream, rate_one, attn_gain, model_width)
    ).astype(BF16)
    grad_attn_gain, grad_moe_gain = lax.psum((gain_one, gain_two), ROW)
    grad_query_gain, grad_key_gain = lax.psum((gain_query, gain_key), ALL)
    return (
        output,
        grad_tokens,
        grad_attn_gain,
        grad_qkv,
        grad_query_gain,
        grad_key_gain,
        grad_out_weight,
        grad_moe_gain,
        grad_gate_up,
        grad_down,
    )


def solution(mesh):
    rows, cols = mesh.devices.shape
    fine = Mesh(mesh.devices.reshape(rows // 2, 2, cols), ("chip", "core", "col"))
    return jax.shard_map(
        local,
        mesh=fine,
        in_specs=(
            P(ROW, "col"),
            P("col"),
            P(None, "col", ROW),
            P(),
            P(),
            P(ROW, "col"),
            P("col"),
            P(ROW, "col", None),
            P(ROW, None, "col"),
            P("col", None),
            P(),
            P(),
            P(ROW, "col"),
        ),
        out_specs=(
            P(ROW, "col"),
            P(ROW, "col"),
            P("col"),
            P(None, "col", ROW),
            P(),
            P(),
            P(ROW, "col"),
            P("col"),
            P(ROW, "col", None),
            P(ROW, None, "col"),
        ),
        check_vma=False,
    )
```

time: 3790 us -> 2400 us (0.63)
  local copies, waits for them, and re-layouts: 949 us -> 313 us
  waiting for transfers between devices: 1860 us -> 1290 us
  other arithmetic: 500 us -> 115 us
  Pallas kernels: 0 us -> 184 us
  matrix products: 389 us -> 330 us
    reduce_scatter x8 -> x4, waiting for transfers between devices: 892 us -> 142 us  [the longest x2 142 us: sum_over_devices(): lax.psum_scatter(total, 'chip', scatter_dimension=0, tiled=True)[0]]
    unnamed x129 -> x126, local copies, waits for them, and re-layouts: 738 us -> 43.6 us
    all_gather x8 -> x6, waiting for transfers between devices: 964 us -> 283 us  [the longest x1 163 us: local(): lax.all_gather(moe_in, ALL, axis=0).reshape(rows, cols, per_row, col_width)]
    ppermute x0 -> x18, waiting for transfers between devices: none -> 615 us  [the longest x12 555 us: swap_cols(): return lax.ppermute(values, 'col', [(i, i ^ mask) for i in range(count)])]
    scatter-add x2 -> x0, other arithmetic: 280 us -> none  [combine_slots(): return total.at[token_slots.reshape(-1)].add(flat_values)]
    unnamed x16 -> x18, waiting for transfers between devices: 1.28 us -> 245 us
    pallas_call x0 -> x6, Pallas kernels: none -> 184 us  [the longest x4 111 us: combine_slots(): pl.pallas_call(partial(combine_kernel, scaled, each), grid_spec=pltpu.Pre...]
    gather x2 -> x0, local copies, waits for them, and re-layouts: 143 us -> none  [the longest x1 71.6 us: local(): cot_all[token_slots].astype(jnp.float32)]
  transfers between devices with their start and end apart: 16 -> 32, of which waited for: 12 -> 17; matrix products, arithmetic and copies ran while one was open for 36% -> 23% of each run, Pallas kernels for 0% -> 5%
where the time goes in v1:
time: 2400 us; the launch traced here: 2380 us
  waiting for transfers between devices  1290 us (54%)
  matrix products  330 us (14%)
  local copies, waits for them, and re-layouts  313 us (13%)
  Pallas kernels  184 us (8%)
  other arithmetic  115 us (5%)
  blocking collectives  106 us (4%)
  starting transfers between devices  26.3 us (1%)
    ppermute x12, waiting for transfers between devices, swap_cols(): return lax.ppermute(values, 'col', [(i, i ^ mask) for i in range(count)])  555 us
    unnamed x18, waiting for transfers between devices  245 us
    all_gather x1, waiting for transfers between devices, local(): lax.all_gather(moe_in, ALL, axis=0).reshape(rows, cols, per_row, col_width)  163 us
    reduce_scatter x2, waiting for transfers between devices, sum_over_devices(): lax.psum_scatter(total, 'chip', scatter_dimension=0, tiled=True)[0]  142 us
    pallas_call x4, Pallas kernels, combine_slots(): pl.pallas_call(partial(combine_kernel, scaled, each), grid_spec=pltpu.Pre...  111 us
    pallas_call x2, Pallas kernels, gather_slots(): pl.pallas_call(partial(gather_kernel, scaled), grid_spec=pltpu.PrefetchSc...  73.5 us
    dynamic_update_slice x16, local copies, waits for them, and re-layouts, spread_parts(): lax.dynamic_update_slice_in_dim(result, piece, there * size, axis_out)  51.2 us
    ppermute x2, waiting for transfers between devices, heads_in(): piece = lax.ppermute(piece, ALL, pairs)  50.5 us
  transfers between devices with their start and end apart: 32, of which 17 were waited for; matrix products, arithmetic and copies ran while one was open for 23% of the time, Pallas kernels for 5%

profile of v1, /device:TPU:3, one launch (start us, length us, event | category | flops | bytes accessed | tf_op | source)
XLA Modules:
  0.0 2375.9 jit_solution(10495004155555171757)
XLA Ops:
  14.4 41.5 %collective-permute-done = bf16[256,3,256]{2,0,1:T(8,128)(2,1)S(1)} collective-permute-done((bf16[256,3,256]{2,0,1:T(8,128)(2,1)S(1)}, bf16[256,3,256]{2,0,1:T(8,128)(2,1)S(1)}, u32[]{:S(2)}, u32[]{:S(2)}) %collective-permute-start) | collective-permute-done | bytes 393248 | tf_op jit(solution)/shard_map/ppermute | solution.py:305
  109.7 48.5 %all-gather.13.cloned.1.call-done = bf16[2048,1536]{0,1:T(8,128)(2,1)} async-done(((bf16[256,1536]{0,1:T(8,128)(2,1)}), bf16[2048,1536]{0,1:T(8,128)(2,1)}) %all-gather.13.cloned.1.call-update) | async-done | bytes 6291472 | tf_op jit(solution)/shard_map/all_gather | solution.py:309
  178.8 28.8 %while.26 = (s32[]{:T(128)}, bf16[4,1024,128]{2,1,0:T(8,128)(2,1)}, f32[4,1024]{1,0:T(4,128)}, s32[1024]{0:T(1024)S(1)}, bf16[4,1024,128]{2,1,0:T(8,128)(2,1)}, ...) while((s32[]{:T(128)}, bf16[4,1024,128]{2,1,0:T(8,128)(2,1)}, ...), condition=%wide.region_8.9_spmd, body=%wide.region_5.8_spmd.sunk | while | flops 551681024 | bytes 13690985 | solution.py:404
  212.3 49.4 %all-gather.15.cloned.1.call-done = bf16[4,1024,512]{2,1,0:T(8,128)(2,1)} async-done(((bf16[1,1024,512]{2,1,0:T(8,128)(2,1)}), bf16[4,1024,512]{2,1,0:T(8,128)(2,1)}) %all-gather.15.cloned.1.call-update) | async-done | bytes 4194320 | tf_op jit(solution)/shard_map/all_gather | solution.py:408
  318.1 27.4 %collective-permute-done.5 = bf16[2,1024,512]{2,1,0:T(8,128)(2,1)} collective-permute-done((bf16[2,1024,512]{2,1,0:T(8,128)(2,1)}, bf16[2,1024,512]{2,1,0:T(8,128)(2,1)}, u32[]{:S(2)}, u32[]{:S(2)}) %collective-permute-start.5) | collective-permute-done | bytes 2097184 | tf_op jit(solution)/shard_map/ppermute | solution.py:265
  369.0 281.9 %collective-permute-done.6 = bf16[2,1024,512]{2,1,0:T(8,128)(2,1)} collective-permute-done((bf16[2,1024,512]{2,1,0:T(8,128)(2,1)}, bf16[2,1024,512]{2,1,0:T(8,128)(2,1)}, u32[]{:S(2)}, u32[]{:S(2)}) %collective-permute-start.6) | collective-permute-done | bytes 2097184 | tf_op jit(solution)/shard_map/ppermute | solution.py:265
  685.0 37.1 %gather_slots.3 = bf16[2,2048,2048]{2,1,0:T(8,128)(2,1)} custom-call(s32[2,16]{1,0:T(2,128)} %get-tuple-element.248.low_ref, s32[2,16]{1,0:T(2,128)} %get-tuple-element.247.high_ref, bf16[8,4,1024,512]{3,2,1,0:T(8,128)(2,1)} %bitcast.356, s32[2,16,1,512]{3,2,1,0:T(1,128)} %broadcast_select_fusion.place_ref, f32[2,16,1,512]{3,2,1,0:T(1,128)} %reshape.307.gate_ref), custom_call_target="tpu_custom_call" | custom-call | flops 25769803776 | bytes 50331648 | tf_op jit(solution)/shard_map/gather_slots/pallas_call | solution.py:156
  722.1 163.4 %all-gather.21.cloned.1.call-done = bf16[32768,512]{0,1:T(8,128)(2,1)} async-done(((bf16[1024,512]{0,1:T(8,128)(2,1)}), bf16[32768,512]{0,1:T(8,128)(2,1)}) %all-gather.21.cloned.1.call-update) | async-done | bytes 33554448 | tf_op jit(solution)/shard_map/all_gather | solution.py:417
  885.6 44.0 %copy.162 = bf16[32768,512]{1,0:T(8,128)(2,1)} copy(bf16[32768,512]{0,1:T(8,128)(2,1)} %all-gather.21.cloned.1.call-done) | data formatting | bytes 67108864 | tf_op jit(solution)/shard_map/all_gather | solution.py:417
  929.5 36.3 %gather_slots.2 = bf16[2,2048,2048]{2,1,0:T(8,128)(2,1)} custom-call(s32[2,16]{1,0:T(2,128)} %get-tuple-element.248.low_ref, s32[2,16]{1,0:T(2,128)} %get-tuple-element.247.high_ref, bf16[8,4,1024,512]{3,2,1,0:T(8,128)(2,1)} %bitcast.317, s32[2,16,1,512]{3,2,1,0:T(1,128)} %broadcast_select_fusion.place_ref, f32[2,16,1,512]{3,2,1,0:T(1,128)} %reshape.307.gate_ref), custom_call_target="tpu_custom_call" | custom-call | flops 25769803776 | bytes 50331648 | tf_op jit(solution)/shard_map/gather_slots/pallas_call | solution.py:156
  965.9 24.4 %fusion.69 = bf16[2,2048,1024]{1,2,0:T(8,128)(2,1)} fusion(bf16[2,2048,2048]{2,1,0:T(8,128)(2,1)} %gather_slots.2, bf16[2,2048,2048]{1,2,0:T(8,128)(2,1)} %constant_dynamic-update-slice_fusion.12), kind=kOutput, calls=%fused_computation.89 | convolution fusion | flops 17184063488 | bytes 33554432 | tf_op jit(solution)/shard_map/ecd,edf->ecf/dot_general | solution.py:429
  990.2 24.2 %fusion.66 = bf16[2,2048,1024]{1,2,0:T(8,128)(2,1)} fusion(bf16[2,2048,2048]{2,1,0:T(8,128)(2,1)} %gather_slots.2, bf16[2,2048,2048]{1,2,0:T(8,128)(2,1)} %constant_dynamic-update-slice_fusion.12), kind=kOutput, calls=%fused_computation.88 | convolution fusion | flops 17184063488 | bytes 33554432 | tf_op jit(solution)/shard_map/ecd,edf->ecf/dot_general | solution.py:426
  1014.5 32.3 %fusion.50 = (bf16[2,2048,1024]{1,2,0:T(8,128)(2,1)}, bf16[2,2048,1024]{1,2,0:T(8,128)(2,1)}) fusion(bf16[2,2048,1024]{1,2,0:T(8,128)(2,1)} %fusion.69, bf16[2,2048,1024]{1,2,0:T(8,128)(2,1)} %fusion.66, bf16[2,2048,2048]{2,1,0:T(8,128)(2,1)} %gather_slots.3, bf16[2,1024,2048]{2,1,0:T(8,128)(2,1)} %copy-done.13), kind=kOutput, calls=%fused_computation.64 | convolution fusion | flops 17242783744 | bytes 58720256 | tf_op jit(solution)/shard_map/ecd,efd->ecf/dot_general | solution.py:432
  1046.8 42.8 %fusion.57.slots_ref = bf16[2,2048,2048]{2,1,0:T(8,128)(2,1)} fusion(bf16[2,2048,2048]{1,2,0:T(8,128)(2,1)} %constant_dynamic-update-slice_fusion.12, bf16[2,2048,1024]{1,2,0:T(8,128)(2,1)} %get-tuple-element.256, bf16[2,2048,1024]{1,2,0:T(8,128)(2,1)} %get-tuple-element.255), kind=kOutput, calls=%fused_computation.74 | convolution fusion | flops 34401681408 | bytes 50331648 | tf_op jit(solution)/shard_map/ecf,edf->ecd/dot_general | solution.py:443
  1089.6 26.7 %combine_slots.7 = bf16[4,4,1024,512]{3,2,1,0:T(8,128)(2,1)} custom-call(s32[2,16]{1,0:T(2,128)} %get-tuple-element.248.low_ref, s32[2,16]{1,0:T(2,128)} %get-tuple-element.247.high_ref, s32[1]{0:T(128)S(6)} %sub.84.core_ref, bf16[2,2048,2048]{2,1,0:T(8,128)(2,1)} %fusion.57.slots_ref, s32[2,16,1,512]{3,2,1,0:T(1,128)} %broadcast_select_fusion.place_ref, ...), custom_call_target="tpu_custom_call" | custom-call | flops 12884901888 | bytes 33554432 | tf_op jit(solution)/shard_map/combine_slots/pallas_call | solution.py:224
  1117.4 26.6 %combine_slots.6 = bf16[4,4,1024,512]{3,2,1,0:T(8,128)(2,1)} custom-call(s32[2,16]{1,0:T(2,128)} %get-tuple-element.248.low_ref, s32[2,16]{1,0:T(2,128)} %get-tuple-element.247.high_ref, s32[1]{0:T(128)} %bitcast.41.core_ref, bf16[2,2048,2048]{2,1,0:T(8,128)(2,1)} %fusion.57.slots_ref, s32[2,16,1,512]{3,2,1,0:T(1,128)} %broadcast_select_fusion.place_ref, ...), custom_call_target="tpu_custom_call" | custom-call | flops 12884901888 | bytes 33554432 | tf_op jit(solution)/shard_map/combine_slots/pallas_call | solution.py:224
  1162.8 26.5 %convolution_convert_fusion.slots_ref = bf16[2,2048,2048]{2,1,0:T(8,128)(2,1)} fusion(bf16[2,1024,2048]{2,1,0:T(8,128)(2,1)} %copy-done.13, bf16[2,2048,1024]{1,2,0:T(8,128)(2,1)} %fusion.69, bf16[2,2048,1024]{1,2,0:T(8,128)(2,1)} %fusion.66), kind=kOutput, calls=%fused_computation.75 | convolution fusion | flops 17221812224 | bytes 41943040 | tf_op jit(solution)/shard_map/ecf,efd->ecd/dot_general | solution.py:457
  1189.3 28.6 %combine_slots.5 = bf16[4,4,1024,512]{3,2,1,0:T(8,128)(2,1)} custom-call(s32[2,16]{1,0:T(2,128)} %get-tuple-element.248.low_ref, s32[2,16]{1,0:T(2,128)} %get-tuple-element.247.high_ref, s32[1]{0:T(128)S(6)} %sub.84.core_ref, bf16[2,2048,2048]{2,1,0:T(8,128)(2,1)} %convolution_convert_fusion.slots_ref, s32[2,16,1,512]{3,2,1,0:T(1,128)} %broadcast_select_fusion.place_ref, ...), custom_call_target="tpu_custom_call" | custom-call | flops 12884901888 | bytes 33554432 | tf_op jit(solution)/shard_map/combine_slots/pallas_call | solution.py:224
  1217.9 28.6 %combine_slots.4 = bf16[4,4,1024,512]{3,2,1,0:T(8,128)(2,1)} custom-call(s32[2,16]{1,0:T(2,128)} %get-tuple-element.248.low_ref, s32[2,16]{1,0:T(2,128)} %get-tuple-element.247.high_ref, s32[1]{0:T(128)} %bitcast.41.core_ref, bf16[2,2048,2048]{2,1,0:T(8,128)(2,1)} %convolution_convert_fusion.slots_ref, s32[2,16,1,512]{3,2,1,0:T(1,128)} %broadcast_select_fusion.place_ref, ...), custom_call_target="tpu_custom_call" | custom-call | flops 12884901888 | bytes 33554432 | tf_op jit(solution)/shard_map/combine_slots/pallas_call | solution.py:224
  1246.5 19.3 add.303
  1265.9 58.8 %reduce-scatter.27.cloned.1.call-done = bf16[1,4,1024,512]{3,2,1,0:T(8,128)(2,1)} async-done(((bf16[4,4,1024,512]{3,2,1,0:T(8,128)(2,1)}), bf16[1,4,1024,512]{3,2,1,0:T(8,128)(2,1)}) %reduce-scatter.27.cloned.1.call-update) | async-done | bytes 4194320
  1331.0 151.2 %reduce-scatter.25.cloned.1.call-done = bf16[1,4,1024,512]{3,2,1,0:T(8,128)(2,1)} async-done(((bf16[4,4,1024,512]{3,2,1,0:T(8,128)(2,1)}), bf16[1,4,1024,512]{3,2,1,0:T(8,128)(2,1)}) %reduce-scatter.25.cloned.1.call-update) | async-done | bytes 4194320
  1490.9 71.1 %reduce-scatter.19.cloned.1.call-done = bf16[1,1024,512]{1,2,0:T(8,128)(2,1)} async-done(((bf16[4,1024,512]{1,2,0:T(8,128)(2,1)}), bf16[1,1024,512]{1,2,0:T(8,128)(2,1)}) %reduce-scatter.19.cloned.1.call-update) | async-done | bytes 1048592 | tf_op jit(solution)/shard_map/reduce_scatter | solution.py:287
  1570.9 71.3 %reduce-scatter.17.cloned.1.call-done = bf16[1,1024,512]{1,2,0:T(8,128)(2,1)} async-done(((bf16[4,1024,512]{1,2,0:T(8,128)(2,1)}), bf16[1,1024,512]{1,2,0:T(8,128)(2,1)}) %reduce-scatter.17.cloned.1.call-update) | async-done | bytes 1048592 | tf_op jit(solution)/shard_map/reduce_scatter | solution.py:287
  1671.9 33.4 %reduce-scatter.29.cloned.1.call-done = bf16[1,1024,512]{2,1,0:T(8,128)(2,1)} async-done(((bf16[4,1024,512]{2,1,0:T(8,128)(2,1)}), bf16[1,1024,512]{2,1,0:T(8,128)(2,1)}) %reduce-scatter.29.cloned.1.call-update) | async-done | bytes 1048592
  1707.7 63.3 %while.27 = (s32[]{:T(128)}, f32[4,1024,128]{1,2,0:T(8,128)}, f32[4,1024,128]{1,2,0:T(8,128)}, bf16[4,1024,128]{1,2,0:T(8,128)(2,1)}, s32[1024]{0:T(1024)S(1)}, ...) while((s32[]{:T(128)}, f32[4,1024,128]{1,2,0:T(8,128)}, ...), condition=%wide.region_24.25_spmd, body=%wide.region_22.24_spmd.sunk | while | flops 1353055232 | bytes 56653992 | solution.py:505
  1798.5 28.1 %convolution_convert_fusion.2 = bf16[2,1024,2048]{2,1,0:T(8,128)(2,1)} fusion(bf16[2,2048,2048]{2,1,0:T(8,128)(2,1)} %gather_slots.3, bf16[2,2048,1024]{1,2,0:T(8,128)(2,1)} %fusion.69, bf16[2,2048,1024]{1,2,0:T(8,128)(2,1)} %fusion.66), kind=kOutput, calls=%fused_computation.90 | convolution fusion | flops 17217617920 | bytes 41943040 | tf_op jit(solution)/shard_map/ecf,ecd->efd/dot_general | solution.py:460
  1841.2 27.1 %constant_dynamic-slice_fusion.6 = (bf16[2,1024,1,512]{3,2,1,0:T(2,128)(2,1)}, bf16[2,1024,1,512]{3,2,1,0:T(2,128)(2,1)}, bf16[2,1024,1,512]{3,2,1,0:T(2,128)(2,1)S(1)}, bf16[2,1024,1,512]{3,2,1,0:T(2,128)(2,1)}) fusion(bf16[2,1024,4,512]{3,2,1,0:T(4,128)(2,1)} %reshape.315, s32[]{:T(128)S(6)} %select_n.171, s32[]{:T(128)S(6)} %select_n.169, ...), kind=kLoop, calls=%fused_computation.225 | loop fusion | bytes 16777232 | tf_op jit(solution)/shard_map/dynamic-slice.17
  1880.2 46.5 %fusion.58 = bf16[2,2048,2048]{2,1,0:T(8,128)(2,1)} fusion(bf16[2,2048,2048]{2,1,0:T(8,128)(2,1)} %gather_slots.2, bf16[2,2048,1024]{1,2,0:T(8,128)(2,1)} %get-tuple-element.256, bf16[2,2048,1024]{1,2,0:T(8,128)(2,1)} %get-tuple-element.255), kind=kOutput, calls=%fused_computation.76 | convolution fusion | flops 34401681408 | bytes 50331648 | tf_op jit(solution)/shard_map/ecd,ecf->edf/dot_general | solution.py:463
  1962.0 245.5 %collective-permute-done.16 = bf16[1,2,1024,512]{3,2,1,0:T(8,128)(2,1)S(1)} collective-permute-done((bf16[1,2,1024,512]{3,2,1,0:T(8,128)(2,1)S(1)}, bf16[1,2,1024,512]{3,2,1,0:T(8,128)(2,1)S(1)}, u32[]{:S(2)}, u32[]{:S(2)}) %collective-permute-start.16) | collective-permute-done | bytes 2097184 | tf_op jit(solution)/shard_map/ppermute | solution.py:265
  2256.4 40.8 %all-reduce.4 = (f32[128]{0:T(128)}, f32[128]{0:T(128)}) all-reduce(f32[128]{0:T(128)S(1)} %copy-done.50, f32[128]{0:T(128)S(1)} %copy-done.49), channel_id=1, replica_groups=mesh['chip'=4,'core'=2,'col'=4] {'chip','core','col'}, use_global_device_ids=true, to_apply=%region_34.35 | all-reduce | flops 256 | bytes 2048 | tf_op jit(solution)/shard_map/psum | solution.py:544
  2322.7 33.7 %all-reduce.5 = (f32[512]{0:T(512)}, f32[512]{0:T(512)}) all-reduce(f32[512]{0:T(512)} %get-tuple-element.205, f32[512]{0:T(512)S(1)} %copy-done.43), channel_id=1, replica_groups=mesh['chip'=4,'core'=2,'col'=4] {'chip','core'}, use_global_device_ids=true, to_apply=%region_31.32 | all-reduce | flops 1024 | bytes 8192 | tf_op jit(solution)/shard_map/psum | solution.py:543
  (386 shorter events, 543.1 us)
Async XLA Ops:
  7.2 83.2 %all-gather.19.cloned.1.call-start = ((), (), s32[]{:S(2)}) async-start(), calls=%async_computation.15 | async-start | bytes 5242880 | tf_op jit(solution)/shard_map/all_gather | solution.py:376
  7.9 150.2 %all-gather.13.cloned.1.call-start = ((), (), s32[]{:S(2)}) async-start(), calls=%async_computation.8 | async-start | bytes 7077888 | tf_op jit(solution)/shard_map/all_gather | solution.py:309
  9.2 46.7 %collective-permute-start = (bf16[256,3,256]{2,0,1:T(8,128)(2,1)S(1)}, bf16[256,3,256]{2,0,1:T(8,128)(2,1)S(1)}, u32[]{:S(2)}, u32[]{:S(2)}) collective-permute-start(bf16[256,3,256]{2,0,1:T(8,128)(2,1)S(1)} %get-tuple-element.292), channel_id=1, source_target_pairs={{0,0},{1,8},{2,16},{3,24},{4,4},{5,12},{6,20},{7,28},{8,1},{9,9},{... | collective-permute-start | bytes 1179656 | tf_op jit(solution)/shard_map/ppermute | solution.py:305
  12.4 52.6 %collective-permute-start.1 = (bf16[256,3,256]{2,0,1:T(8,128)(2,1)S(1)}, bf16[256,3,256]{2,0,1:T(8,128)(2,1)S(1)}, u32[]{:S(2)}, u32[]{:S(2)}) collective-permute-start(bf16[256,3,256]{2,0,1:T(8,128)(2,1)S(1)} %get-tuple-element.291), channel_id=1, source_target_pairs={{0,4},{1,12},{2,20},{3,28},{4,0},{5,8},{6,16},{7,24},{8,5},{9,13},... | collective-permute-start | bytes 1179656 | tf_op jit(solution)/shard_map/ppermute | solution.py:305
  66.3 146.0 %all-gather.17.cloned.1.call-start = ((), (), s32[]{:S(2)}) async-start(), calls=%async_computation.10 | async-start | bytes 2359296 | tf_op jit(solution)/shard_map/all_gather | solution.py:378
  67.0 194.7 %all-gather.15.cloned.1.call-start = ((), (), s32[]{:S(2)}) async-start(), calls=%async_computation.9 | async-start | bytes 5242880 | tf_op jit(solution)/shard_map/all_gather | solution.py:408
  211.0 474.0 %all-gather.23.cloned.1.call-start = ((), (), s32[]{:S(2)}) async-start(), calls=%async_computation.17 | async-start | bytes 34603008 | tf_op jit(solution)/shard_map/all_gather | solution.py:384
  211.6 673.9 %all-gather.21.cloned.1.call-start = ((), (), s32[]{:S(2)}) async-start(), calls=%async_computation.16 | async-start | bytes 34603008 | tf_op jit(solution)/shard_map/all_gather | solution.py:417
  275.0 1049.7 %reduce-scatter.27.cloned.1.call-start = ((), (), s32[]{:S(2)}) async-start(), calls=%async_computation.19 | async-start | bytes 20971520
  280.9 64.6 %collective-permute-start.5 = (bf16[2,1024,512]{2,1,0:T(8,128)(2,1)}, bf16[2,1024,512]{2,1,0:T(8,128)(2,1)}, u32[]{:S(2)}, u32[]{:S(2)}) collective-permute-start(bf16[2,1024,512]{2,1,0:T(8,128)(2,1)} %get-tuple-element.270), channel_id=1, source_target_pairs={{0,1},{1,0},{2,3},{3,2},{4,5},{5,4},{6,7},{7,6},{8,9},{9,8},{10,11... | collective-permute-start | bytes 6291464 | tf_op jit(solution)/shard_map/ppermute | solution.py:265
  301.1 353.6 %collective-permute-start.2 = (bf16[2,512,2048]{1,2,0:T(8,128)(2,1)}, bf16[2,512,2048]{1,2,0:T(8,128)(2,1)}, u32[]{:S(2)}, u32[]{:S(2)}) collective-permute-start(bf16[2,512,2048]{1,2,0:T(8,128)(2,1)} %bitcast.333), channel_id=1, source_target_pairs={{0,1},{1,0},{2,3},{3,2},{4,5},{5,4},{6,7},{7,6},{8,9},{9,8},{10,11... | collective-permute-start | bytes 12582920 | tf_op jit(solution)/shard_map/ppermute | solution.py:265
  308.2 354.2 %collective-permute-start.3 = (bf16[2,512,2048]{1,2,0:T(8,128)(2,1)}, bf16[2,512,2048]{1,2,0:T(8,128)(2,1)}, u32[]{:S(2)}, u32[]{:S(2)}) collective-permute-start(bf16[2,512,2048]{1,2,0:T(8,128)(2,1)} %bitcast.332), channel_id=1, source_target_pairs={{0,2},{1,3},{2,0},{3,1},{4,6},{5,7},{6,4},{7,5},{8,10},{9,11},{10,... | collective-permute-start | bytes 12582920 | tf_op jit(solution)/shard_map/ppermute | solution.py:265
  315.7 351.2 %collective-permute-start.4 = (bf16[2,512,2048]{1,2,0:T(8,128)(2,1)}, bf16[2,512,2048]{1,2,0:T(8,128)(2,1)}, u32[]{:S(2)}, u32[]{:S(2)}) collective-permute-start(bf16[2,512,2048]{1,2,0:T(8,128)(2,1)} %bitcast.331), channel_id=1, source_target_pairs={{0,3},{1,2},{2,1},{3,0},{4,7},{5,6},{6,5},{7,4},{8,11},{9,10},{10,... | collective-permute-start | bytes 12582920 | tf_op jit(solution)/shard_map/ppermute | solution.py:265
  316.6 334.2 %collective-permute-start.6 = (bf16[2,1024,512]{2,1,0:T(8,128)(2,1)}, bf16[2,1024,512]{2,1,0:T(8,128)(2,1)}, u32[]{:S(2)}, u32[]{:S(2)}) collective-permute-start(bf16[2,1024,512]{2,1,0:T(8,128)(2,1)} %get-tuple-element.269), channel_id=1, source_target_pairs={{0,2},{1,3},{2,0},{3,1},{4,6},{5,7},{6,4},{7,5},{8,10},{9,11},{10,... | collective-permute-start | bytes 6291464 | tf_op jit(solution)/shard_map/ppermute | solution.py:265
  345.5 307.3 %collective-permute-start.7 = (bf16[2,1024,512]{2,1,0:T(8,128)(2,1)S(1)}, bf16[2,1024,512]{2,1,0:T(8,128)(2,1)}, u32[]{:S(2)}, u32[]{:S(2)}) collective-permute-start(bf16[2,1024,512]{2,1,0:T(8,128)(2,1)S(1)} %copy-done.27), channel_id=1, source_target_pairs={{0,3},{1,2},{2,1},{3,0},{4,7},{5,6},{6,5},{7,4},{8,11},{9,10},{10,... | collective-permute-start | bytes 6291464 | tf_op jit(solution)/shard_map/ppermute | solution.py:265
  1116.3 27.7 %collective-permute-start.9 = (bf16[4,4,1024,512]{3,2,1,0:T(8,128)(2,1)}, bf16[4,4,1024,512]{3,2,1,0:T(8,128)(2,1)}, u32[]{:S(2)}, u32[]{:S(2)}) collective-permute-start(bf16[4,4,1024,512]{3,2,1,0:T(8,128)(2,1)} %combine_slots.7), channel_id=1, source_target_pairs={{0,4},{4,0},{1,5},{5,1},{2,6},{6,2},{3,7},{7,3},{8,12},{12,8},{9,1... | collective-permute-start | bytes 50331656 | tf_op jit(solution)/shard_map/ppermute | solution.py:260
  1162.8 319.4 %reduce-scatter.25.cloned.1.call-start = ((), (), s32[]{:S(2)}) async-start(), calls=%async_computation.18 | async-start | bytes 20971520
  1217.9 28.6 %collective-permute-start.8 = (bf16[4,4,1024,512]{3,2,1,0:T(8,128)(2,1)}, bf16[4,4,1024,512]{3,2,1,0:T(8,128)(2,1)}, u32[]{:S(2)}, u32[]{:S(2)}) collective-permute-start(bf16[4,4,1024,512]{3,2,1,0:T(8,128)(2,1)} %combine_slots.5), channel_id=1, source_target_pairs={{0,4},{4,0},{1,5},{5,1},{2,6},{6,2},{3,7},{7,3},{8,12},{12,8},{9,1... | collective-permute-start | bytes 50331656 | tf_op jit(solution)/shard_map/ppermute | solution.py:260
  1265.8 296.2 %reduce-scatter.19.cloned.1.call-start = ((), (), s32[]{:S(2)}) async-start(), calls=%async_computation.12 | async-start | bytes 5242880 | tf_op jit(solution)/shard_map/reduce_scatter | solution.py:287
  1330.9 311.2 %reduce-scatter.17.cloned.1.call-start = ((), (), s32[]{:S(2)}) async-start(), calls=%async_computation.11 | async-start | bytes 5242880 | tf_op jit(solution)/shard_map/reduce_scatter | solution.py:287
  1488.4 216.8 %reduce-scatter.29.cloned.1.call-start = ((), (), s32[]{:S(2)}) async-start(), calls=%async_computation.20 | async-start | bytes 5242880
  1652.0 602.6 %reduce-scatter.23.cloned.1.call-start = ((), (), s32[]{:S(2)}) async-start(), calls=%async_computation.14 | async-start | bytes 2359296 | tf_op jit(solution)/shard_map/reduce_scatter | solution.py:496
  1671.4 625.8 %reduce-scatter.31.cloned.1.call-start = ((), (), s32[]{:S(2)}) async-start(), calls=%async_computation.21 | async-start | bytes 5242880
  1798.3 508.0 %reduce-scatter.21.cloned.1.call-start = ((), (), s32[]{:S(2)}) async-start(), calls=%async_computation.13 | async-start | bytes 7077888 | tf_op jit(solution)/shard_map/reduce_scatter | solution.py:317
  1870.1 70.4 %collective-permute-start.15 = (bf16[1,2,1024,512]{3,2,1,0:T(8,128)(2,1)}, bf16[1,2,1024,512]{3,2,1,0:T(8,128)(2,1)}, u32[]{:S(2)}, u32[]{:S(2)}) collective-permute-start(bf16[1,2,1024,512]{3,2,1,0:T(8,128)(2,1)} %bitcast.274), channel_id=1, source_target_pairs={{0,1},{1,0},{2,3},{3,2},{4,5},{5,4},{6,7},{7,6},{8,9},{9,8},{10,11... | collective-permute-start | bytes 6291464 | tf_op jit(solution)/shard_map/ppermute | solution.py:265
  1936.1 286.2 %collective-permute-start.12 = (bf16[1,2,512,2048]{3,2,1,0:T(8,128)(2,1)}, bf16[1,2,512,2048]{3,2,1,0:T(8,128)(2,1)}, u32[]{:S(2)}, u32[]{:S(2)}) collective-permute-start(bf16[1,2,512,2048]{3,2,1,0:T(8,128)(2,1)} %get-tuple-element.259), channel_id=1, source_target_pairs={{0,1},{1,0},{2,3},{3,2},{4,5},{5,4},{6,7},{7,6},{8,9},{9,8},{10,11... | collective-permute-start | bytes 12582920 | tf_op jit(solution)/shard_map/ppermute | solution.py:265
  1936.9 290.2 %collective-permute-start.13 = (bf16[1,2,512,2048]{3,2,1,0:T(8,128)(2,1)}, bf16[1,2,512,2048]{3,2,1,0:T(8,128)(2,1)S(1)}, u32[]{:S(2)}, u32[]{:S(2)}) collective-permute-start(bf16[1,2,512,2048]{3,2,1,0:T(8,128)(2,1)} %get-tuple-element.258), channel_id=1, source_target_pairs={{0,2},{1,3},{2,0},{3,1},{4,6},{5,7},{6,4},{7,5},{8,10},{9,11},{10,... | collective-permute-start | bytes 12582920 | tf_op jit(solution)/shard_map/ppermute | solution.py:265
  1938.2 269.4 %collective-permute-start.16 = (bf16[1,2,1024,512]{3,2,1,0:T(8,128)(2,1)S(1)}, bf16[1,2,1024,512]{3,2,1,0:T(8,128)(2,1)S(1)}, u32[]{:S(2)}, u32[]{:S(2)}) collective-permute-start(bf16[1,2,1024,512]{3,2,1,0:T(8,128)(2,1)S(1)} %bitcast.341), channel_id=1, source_target_pairs={{0,2},{1,3},{2,0},{3,1},{4,6},{5,7},{6,4},{7,5},{8,10},{9,11},{10,... | collective-permute-start | bytes 6291464 | tf_op jit(solution)/shard_map/ppermute | solution.py:265
  1939.6 269.4 %collective-permute-start.17 = (bf16[1,2,1024,512]{3,2,1,0:T(8,128)(2,1)S(1)}, bf16[1,2,1024,512]{3,2,1,0:T(8,128)(2,1)S(1)}, u32[]{:S(2)}, u32[]{:S(2)}) collective-permute-start(bf16[1,2,1024,512]{3,2,1,0:T(8,128)(2,1)S(1)} %bitcast.340), channel_id=1, source_target_pairs={{0,3},{1,2},{2,1},{3,0},{4,7},{5,6},{6,5},{7,4},{8,11},{9,10},{10,... | collective-permute-start | bytes 6291464 | tf_op jit(solution)/shard_map/ppermute | solution.py:265
  1940.5 288.8 %collective-permute-start.14 = (bf16[1,2,512,2048]{3,2,1,0:T(8,128)(2,1)}, bf16[1,2,512,2048]{3,2,1,0:T(8,128)(2,1)}, u32[]{:S(2)}, u32[]{:S(2)}) collective-permute-start(bf16[1,2,512,2048]{3,2,1,0:T(8,128)(2,1)} %get-tuple-element.257), channel_id=1, source_target_pairs={{0,3},{1,2},{2,1},{3,0},{4,7},{5,6},{6,5},{7,4},{8,11},{9,10},{10,... | collective-permute-start | bytes 12582920 | tf_op jit(solution)/shard_map/ppermute | solution.py:265
  2311.0 47.1 %collective-permute-start.10 = (bf16[256,3,256]{2,0,1:T(8,128)(2,1)}, bf16[256,3,256]{2,0,1:T(8,128)(2,1)}, u32[]{:S(2)}, u32[]{:S(2)}) collective-permute-start(bf16[256,3,256]{2,0,1:T(8,128)(2,1)} %bitcast.277), channel_id=1, source_target_pairs={{0,0},{1,8},{2,16},{3,24},{4,4},{5,12},{6,20},{7,28},{8,1},{9,9},{... | collective-permute-start | bytes 1179656 | tf_op jit(solution)/shard_map/ppermute | solution.py:328
  2316.5 51.0 %collective-permute-start.11 = (bf16[256,3,256]{2,0,1:T(8,128)(2,1)}, bf16[256,3,256]{2,0,1:T(8,128)(2,1)S(1)}, u32[]{:S(2)}, u32[]{:S(2)}) collective-permute-start(bf16[256,3,256]{2,0,1:T(8,128)(2,1)} %bitcast.276), channel_id=1, source_target_pairs={{0,4},{1,12},{2,20},{3,28},{4,0},{5,8},{6,16},{7,24},{8,5},{9,13},... | collective-permute-start | bytes 1179656 | tf_op jit(solution)/shard_map/ppermute | solution.py:328
  (59 other events, 1034.6 us)
Sparse Core Ops, SparseCore 0:
  9.9 80.4 all-gather.18
  92.5 65.5 all-gather.12
  159.8 27.2 all-gather.16
  211.2 50.4 all-gather.14
  264.4 420.5 all-gather.22
  688.4 197.1 all-gather.20
  1162.9 161.7 reduce-scatter.26
  1328.3 153.8 reduce-scatter.24
  1485.1 76.9 reduce-scatter.18
  1564.9 77.2 reduce-scatter.16
  1652.1 53.0 reduce-scatter.28
  1707.5 32.9 reduce-scatter.22
  1798.4 52.6 reduce-scatter.30
  1880.3 68.4 reduce-scatter.20

commit v2 on v1

v2 whole, which is shorter than its diff:
```python
from functools import partial

import jax
import jax.numpy as jnp
from jax import lax
from jax.experimental import pallas as pl
from jax.experimental.layout import Layout, with_layout_constraint
from jax.experimental.pallas import tpu as pltpu
from jax.sharding import Mesh, PartitionSpec as P

DOCS = 4
epsilon = 1e-06
rope_base = 10000.0
neg_large = -1e30

ROW = ("chip", "core")
ALL = ("chip", "core", "col")
TILE = 256
BLOCK = 512
VMEM_BYTES = 58 * 1024 * 1024
F32 = jnp.float32
BF16 = jnp.bfloat16


def rope_tables(seg_row, head_size):
    docs = jnp.arange(DOCS, dtype=jnp.int32)
    starts = jnp.sum((seg_row[:, None] < docs[None, :]).astype(jnp.int32), axis=0)
    first_index = jnp.sum(
        jnp.where(seg_row[:, None] == docs[None, :], starts[None, :], 0), axis=-1
    )
    places = (jnp.arange(seg_row.shape[0], dtype=jnp.int32) - first_index).astype(F32)
    rates = rope_base ** (-jnp.arange(0, head_size, 2, dtype=F32) / head_size)
    angles = places[..., None] * rates
    angles = jnp.concatenate([angles, angles], axis=-1)
    return (jnp.cos(angles), jnp.sin(angles))


def width_total(values):
    return lax.psum(values, "col")


def norm_back(grad_normed, stream, rate, gain, model_width):
    scaled_grad = grad_normed * gain
    across = width_total(jnp.sum(scaled_grad * stream, axis=-1))[:, None]
    return rate * scaled_grad - stream * rate * rate * rate * across / model_width


def half_turn(values, sign):
    lane = lax.broadcasted_iota(jnp.int32, values.shape, 1)
    half = values.shape[1] // 2
    return jnp.where(lane < half, sign, -sign) * pltpu.roll(values, half, 1)


def head_norm(raw, gain, cosine, sine):
    rate = lax.rsqrt(jnp.mean(raw * raw, axis=-1, keepdims=True) + epsilon)
    normed = raw * rate
    gained = normed * gain
    return normed, rate, (gained * cosine + half_turn(gained, -1.0) * sine).astype(BF16)


def masked_scores(query, key, seg_col, seg_row, factor):
    scores = lax.dot_general(
        query, key, (((1,), (1,)), ((), ())), preferred_element_type=F32
    ) * factor
    return jnp.where(seg_col == seg_row, scores, neg_large)


def attend_kernel(
    factor, query_ref, key_ref, value_ref, cos_ref, sin_ref, row_ref, col_ref, gains_ref,
    out_ref, log_ref, low_ref,
):
    cosine, sine = cos_ref[...], sin_ref[...]
    low_ref[...] = head_norm(query_ref[...], gains_ref[0:1], cosine, sine)[2]
    key = head_norm(key_ref[...], gains_ref[1:2], cosine, sine)[2]
    value = value_ref[...].astype(BF16)
    seg_row = row_ref[...]

    def body(i, carry):
        rows = pl.ds(pl.multiple_of(i * TILE, TILE), TILE)
        scores = masked_scores(low_ref[rows], key, col_ref[rows], seg_row, factor)
        top = jnp.max(scores, axis=-1, keepdims=True)
        log_total = top + jnp.log(jnp.sum(jnp.exp(scores - top), axis=-1, keepdims=True))
        probs = jnp.exp(scores - log_total).astype(BF16)
        out_ref[rows] = jnp.dot(probs, value, preferred_element_type=F32).astype(BF16)
        log_ref[rows] = jnp.broadcast_to(log_total, (TILE, log_ref.shape[1]))
        return carry

    lax.fori_loop(0, query_ref.shape[0] // TILE, body, 0)


def attend_specs(tokens, size, heads):
    def part(k):
        return pl.BlockSpec((tokens, size), lambda h: (0, k * heads + h))

    whole = [
        pl.BlockSpec(shape, lambda h: (0, 0))
        for shape in ((tokens, size), (tokens, size), (1, tokens), (tokens, 1), (2, size))
    ]
    return [part(0), part(1), part(2)], whole


def attend_forward(qkv, cosine, sine, seg_row, gains):
    tokens, size = cosine.shape
    heads = qkv.shape[1] // (3 * size)
    parts, whole = attend_specs(tokens, size, heads)
    by_head = pl.BlockSpec((tokens, size), lambda h: (0, h))
    return pl.pallas_call(
        partial(attend_kernel, size ** (-0.5)),
        grid=(heads,),
        in_specs=parts + whole,
        out_specs=[by_head, by_head],
        out_shape=[
            jax.ShapeDtypeStruct((tokens, heads * size), BF16),
            jax.ShapeDtypeStruct((tokens, heads * size), F32),
        ],
        scratch_shapes=[pltpu.VMEM((tokens, size), BF16)],
        compiler_params=pltpu.CompilerParams(vmem_limit_bytes=VMEM_BYTES),
        cost_estimate=pl.CostEstimate(
            flops=4 * heads * tokens * tokens * size,
            bytes_accessed=qkv.size * 4 + tokens * heads * size * 6,
            transcendentals=2 * heads * tokens * tokens,
        ),
        name="attend_forward",
    )(qkv, qkv, qkv, cosine, sine, seg_row[None, :], seg_row[:, None], gains)


def attend_back_kernel(
    factor, query_ref, key_ref, value_ref, cos_ref, sin_ref, row_ref, col_ref, gains_ref,
    grad_ref, log_ref, out_ref, gain_ref, low_ref, query_grad, key_grad, value_grad,
):
    head, heads = pl.program_id(0), pl.num_programs(0)
    cosine, sine = cos_ref[...], sin_ref[...]
    gains = gains_ref[...]
    low_ref[...] = head_norm(query_ref[...], gains[0:1], cosine, sine)[2]
    key = head_norm(key_ref[...], gains[1:2], cosine, sine)[2]
    value = value_ref[...].astype(BF16)
    seg_row = row_ref[...]
    size = value.shape[1]
    key_grad[...] = jnp.zeros_like(key_grad)
    value_grad[...] = jnp.zeros_like(value_grad)

    def body(i, carry):
        rows = pl.ds(pl.multiple_of(i * TILE, TILE), TILE)
        query = low_ref[rows]
        grad_out = grad_ref[rows]
        scores = masked_scores(query, key, col_ref[rows], seg_row, factor)
        probs = jnp.exp(scores - log_ref[rows][:, :1])
        grad_probs = lax.dot_general(
            grad_out, value, (((1,), (1,)), ((), ())), preferred_element_type=F32
        )
        weighted = probs * grad_probs
        center = jnp.sum(weighted, axis=-1, keepdims=True)
        grad_scores = (weighted - probs * center).astype(BF16)
        query_grad[rows] = jnp.dot(grad_scores, key, preferred_element_type=F32) * factor
        first = (((0,), (0,)), ((), ()))
        key_grad[...] += lax.dot_general(grad_scores, query, first, preferred_element_type=F32)
        value_grad[...] += lax.dot_general(
            probs.astype(BF16), grad_out, first, preferred_element_type=F32
        )
        return carry

    lax.fori_loop(0, query_ref.shape[0] // TILE, body, 0)

    @pl.when(head == 0)
    def _():
        gain_ref[...] = jnp.zeros_like(gain_ref)

    for k, (raw_ref, grad) in enumerate(
        ((query_ref, query_grad[...]), (key_ref, key_grad[...] * factor))
    ):
        raw = raw_ref[...]
        rate = lax.rsqrt(jnp.mean(raw * raw, axis=-1, keepdims=True) + epsilon)
        normed = raw * rate
        grad_normed = grad * cosine + half_turn(grad * sine, 1.0)
        gain_ref[k : k + 1] += jnp.sum(grad_normed * normed, axis=0, keepdims=True)
        scaled = grad_normed * gains[k : k + 1]
        raw_grad = rate * (
            scaled - normed * jnp.mean(scaled * normed, axis=-1, keepdims=True)
        )
        columns = pl.ds(pl.multiple_of((k * heads + head) * size, size), size)
        out_ref[:, columns] = raw_grad.astype(BF16)
    columns = pl.ds(pl.multiple_of((2 * heads + head) * size, size), size)
    out_ref[:, columns] = value_grad[...].astype(BF16)


def attend_backward(qkv, cosine, sine, seg_row, gains, grad_heads, logs):
    tokens, size = cosine.shape
    heads = qkv.shape[1] // (3 * size)
    parts, whole = attend_specs(tokens, size, heads)
    by_head = pl.BlockSpec((tokens, size), lambda h: (0, h))
    return pl.pallas_call(
        partial(attend_back_kernel, size ** (-0.5)),
        grid=(heads,),
        in_specs=parts + whole + [by_head, by_head],
        out_specs=[
            pl.BlockSpec((tokens, 3 * heads * size), lambda h: (0, 0)),
            pl.BlockSpec((2, size), lambda h: (0, 0)),
        ],
        out_shape=[
            jax.ShapeDtypeStruct((tokens, 3 * heads * size), BF16),
            jax.ShapeDtypeStruct((2, size), F32),
        ],
        scratch_shapes=[
            pltpu.VMEM((tokens, size), BF16),
            pltpu.VMEM((tokens, size), F32),
            pltpu.VMEM((tokens, size), F32),
            pltpu.VMEM((tokens, size), F32),
        ],
        compiler_params=pltpu.CompilerParams(vmem_limit_bytes=VMEM_BYTES),
        cost_estimate=pl.CostEstimate(
            flops=10 * heads * tokens * tokens * size,
            bytes_accessed=qkv.size * 6 + tokens * heads * size * 6,
            transcendentals=heads * tokens * tokens,
        ),
        name="attend_backward",
    )(qkv, qkv, qkv, cosine, sine, seg_row[None, :], seg_row[:, None], gains, grad_heads, logs)


def slot_places(routes, route_gates, expert_ids):
    chosen = routes[None] == expert_ids[:, None, None]
    hit = jnp.any(chosen, axis=-1)
    gate = jnp.sum(jnp.where(chosen, route_gates[None], 0.0), axis=-1)
    count, tok_total = hit.shape
    grouped = hit.astype(BF16).reshape(count, tok_total // 128, 128)
    lane = jnp.arange(128)
    before = (lane[:, None] < lane[None, :]).astype(BF16)
    inside = jnp.einsum("egt,tu->egu", grouped, before, preferred_element_type=F32)
    totals = jnp.sum(grouped.astype(F32), axis=-1).astype(BF16)
    group = jnp.arange(tok_total // 128)
    earlier = (group[:, None] < group[None, :]).astype(BF16)
    offset = jnp.einsum("eg,gh->eh", totals, earlier, preferred_element_type=F32)
    place = (inside + offset[..., None]).reshape(count, tok_total).astype(jnp.int32)
    per_block = jnp.sum(hit.astype(jnp.int32).reshape(count, tok_total // BLOCK, BLOCK), axis=-1)
    begin = place.reshape(count, tok_total // BLOCK, BLOCK)[:, :, 0]
    end = begin + per_block
    low = begin // TILE
    high = jnp.where(end > begin, (end + TILE - 1) // TILE, low)
    return (jnp.where(hit, place, -1), gate, low, high)


def gather_kernel(scaled, each, low_ref, high_ref, *refs):
    rows_refs, place_refs, gate_refs, slots_ref = refs[0:2], refs[2:4], refs[4:6], refs[6]
    chip, piece = pl.program_id(0), pl.program_id(1)
    experts = slots_ref.shape[0]

    @pl.when((chip == 0) & (piece == 0))
    def _():
        slots_ref[...] = jnp.zeros_like(slots_ref)

    for k in range(2):
        rows_ref = rows_refs[k]
        parts, width = rows_ref.shape[1], rows_ref.shape[3]
        block = (2 * chip + k) * each + piece
        for e in range(experts):
            place = place_refs[k][e, 0]
            gate = gate_refs[k][e, 0]

            def body(i, carry):
                base = pl.multiple_of(i * TILE, TILE)
                wanted = lax.broadcasted_iota(jnp.int32, (TILE, BLOCK), 0) + base
                mask = place == wanted
                onehot = mask.astype(F32).astype(BF16)
                if scaled:
                    factor = jnp.sum(jnp.where(mask, gate, 0.0), axis=1, keepdims=True)
                for c in range(parts):
                    picked = jnp.dot(onehot, rows_ref[0, c], preferred_element_type=F32)
                    if scaled:
                        picked = picked * factor
                    where = (e, pl.ds(base, TILE), slice(c * width, (c + 1) * width))
                    slots_ref[where] = slots_ref[where] + picked.astype(BF16)
                return carry

            lax.fori_loop(low_ref[e, block], high_ref[e, block], body, 0)


def gather_slots(rows, place, gate, low, high, capacity, scaled):
    row_count, parts, per_row, width = rows.shape
    experts, tok_total = place.shape
    blocks = tok_total // BLOCK
    each = per_row // BLOCK

    def row_spec(k):
        return pl.BlockSpec(
            (1, parts, BLOCK, width),
            lambda z, j, *_: (2 * z + k, 0, j, 0),
        )

    def token_spec(k):
        return pl.BlockSpec(
            (experts, 1, 1, BLOCK),
            lambda z, j, *_: (0, (2 * z + k) * each + j, 0, 0),
        )

    places = place.reshape(experts, blocks, 1, BLOCK)
    gates = gate.reshape(experts, blocks, 1, BLOCK)
    return pl.pallas_call(
        partial(gather_kernel, scaled, each),
        grid_spec=pltpu.PrefetchScalarGridSpec(
            num_scalar_prefetch=2,
            grid=(row_count // 2, each),
            in_specs=[
                row_spec(0), row_spec(1), token_spec(0), token_spec(1), token_spec(0), token_spec(1),
            ],
            out_specs=pl.BlockSpec((experts, capacity, parts * width), lambda *_: (0, 0, 0)),
        ),
        out_shape=jax.ShapeDtypeStruct((experts, capacity, parts * width), BF16),
        compiler_params=pltpu.CompilerParams(vmem_limit_bytes=VMEM_BYTES),
        cost_estimate=pl.CostEstimate(
            flops=2 * 24 * experts * TILE * BLOCK * parts * width,
            bytes_accessed=(tok_total + experts * capacity) * parts * width * 2,
            transcendentals=0,
        ),
        name="gather_slots",
    )(low, high, rows, rows, places, places, gates, gates)


def combine_kernel(scaled, each, low_ref, high_ref, core_ref, slots_ref, place_ref, gate_ref, *refs):
    out_ref, total_ref = refs[-2:]
    chip, piece = pl.program_id(0), pl.program_id(1)
    block = (2 * chip + core_ref[0]) * each + piece
    experts = slots_ref.shape[0]
    parts, width = out_ref.shape[0], out_ref.shape[3]
    total_ref[...] = jnp.zeros_like(total_ref)
    for e in range(experts):
        place = jnp.broadcast_to(place_ref[e, 0].astype(F32), (8, BLOCK)).T[:, :1]
        if scaled:
            gate = jnp.broadcast_to(gate_ref[e, 0], (8, BLOCK)).T[:, :1]

        def body(i, carry):
            base = pl.multiple_of(i * TILE, TILE)
            wanted = lax.broadcasted_iota(jnp.int32, (BLOCK, TILE), 1) + base
            onehot = (place == wanted.astype(F32)).astype(F32).astype(BF16)
            for c in range(parts):
                columns = slice(c * width, (c + 1) * width)
                picked = jnp.dot(
                    onehot, slots_ref[e, pl.ds(base, TILE), columns], preferred_element_type=F32
                )
                if scaled:
                    picked = picked * gate
                total_ref[:, columns] = total_ref[:, columns] + picked
            return carry

        lax.fori_loop(low_ref[e, block], high_ref[e, block], body, 0)
    for c in range(parts):
        total = total_ref[:, c * width : (c + 1) * width]
        if len(refs) == 3:
            total = total + refs[0][c, 0].astype(F32)
        out_ref[c, 0] = total.astype(BF16)


def combine_slots(slots, place, gate, low, high, core, chips, per_row, parts, scaled, more=()):
    experts, capacity, model_width = slots.shape
    width = model_width // parts
    each = per_row // BLOCK
    blocks = place.shape[1] // BLOCK

    def token_block(z, j, low_ref, high_ref, core_ref):
        return (0, (2 * z + core_ref[0]) * each + j, 0, 0)

    sums = pl.BlockSpec((parts, 1, BLOCK, width), lambda z, j, *_: (0, z, j, 0))
    return pl.pallas_call(
        partial(combine_kernel, scaled, each),
        grid_spec=pltpu.PrefetchScalarGridSpec(
            num_scalar_prefetch=3,
            grid=(chips, each),
            in_specs=[
                pl.BlockSpec(
                    (experts, capacity, model_width),
                    lambda *_: (0, 0, 0),
                    pipeline_mode=pl.Buffered(1),
                ),
                pl.BlockSpec((experts, 1, 1, BLOCK), token_block),
                pl.BlockSpec((experts, 1, 1, BLOCK), token_block),
            ]
            + [sums] * len(more),
            out_specs=sums,
            scratch_shapes=[pltpu.VMEM((BLOCK, model_width), F32)],
        ),
        out_shape=jax.ShapeDtypeStruct((parts, chips, per_row, width), BF16),
        compiler_params=pltpu.CompilerParams(vmem_limit_bytes=VMEM_BYTES),
        cost_estimate=pl.CostEstimate(
            flops=24 * experts * TILE * BLOCK * model_width,
            bytes_accessed=slots.size * 2 + parts * chips * per_row * width * 2,
            transcendentals=0,
        ),
        name="combine_slots",
    )(
        low,
        high,
        core,
        slots,
        place.reshape(experts, blocks, 1, BLOCK),
        gate.reshape(experts, blocks, 1, BLOCK),
        *more,
    )


def swap_cores(values):
    return lax.ppermute(values, "core", [(0, 1), (1, 0)])


def swap_cols(values, mask):
    count = lax.axis_size("col")
    return lax.ppermute(values, "col", [(i, i ^ mask) for i in range(count)])


def fence(*values):
    return lax.optimization_barrier(values)


def plain(values):
    return with_layout_constraint(values, Layout(tuple(range(values.ndim))))


def gather_cols(values):
    count = lax.axis_size("col")
    me = lax.axis_index("col")
    result = jnp.zeros((count,) + values.shape, values.dtype)
    for mask in range(count):
        piece = swap_cols(values, mask) if mask else values
        result = lax.dynamic_update_index_in_dim(result, piece, me ^ mask, 0)
    return result


def sum_cols(parts):
    count = lax.axis_size("col")
    me = lax.axis_index("col")
    total = 0.0
    for mask in range(count):
        piece = lax.dynamic_index_in_dim(parts, me ^ mask, 0, keepdims=False)
        if mask:
            piece = swap_cols(piece, mask)
        total = total + piece.astype(F32)
    return total


def send_parts(parts):
    me = lax.axis_index("col")
    pieces = []
    for mask in range(lax.axis_size("col")):
        piece = plain(lax.dynamic_index_in_dim(parts, me ^ mask, 0, keepdims=False))
        pieces.append(swap_cols(piece, mask) if mask else piece)
    return pieces


def join_parts(pieces, axis, result=None, offset=0):
    me = lax.axis_index("col")
    if result is None:
        shape = list(pieces[0].shape)
        shape[axis] *= len(pieces)
        result = jnp.zeros(shape, pieces[0].dtype)
    size = result.shape[axis] // len(pieces)
    for mask, piece in enumerate(pieces):
        start = (me ^ mask) * size + offset
        result = lax.dynamic_update_slice_in_dim(result, piece, start, axis)
    return result


def swap_chips(values, mask):
    count = lax.axis_size("chip")
    return lax.ppermute(values, "chip", [(i, i ^ mask) for i in range(count)])


def over_chips(values):
    chips = lax.axis_size("chip")
    chip = lax.axis_index("chip")
    same = jnp.zeros((chips,) + values.shape, values.dtype)
    for mask in range(chips):
        piece = swap_chips(values, mask) if mask else values
        same = lax.dynamic_update_index_in_dim(same, piece, chip ^ mask, 0)
    return same


def over_cores(same):
    core = lax.axis_index("core")
    other = swap_cores(same)
    both = jnp.stack([jnp.where(core == 0, same, other), jnp.where(core == 0, other, same)], axis=1)
    return both.reshape(-1, same.shape[-1])


def pick(pieces, index):
    chosen = pieces[0]
    for k in range(1, len(pieces)):
        chosen = jnp.where(index == k, pieces[k], chosen)
    return chosen


def heads_in(weight, ratio):
    chips, cols = lax.axis_size("chip"), lax.axis_size("col")
    rows = 2 * chips
    row = 2 * lax.axis_index("chip") + lax.axis_index("core")
    kinds, features, width = weight.shape
    block = features // ratio
    pieces = []
    for k in range(ratio):
        pairs = []
        for r in range(rows):
            for c in range(cols):
                h = (k + r) % ratio
                pairs.append((r * cols + c, (ratio * c + h) * cols + r // ratio))
        piece = lax.dynamic_slice_in_dim(weight, (k + row) % ratio * block, block, 1)
        pieces.append(lax.ppermute(piece, ALL, pairs))
    joined = jnp.concatenate(
        [pick([p[a] for p in pieces], (row - s) % ratio) for a in range(kinds) for s in range(ratio)],
        axis=1,
    )
    return joined


def heads_out(grad, kinds, ratio):
    chips, cols = lax.axis_size("chip"), lax.axis_size("col")
    rows = 2 * chips
    row = 2 * lax.axis_index("chip") + lax.axis_index("core")
    block = grad.shape[0] // rows
    mine = lax.psum_scatter(grad, ROW, scatter_dimension=0, tiled=True)
    width = grad.shape[1] // (kinds * ratio)
    pieces = []
    for k in range(ratio):
        pairs = []
        for r in range(rows):
            for c in range(cols):
                s = (r - k) % ratio
                pairs.append((r * cols + c, (ratio * c + s) * cols + r // ratio))
        start = (row - k) % ratio * width
        piece = jnp.stack(
            [
                lax.dynamic_slice_in_dim(mine, a * ratio * width + start, width, 1)
                for a in range(kinds)
            ]
        )
        pieces.append(lax.ppermute(piece, ALL, pairs))
    return jnp.concatenate(
        [pick(pieces, (h - row) % ratio) for h in range(ratio)], axis=1
    ).astype(F32)


def sum_rows(values):
    total = values
    for axis in ROW:
        count = lax.axis_size(axis)
        step = 1
        while step < count:
            total = total + lax.ppermute(total, axis, [(i, i ^ step) for i in range(count)])
            step *= 2
    return total


def local(
    tokens,
    attn_gain,
    qkv_weight,
    query_gain,
    key_gain,
    out_weight,
    moe_gain,
    gate_up_weight,
    down_weight,
    segments,
    routes,
    route_gates,
    cotangent,
):
    cols = lax.axis_size("col")
    chips = lax.axis_size("chip")
    rows = 2 * chips
    col = lax.axis_index("col")
    core = lax.axis_index("core")
    row = 2 * lax.axis_index("chip") + core
    per_row, col_width = tokens.shape
    model_width = col_width * cols
    head_size = query_gain.shape[0]
    ratio = rows // cols
    head_width = model_width // cols

    experts_here, _, double_units = gate_up_weight.shape
    units = double_units // 2
    split = max(1, cols // experts_here)
    mine_count = experts_here * split // cols
    part_units = units // split
    capacity = 2 * rows * per_row * routes.shape[1] // (experts_here * rows)

    gate_up_parts = (
        gate_up_weight.reshape(experts_here, col_width, 2, split, part_units)
        .transpose(0, 3, 1, 2, 4)
        .reshape(cols, mine_count, col_width, 2 * part_units)
    )
    down_parts = down_weight.reshape(cols, mine_count, part_units, col_width)

    segs = gather_cols(segments)
    gain_all = gather_cols(attn_gain)
    tokens_all = gather_cols(tokens)
    quarter = col_width // 4
    gate_up_first = send_parts(gate_up_parts[:, :, :quarter])
    gate_up_second = send_parts(gate_up_parts[:, :, quarter : 2 * quarter])
    gate_up_last = send_parts(gate_up_parts[:, :, 2 * quarter :])
    qkv_in, out_in, cot_in, segs, gain_all, tokens_all, gate_up_first = fence(
        qkv_weight, out_weight, cotangent, segs, gain_all, tokens_all, gate_up_first
    )
    qkv_all = over_cores(over_chips(heads_in(qkv_in, ratio)))
    out_all = over_cores(over_chips(out_in))
    seg_row = lax.dynamic_index_in_dim(segs.reshape(rows, per_row), row, 0, keepdims=False)
    cot_all = lax.all_gather(cot_in, ALL, axis=0).reshape(rows, cols, per_row, col_width)

    first = row * experts_here
    expert_ids = first + (col * mine_count + jnp.arange(mine_count, dtype=jnp.int32)) // split
    place, gate, low, high = slot_places(routes, route_gates, expert_ids)

    cosine, sine = rope_tables(seg_row, head_size)
    stream_all = tokens_all.astype(F32)
    rate_one = lax.rsqrt(jnp.sum(stream_all * stream_all, axis=(0, 2)) / model_width + epsilon)
    rate_one = rate_one[:, None]
    normed_all = jnp.concatenate(
        [(stream_all[c] * rate_one * gain_all[c]).astype(BF16) for c in range(cols)], axis=1
    )
    qkv = jnp.dot(normed_all, qkv_all, preferred_element_type=F32)
    head_gains = jnp.stack([query_gain, key_gain])
    heads_low, logs = attend_forward(qkv, cosine, sine, seg_row, head_gains)
    heads_low, gate_up_second = fence(heads_low, gate_up_second)
    heads_all = gather_cols(heads_low)
    out_split = out_all.reshape(cols, head_width, col_width)
    stream = tokens.astype(F32)
    hidden_one = plain(
        stream + jnp.einsum("ctk,ckd->td", heads_all, out_split, preferred_element_type=F32)
    )
    rate_two = lax.rsqrt(
        width_total(jnp.sum(hidden_one * hidden_one, axis=-1)) / model_width + epsilon
    )[:, None]
    moe_in = plain((hidden_one * rate_two * moe_gain).astype(BF16))
    moe_in, gate_up_last, cot_all = fence(moe_in, gate_up_last, cot_all)
    gate_up = jnp.zeros((mine_count, model_width, 2 * part_units), BF16)
    gate_up = join_parts(gate_up_first, 1, gate_up, 0)
    gate_up = join_parts(gate_up_second, 1, gate_up, quarter)
    gate_up = join_parts(gate_up_last, 1, gate_up, 2 * quarter)

    moe_all = lax.all_gather(moe_in, ALL, axis=0).reshape(rows, cols, per_row, col_width)
    mine = jnp.reshape(core, (1,))
    others = 1 - mine
    grad_slot = gather_slots(cot_all, place, gate, low, high, capacity, True)
    moe_all, down_parts, grad_slot = fence(moe_all, down_parts, grad_slot)
    down = join_parts(send_parts(down_parts), 2)
    slot_inputs = gather_slots(moe_all, place, gate, low, high, capacity, False)

    gate_weight = gate_up[..., :part_units]
    up_weight = gate_up[..., part_units:]
    gate_pre = jnp.einsum(
        "ecd,edf->ecf", slot_inputs, gate_weight, preferred_element_type=F32
    ).astype(BF16)
    up_pre = jnp.einsum(
        "ecd,edf->ecf", slot_inputs, up_weight, preferred_element_type=F32
    ).astype(BF16)
    gate_wide = gate_pre.astype(F32)
    up_wide = up_pre.astype(F32)
    sigmoid_gate = jax.nn.sigmoid(gate_wide)
    activated = gate_wide * sigmoid_gate
    hidden = (activated * up_wide).astype(BF16)
    hidden, down = fence(hidden, down)

    combine = partial(
        combine_slots, place=place, gate=gate, low=low, high=high,
        chips=chips, per_row=per_row, parts=cols,
    )

    def feature_block(values, index):
        return lax.dynamic_slice_in_dim(values, index * col_width, col_width, 2)

    down_grads = []
    for mask in range(cols):
        part = jnp.einsum(
            "ecf,ecd->efd", hidden, feature_block(grad_slot, col ^ mask),
            preferred_element_type=F32,
        )
        down_grads.append(part.astype(BF16) if mask else part)
    down_grads, hidden = fence(down_grads, hidden)
    got_down = down_grads[:1] + [swap_cols(down_grads[mask], mask) for mask in range(1, cols)]

    expert_out = jnp.einsum("ecf,efd->ecd", hidden, down, preferred_element_type=F32).astype(BF16)
    out_other = combine(expert_out, core=others, scaled=True)
    out_other, grad_slot = fence(out_other, grad_slot)
    out_other = swap_cores(out_other)
    grad_hidden = jnp.einsum("ecd,efd->ecf", grad_slot, down, preferred_element_type=F32)
    grad_gate_pre = (
        grad_hidden * up_wide * sigmoid_gate * (1.0 + gate_wide * (1.0 - sigmoid_gate))
    ).astype(BF16)
    grad_up_pre = (grad_hidden * activated).astype(BF16)
    grad_inner = jnp.concatenate([grad_gate_pre, grad_up_pre], axis=-1)
    out_other, grad_inner = fence(out_other, grad_inner)
    out_partial = combine(expert_out, core=mine, scaled=True, more=(out_other,))
    out_partial, grad_inner, got_down = fence(out_partial, grad_inner, got_down)
    out_partial = plain(lax.psum_scatter(out_partial, "col", scatter_dimension=0, tiled=True)[0])

    grad_slot_in = jnp.einsum(
        "ecf,edf->ecd", grad_inner, gate_up, preferred_element_type=F32
    ).astype(BF16)
    grad_other = combine(grad_slot_in, core=others, scaled=False)
    grad_other, grad_inner = fence(grad_other, grad_inner)
    grad_other = swap_cores(grad_other)
    inner_parts = []
    for mask in range(cols):
        part = jnp.einsum(
            "ecd,ecf->edf", feature_block(slot_inputs, col ^ mask), grad_inner,
            preferred_element_type=F32,
        )
        inner_parts.append(part.astype(BF16) if mask else part)
    grad_other, inner_parts[1] = fence(grad_other, inner_parts[1])
    grad_partial = combine(grad_slot_in, core=mine, scaled=False, more=(grad_other,))
    grad_partial, out_partial = fence(grad_partial, out_partial)
    grad_partial = plain(lax.psum_scatter(grad_partial, "col", scatter_dimension=0, tiled=True)[0])
    grad_partial, inner_parts, out_partial = fence(grad_partial, inner_parts, out_partial)
    grad_moe_in = plain(lax.psum_scatter(grad_partial, "chip", scatter_dimension=0, tiled=True)[0])
    near = cols // 2 + 1
    far_parts = inner_parts[near:]
    got_inner = inner_parts[:1] + [swap_cols(inner_parts[mask], mask) for mask in range(1, near)]
    grad_moe_in, got_inner, out_partial, far_parts = fence(
        grad_moe_in, got_inner, out_partial, far_parts
    )
    grad_moe_in = grad_moe_in.astype(F32)

    gain_two = jnp.sum(grad_moe_in * hidden_one * rate_two, axis=0)
    grad_hidden_one = cotangent.astype(F32) + norm_back(
        grad_moe_in, hidden_one, rate_two, moe_gain, model_width
    )
    grad_branch = plain(grad_hidden_one.astype(BF16))
    grad_heads = sum_cols(
        jnp.einsum("td,ckd->ctk", grad_branch, out_split, preferred_element_type=F32).astype(BF16)
    ).astype(BF16)
    grad_heads, out_partial, far_parts = fence(grad_heads, out_partial, far_parts)
    far_parts = [swap_cols(part, near + i) for i, part in enumerate(far_parts)]
    moe_result = lax.psum_scatter(out_partial, "chip", scatter_dimension=0, tiled=True)[0]
    grad_out_weight = lax.psum_scatter(
        jnp.einsum("ctk,td->ckd", heads_all, grad_branch, preferred_element_type=F32)
        .astype(BF16)
        .reshape(model_width, col_width),
        ROW,
        scatter_dimension=0,
        tiled=True,
    ).astype(F32)
    grad_projected, grad_gains = attend_backward(
        qkv, cosine, sine, seg_row, head_gains, grad_heads, logs
    )
    grad_projected, far_parts, moe_result = fence(grad_projected, far_parts, moe_result)
    output = (hidden_one + moe_result.astype(F32)).astype(BF16)
    got_inner = got_inner + far_parts
    normed_parts = jnp.einsum(
        "tk,cfk->ctf",
        grad_projected,
        qkv_all.reshape(cols, col_width, 3 * head_width),
        preferred_element_type=F32,
    ).astype(BF16)
    normed_parts, grad_projected, got_inner, got_down = fence(
        normed_parts, grad_projected, got_inner, got_down
    )
    grad_normed = sum_cols(normed_parts)
    grad_qkv = heads_out(
        jnp.einsum("td,tk->dk", normed_all, grad_projected, preferred_element_type=F32).astype(BF16),
        3,
        ratio,
    )

    scaled_grad = grad_normed * attn_gain
    gain_one = jnp.sum(grad_normed * stream * rate_one, axis=0)
    across = jnp.sum(scaled_grad * stream, axis=-1)
    small = width_total(jnp.concatenate([across, grad_gains.reshape(-1)]))
    across = small[:per_row, None]
    gains = sum_rows(jnp.concatenate([gain_one, gain_two, small[per_row:]]))
    grad_attn_gain = gains[:col_width]
    grad_moe_gain = gains[col_width : 2 * col_width]
    grad_query_gain = gains[2 * col_width : 2 * col_width + head_size]
    grad_key_gain = gains[2 * col_width + head_size :]
    grad_tokens = (
        grad_hidden_one
        + rate_one * scaled_grad
        - stream * rate_one * rate_one * rate_one * across / model_width
    ).astype(BF16)

    grad_gate_up = jnp.zeros((cols, mine_count, col_width, 2 * part_units), F32)
    grad_down = jnp.zeros((cols, mine_count, part_units, col_width), F32)
    for mask in range(cols):
        there = col ^ mask
        grad_gate_up = lax.dynamic_update_index_in_dim(
            grad_gate_up, got_inner[mask].astype(F32), there, 0
        )
        grad_down = lax.dynamic_update_index_in_dim(grad_down, got_down[mask].astype(F32), there, 0)
    grad_gate_up = (
        grad_gate_up.reshape(experts_here, split, col_width, 2, part_units)
        .transpose(0, 2, 3, 1, 4)
        .reshape(experts_here, col_width, double_units)
    )
    grad_down = grad_down.reshape(experts_here, units, col_width)
    return (
        output,
        grad_tokens,
        grad_attn_gain,
        grad_qkv,
        grad_query_gain,
        grad_key_gain,
        grad_out_weight,
        grad_moe_gain,
        grad_gate_up,
        grad_down,
    )


def solution(mesh):
    rows, cols = mesh.devices.shape
    fine = Mesh(mesh.devices.reshape(rows // 2, 2, cols), ("chip", "core", "col"))
    return jax.shard_map(
        local,
        mesh=fine,
        in_specs=(
            P(ROW, "col"),
            P("col"),
            P(None, "col", ROW),
            P(),
            P(),
            P(ROW, "col"),
            P("col"),
            P(ROW, "col", None),
            P(ROW, None, "col"),
            P("col", None),
            P(),
            P(),
            P(ROW, "col"),
        ),
        out_specs=(
            P(ROW, "col"),
            P(ROW, "col"),
            P("col"),
            P(None, "col", ROW),
            P(),
            P(),
            P(ROW, "col"),
            P("col"),
            P(ROW, "col", None),
            P(ROW, None, "col"),
        ),
        check_vma=False,
    )
```

time: 2400 us -> 1810 us (0.75)
  waiting for transfers between devices: 1290 us -> 882 us
  local copies, waits for them, and re-layouts: 313 us -> 164 us
  blocking collectives: 106 us -> 22.3 us
  Pallas kernels: 184 us -> 254 us
  starting transfers between devices: 26.3 us -> 77.7 us
  matrix products: 330 us -> 298 us
    ppermute x4 -> x13, waiting for transfers between devices: 60.5 us -> 233 us  [the longest x6 111 us: swap_chips(): return lax.ppermute(values, 'chip', [(i, i ^ mask) for i in range(count)])]
    ppermute x12 -> x36, waiting for transfers between devices: 555 us -> 385 us  [swap_cols(): return lax.ppermute(values, 'col', [(i, i ^ mask) for i in range(count)])]
    reduce_scatter x2, waiting for transfers between devices: 142 us -> 0.01 us  [the longest x1 0.01 us: local(): lax.psum_scatter(grad_partial, 'chip', scatter_dimension=0, tiled=True)[0]]
    all_gather x5 -> x1, waiting for transfers between devices: 120 us -> 0.02 us  [local(): lax.all_gather(cot_in, ALL, axis=0).reshape(rows, cols, per_row, col_width)]
    unnamed x18 -> x10, waiting for transfers between devices: 245 us -> 137 us
    psum x2 -> x0, blocking collectives: 74.5 us -> none  [the longest x1 40.8 us: local(): grad_query_gain, grad_key_gain = lax.psum((gain_query, gain_key), ALL)]
    pallas_call x2 -> x4, Pallas kernels: 73.5 us -> 131 us  [the longest x2 82.5 us: gather_slots(): pl.pallas_call(partial(gather_kernel, scaled, each), grid_spec=pltpu.Pref...]
    all_gather x1, waiting for transfers between devices: 163 us -> 108 us  [local(): lax.all_gather(moe_in, ALL, axis=0).reshape(rows, cols, per_row, col_width)]
  transfers between devices with their start and end apart: 32 -> 61, of which waited for: 17 -> 24; matrix products, arithmetic and copies ran while one was open for 23% -> 26% of each run, Pallas kernels for 5% -> 12%
where the time goes in v2:
time: 1810 us
  waiting for transfers between devices  882 us (49%)
  matrix products  298 us (16%)
  Pallas kernels  254 us (14%)
  local copies, waits for them, and re-layouts  164 us (9%)
  other arithmetic  91.8 us (5%)
  starting transfers between devices  77.7 us (4%)
  blocking collectives  22.3 us (1%)
    ppermute x36, waiting for transfers between devices, swap_cols(): return lax.ppermute(values, 'col', [(i, i ^ mask) for i in range(count)])  385 us
    unnamed x10, waiting for transfers between devices  137 us
    pallas_call x4, Pallas kernels, combine_slots(): pl.pallas_call(partial(combine_kernel, scaled, each), grid_spec=pltpu.Pre...  123 us
    ppermute x6, waiting for transfers between devices, swap_chips(): return lax.ppermute(values, 'chip', [(i, i ^ mask) for i in range(count)])  111 us
    all_gather x1, waiting for transfers between devices, local(): lax.all_gather(moe_in, ALL, axis=0).reshape(rows, cols, per_row, col_width)  108 us
    pallas_call x2, Pallas kernels, gather_slots(): pl.pallas_call(partial(gather_kernel, scaled, each), grid_spec=pltpu.Pref...  82.5 us
    ppermute x2, waiting for transfers between devices, heads_in(): pieces.append(lax.ppermute(piece, ALL, pairs))  72.3 us
    dot_general x4, matrix products, local(): jnp.einsum('ecd,ecf->edf', feature_block(slot_inputs, col ^ mask), grad_i...  67.6 us
  transfers between devices with their start and end apart: 61, of which 24 were waited for; matrix products, arithmetic and copies ran while one was open for 26% of the time, Pallas kernels for 12%

profile of v2, /device:TPU:3, one launch (start us, length us, event | category | flops | bytes accessed | tf_op | source)
XLA Modules:
  0.0 1805.7 jit_solution(11468290366821455170)
XLA Ops:
  37.4 19.3 %collective-permute-done.2 = s32[2,1024]{1,0:T(2,128)S(1)} collective-permute-done((s32[2,1024]{1,0:T(2,128)S(1)}, s32[2,1024]{1,0:T(2,128)S(1)}, u32[]{:S(2)}, u32[]{:S(2)}) %collective-permute-start.2) | collective-permute-done | bytes 8224 | tf_op jit(solution)/shard_map/ppermute | solution.py:404
  65.6 36.2 %collective-permute-done.10 = bf16[2,128,2048]{2,1,0:T(8,128)(2,1)S(1)} collective-permute-done((bf16[2,128,2048]{2,1,0:T(8,128)(2,1)}, bf16[2,128,2048]{2,1,0:T(8,128)(2,1)S(1)}, u32[]{:S(2)}, u32[]{:S(2)}) %collective-permute-start.10) | collective-permute-done | bytes 1048608 | tf_op jit(solution)/shard_map/ppermute | solution.py:404
  111.9 59.8 %collective-permute-done.12 = bf16[3,256,256]{2,1,0:T(8,128)(2,1)S(1)} collective-permute-done((bf16[3,256,256]{2,1,0:T(8,128)(2,1)S(1)}, bf16[3,256,256]{2,1,0:T(8,128)(2,1)S(1)}, u32[]{:S(2)}, u32[]{:S(2)}) %collective-permute-start.12) | collective-permute-done | bytes 393248 | tf_op jit(solution)/shard_map/ppermute | solution.py:502
  199.5 50.7 %collective-permute-done.14 = bf16[256,1536]{1,0:T(8,128)(2,1)} collective-permute-done((bf16[256,1536]{1,0:T(8,128)(2,1)}, bf16[256,1536]{1,0:T(8,128)(2,1)}, u32[]{:S(2)}, u32[]{:S(2)}) %collective-permute-start.14) | collective-permute-done | bytes 786464 | tf_op jit(solution)/shard_map/ppermute | solution.py:461
  251.5 34.5 %collective-permute-done.15 = bf16[256,1536]{1,0:T(8,128)(2,1)S(1)} collective-permute-done((bf16[256,1536]{1,0:T(8,128)(2,1)}, bf16[256,1536]{1,0:T(8,128)(2,1)S(1)}, u32[]{:S(2)}, u32[]{:S(2)}) %collective-permute-start.15) | collective-permute-done | bytes 786464 | tf_op jit(solution)/shard_map/ppermute | solution.py:461
  307.5 25.4 %collective-permute-done.25 = bf16[256,512]{1,0:T(8,128)(2,1)} collective-permute-done((bf16[256,512]{1,0:T(8,128)(2,1)S(1)}, bf16[256,512]{1,0:T(8,128)(2,1)}, u32[]{:S(2)}, u32[]{:S(2)}) %collective-permute-start.25) | collective-permute-done | bytes 262176 | tf_op jit(solution)/shard_map/ppermute | solution.py:461
  332.8 18.3 %collective-permute-start.20 = (bf16[2,128,2048]{2,1,0:T(8,128)(2,1)}, bf16[2,128,2048]{2,1,0:T(8,128)(2,1)}, u32[]{:S(2)}, u32[]{:S(2)}) collective-permute-start(bf16[2,128,2048]{2,1,0:T(8,128)(2,1)} %get-tuple-element.198), channel_id=1, source_target_pairs={{0,3},{1,2},{2,1},{3,0},{4,7},{5,6},{6,5},{7,4},{8,11},{9,10},{10,... | collective-permute-start | bytes 3145736 | tf_op jit(solution)/shard_map/ppermute | solution.py:404
  368.9 19.2 %attend_forward.1 = (bf16[1024,512]{1,0:T(8,128)(2,1)}, f32[1024,512]{1,0:T(8,128)}) custom-call(f32[1024,1536]{1,0:T(8,128)} %fusion.92.query_ref.key_ref.value_ref, f32[1024,1536]{1,0:T(8,128)} %fusion.92.query_ref.key_ref.value_ref, f32[1024,1536]{1,0:T(8,128)} %fusion.92.query_ref.key_ref.value_ref, f32[1024,128]{1,0:T(8,128)} %get-tuple-element.219.cos_ref, ...), custom_call_target="tpu_custom_call" | custom-call | flops 2147483648 | bytes 9437184 | tf_op jit(solution)/shard_map/attend_forward/pallas_call | solution.py:107
  413.9 129.2 %collective-permute-done.22 = bf16[1024,512]{1,0:T(8,128)(2,1)S(1)} collective-permute-done((bf16[1024,512]{1,0:T(8,128)(2,1)S(1)}, bf16[1024,512]{1,0:T(8,128)(2,1)S(1)}, u32[]{:S(2)}, u32[]{:S(2)}) %collective-permute-start.22) | collective-permute-done | bytes 1048608 | tf_op jit(solution)/shard_map/ppermute | solution.py:404
  619.6 41.4 %gather_slots.2 = bf16[2,2048,2048]{2,1,0:T(8,128)(2,1)} custom-call(s32[2,16]{1,0:T(2,128)} %get-tuple-element.174.low_ref, s32[2,16]{1,0:T(2,128)} %get-tuple-element.173.high_ref, bf16[8,4,1024,512]{3,2,1,0:T(8,128)(2,1)} %bitcast.323, bf16[8,4,1024,512]{3,2,1,0:T(8,128)(2,1)} %bitcast.324, ...), custom_call_target="tpu_custom_call" | custom-call | flops 25769803776 | bytes 50331648 | tf_op jit(solution)/shard_map/gather_slots/pallas_call | solution.py:296
  661.0 108.3 %all-gather.7.cloned.1.call-done = bf16[32768,512]{1,0:T(8,128)(2,1)} async-done(((bf16[1024,512]{1,0:T(8,128)(2,1)}), bf16[32768,512]{1,0:T(8,128)(2,1)}) %all-gather.7.cloned.1.call-update) | async-done | bytes 33554448 | tf_op jit(solution)/shard_map/all_gather | solution.py:635
  777.4 41.1 %gather_slots.3 = bf16[2,2048,2048]{2,1,0:T(8,128)(2,1)} custom-call(s32[2,16]{1,0:T(2,128)} %get-tuple-element.174.low_ref, s32[2,16]{1,0:T(2,128)} %get-tuple-element.173.high_ref, bf16[8,4,1024,512]{3,2,1,0:T(8,128)(2,1)} %bitcast.325, bf16[8,4,1024,512]{3,2,1,0:T(8,128)(2,1)} %bitcast.326, ...), custom_call_target="tpu_custom_call" | custom-call | flops 25769803776 | bytes 50331648 | tf_op jit(solution)/shard_map/gather_slots/pallas_call | solution.py:296
  818.5 24.5 %fusion.12 = bf16[2,2048,1024]{1,2,0:T(8,128)(2,1)} fusion(bf16[2,2048,2048]{2,1,0:T(8,128)(2,1)} %gather_slots.3, bf16[2,2048,2048]{1,2,0:T(8,128)(2,1)} %constant_dynamic-update-slice_fusion.3), kind=kOutput, calls=%fused_computation.28 | convolution fusion | flops 17184063488 | bytes 33554432 | tf_op jit(solution)/shard_map/ecd,edf->ecf/dot_general | solution.py:645
  843.0 27.9 %fusion = (bf16[2,2048,1024]{1,2,0:T(8,128)(2,1)}, bf16[2,2048,1024]{1,2,0:T(8,128)(2,1)}) fusion(bf16[2,2048,1024]{1,2,0:T(8,128)(2,1)} %fusion.12, bf16[2,2048,2048]{2,1,0:T(8,128)(2,1)} %gather_slots.3, bf16[2,2048,2048]{1,2,0:T(8,128)(2,1)} %constant_dynamic-update-slice_fusion.3), kind=kOutput, calls=%fused_computation.5 | convolution fusion | flops 17217617920 | bytes 50331648 | tf_op jit(solution)/shard_map/ecd,edf->ecf/dot_general | solution.py:648
  915.4 25.8 %convolution_convert_fusion.slots_ref = bf16[2,2048,2048]{2,1,0:T(8,128)(2,1)} fusion(bf16[2,2048,1024]{1,2,0:T(8,128)(2,1)} %get-tuple-element.115, bf16[2,1024,2048]{2,1,0:T(8,128)(2,1)} %copy-done.8), kind=kOutput, calls=%fused_computation.15 | convolution fusion | flops 17188257792 | bytes 33554432 | tf_op jit(solution)/shard_map/ecf,efd->ecd/dot_general | solution.py:676
  941.2 29.6 %combine_slots.4 = bf16[4,4,1024,512]{3,2,1,0:T(8,128)(2,1)} custom-call(s32[2,16]{1,0:T(2,128)} %get-tuple-element.174.low_ref, s32[2,16]{1,0:T(2,128)} %get-tuple-element.173.high_ref, s32[1]{0:T(128)S(6)} %sub.52.core_ref, bf16[2,2048,2048]{2,1,0:T(8,128)(2,1)} %convolution_convert_fusion.slots_ref, ...), custom_call_target="tpu_custom_call" | custom-call | flops 12884901888 | bytes 33554432 | tf_op jit(solution)/shard_map/combine_slots/pallas_call | solution.py:361
  973.4 32.9 %fusion.3 = (bf16[2,2048,1024]{1,2,0:T(8,128)(2,1)}, bf16[2,2048,1024]{1,2,0:T(8,128)(2,1)}) fusion(bf16[2,2048,1024]{1,2,0:T(8,128)(2,1)} %get-tuple-element.231, bf16[2,2048,1024]{1,2,0:T(8,128)(2,1)} %fusion.12, bf16[2,2048,2048]{2,1,0:T(8,128)(2,1)} %gather_slots.2, bf16[2,1024,2048]{2,1,0:T(8,128)(2,1)} %copy-done.8), kind=kOutput, calls=%fused_computation.8 | convolution fusion | flops 17242783744 | bytes 58720256 | tf_op jit(solution)/shard_map/ecd,efd->ecf/dot_general | solution.py:680
  1020.1 33.0 %combine_slots.5 = bf16[4,4,1024,512]{3,2,1,0:T(8,128)(2,1)} custom-call(s32[2,16]{1,0:T(2,128)} %get-tuple-element.174.low_ref, s32[2,16]{1,0:T(2,128)} %get-tuple-element.173.high_ref, s32[1]{0:T(128)} %bitcast.62.core_ref, bf16[2,2048,2048]{2,1,0:T(8,128)(2,1)} %convolution_convert_fusion.slots_ref, ...), custom_call_target="tpu_custom_call" | custom-call | flops 12884901888 | bytes 33554432 | tf_op jit(solution)/shard_map/combine_slots/pallas_call | solution.py:361
  1064.0 42.5 %convolution_convert_fusion.1.slots_ref = bf16[2,2048,2048]{2,1,0:T(8,128)(2,1)} fusion(bf16[2,2048,2048]{1,2,0:T(8,128)(2,1)} %pad_maximum_fusion, bf16[2,2048,2048]{1,2,0:T(8,128)(2,1)} %constant_dynamic-update-slice_fusion.3), kind=kOutput, calls=%fused_computation.16 | convolution fusion | flops 34368126976 | bytes 50331648 | tf_op jit(solution)/shard_map/ecf,edf->ecd/dot_general | solution.py:691
  1106.5 28.6 %combine_slots.6 = bf16[4,4,1024,512]{3,2,1,0:T(8,128)(2,1)} custom-call(s32[2,16]{1,0:T(2,128)} %get-tuple-element.174.low_ref, s32[2,16]{1,0:T(2,128)} %get-tuple-element.173.high_ref, s32[1]{0:T(128)S(6)} %sub.52.core_ref, bf16[2,2048,2048]{2,1,0:T(8,128)(2,1)} %convolution_convert_fusion.1.slots_ref, ...), custom_call_target="tpu_custom_call" | custom-call | flops 12884901888 | bytes 33554432 | tf_op jit(solution)/shard_map/combine_slots/pallas_call | solution.py:361
  1135.1 16.8 fusion.34
  1160.6 32.2 %combine_slots.7 = bf16[4,4,1024,512]{3,2,1,0:T(8,128)(2,1)} custom-call(s32[2,16]{1,0:T(2,128)} %get-tuple-element.174.low_ref, s32[2,16]{1,0:T(2,128)} %get-tuple-element.173.high_ref, s32[1]{0:T(128)} %bitcast.62.core_ref, bf16[2,2048,2048]{2,1,0:T(8,128)(2,1)} %convolution_convert_fusion.1.slots_ref, ...), custom_call_target="tpu_custom_call" | custom-call | flops 12884901888 | bytes 33554432 | tf_op jit(solution)/shard_map/combine_slots/pallas_call | solution.py:361
  1192.7 30.1 %reduce-scatter.19.cloned.1.call-done = bf16[1,4,1024,512]{3,2,1,0:T(8,128)(2,1)} async-done(((bf16[4,4,1024,512]{3,2,1,0:T(8,128)(2,1)}), bf16[1,4,1024,512]{3,2,1,0:T(8,128)(2,1)}) %reduce-scatter.19.cloned.1.call-update) | async-done | bytes 4194320
  1222.9 16.8 fusion.40
  1256.3 17.4 fusion.22
  1273.7 106.5 %reduce-scatter.21.cloned.1.call-done = bf16[1,4,1024,512]{3,2,1,0:T(8,128)(2,1)} async-done(((bf16[4,4,1024,512]{3,2,1,0:T(8,128)(2,1)}), bf16[1,4,1024,512]{3,2,1,0:T(8,128)(2,1)}) %reduce-scatter.21.cloned.1.call-update) | async-done | bytes 4194320
  1381.9 90.2 %collective-permute-done.39 = bf16[2,512,2048]{2,1,0:T(8,128)(2,1)} collective-permute-done((bf16[2,512,2048]{2,1,0:T(8,128)(2,1)}, bf16[2,512,2048]{2,1,0:T(8,128)(2,1)}, u32[]{:S(2)}, u32[]{:S(2)}) %collective-permute-start.39) | collective-permute-done | bytes 4194336 | tf_op jit(solution)/shard_map/ppermute | solution.py:404
  1488.8 18.4 %collective-permute-done.41 = bf16[1024,512]{1,0:T(8,128)(2,1)S(1)} collective-permute-done((bf16[1024,512]{1,0:T(8,128)(2,1)S(1)}, bf16[1024,512]{1,0:T(8,128)(2,1)S(1)}, u32[]{:S(2)}, u32[]{:S(2)}) %collective-permute-start.41) | collective-permute-done | bytes 1048608 | tf_op jit(solution)/shard_map/ppermute | solution.py:404
  1508.6 20.7 %collective-permute-done.43 = bf16[1024,512]{1,0:T(8,128)(2,1)S(1)} collective-permute-done((bf16[1024,512]{1,0:T(8,128)(2,1)S(1)}, bf16[1024,512]{1,0:T(8,128)(2,1)S(1)}, u32[]{:S(2)}, u32[]{:S(2)}) %collective-permute-start.43) | collective-permute-done | bytes 1048608 | tf_op jit(solution)/shard_map/ppermute | solution.py:404
  1539.9 28.9 %attend_backward.1 = (bf16[1024,1536]{1,0:T(8,128)(2,1)}, f32[2,128]{1,0:T(2,128)}) custom-call(f32[1024,1536]{1,0:T(8,128)} %fusion.92.query_ref.key_ref.value_ref, f32[1024,1536]{1,0:T(8,128)} %fusion.92.query_ref.key_ref.value_ref, f32[1024,1536]{1,0:T(8,128)} %fusion.92.query_ref.key_ref.value_ref, f32[1024,128]{1,0:T(8,128)} %get-tuple-element.219.cos_ref, ...), custom_call_target="tpu_custom_call" | custom-call | flops 5368709120 | bytes 12582912 | tf_op jit(solution)/shard_map/attend_backward/pallas_call | solution.py:191
  1568.8 49.7 %collective-permute-done.44 = bf16[2,512,2048]{2,1,0:T(8,128)(2,1)} collective-permute-done((bf16[2,512,2048]{2,1,0:T(8,128)(2,1)}, bf16[2,512,2048]{2,1,0:T(8,128)(2,1)}, u32[]{:S(2)}, u32[]{:S(2)}) %collective-permute-start.44) | collective-permute-done | bytes 4194336 | tf_op jit(solution)/shard_map/ppermute | solution.py:404
  1746.7 41.9 %collective-permute-done.52 = bf16[3,256,256]{2,1,0:T(8,128)(2,1)S(1)} collective-permute-done((bf16[3,256,256]{2,1,0:T(8,128)(2,1)S(1)}, bf16[3,256,256]{2,1,0:T(8,128)(2,1)S(1)}, u32[]{:S(2)}, u32[]{:S(2)}) %collective-permute-start.52) | collective-permute-done | bytes 393248 | tf_op jit(solution)/shard_map/ppermute | solution.py:531
  (388 shorter events, 492.1 us)
Async XLA Ops:
  7.2 548.9 %all-gather.5.cloned.1.call-start = ((), (), s32[]{:S(2)}) async-start(), calls=%async_computation.10 | async-start | bytes 34603008 | tf_op jit(solution)/shard_map/all_gather | solution.py:602
  37.3 64.5 %collective-permute-start.10 = (bf16[2,128,2048]{2,1,0:T(8,128)(2,1)}, bf16[2,128,2048]{2,1,0:T(8,128)(2,1)S(1)}, u32[]{:S(2)}, u32[]{:S(2)}) collective-permute-start(bf16[2,128,2048]{2,1,0:T(8,128)(2,1)} %get-tuple-element.203), channel_id=1, source_target_pairs={{0,2},{1,3},{2,0},{3,1},{4,6},{5,7},{6,4},{7,5},{8,10},{9,11},{10,... | collective-permute-start | bytes 3145736 | tf_op jit(solution)/shard_map/ppermute | solution.py:404
  104.1 665.2 %all-gather.7.cloned.1.call-start = ((), (), s32[]{:S(2)}) async-start(), calls=%async_computation.11 | async-start | bytes 34603008 | tf_op jit(solution)/shard_map/all_gather | solution.py:635
  105.4 66.3 %collective-permute-start.12 = (bf16[3,256,256]{2,1,0:T(8,128)(2,1)S(1)}, bf16[3,256,256]{2,1,0:T(8,128)(2,1)S(1)}, u32[]{:S(2)}, u32[]{:S(2)}) collective-permute-start(bf16[3,256,256]{2,1,0:T(8,128)(2,1)S(1)} %get-tuple-element.216), channel_id=1, source_target_pairs={{0,4},{1,12},{2,20},{3,28},{4,0},{5,8},{6,16},{7,24},{8,5},{9,13},... | collective-permute-start | bytes 1179656 | tf_op jit(solution)/shard_map/ppermute | solution.py:502
  109.7 74.5 %collective-permute-start.13 = (bf16[3,256,256]{2,1,0:T(8,128)(2,1)S(1)}, bf16[3,256,256]{2,1,0:T(8,128)(2,1)S(1)}, u32[]{:S(2)}, u32[]{:S(2)}) collective-permute-start(bf16[3,256,256]{2,1,0:T(8,128)(2,1)S(1)} %get-tuple-element.217), channel_id=1, source_target_pairs={{0,0},{1,8},{2,16},{3,24},{4,4},{5,12},{6,20},{7,28},{8,1},{9,9},{... | collective-permute-start | bytes 1179656 | tf_op jit(solution)/shard_map/ppermute | solution.py:502
  188.3 61.9 %collective-permute-start.14 = (bf16[256,1536]{1,0:T(8,128)(2,1)}, bf16[256,1536]{1,0:T(8,128)(2,1)}, u32[]{:S(2)}, u32[]{:S(2)}) collective-permute-start(bf16[256,1536]{1,0:T(8,128)(2,1)} %bitcast_dynamic-update-slice_fusion.19), channel_id=1, source_target_pairs={{0,8},{8,0},{16,24},{24,16},{1,9},{9,1},{17,25},{25,17},{2,10},{10... | collective-permute-start | bytes 2359304 | tf_op jit(solution)/shard_map/ppermute | solution.py:461
  192.8 195.3 %collective-permute-start.18 = (bf16[2,128,2048]{2,1,0:T(8,128)(2,1)}, bf16[2,128,2048]{2,1,0:T(8,128)(2,1)}, u32[]{:S(2)}, u32[]{:S(2)}) collective-permute-start(bf16[2,128,2048]{2,1,0:T(8,128)(2,1)} %get-tuple-element.200), channel_id=1, source_target_pairs={{0,1},{1,0},{2,3},{3,2},{4,5},{5,4},{6,7},{7,6},{8,9},{9,8},{10,11... | collective-permute-start | bytes 3145736 | tf_op jit(solution)/shard_map/ppermute | solution.py:404
  192.8 195.3 %collective-permute-start.19 = (bf16[2,128,2048]{2,1,0:T(8,128)(2,1)}, bf16[2,128,2048]{2,1,0:T(8,128)(2,1)}, u32[]{:S(2)}, u32[]{:S(2)}) collective-permute-start(bf16[2,128,2048]{2,1,0:T(8,128)(2,1)} %get-tuple-element.199), channel_id=1, source_target_pairs={{0,2},{1,3},{2,0},{3,1},{4,6},{5,7},{6,4},{7,5},{8,10},{9,11},{10,... | collective-permute-start | bytes 3145736 | tf_op jit(solution)/shard_map/ppermute | solution.py:404
  193.5 109.7 %collective-permute-start.24 = (bf16[256,512]{1,0:T(8,128)(2,1)S(1)}, bf16[256,512]{1,0:T(8,128)(2,1)}, u32[]{:S(2)}, u32[]{:S(2)}) collective-permute-start(bf16[256,512]{1,0:T(8,128)(2,1)S(1)} %copy-done.38), channel_id=1, source_target_pairs={{0,8},{8,0},{16,24},{24,16},{1,9},{9,1},{17,25},{25,17},{2,10},{10... | collective-permute-start | bytes 786440 | tf_op jit(solution)/shard_map/ppermute | solution.py:461
  195.0 91.0 %collective-permute-start.15 = (bf16[256,1536]{1,0:T(8,128)(2,1)}, bf16[256,1536]{1,0:T(8,128)(2,1)S(1)}, u32[]{:S(2)}, u32[]{:S(2)}) collective-permute-start(bf16[256,1536]{1,0:T(8,128)(2,1)} %bitcast_dynamic-update-slice_fusion.19), channel_id=1, source_target_pairs={{0,16},{8,24},{16,0},{24,8},{1,17},{9,25},{17,1},{25,9},{2,18},{10... | collective-permute-start | bytes 2359304 | tf_op jit(solution)/shard_map/ppermute | solution.py:461
  286.1 68.2 %collective-permute-start.17 = (bf16[4,256,1536]{2,1,0:T(8,128)(2,1)S(1)}, bf16[4,256,1536]{2,1,0:T(8,128)(2,1)}, u32[]{:S(2)}, u32[]{:S(2)}) collective-permute-start(bf16[4,256,1536]{2,1,0:T(8,128)(2,1)S(1)} %bitcast_dynamic-update-slice_fusion.11), channel_id=1, source_target_pairs={{0,4},{4,0},{1,5},{5,1},{2,6},{6,2},{3,7},{7,3},{8,12},{12,8},{9,1... | collective-permute-start | bytes 9437192 | tf_op jit(solution)/shard_map/ppermute | solution.py:399
  406.4 149.6 %collective-permute-start.28 = (bf16[2,256,2048]{2,1,0:T(8,128)(2,1)}, bf16[2,256,2048]{2,1,0:T(8,128)(2,1)}, u32[]{:S(2)}, u32[]{:S(2)}) collective-permute-start(bf16[2,256,2048]{2,1,0:T(8,128)(2,1)} %get-tuple-element.188), channel_id=1, source_target_pairs={{0,1},{1,0},{2,3},{3,2},{4,5},{5,4},{6,7},{7,6},{8,9},{9,8},{10,11... | collective-permute-start | bytes 6291464 | tf_op jit(solution)/shard_map/ppermute | solution.py:404
  406.4 149.6 %collective-permute-start.29 = (bf16[2,256,2048]{2,1,0:T(8,128)(2,1)}, bf16[2,256,2048]{2,1,0:T(8,128)(2,1)}, u32[]{:S(2)}, u32[]{:S(2)}) collective-permute-start(bf16[2,256,2048]{2,1,0:T(8,128)(2,1)} %get-tuple-element.187), channel_id=1, source_target_pairs={{0,2},{1,3},{2,0},{3,1},{4,6},{5,7},{6,4},{7,5},{8,10},{9,11},{10,... | collective-permute-start | bytes 6291464 | tf_op jit(solution)/shard_map/ppermute | solution.py:404
  406.5 136.6 %collective-permute-start.22 = (bf16[1024,512]{1,0:T(8,128)(2,1)S(1)}, bf16[1024,512]{1,0:T(8,128)(2,1)S(1)}, u32[]{:S(2)}, u32[]{:S(2)}) collective-permute-start(bf16[1024,512]{1,0:T(8,128)(2,1)S(1)} %copy-done.32), channel_id=1, source_target_pairs={{0,2},{1,3},{2,0},{3,1},{4,6},{5,7},{6,4},{7,5},{8,10},{9,11},{10,... | collective-permute-start | bytes 3145736 | tf_op jit(solution)/shard_map/ppermute | solution.py:404
  407.9 135.2 %collective-permute-start.23 = (bf16[1024,512]{1,0:T(8,128)(2,1)S(1)}, bf16[1024,512]{1,0:T(8,128)(2,1)S(1)}, u32[]{:S(2)}, u32[]{:S(2)}) collective-permute-start(bf16[1024,512]{1,0:T(8,128)(2,1)S(1)} %copy-done.32), channel_id=1, source_target_pairs={{0,3},{1,2},{2,1},{3,0},{4,7},{5,6},{6,5},{7,4},{8,11},{9,10},{10,... | collective-permute-start | bytes 3145736 | tf_op jit(solution)/shard_map/ppermute | solution.py:404
  413.3 142.8 %collective-permute-start.30 = (bf16[2,256,2048]{2,1,0:T(8,128)(2,1)}, bf16[2,256,2048]{2,1,0:T(8,128)(2,1)}, u32[]{:S(2)}, u32[]{:S(2)}) collective-permute-start(bf16[2,256,2048]{2,1,0:T(8,128)(2,1)} %get-tuple-element.186), channel_id=1, source_target_pairs={{0,3},{1,2},{2,1},{3,0},{4,7},{5,6},{6,5},{7,4},{8,11},{9,10},{10,... | collective-permute-start | bytes 6291464 | tf_op jit(solution)/shard_map/ppermute | solution.py:404
  556.1 666.7 %reduce-scatter.19.cloned.1.call-start = ((), (), s32[]{:S(2)}) async-start(), calls=%async_computation.12 | async-start | bytes 20971520
  774.8 99.4 %collective-permute-start.31 = (bf16[2,1024,512]{2,1,0:T(8,128)(2,1)}, bf16[2,1024,512]{2,1,0:T(8,128)(2,1)}, u32[]{:S(2)}, u32[]{:S(2)}) collective-permute-start(bf16[2,1024,512]{2,1,0:T(8,128)(2,1)} %get-tuple-element.185), channel_id=1, source_target_pairs={{0,1},{1,0},{2,3},{3,2},{4,5},{5,4},{6,7},{7,6},{8,9},{9,8},{10,11... | collective-permute-start | bytes 6291464 | tf_op jit(solution)/shard_map/ppermute | solution.py:404
  775.1 101.0 %collective-permute-start.32 = (bf16[2,1024,512]{2,1,0:T(8,128)(2,1)}, bf16[2,1024,512]{2,1,0:T(8,128)(2,1)}, u32[]{:S(2)}, u32[]{:S(2)}) collective-permute-start(bf16[2,1024,512]{2,1,0:T(8,128)(2,1)} %get-tuple-element.184), channel_id=1, source_target_pairs={{0,2},{1,3},{2,0},{3,1},{4,6},{5,7},{6,4},{7,5},{8,10},{9,11},{10,... | collective-permute-start | bytes 6291464 | tf_op jit(solution)/shard_map/ppermute | solution.py:404
  776.3 101.9 %collective-permute-start.33 = (bf16[2,1024,512]{2,1,0:T(8,128)(2,1)S(1)}, bf16[2,1024,512]{2,1,0:T(8,128)(2,1)}, u32[]{:S(2)}, u32[]{:S(2)}) collective-permute-start(bf16[2,1024,512]{2,1,0:T(8,128)(2,1)S(1)} %get-tuple-element.183), channel_id=1, source_target_pairs={{0,3},{1,2},{2,1},{3,0},{4,7},{5,6},{6,5},{7,4},{8,11},{9,10},{10,... | collective-permute-start | bytes 6291464 | tf_op jit(solution)/shard_map/ppermute | solution.py:404
  970.8 82.3 %collective-permute-start.35 = (bf16[2,1024,512]{2,1,0:T(8,128)(2,1)}, bf16[2,1024,512]{2,1,0:T(8,128)(2,1)}, u32[]{:S(2)}, u32[]{:S(2)}) collective-permute-start(bf16[2,1024,512]{2,1,0:T(8,128)(2,1)} %fusion.80), channel_id=1, source_target_pairs={{0,1},{1,0},{2,3},{3,2},{4,5},{5,4},{6,7},{7,6},{8,9},{9,8},{10,11... | collective-permute-start | bytes 6291464 | tf_op jit(solution)/shard_map/ppermute | solution.py:404
  970.8 82.3 %collective-permute-start.36 = (bf16[2,1024,512]{2,1,0:T(8,128)(2,1)}, bf16[2,1024,512]{2,1,0:T(8,128)(2,1)}, u32[]{:S(2)}, u32[]{:S(2)}) collective-permute-start(bf16[2,1024,512]{2,1,0:T(8,128)(2,1)} %fusion.83), channel_id=1, source_target_pairs={{0,2},{1,3},{2,0},{3,1},{4,6},{5,7},{6,4},{7,5},{8,10},{9,11},{10,... | collective-permute-start | bytes 6291464 | tf_op jit(solution)/shard_map/ppermute | solution.py:404
  971.2 91.5 %collective-permute-start.37 = (bf16[2,1024,512]{2,1,0:T(8,128)(2,1)}, bf16[2,1024,512]{2,1,0:T(8,128)(2,1)S(1)}, u32[]{:S(2)}, u32[]{:S(2)}) collective-permute-start(bf16[2,1024,512]{2,1,0:T(8,128)(2,1)} %fusion.86), channel_id=1, source_target_pairs={{0,3},{1,2},{2,1},{3,0},{4,7},{5,6},{6,5},{7,4},{8,11},{9,10},{10,... | collective-permute-start | bytes 6291464 | tf_op jit(solution)/shard_map/ppermute | solution.py:404
  1064.0 316.2 %reduce-scatter.21.cloned.1.call-start = ((), (), s32[]{:S(2)}) async-start(), calls=%async_computation.13 | async-start | bytes 20971520
  1222.9 249.2 %reduce-scatter.11.cloned.1.call-start = ((), (), s32[]{:S(2)}) async-start(), calls=%async_computation.6 | async-start | bytes 5242880 | tf_op jit(solution)/shard_map/reduce_scatter | solution.py:709
  1380.2 238.2 %reduce-scatter.13.cloned.1.call-start = ((), (), s32[]{:S(2)}) async-start(), calls=%async_computation.7 | async-start | bytes 5242880 | tf_op jit(solution)/shard_map/reduce_scatter | solution.py:728
  1380.3 91.8 %collective-permute-start.39 = (bf16[2,512,2048]{2,1,0:T(8,128)(2,1)}, bf16[2,512,2048]{2,1,0:T(8,128)(2,1)}, u32[]{:S(2)}, u32[]{:S(2)}) collective-permute-start(bf16[2,512,2048]{2,1,0:T(8,128)(2,1)} %fusion.34), channel_id=1, source_target_pairs={{0,1},{1,0},{2,3},{3,2},{4,5},{5,4},{6,7},{7,6},{8,9},{9,8},{10,11... | collective-permute-start | bytes 12582920 | tf_op jit(solution)/shard_map/ppermute | solution.py:404
  1380.7 91.4 %collective-permute-start.40 = (bf16[2,512,2048]{2,1,0:T(8,128)(2,1)}, bf16[2,512,2048]{2,1,0:T(8,128)(2,1)}, u32[]{:S(2)}, u32[]{:S(2)}) collective-permute-start(bf16[2,512,2048]{2,1,0:T(8,128)(2,1)} %fusion.37), channel_id=1, source_target_pairs={{0,2},{1,3},{2,0},{3,1},{4,6},{5,7},{6,4},{7,5},{8,10},{9,11},{10,... | collective-permute-start | bytes 12582920 | tf_op jit(solution)/shard_map/ppermute | solution.py:404
  1530.9 118.7 %reduce-scatter.17.cloned.1.call-start = ((), (), s32[]{:S(2)}) async-start(), calls=%async_computation.9 | async-start | bytes 2359296 | tf_op jit(solution)/shard_map/reduce_scatter | solution.py:729
  1531.0 87.5 %collective-permute-start.44 = (bf16[2,512,2048]{2,1,0:T(8,128)(2,1)}, bf16[2,512,2048]{2,1,0:T(8,128)(2,1)}, u32[]{:S(2)}, u32[]{:S(2)}) collective-permute-start(bf16[2,512,2048]{2,1,0:T(8,128)(2,1)} %fusion.40), channel_id=1, source_target_pairs={{0,3},{1,2},{2,1},{3,0},{4,7},{5,6},{6,5},{7,4},{8,11},{9,10},{10,... | collective-permute-start | bytes 12582920 | tf_op jit(solution)/shard_map/ppermute | solution.py:404
  1539.7 199.3 %reduce-scatter.15.cloned.1.call-start = ((), (), s32[]{:S(2)}) async-start(), calls=%async_computation.8 | async-start | bytes 7077888 | tf_op jit(solution)/shard_map/reduce_scatter | solution.py:515
  1653.5 58.5 %collective-permute-start.45 = (bf16[1024,512]{1,0:T(8,128)(2,1)S(1)}, bf16[1024,512]{1,0:T(8,128)(2,1)S(1)}, u32[]{:S(2)}, u32[]{:S(2)}) collective-permute-start(bf16[1024,512]{1,0:T(8,128)(2,1)S(1)} %get-tuple-element.192), channel_id=1, source_target_pairs={{0,1},{1,0},{2,3},{3,2},{4,5},{5,4},{6,7},{7,6},{8,9},{9,8},{10,11... | collective-permute-start | bytes 3145736 | tf_op jit(solution)/shard_map/ppermute | solution.py:404
  (86 other events, 2415.9 us)
Sparse Core Ops, SparseCore 0:
  104.2 313.0 all-gather.4
  556.2 212.9 all-gather.6
  1062.9 159.9 reduce-scatter.18
  1226.4 153.8 reduce-scatter.20
  1382.4 76.9 reduce-scatter.10
  1531.0 82.0 reduce-scatter.12
  1616.1 33.4 reduce-scatter.16
  1651.9 69.0 reduce-scatter.14

commit v3 on v2

--- a/solution.py
+++ b/solution.py
@@ -88,9 +88,9 @@
     lax.fori_loop(0, query_ref.shape[0] // TILE, body, 0)
 
 
-def attend_specs(tokens, size, heads):
+def attend_specs(tokens, size, each):
     def part(k):
-        return pl.BlockSpec((tokens, size), lambda h: (0, k * heads + h))
+        return pl.BlockSpec((None, tokens, size), lambda h: (h // each, 0, k * each + h % each))
 
     whole = [
         pl.BlockSpec(shape, lambda h: (0, 0))
@@ -101,8 +101,9 @@
 
 def attend_forward(qkv, cosine, sine, seg_row, gains):
     tokens, size = cosine.shape
-    heads = qkv.shape[1] // (3 * size)
-    parts, whole = attend_specs(tokens, size, heads)
+    each = qkv.shape[2] // (3 * size)
+    heads = qkv.shape[0] * each
+    parts, whole = attend_specs(tokens, size, each)
     by_head = pl.BlockSpec((tokens, size), lambda h: (0, h))
     return pl.pallas_call(
         partial(attend_kernel, size ** (-0.5)),
@@ -125,10 +126,11 @@
 
 
 def attend_back_kernel(
-    factor, query_ref, key_ref, value_ref, cos_ref, sin_ref, row_ref, col_ref, gains_ref,
+    factor, each, query_ref, key_ref, value_ref, cos_ref, sin_ref, row_ref, col_ref, gains_ref,
     grad_ref, log_ref, out_ref, gain_ref, low_ref, query_grad, key_grad, value_grad,
 ):
-    head, heads = pl.program_id(0), pl.num_programs(0)
+    head = pl.program_id(0)
+    group, place = head // each, head % each
     cosine, sine = cos_ref[...], sin_ref[...]
     gains = gains_ref[...]
     low_ref[...] = head_norm(query_ref[...], gains[0:1], cosine, sine)[2]
@@ -177,27 +179,28 @@
         raw_grad = rate * (
             scaled - normed * jnp.mean(scaled * normed, axis=-1, keepdims=True)
         )
-        columns = pl.ds(pl.multiple_of((k * heads + head) * size, size), size)
-        out_ref[:, columns] = raw_grad.astype(BF16)
-    columns = pl.ds(pl.multiple_of((2 * heads + head) * size, size), size)
-    out_ref[:, columns] = value_grad[...].astype(BF16)
+        columns = pl.ds(pl.multiple_of((k * each + place) * size, size), size)
+        out_ref[group, :, columns] = raw_grad.astype(BF16)
+    columns = pl.ds(pl.multiple_of((2 * each + place) * size, size), size)
+    out_ref[group, :, columns] = value_grad[...].astype(BF16)
 
 
 def attend_backward(qkv, cosine, sine, seg_row, gains, grad_heads, logs):
     tokens, size = cosine.shape
-    heads = qkv.shape[1] // (3 * size)
-    parts, whole = attend_specs(tokens, size, heads)
+    each = qkv.shape[2] // (3 * size)
+    heads = qkv.shape[0] * each
+    parts, whole = attend_specs(tokens, size, each)
     by_head = pl.BlockSpec((tokens, size), lambda h: (0, h))
     return pl.pallas_call(
-        partial(attend_back_kernel, size ** (-0.5)),
+        partial(attend_back_kernel, size ** (-0.5), each),
         grid=(heads,),
         in_specs=parts + whole + [by_head, by_head],
         out_specs=[
-            pl.BlockSpec((tokens, 3 * heads * size), lambda h: (0, 0)),
+            pl.BlockSpec(qkv.shape, lambda h: (0, 0, 0)),
             pl.BlockSpec((2, size), lambda h: (0, 0)),
         ],
         out_shape=[
-            jax.ShapeDtypeStruct((tokens, 3 * heads * size), BF16),
+            jax.ShapeDtypeStruct(qkv.shape, BF16),
             jax.ShapeDtypeStruct((2, size), F32),
         ],
         scratch_shapes=[
@@ -422,25 +425,23 @@
     return result
 
 
-def sum_cols(parts):
-    count = lax.axis_size("col")
-    me = lax.axis_index("col")
+def sum_cols(pieces):
     total = 0.0
-    for mask in range(count):
-        piece = lax.dynamic_index_in_dim(parts, me ^ mask, 0, keepdims=False)
-        if mask:
-            piece = swap_cols(piece, mask)
+    for piece in send_parts(pieces):
         total = total + piece.astype(F32)
     return total
 
 
-def send_parts(parts):
+def split_parts(parts):
     me = lax.axis_index("col")
-    pieces = []
-    for mask in range(lax.axis_size("col")):
-        piece = plain(lax.dynamic_index_in_dim(parts, me ^ mask, 0, keepdims=False))
-        pieces.append(swap_cols(piece, mask) if mask else piece)
-    return pieces
+    return [
+        plain(lax.dynamic_index_in_dim(parts, me ^ mask, 0, keepdims=False))
+        for mask in range(lax.axis_size("col"))
+    ]
+
+
+def send_parts(pieces):
+    return pieces[:1] + [swap_cols(pieces[mask], mask) for mask in range(1, len(pieces))]
 
 
 def join_parts(pieces, axis, result=None, offset=0):
@@ -485,13 +486,32 @@
     return chosen
 
 
-def heads_in(weight, ratio):
+def own_heads(cols, heads_row):
+    return 2 * heads_row == cols
+
+
+def heads_in(weight, ratio, size):
     chips, cols = lax.axis_size("chip"), lax.axis_size("col")
+    core, col = lax.axis_index("core"), lax.axis_index("col")
     rows = 2 * chips
-    row = 2 * lax.axis_index("chip") + lax.axis_index("core")
+    row = 2 * lax.axis_index("chip") + core
     kinds, features, width = weight.shape
+    pieces = []
+    if own_heads(cols, width // size):
+        p = width // size
+        for t in range(p):
+            pairs = [
+                (k * cols + c, c // p * cols + k * p + (t + c) % p)
+                for k in range(2)
+                for c in range(cols)
+            ]
+            piece = lax.dynamic_slice_in_dim(weight, (t + col) % p * size, size, 2)
+            pieces.append(lax.ppermute(piece, ("core", "col"), pairs))
+        pieces = [pick(pieces, (col - b) % p) for b in range(p)]
+        return jnp.concatenate(
+            [jnp.concatenate([p[a] for a in range(kinds)], axis=1) for p in pieces], axis=0
+        )
     block = features // ratio
-    pieces = []
     for k in range(ratio):
         pairs = []
         for r in range(rows):
@@ -500,21 +520,40 @@
                 pairs.append((r * cols + c, (ratio * c + h) * cols + r // ratio))
         piece = lax.dynamic_slice_in_dim(weight, (k + row) % ratio * block, block, 1)
         pieces.append(lax.ppermute(piece, ALL, pairs))
-    joined = jnp.concatenate(
+    return jnp.concatenate(
         [pick([p[a] for p in pieces], (row - s) % ratio) for a in range(kinds) for s in range(ratio)],
         axis=1,
     )
-    return joined
-
-
-def heads_out(grad, kinds, ratio):
+
+
+def heads_out(grad, kinds, ratio, heads_row):
     chips, cols = lax.axis_size("chip"), lax.axis_size("col")
+    col = lax.axis_index("col")
     rows = 2 * chips
     row = 2 * lax.axis_index("chip") + lax.axis_index("core")
-    block = grad.shape[0] // rows
-    mine = lax.psum_scatter(grad, ROW, scatter_dimension=0, tiled=True)
-    width = grad.shape[1] // (kinds * ratio)
+    mine = grad.reshape(rows, -1, grad.shape[2])
+    mine = lax.psum_scatter(mine, ROW, scatter_dimension=0, tiled=True)[0]
+    block = mine.shape[0]
     pieces = []
+    if own_heads(cols, heads_row):
+        p = heads_row
+        size = mine.shape[1] // kinds
+        for t in range(p):
+            pairs = [
+                (k * cols + c, c // p * cols + k * p + (c - t) % p)
+                for k in range(2)
+                for c in range(cols)
+            ]
+            piece = lax.dynamic_slice_in_dim(mine, (col - t) % p * (block // p), block // p, 0)
+            pieces.append(lax.ppermute(piece, ("core", "col"), pairs))
+        pieces = [pick(pieces, (i - col) % p) for i in range(p)]
+        return jnp.stack(
+            [
+                jnp.concatenate([q[:, a * size : (a + 1) * size] for q in pieces], axis=1)
+                for a in range(kinds)
+            ]
+        ).astype(F32)
+    width = mine.shape[1] // (kinds * ratio)
     for k in range(ratio):
         pairs = []
         for r in range(rows):
@@ -586,18 +625,43 @@
     )
     down_parts = down_weight.reshape(cols, mine_count, part_units, col_width)
 
+    heads_row = qkv_weight.shape[2] // head_size
+    groups = chips if own_heads(cols, heads_row) else 1
+
+    def by_col(values):
+        if groups == 1:
+            return values.reshape(cols, head_width, col_width)
+        values = values.reshape(groups, cols, head_width // groups, col_width)
+        return values.transpose(1, 0, 2, 3).reshape(cols, head_width, col_width)
+
+    def by_head(values):
+        if groups > 1:
+            values = values.reshape(cols, groups, head_width // groups, col_width)
+            values = values.transpose(1, 0, 2, 3)
+        return values.reshape(model_width, col_width)
+
     segs = gather_cols(segments)
     gain_all = gather_cols(attn_gain)
     tokens_all = gather_cols(tokens)
-    quarter = col_width // 4
-    gate_up_first = send_parts(gate_up_parts[:, :, :quarter])
-    gate_up_second = send_parts(gate_up_parts[:, :, quarter : 2 * quarter])
-    gate_up_last = send_parts(gate_up_parts[:, :, 2 * quarter :])
-    qkv_in, out_in, cot_in, segs, gain_all, tokens_all, gate_up_first = fence(
-        qkv_weight, out_weight, cotangent, segs, gain_all, tokens_all, gate_up_first
-    )
-    qkv_all = over_cores(over_chips(heads_in(qkv_in, ratio)))
-    out_all = over_cores(over_chips(out_in))
+    qkv_rows, segs, gain_all, tokens_all, out_in = fence(
+        heads_in(qkv_weight, ratio, head_size), segs, gain_all, tokens_all, out_weight
+    )
+    cuts = (0, col_width // 2, 3 * col_width // 4, col_width)
+    first, second, last = (
+        split_parts(gate_up_parts[:, :, cuts[i] : cuts[i + 1]]) for i in range(3)
+    )
+    gate_up_first = send_parts(first)
+    qkv_rows, out_rows, gate_up_first, second, last, cot_in = fence(
+        over_chips(qkv_rows), over_chips(out_in), gate_up_first, second, last, cotangent
+    )
+    gate_up_second, gate_up_last = send_parts(second), send_parts(last)
+    if groups > 1:
+        half = model_width // 2
+        qkv_halves = [(qkv_rows, core * half), (swap_cores(qkv_rows), (1 - core) * half)]
+    else:
+        half = model_width
+        qkv_halves = [(over_cores(qkv_rows)[None], 0)]
+    out_split = by_col(over_cores(out_rows))
     seg_row = lax.dynamic_index_in_dim(segs.reshape(rows, per_row), row, 0, keepdims=False)
     cot_all = lax.all_gather(cot_in, ALL, axis=0).reshape(rows, cols, per_row, col_width)
 
@@ -612,12 +676,19 @@
     normed_all = jnp.concatenate(
         [(stream_all[c] * rate_one * gain_all[c]).astype(BF16) for c in range(cols)], axis=1
     )
-    qkv = jnp.dot(normed_all, qkv_all, preferred_element_type=F32)
+    qkv = sum(
+        jnp.einsum(
+            "td,gdk->gtk",
+            lax.dynamic_slice_in_dim(normed_all, begin, half, 1),
+            weight,
+            preferred_element_type=F32,
+        )
+        for weight, begin in qkv_halves
+    )
     head_gains = jnp.stack([query_gain, key_gain])
     heads_low, logs = attend_forward(qkv, cosine, sine, seg_row, head_gains)
     heads_low, gate_up_second = fence(heads_low, gate_up_second)
     heads_all = gather_cols(heads_low)
-    out_split = out_all.reshape(cols, head_width, col_width)
     stream = tokens.astype(F32)
     hidden_one = plain(
         stream + jnp.einsum("ctk,ckd->td", heads_all, out_split, preferred_element_type=F32)
@@ -626,18 +697,20 @@
         width_total(jnp.sum(hidden_one * hidden_one, axis=-1)) / model_width + epsilon
     )[:, None]
     moe_in = plain((hidden_one * rate_two * moe_gain).astype(BF16))
-    moe_in, gate_up_last, cot_all = fence(moe_in, gate_up_last, cot_all)
+    moe_in, gate_up_last, cot_all, down_first = fence(
+        moe_in, gate_up_last, cot_all, split_parts(down_parts)
+    )
     gate_up = jnp.zeros((mine_count, model_width, 2 * part_units), BF16)
     gate_up = join_parts(gate_up_first, 1, gate_up, 0)
-    gate_up = join_parts(gate_up_second, 1, gate_up, quarter)
-    gate_up = join_parts(gate_up_last, 1, gate_up, 2 * quarter)
+    gate_up = join_parts(gate_up_second, 1, gate_up, cuts[1])
+    gate_up = join_parts(gate_up_last, 1, gate_up, cuts[2])
 
     moe_all = lax.all_gather(moe_in, ALL, axis=0).reshape(rows, cols, per_row, col_width)
     mine = jnp.reshape(core, (1,))
     others = 1 - mine
     grad_slot = gather_slots(cot_all, place, gate, low, high, capacity, True)
-    moe_all, down_parts, grad_slot = fence(moe_all, down_parts, grad_slot)
-    down = join_parts(send_parts(down_parts), 2)
+    moe_all, down_first, grad_slot = fence(moe_all, down_first, grad_slot)
+    down = join_parts(send_parts(down_first), 2)
     slot_inputs = gather_slots(moe_all, place, gate, low, high, capacity, False)
 
     gate_weight = gate_up[..., :part_units]
@@ -675,7 +748,9 @@
 
     expert_out = jnp.einsum("ecf,efd->ecd", hidden, down, preferred_element_type=F32).astype(BF16)
     out_other = combine(expert_out, core=others, scaled=True)
-    out_other, grad_slot = fence(out_other, grad_slot)
+    near = cols // 2 + 1
+    out_other, grad_slot, near_down = fence(out_other, grad_slot, got_down[1:near])
+    got_down[1:near] = near_down
     out_other = swap_cores(out_other)
     grad_hidden = jnp.einsum("ecd,efd->ecf", grad_slot, down, preferred_element_type=F32)
     grad_gate_pre = (
@@ -707,7 +782,6 @@
     grad_partial = plain(lax.psum_scatter(grad_partial, "col", scatter_dimension=0, tiled=True)[0])
     grad_partial, inner_parts, out_partial = fence(grad_partial, inner_parts, out_partial)
     grad_moe_in = plain(lax.psum_scatter(grad_partial, "chip", scatter_dimension=0, tiled=True)[0])
-    near = cols // 2 + 1
     far_parts = inner_parts[near:]
     got_inner = inner_parts[:1] + [swap_cols(inner_parts[mask], mask) for mask in range(1, near)]
     grad_moe_in, got_inner, out_partial, far_parts = fence(
@@ -721,15 +795,24 @@
     )
     grad_branch = plain(grad_hidden_one.astype(BF16))
     grad_heads = sum_cols(
-        jnp.einsum("td,ckd->ctk", grad_branch, out_split, preferred_element_type=F32).astype(BF16)
+        split_parts(
+            jnp.einsum("td,ckd->ctk", grad_branch, out_split, preferred_element_type=F32).astype(BF16)
+        )
     ).astype(BF16)
-    grad_heads, out_partial, far_parts = fence(grad_heads, out_partial, far_parts)
+    grad_down = jnp.zeros((cols, mine_count, part_units, col_width), F32)
+    for mask in range(cols):
+        grad_down = lax.dynamic_update_index_in_dim(
+            grad_down, got_down[mask].astype(F32), col ^ mask, 0
+        )
+    grad_heads, out_partial, far_parts, grad_down = fence(
+        grad_heads, out_partial, far_parts, grad_down
+    )
     far_parts = [swap_cols(part, near + i) for i, part in enumerate(far_parts)]
     moe_result = lax.psum_scatter(out_partial, "chip", scatter_dimension=0, tiled=True)[0]
     grad_out_weight = lax.psum_scatter(
-        jnp.einsum("ctk,td->ckd", heads_all, grad_branch, preferred_element_type=F32)
-        .astype(BF16)
-        .reshape(model_width, col_width),
+        by_head(
+            jnp.einsum("ctk,td->ckd", heads_all, grad_branch, preferred_element_type=F32).astype(BF16)
+        ),
         ROW,
         scatter_dimension=0,
         tiled=True,
@@ -737,23 +820,43 @@
     grad_projected, grad_gains = attend_backward(
         qkv, cosine, sine, seg_row, head_gains, grad_heads, logs
     )
-    grad_projected, far_parts, moe_result = fence(grad_projected, far_parts, moe_result)
+    grad_gate_up = jnp.zeros((cols, mine_count, col_width, 2 * part_units), F32)
+    for mask in range(near):
+        grad_gate_up = lax.dynamic_update_index_in_dim(
+            grad_gate_up, got_inner[mask].astype(F32), col ^ mask, 0
+        )
+    grad_projected, far_parts, moe_result, grad_gate_up = fence(
+        grad_projected, far_parts, moe_result, grad_gate_up
+    )
     output = (hidden_one + moe_result.astype(F32)).astype(BF16)
-    got_inner = got_inner + far_parts
-    normed_parts = jnp.einsum(
-        "tk,cfk->ctf",
-        grad_projected,
-        qkv_all.reshape(cols, col_width, 3 * head_width),
-        preferred_element_type=F32,
-    ).astype(BF16)
-    normed_parts, grad_projected, got_inner, got_down = fence(
-        normed_parts, grad_projected, got_inner, got_down
-    )
-    grad_normed = sum_cols(normed_parts)
+    normed_parts = [
+        plain(
+            jnp.einsum("gtk,gdk->td", grad_projected, weight, preferred_element_type=F32).astype(BF16)
+        )
+        for weight, _ in qkv_halves
+    ]
+    if groups > 1:
+        mine_first = jnp.concatenate(normed_parts, axis=1)
+        mine_last = jnp.concatenate(normed_parts[::-1], axis=1)
+        normed_parts = jnp.where(core == 0, mine_first, mine_last)
+    else:
+        normed_parts = normed_parts[0]
+    normed_parts, grad_projected, far_parts = fence(normed_parts, grad_projected, far_parts)
+    grad_normed = sum_cols(
+        [
+            lax.dynamic_slice_in_dim(normed_parts, (col ^ mask) * col_width, col_width, 1)
+            for mask in range(cols)
+        ]
+    )
     grad_qkv = heads_out(
-        jnp.einsum("td,tk->dk", normed_all, grad_projected, preferred_element_type=F32).astype(BF16),
+        plain(
+            jnp.einsum(
+                "td,gtk->gdk", normed_all, grad_projected, preferred_element_type=F32
+            ).astype(BF16)
+        ),
         3,
         ratio,
+        heads_row,
     )
 
     scaled_grad = grad_normed * attn_gain
@@ -772,14 +875,10 @@
         - stream * rate_one * rate_one * rate_one * across / model_width
     ).astype(BF16)
 
-    grad_gate_up = jnp.zeros((cols, mine_count, col_width, 2 * part_units), F32)
-    grad_down = jnp.zeros((cols, mine_count, part_units, col_width), F32)
-    for mask in range(cols):
-        there = col ^ mask
+    for mask in range(near, cols):
         grad_gate_up = lax.dynamic_update_index_in_dim(
-            grad_gate_up, got_inner[mask].astype(F32), there, 0
-        )
-        grad_down = lax.dynamic_update_index_in_dim(grad_down, got_down[mask].astype(F32), there, 0)
+            grad_gate_up, far_parts[mask - near].astype(F32), col ^ mask, 0
+        )
     grad_gate_up = (
         grad_gate_up.reshape(experts_here, split, col_width, 2, part_units)
         .transpose(0, 2, 3, 1, 4)

time: 1810 us -> 1670 us (0.923)
  waiting for transfers between devices: 882 us -> 725 us
  blocking collectives: 22.3 us -> 60.9 us
    ppermute x4, waiting for transfers between devices: 123 us -> 35.4 us  [the longest x2 27.9 us: heads_in(): pieces.append(lax.ppermute(piece, ('core', 'col'), pairs))]
    ppermute x36, waiting for transfers between devices: 385 us -> 316 us  [swap_cols(): return lax.ppermute(values, 'col', [(i, i ^ mask) for i in range(count)])]
    all_gather x1, waiting for transfers between devices: 0.02 us -> 52.1 us  [local(): lax.all_gather(cot_in, ALL, axis=0).reshape(rows, cols, per_row, col_width)]
    ppermute x6, waiting for transfers between devices: 111 us -> 68.1 us  [swap_chips(): return lax.ppermute(values, 'chip', [(i, i ^ mask) for i in range(count)])]
    psum x3, blocking collectives: 22.3 us -> 60.9 us  [width_total(): return lax.psum(values, 'col')]
  transfers between devices with their start and end apart: 61 -> 61, of which waited for: 24 -> 28; matrix products, arithmetic and copies ran while one was open for 26% -> 29% of each run, Pallas kernels for 12% -> 15%
where the time goes in v3:
time: 1670 us; the launch traced here: 1660 us
  waiting for transfers between devices  725 us (43%)
  matrix products  301 us (18%)
  Pallas kernels  244 us (15%)
  local copies, waits for them, and re-layouts  152 us (9%)
  other arithmetic  87.8 us (5%)
  starting transfers between devices  70.5 us (4%)
  blocking collectives  60.9 us (4%)
    ppermute x36, waiting for transfers between devices, swap_cols(): return lax.ppermute(values, 'col', [(i, i ^ mask) for i in range(count)])  316 us
    unnamed x10, waiting for transfers between devices  140 us
    pallas_call x4, Pallas kernels, combine_slots(): pl.pallas_call(partial(combine_kernel, scaled, each), grid_spec=pltpu.Pre...  118 us
    all_gather x1, waiting for transfers between devices, local(): lax.all_gather(moe_in, ALL, axis=0).reshape(rows, cols, per_row, col_width)  103 us
    pallas_call x2, Pallas kernels, gather_slots(): pl.pallas_call(partial(gather_kernel, scaled, each), grid_spec=pltpu.Pref...  78.2 us
    ppermute x6, waiting for transfers between devices, swap_chips(): return lax.ppermute(values, 'chip', [(i, i ^ mask) for i in range(count)])  68.1 us
    dot_general x4, matrix products, local(): jnp.einsum('ecd,ecf->edf', feature_block(slot_inputs, col ^ mask), grad_i...  67.7 us
    psum x3, blocking collectives, width_total(): return lax.psum(values, 'col')  60.9 us
  transfers between devices with their start and end apart: 61, of which 28 were waited for; matrix products, arithmetic and copies ran while one was open for 29% of the time, Pallas kernels for 15%

profile of v3, /device:TPU:3, one launch (start us, length us, event | category | flops | bytes accessed | tf_op | source)
XLA Modules:
  0.0 1657.0 jit_solution(5696543964080540240)
XLA Ops:
  38.7 20.2 %collective-permute-done.3 = s32[2,1024]{1,0:T(2,128)S(1)} collective-permute-done((s32[2,1024]{1,0:T(2,128)S(1)}, s32[2,1024]{1,0:T(2,128)S(1)}, u32[]{:S(2)}, u32[]{:S(2)}) %collective-permute-start.3) | collective-permute-done | bytes 8224 | tf_op jit(solution)/shard_map/ppermute | solution.py:407
  65.3 27.9 %collective-permute-done.1 = bf16[3,512,128]{1,2,0:T(8,128)(2,1)S(1)} collective-permute-done((bf16[3,512,128]{1,2,0:T(8,128)(2,1)S(1)}, bf16[3,512,128]{1,2,0:T(8,128)(2,1)S(1)}, u32[]{:S(2)}, u32[]{:S(2)}) %collective-permute-start.1) | collective-permute-done | bytes 393248 | tf_op jit(solution)/shard_map/ppermute | solution.py:509
  141.6 48.5 %collective-permute-done.12 = bf16[1024,384]{0,1:T(8,128)(2,1)S(1)} collective-permute-done((bf16[1024,384]{0,1:T(8,128)(2,1)S(1)}, bf16[1024,384]{0,1:T(8,128)(2,1)S(1)}, u32[]{:S(2)}, u32[]{:S(2)}) %collective-permute-start.12) | collective-permute-done | bytes 786464 | tf_op jit(solution)/shard_map/ppermute | solution.py:462
  229.5 19.2 %attend_forward.1 = (bf16[1024,512]{1,0:T(8,128)(2,1)}, f32[1024,512]{1,0:T(8,128)}) custom-call(f32[4,1024,384]{2,1,0:T(8,128)} %add_bitcast_fusion.query_ref.key_ref.value_ref, f32[4,1024,384]{2,1,0:T(8,128)} %add_bitcast_fusion.query_ref.key_ref.value_ref, f32[4,1024,384]{2,1,0:T(8,128)} %add_bitcast_fusion.query_ref.key_ref.value_ref, ...), custom_call_target="tpu_custom_call" | custom-call | flops 2147483648 | bytes 9437184 | tf_op jit(solution)/shard_map/attend_forward/pallas_call | solution.py:108
  262.5 23.3 %collective-permute-done.23 = bf16[2,128,2048]{2,1,0:T(8,128)(2,1)} collective-permute-done((bf16[2,128,2048]{2,1,0:T(8,128)(2,1)S(1)}, bf16[2,128,2048]{2,1,0:T(8,128)(2,1)}, u32[]{:S(2)}, u32[]{:S(2)}) %collective-permute-start.23) | collective-permute-done | bytes 1048608 | tf_op jit(solution)/shard_map/ppermute | solution.py:407
  301.4 19.8 %collective-permute-done.24 = bf16[1024,512]{1,0:T(8,128)(2,1)S(1)} collective-permute-done((bf16[1024,512]{1,0:T(8,128)(2,1)}, bf16[1024,512]{1,0:T(8,128)(2,1)S(1)}, u32[]{:S(2)}, u32[]{:S(2)}) %collective-permute-start.24) | collective-permute-done | bytes 1048608 | tf_op jit(solution)/shard_map/ppermute | solution.py:407
  321.3 24.7 %collective-permute-done.25 = bf16[1024,512]{1,0:T(8,128)(2,1)S(1)} collective-permute-done((bf16[1024,512]{1,0:T(8,128)(2,1)S(1)}, bf16[1024,512]{1,0:T(8,128)(2,1)S(1)}, u32[]{:S(2)}, u32[]{:S(2)}) %collective-permute-start.25) | collective-permute-done | bytes 1048608 | tf_op jit(solution)/shard_map/ppermute | solution.py:407
  346.1 50.2 %collective-permute-done.26 = bf16[1024,512]{1,0:T(8,128)(2,1)S(1)} collective-permute-done((bf16[1024,512]{1,0:T(8,128)(2,1)S(1)}, bf16[1024,512]{1,0:T(8,128)(2,1)S(1)}, u32[]{:S(2)}, u32[]{:S(2)}) %collective-permute-start.26) | collective-permute-done | bytes 1048608 | tf_op jit(solution)/shard_map/ppermute | solution.py:407
  398.9 46.5 %psum.21 = f32[1024]{0:T(1024)S(1)} all-reduce(f32[1024]{0:T(1024)S(1)} %get-tuple-element.265), channel_id=1, replica_groups=mesh['chip'=4,'core'=2,'col'=4] {'col'}, use_global_device_ids=true, to_apply=%region_4.5 | all-reduce | flops 1024 | bytes 8192 | tf_op jit(solution)/shard_map/psum | solution.py:39
  446.6 52.1 %all-gather.5.cloned.1.call-done = bf16[32768,512]{1,0:T(8,128)(2,1)} async-done(((bf16[1024,512]{1,0:T(8,128)(2,1)}), bf16[32768,512]{1,0:T(8,128)(2,1)}) %all-gather.5.cloned.1.call-update) | async-done | bytes 33554448 | tf_op jit(solution)/shard_map/all_gather | solution.py:666
  554.9 39.3 %gather_slots.2 = bf16[2,2048,2048]{2,1,0:T(8,128)(2,1)} custom-call(s32[2,16]{1,0:T(2,128)} %get-tuple-element.202.low_ref, s32[2,16]{1,0:T(2,128)} %get-tuple-element.201.high_ref, bf16[8,4,1024,512]{3,2,1,0:T(8,128)(2,1)} %bitcast.316, bf16[8,4,1024,512]{3,2,1,0:T(8,128)(2,1)} %bitcast.317, ...), custom_call_target="tpu_custom_call" | custom-call | flops 25769803776 | bytes 50331648 | tf_op jit(solution)/shard_map/gather_slots/pallas_call | solution.py:299
  594.2 102.9 %all-gather.7.cloned.1.call-done = bf16[32768,512]{1,0:T(8,128)(2,1)} async-done(((bf16[1024,512]{1,0:T(8,128)(2,1)}), bf16[32768,512]{1,0:T(8,128)(2,1)}) %all-gather.7.cloned.1.call-update) | async-done | bytes 33554448 | tf_op jit(solution)/shard_map/all_gather | solution.py:708
  699.7 39.0 %gather_slots.3 = bf16[2,2048,2048]{2,1,0:T(8,128)(2,1)} custom-call(s32[2,16]{1,0:T(2,128)} %get-tuple-element.202.low_ref, s32[2,16]{1,0:T(2,128)} %get-tuple-element.201.high_ref, bf16[8,4,1024,512]{3,2,1,0:T(8,128)(2,1)} %bitcast.318, bf16[8,4,1024,512]{3,2,1,0:T(8,128)(2,1)} %bitcast.319, ...), custom_call_target="tpu_custom_call" | custom-call | flops 25769803776 | bytes 50331648 | tf_op jit(solution)/shard_map/gather_slots/pallas_call | solution.py:299
  738.7 24.4 %fusion.12 = bf16[2,2048,1024]{1,2,0:T(8,128)(2,1)} fusion(bf16[2,2048,2048]{2,1,0:T(8,128)(2,1)} %gather_slots.3, bf16[2,2048,2048]{1,2,0:T(8,128)(2,1)} %constant_dynamic-update-slice_fusion.4), kind=kOutput, calls=%fused_computation.27 | convolution fusion | flops 17184063488 | bytes 33554432 | tf_op jit(solution)/shard_map/ecd,edf->ecf/dot_general | solution.py:718
  763.1 27.9 %fusion = (bf16[2,2048,1024]{1,2,0:T(8,128)(2,1)}, bf16[2,2048,1024]{1,2,0:T(8,128)(2,1)}) fusion(bf16[2,2048,1024]{1,2,0:T(8,128)(2,1)} %fusion.12, bf16[2,2048,2048]{2,1,0:T(8,128)(2,1)} %gather_slots.3, bf16[2,2048,2048]{1,2,0:T(8,128)(2,1)} %constant_dynamic-update-slice_fusion.4), kind=kOutput, calls=%fused_computation.5 | convolution fusion | flops 17217617920 | bytes 50331648 | tf_op jit(solution)/shard_map/ecd,edf->ecf/dot_general | solution.py:721
  836.5 25.9 %convolution_convert_fusion.slots_ref = bf16[2,2048,2048]{2,1,0:T(8,128)(2,1)} fusion(bf16[2,2048,1024]{1,2,0:T(8,128)(2,1)} %get-tuple-element.146, bf16[2,1024,2048]{2,1,0:T(8,128)(2,1)} %copy-done.7), kind=kOutput, calls=%fused_computation.15 | convolution fusion | flops 17188257792 | bytes 33554432 | tf_op jit(solution)/shard_map/ecf,efd->ecd/dot_general | solution.py:749
  862.4 28.8 %combine_slots.4 = bf16[4,4,1024,512]{3,2,1,0:T(8,128)(2,1)} custom-call(s32[2,16]{1,0:T(2,128)} %get-tuple-element.202.low_ref, s32[2,16]{1,0:T(2,128)} %get-tuple-element.201.high_ref, s32[1]{0:T(128)S(6)} %sub.54.core_ref, bf16[2,2048,2048]{2,1,0:T(8,128)(2,1)} %convolution_convert_fusion.slots_ref, ...), custom_call_target="tpu_custom_call" | custom-call | flops 12884901888 | bytes 33554432 | tf_op jit(solution)/shard_map/combine_slots/pallas_call | solution.py:364
  891.9 32.7 %fusion.3 = (bf16[2,2048,1024]{1,2,0:T(8,128)(2,1)}, bf16[2,2048,1024]{1,2,0:T(8,128)(2,1)}) fusion(bf16[2,2048,1024]{1,2,0:T(8,128)(2,1)} %get-tuple-element.268, bf16[2,2048,1024]{1,2,0:T(8,128)(2,1)} %fusion.12, bf16[2,2048,2048]{2,1,0:T(8,128)(2,1)} %gather_slots.2, bf16[2,1024,2048]{2,1,0:T(8,128)(2,1)} %copy-done.7), kind=kOutput, calls=%fused_computation.8 | convolution fusion | flops 17242783744 | bytes 58720256 | tf_op jit(solution)/shard_map/ecd,efd->ecf/dot_general | solution.py:755
  938.3 31.5 %combine_slots.5 = bf16[4,4,1024,512]{3,2,1,0:T(8,128)(2,1)} custom-call(s32[2,16]{1,0:T(2,128)} %get-tuple-element.202.low_ref, s32[2,16]{1,0:T(2,128)} %get-tuple-element.201.high_ref, s32[1]{0:T(128)} %bitcast.67.core_ref, bf16[2,2048,2048]{2,1,0:T(8,128)(2,1)} %convolution_convert_fusion.slots_ref, ...), custom_call_target="tpu_custom_call" | custom-call | flops 12884901888 | bytes 33554432 | tf_op jit(solution)/shard_map/combine_slots/pallas_call | solution.py:364
  969.9 42.5 %convolution_convert_fusion.1.slots_ref = bf16[2,2048,2048]{2,1,0:T(8,128)(2,1)} fusion(bf16[2,2048,2048]{1,2,0:T(8,128)(2,1)} %pad_maximum_fusion, bf16[2,2048,2048]{1,2,0:T(8,128)(2,1)} %constant_dynamic-update-slice_fusion.4), kind=kOutput, calls=%fused_computation.16 | convolution fusion | flops 34368126976 | bytes 50331648 | tf_op jit(solution)/shard_map/ecf,edf->ecd/dot_general | solution.py:766
  1012.4 27.9 %combine_slots.6 = bf16[4,4,1024,512]{3,2,1,0:T(8,128)(2,1)} custom-call(s32[2,16]{1,0:T(2,128)} %get-tuple-element.202.low_ref, s32[2,16]{1,0:T(2,128)} %get-tuple-element.201.high_ref, s32[1]{0:T(128)S(6)} %sub.54.core_ref, bf16[2,2048,2048]{2,1,0:T(8,128)(2,1)} %convolution_convert_fusion.1.slots_ref, ...), custom_call_target="tpu_custom_call" | custom-call | flops 12884901888 | bytes 33554432 | tf_op jit(solution)/shard_map/combine_slots/pallas_call | solution.py:364
  1040.6 17.0 %fusion.35 = bf16[2,512,2048]{2,1,0:T(8,128)(2,1)} fusion(bf16[2,2048,2048]{1,2,0:T(8,128)(2,1)} %pad_maximum_fusion, bf16[2,2048,2048]{2,1,0:T(8,128)(2,1)} %gather_slots.3, s32[]{:T(128)S(6)} %select_n.294), kind=kOutput, calls=%fused_computation.55 | convolution fusion | flops 8592031744 | bytes 25165828 | tf_op jit(solution)/shard_map/ecd,ecf->edf/dot_general | solution.py:774
  1065.8 30.2 %combine_slots.7 = bf16[4,4,1024,512]{3,2,1,0:T(8,128)(2,1)} custom-call(s32[2,16]{1,0:T(2,128)} %get-tuple-element.202.low_ref, s32[2,16]{1,0:T(2,128)} %get-tuple-element.201.high_ref, s32[1]{0:T(128)} %bitcast.67.core_ref, bf16[2,2048,2048]{2,1,0:T(8,128)(2,1)} %convolution_convert_fusion.1.slots_ref, ...), custom_call_target="tpu_custom_call" | custom-call | flops 12884901888 | bytes 33554432 | tf_op jit(solution)/shard_map/combine_slots/pallas_call | solution.py:364
  1096.0 33.3 %reduce-scatter.19.cloned.1.call-done = bf16[1,4,1024,512]{3,2,1,0:T(8,128)(2,1)} async-done(((bf16[4,4,1024,512]{3,2,1,0:T(8,128)(2,1)}), bf16[1,4,1024,512]{3,2,1,0:T(8,128)(2,1)}) %reduce-scatter.19.cloned.1.call-update) | async-done | bytes 4194320
  1129.4 16.7 %fusion.41 = bf16[2,512,2048]{2,1,0:T(8,128)(2,1)} fusion(bf16[2,2048,2048]{1,2,0:T(8,128)(2,1)} %pad_maximum_fusion, bf16[2,2048,2048]{2,1,0:T(8,128)(2,1)} %gather_slots.3, s32[]{:T(128)S(6)} %select_n.296), kind=kOutput, calls=%fused_computation.57 | convolution fusion | flops 8592031744 | bytes 25165828 | tf_op jit(solution)/shard_map/ecd,ecf->edf/dot_general | solution.py:774
  1162.7 17.4 %fusion.23 = f32[2,512,2048]{2,1,0:T(8,128)} fusion(bf16[2,2048,2048]{1,2,0:T(8,128)(2,1)} %pad_maximum_fusion, bf16[2,2048,2048]{2,1,0:T(8,128)(2,1)} %gather_slots.3, s32[]{:T(128)S(6)} %select_n.293), kind=kOutput, calls=%fused_computation.43 | convolution fusion | flops 8589934592 | bytes 29360132 | tf_op jit(solution)/shard_map/ecd,ecf->edf/dot_general | solution.py:774
  1180.1 106.6 %reduce-scatter.21.cloned.1.call-done = bf16[1,4,1024,512]{3,2,1,0:T(8,128)(2,1)} async-done(((bf16[4,4,1024,512]{3,2,1,0:T(8,128)(2,1)}), bf16[1,4,1024,512]{3,2,1,0:T(8,128)(2,1)}) %reduce-scatter.21.cloned.1.call-update) | async-done | bytes 4194320
  1299.3 79.2 %collective-permute-done.39 = bf16[2,512,2048]{2,1,0:T(8,128)(2,1)} collective-permute-done((bf16[2,512,2048]{2,1,0:T(8,128)(2,1)}, bf16[2,512,2048]{2,1,0:T(8,128)(2,1)}, u32[]{:S(2)}, u32[]{:S(2)}) %collective-permute-start.39) | collective-permute-done | bytes 4194336 | tf_op jit(solution)/shard_map/ppermute | solution.py:407
  1415.3 20.7 %collective-permute-done.43 = bf16[1024,512]{1,0:T(8,128)(2,1)S(1)} collective-permute-done((bf16[1024,512]{1,0:T(8,128)(2,1)S(1)}, bf16[1024,512]{1,0:T(8,128)(2,1)S(1)}, u32[]{:S(2)}, u32[]{:S(2)}) %collective-permute-start.43) | collective-permute-done | bytes 1048608 | tf_op jit(solution)/shard_map/ppermute | solution.py:407
  1479.6 28.6 %attend_backward.1 = (bf16[4,1024,384]{2,1,0:T(8,128)(2,1)}, f32[2,128]{1,0:T(2,128)}) custom-call(f32[4,1024,384]{2,1,0:T(8,128)} %add_bitcast_fusion.query_ref.key_ref.value_ref, f32[4,1024,384]{2,1,0:T(8,128)} %add_bitcast_fusion.query_ref.key_ref.value_ref, f32[4,1024,384]{2,1,0:T(8,128)} %add_bitcast_fusion.query_ref.key_ref.value_ref, ...), custom_call_target="tpu_custom_call" | custom-call | flops 5368709120 | bytes 12582912 | tf_op jit(solution)/shard_map/attend_backward/pallas_call | solution.py:194
  1508.3 16.9 %collective-permute-done.44 = bf16[2,512,2048]{2,1,0:T(8,128)(2,1)} collective-permute-done((bf16[2,512,2048]{2,1,0:T(8,128)(2,1)}, bf16[2,512,2048]{2,1,0:T(8,128)(2,1)}, u32[]{:S(2)}, u32[]{:S(2)}) %collective-permute-start.44) | collective-permute-done | bytes 4194336 | tf_op jit(solution)/shard_map/ppermute | solution.py:407
  1576.0 22.2 %collective-permute-done.47 = bf16[1024,512]{1,0:T(8,128)(2,1)} collective-permute-done((bf16[1024,512]{1,0:T(8,128)(2,1)}, bf16[1024,512]{1,0:T(8,128)(2,1)}, u32[]{:S(2)}, u32[]{:S(2)}) %collective-permute-start.47) | collective-permute-done | bytes 1048608 | tf_op jit(solution)/shard_map/ppermute | solution.py:407
  (390 shorter events, 497.2 us)
Async XLA Ops:
  7.2 491.5 %all-gather.5.cloned.1.call-start = ((), (), s32[]{:S(2)}) async-start(), calls=%async_computation.10 | async-start | bytes 34603008 | tf_op jit(solution)/shard_map/all_gather | solution.py:666
  10.0 83.4 %collective-permute-start.8 = (bf16[1024,512]{1,0:T(8,128)(2,1)}, bf16[1024,512]{1,0:T(8,128)(2,1)}, u32[]{:S(2)}, u32[]{:S(2)}) collective-permute-start(bf16[1024,512]{1,0:T(8,128)(2,1)} %param.13), channel_id=1, source_target_pairs={{0,1},{1,0},{2,3},{3,2},{4,5},{5,4},{6,7},{7,6},{8,9},{9,8},{10,11... | collective-permute-start | bytes 3145736 | tf_op jit(solution)/shard_map/ppermute | solution.py:407
  31.6 65.6 %collective-permute-start.9 = (bf16[1024,512]{1,0:T(8,128)(2,1)S(1)}, bf16[1024,512]{1,0:T(8,128)(2,1)S(1)}, u32[]{:S(2)}, u32[]{:S(2)}) collective-permute-start(bf16[1024,512]{1,0:T(8,128)(2,1)S(1)} %copy-done.2), channel_id=1, source_target_pairs={{0,2},{1,3},{2,0},{3,1},{4,6},{5,7},{6,4},{7,5},{8,10},{9,11},{10,... | collective-permute-start | bytes 3145736 | tf_op jit(solution)/shard_map/ppermute | solution.py:407
  65.0 127.0 %collective-permute-start.17 = (bf16[2,256,2048]{2,1,0:T(8,128)(2,1)}, bf16[2,256,2048]{2,1,0:T(8,128)(2,1)}, u32[]{:S(2)}, u32[]{:S(2)}) collective-permute-start(bf16[2,256,2048]{2,1,0:T(8,128)(2,1)} %get-tuple-element.217), channel_id=1, source_target_pairs={{0,1},{1,0},{2,3},{3,2},{4,5},{5,4},{6,7},{7,6},{8,9},{9,8},{10,11... | collective-permute-start | bytes 6291464 | tf_op jit(solution)/shard_map/ppermute | solution.py:407
  93.2 98.8 %collective-permute-start.18 = (bf16[2,256,2048]{2,1,0:T(8,128)(2,1)}, bf16[2,256,2048]{2,1,0:T(8,128)(2,1)}, u32[]{:S(2)}, u32[]{:S(2)}) collective-permute-start(bf16[2,256,2048]{2,1,0:T(8,128)(2,1)} %get-tuple-element.216), channel_id=1, source_target_pairs={{0,2},{1,3},{2,0},{3,1},{4,6},{5,7},{6,4},{7,5},{8,10},{9,11},{10,... | collective-permute-start | bytes 6291464 | tf_op jit(solution)/shard_map/ppermute | solution.py:407
  93.4 98.6 %collective-permute-start.19 = (bf16[2,256,2048]{2,1,0:T(8,128)(2,1)}, bf16[2,256,2048]{2,1,0:T(8,128)(2,1)}, u32[]{:S(2)}, u32[]{:S(2)}) collective-permute-start(bf16[2,256,2048]{2,1,0:T(8,128)(2,1)} %get-tuple-element.215), channel_id=1, source_target_pairs={{0,3},{1,2},{2,1},{3,0},{4,7},{5,6},{6,5},{7,4},{8,11},{9,10},{10,... | collective-permute-start | bytes 6291464 | tf_op jit(solution)/shard_map/ppermute | solution.py:407
  137.0 53.1 %collective-permute-start.12 = (bf16[1024,384]{0,1:T(8,128)(2,1)S(1)}, bf16[1024,384]{0,1:T(8,128)(2,1)S(1)}, u32[]{:S(2)}, u32[]{:S(2)}) collective-permute-start(bf16[1024,384]{0,1:T(8,128)(2,1)S(1)} %maximum_maximum_fusion), channel_id=1, source_target_pairs={{0,16},{8,24},{16,0},{24,8},{1,17},{9,25},{17,1},{25,9},{2,18},{10... | collective-permute-start | bytes 2359304 | tf_op jit(solution)/shard_map/ppermute | solution.py:462
  138.0 53.0 %collective-permute-start.13 = (bf16[1024,384]{0,1:T(8,128)(2,1)S(1)}, bf16[1024,384]{0,1:T(8,128)(2,1)S(1)}, u32[]{:S(2)}, u32[]{:S(2)}) collective-permute-start(bf16[1024,384]{0,1:T(8,128)(2,1)S(1)} %maximum_maximum_fusion), channel_id=1, source_target_pairs={{0,24},{8,16},{16,8},{24,0},{1,25},{9,17},{17,9},{25,1},{2,26},{10... | collective-permute-start | bytes 2359304 | tf_op jit(solution)/shard_map/ppermute | solution.py:462
  192.0 505.1 %all-gather.7.cloned.1.call-start = ((), (), s32[]{:S(2)}) async-start(), calls=%async_computation.11 | async-start | bytes 34603008 | tf_op jit(solution)/shard_map/all_gather | solution.py:708
  214.0 82.6 %collective-permute-start.27 = (bf16[4,256,512]{2,1,0:T(8,128)(2,1)S(1)}, bf16[4,256,512]{2,1,0:T(8,128)(2,1)}, u32[]{:S(2)}, u32[]{:S(2)}) collective-permute-start(bf16[4,256,512]{2,1,0:T(8,128)(2,1)S(1)} %bitcast_dynamic-update-slice_fusion.14), channel_id=1, source_target_pairs={{0,4},{4,0},{1,5},{5,1},{2,6},{6,2},{3,7},{7,3},{8,12},{12,8},{9,1... | collective-permute-start | bytes 3145736 | tf_op jit(solution)/shard_map/ppermute | solution.py:402
  215.4 47.1 %collective-permute-start.22 = (bf16[2,128,2048]{2,1,0:T(8,128)(2,1)S(1)}, bf16[2,128,2048]{2,1,0:T(8,128)(2,1)}, u32[]{:S(2)}, u32[]{:S(2)}) collective-permute-start(bf16[2,128,2048]{2,1,0:T(8,128)(2,1)S(1)} %copy-done.31), channel_id=1, source_target_pairs={{0,2},{1,3},{2,0},{3,1},{4,6},{5,7},{6,4},{7,5},{8,10},{9,11},{10,... | collective-permute-start | bytes 3145736 | tf_op jit(solution)/shard_map/ppermute | solution.py:407
  215.4 70.3 %collective-permute-start.23 = (bf16[2,128,2048]{2,1,0:T(8,128)(2,1)S(1)}, bf16[2,128,2048]{2,1,0:T(8,128)(2,1)}, u32[]{:S(2)}, u32[]{:S(2)}) collective-permute-start(bf16[2,128,2048]{2,1,0:T(8,128)(2,1)S(1)} %copy-done.30), channel_id=1, source_target_pairs={{0,3},{1,2},{2,1},{3,0},{4,7},{5,6},{6,5},{7,4},{8,11},{9,10},{10,... | collective-permute-start | bytes 3145736 | tf_op jit(solution)/shard_map/ppermute | solution.py:407
  293.1 153.6 %collective-permute-start.28 = (bf16[2,128,2048]{2,1,0:T(8,128)(2,1)}, bf16[2,128,2048]{2,1,0:T(8,128)(2,1)}, u32[]{:S(2)}, u32[]{:S(2)}) collective-permute-start(bf16[2,128,2048]{2,1,0:T(8,128)(2,1)} %get-tuple-element.117), channel_id=1, source_target_pairs={{0,1},{1,0},{2,3},{3,2},{4,5},{5,4},{6,7},{7,6},{8,9},{9,8},{10,11... | collective-permute-start | bytes 3145736 | tf_op jit(solution)/shard_map/ppermute | solution.py:407
  294.4 152.2 %collective-permute-start.29 = (bf16[2,128,2048]{2,1,0:T(8,128)(2,1)}, bf16[2,128,2048]{2,1,0:T(8,128)(2,1)}, u32[]{:S(2)}, u32[]{:S(2)}) collective-permute-start(bf16[2,128,2048]{2,1,0:T(8,128)(2,1)} %get-tuple-element.118), channel_id=1, source_target_pairs={{0,2},{1,3},{2,0},{3,1},{4,6},{5,7},{6,4},{7,5},{8,10},{9,11},{10,... | collective-permute-start | bytes 3145736 | tf_op jit(solution)/shard_map/ppermute | solution.py:407
  296.6 49.4 %collective-permute-start.25 = (bf16[1024,512]{1,0:T(8,128)(2,1)S(1)}, bf16[1024,512]{1,0:T(8,128)(2,1)S(1)}, u32[]{:S(2)}, u32[]{:S(2)}) collective-permute-start(bf16[1024,512]{1,0:T(8,128)(2,1)S(1)} %copy-done.32), channel_id=1, source_target_pairs={{0,2},{1,3},{2,0},{3,1},{4,6},{5,7},{6,4},{7,5},{8,10},{9,11},{10,... | collective-permute-start | bytes 3145736 | tf_op jit(solution)/shard_map/ppermute | solution.py:407
  296.7 99.7 %collective-permute-start.26 = (bf16[1024,512]{1,0:T(8,128)(2,1)S(1)}, bf16[1024,512]{1,0:T(8,128)(2,1)S(1)}, u32[]{:S(2)}, u32[]{:S(2)}) collective-permute-start(bf16[1024,512]{1,0:T(8,128)(2,1)S(1)} %copy-done.32), channel_id=1, source_target_pairs={{0,3},{1,2},{2,1},{3,0},{4,7},{5,6},{6,5},{7,4},{8,11},{9,10},{10,... | collective-permute-start | bytes 3145736 | tf_op jit(solution)/shard_map/ppermute | solution.py:407
  321.2 125.4 %collective-permute-start.30 = (bf16[2,128,2048]{2,1,0:T(8,128)(2,1)}, bf16[2,128,2048]{2,1,0:T(8,128)(2,1)}, u32[]{:S(2)}, u32[]{:S(2)}) collective-permute-start(bf16[2,128,2048]{2,1,0:T(8,128)(2,1)} %get-tuple-element.119), channel_id=1, source_target_pairs={{0,3},{1,2},{2,1},{3,0},{4,7},{5,6},{6,5},{7,4},{8,11},{9,10},{10,... | collective-permute-start | bytes 3145736 | tf_op jit(solution)/shard_map/ppermute | solution.py:407
  498.8 630.6 %reduce-scatter.19.cloned.1.call-start = ((), (), s32[]{:S(2)}) async-start(), calls=%async_computation.12 | async-start | bytes 20971520
  697.1 95.9 %collective-permute-start.31 = (bf16[2,1024,512]{2,1,0:T(8,128)(2,1)}, bf16[2,1024,512]{2,1,0:T(8,128)(2,1)}, u32[]{:S(2)}, u32[]{:S(2)}) collective-permute-start(bf16[2,1024,512]{2,1,0:T(8,128)(2,1)} %get-tuple-element.141), channel_id=1, source_target_pairs={{0,1},{1,0},{2,3},{3,2},{4,5},{5,4},{6,7},{7,6},{8,9},{9,8},{10,11... | collective-permute-start | bytes 6291464 | tf_op jit(solution)/shard_map/ppermute | solution.py:407
  697.4 97.7 %collective-permute-start.32 = (bf16[2,1024,512]{2,1,0:T(8,128)(2,1)}, bf16[2,1024,512]{2,1,0:T(8,128)(2,1)}, u32[]{:S(2)}, u32[]{:S(2)}) collective-permute-start(bf16[2,1024,512]{2,1,0:T(8,128)(2,1)} %get-tuple-element.142), channel_id=1, source_target_pairs={{0,2},{1,3},{2,0},{3,1},{4,6},{5,7},{6,4},{7,5},{8,10},{9,11},{10,... | collective-permute-start | bytes 6291464 | tf_op jit(solution)/shard_map/ppermute | solution.py:407
  698.6 98.6 %collective-permute-start.33 = (bf16[2,1024,512]{2,1,0:T(8,128)(2,1)S(1)}, bf16[2,1024,512]{2,1,0:T(8,128)(2,1)}, u32[]{:S(2)}, u32[]{:S(2)}) collective-permute-start(bf16[2,1024,512]{2,1,0:T(8,128)(2,1)S(1)} %copy-done.25), channel_id=1, source_target_pairs={{0,3},{1,2},{2,1},{3,0},{4,7},{5,6},{6,5},{7,4},{8,11},{9,10},{10,... | collective-permute-start | bytes 6291464 | tf_op jit(solution)/shard_map/ppermute | solution.py:407
  834.3 56.9 %collective-permute-start.34 = (bf16[2,1024,512]{2,1,0:T(8,128)(2,1)}, bf16[2,1024,512]{2,1,0:T(8,128)(2,1)S(1)}, u32[]{:S(2)}, u32[]{:S(2)}) collective-permute-start(bf16[2,1024,512]{2,1,0:T(8,128)(2,1)} %fusion.77), channel_id=1, source_target_pairs={{0,1},{1,0},{2,3},{3,2},{4,5},{5,4},{6,7},{7,6},{8,9},{9,8},{10,11... | collective-permute-start | bytes 6291464 | tf_op jit(solution)/shard_map/ppermute | solution.py:407
  834.6 56.6 %collective-permute-start.35 = (bf16[2,1024,512]{2,1,0:T(8,128)(2,1)}, bf16[2,1024,512]{2,1,0:T(8,128)(2,1)}, u32[]{:S(2)}, u32[]{:S(2)}) collective-permute-start(bf16[2,1024,512]{2,1,0:T(8,128)(2,1)} %fusion.80), channel_id=1, source_target_pairs={{0,2},{1,3},{2,0},{3,1},{4,6},{5,7},{6,4},{7,5},{8,10},{9,11},{10,... | collective-permute-start | bytes 6291464 | tf_op jit(solution)/shard_map/ppermute | solution.py:407
  891.6 78.3 %collective-permute-start.37 = (bf16[2,1024,512]{2,1,0:T(8,128)(2,1)}, bf16[2,1024,512]{2,1,0:T(8,128)(2,1)}, u32[]{:S(2)}, u32[]{:S(2)}) collective-permute-start(bf16[2,1024,512]{2,1,0:T(8,128)(2,1)} %fusion.83), channel_id=1, source_target_pairs={{0,3},{1,2},{2,1},{3,0},{4,7},{5,6},{6,5},{7,4},{8,11},{9,10},{10,... | collective-permute-start | bytes 6291464 | tf_op jit(solution)/shard_map/ppermute | solution.py:407
  969.8 316.9 %reduce-scatter.21.cloned.1.call-start = ((), (), s32[]{:S(2)}) async-start(), calls=%async_computation.13 | async-start | bytes 20971520
  1129.4 249.2 %reduce-scatter.11.cloned.1.call-start = ((), (), s32[]{:S(2)}) async-start(), calls=%async_computation.6 | async-start | bytes 5242880 | tf_op jit(solution)/shard_map/reduce_scatter | solution.py:784
  1286.7 238.4 %reduce-scatter.13.cloned.1.call-start = ((), (), s32[]{:S(2)}) async-start(), calls=%async_computation.7 | async-start | bytes 5242880 | tf_op jit(solution)/shard_map/reduce_scatter | solution.py:811
  1286.8 91.8 %collective-permute-start.39 = (bf16[2,512,2048]{2,1,0:T(8,128)(2,1)}, bf16[2,512,2048]{2,1,0:T(8,128)(2,1)}, u32[]{:S(2)}, u32[]{:S(2)}) collective-permute-start(bf16[2,512,2048]{2,1,0:T(8,128)(2,1)} %fusion.35), channel_id=1, source_target_pairs={{0,1},{1,0},{2,3},{3,2},{4,5},{5,4},{6,7},{7,6},{8,9},{9,8},{10,11... | collective-permute-start | bytes 12582920 | tf_op jit(solution)/shard_map/ppermute | solution.py:407
  1287.2 91.4 %collective-permute-start.40 = (bf16[2,512,2048]{2,1,0:T(8,128)(2,1)}, bf16[2,512,2048]{2,1,0:T(8,128)(2,1)}, u32[]{:S(2)}, u32[]{:S(2)}) collective-permute-start(bf16[2,512,2048]{2,1,0:T(8,128)(2,1)} %fusion.38), channel_id=1, source_target_pairs={{0,2},{1,3},{2,0},{3,1},{4,6},{5,7},{6,4},{7,5},{8,10},{9,11},{10,... | collective-permute-start | bytes 12582920 | tf_op jit(solution)/shard_map/ppermute | solution.py:407
  1437.6 120.1 %reduce-scatter.17.cloned.1.call-start = ((), (), s32[]{:S(2)}) async-start(), calls=%async_computation.9 | async-start | bytes 2359296 | tf_op jit(solution)/shard_map/reduce_scatter | solution.py:812
  1437.7 87.5 %collective-permute-start.44 = (bf16[2,512,2048]{2,1,0:T(8,128)(2,1)}, bf16[2,512,2048]{2,1,0:T(8,128)(2,1)}, u32[]{:S(2)}, u32[]{:S(2)}) collective-permute-start(bf16[2,512,2048]{2,1,0:T(8,128)(2,1)} %fusion.41), channel_id=1, source_target_pairs={{0,3},{1,2},{2,1},{3,0},{4,7},{5,6},{6,5},{7,4},{8,11},{9,10},{10,... | collective-permute-start | bytes 12582920 | tf_op jit(solution)/shard_map/ppermute | solution.py:407
  1446.5 186.6 %reduce-scatter.15.cloned.1.call-start = ((), (), s32[]{:S(2)}) async-start(), calls=%async_computation.8 | async-start | bytes 7077888 | tf_op jit(solution)/shard_map/reduce_scatter | solution.py:535
  (85 other events, 2295.6 us)
Sparse Core Ops, SparseCore 0:
  192.1 306.5 all-gather.4
  502.2 194.8 all-gather.6
  970.0 159.3 reduce-scatter.18
  1132.8 153.8 reduce-scatter.20
  1288.8 76.9 reduce-scatter.10
  1437.7 82.0 reduce-scatter.12
  1522.1 33.2 reduce-scatter.16
  1557.8 69.5 reduce-scatter.14

commit v4 on v3

--- a/solution.py
+++ b/solution.py
@@ -640,19 +640,20 @@
             values = values.transpose(1, 0, 2, 3)
         return values.reshape(model_width, col_width)
 
-    segs = gather_cols(segments)
-    gain_all = gather_cols(attn_gain)
     tokens_all = gather_cols(tokens)
-    qkv_rows, segs, gain_all, tokens_all, out_in = fence(
-        heads_in(qkv_weight, ratio, head_size), segs, gain_all, tokens_all, out_weight
-    )
+    small = gather_cols(jnp.concatenate([attn_gain, segments.astype(F32).reshape(-1)]))
+    qkv_rows, small, tokens_all, out_in = fence(
+        heads_in(qkv_weight, ratio, head_size), small, tokens_all, out_weight
+    )
+    gain_all = small[:, :col_width]
+    segs = small[:, col_width:].astype(jnp.int32)
     cuts = (0, col_width // 2, 3 * col_width // 4, col_width)
     first, second, last = (
         split_parts(gate_up_parts[:, :, cuts[i] : cuts[i + 1]]) for i in range(3)
     )
     gate_up_first = send_parts(first)
-    qkv_rows, out_rows, gate_up_first, second, last, cot_in = fence(
-        over_chips(qkv_rows), over_chips(out_in), gate_up_first, second, last, cotangent
+    qkv_rows, out_rows, gate_up_first, second, last = fence(
+        over_chips(qkv_rows), over_chips(out_in), gate_up_first, second, last
     )
     gate_up_second, gate_up_last = send_parts(second), send_parts(last)
     if groups > 1:
@@ -663,7 +664,6 @@
         qkv_halves = [(over_cores(qkv_rows)[None], 0)]
     out_split = by_col(over_cores(out_rows))
     seg_row = lax.dynamic_index_in_dim(segs.reshape(rows, per_row), row, 0, keepdims=False)
-    cot_all = lax.all_gather(cot_in, ALL, axis=0).reshape(rows, cols, per_row, col_width)
 
     first = row * experts_here
     expert_ids = first + (col * mine_count + jnp.arange(mine_count, dtype=jnp.int32)) // split
@@ -697,9 +697,7 @@
         width_total(jnp.sum(hidden_one * hidden_one, axis=-1)) / model_width + epsilon
     )[:, None]
     moe_in = plain((hidden_one * rate_two * moe_gain).astype(BF16))
-    moe_in, gate_up_last, cot_all, down_first = fence(
-        moe_in, gate_up_last, cot_all, split_parts(down_parts)
-    )
+    moe_in, gate_up_last, down_first = fence(moe_in, gate_up_last, split_parts(down_parts))
     gate_up = jnp.zeros((mine_count, model_width, 2 * part_units), BF16)
     gate_up = join_parts(gate_up_first, 1, gate_up, 0)
     gate_up = join_parts(gate_up_second, 1, gate_up, cuts[1])
@@ -708,8 +706,10 @@
     moe_all = lax.all_gather(moe_in, ALL, axis=0).reshape(rows, cols, per_row, col_width)
     mine = jnp.reshape(core, (1,))
     others = 1 - mine
-    grad_slot = gather_slots(cot_all, place, gate, low, high, capacity, True)
-    moe_all, down_first, grad_slot = fence(moe_all, down_first, grad_slot)
+    moe_all, down_first, cot_in, gate_up, place, gate, low, high = fence(
+        moe_all, down_first, cotangent, gate_up, place, gate, low, high
+    )
+    cot_all = lax.all_gather(cot_in, ALL, axis=0).reshape(rows, cols, per_row, col_width)
     down = join_parts(send_parts(down_first), 2)
     slot_inputs = gather_slots(moe_all, place, gate, low, high, capacity, False)
 
@@ -736,6 +736,13 @@
     def feature_block(values, index):
         return lax.dynamic_slice_in_dim(values, index * col_width, col_width, 2)
 
+    expert_out = jnp.einsum("ecf,efd->ecd", hidden, down, preferred_element_type=F32).astype(BF16)
+    out_other = swap_cores(combine(expert_out, core=others, scaled=True))
+    out_partial = combine(expert_out, core=mine, scaled=True, more=(out_other,))
+    out_partial, cot_all = fence(out_partial, cot_all)
+    out_partial = plain(lax.psum_scatter(out_partial, "col", scatter_dimension=0, tiled=True)[0])
+
+    grad_slot = gather_slots(cot_all, place, gate, low, high, capacity, True)
     down_grads = []
     for mask in range(cols):
         part = jnp.einsum(
@@ -743,31 +750,24 @@
             preferred_element_type=F32,
         )
         down_grads.append(part.astype(BF16) if mask else part)
-    down_grads, hidden = fence(down_grads, hidden)
-    got_down = down_grads[:1] + [swap_cols(down_grads[mask], mask) for mask in range(1, cols)]
-
-    expert_out = jnp.einsum("ecf,efd->ecd", hidden, down, preferred_element_type=F32).astype(BF16)
-    out_other = combine(expert_out, core=others, scaled=True)
-    near = cols // 2 + 1
-    out_other, grad_slot, near_down = fence(out_other, grad_slot, got_down[1:near])
-    got_down[1:near] = near_down
-    out_other = swap_cores(out_other)
+    down_grads, grad_slot = fence(down_grads, grad_slot)
+    got_down = send_parts(down_grads)
     grad_hidden = jnp.einsum("ecd,efd->ecf", grad_slot, down, preferred_element_type=F32)
     grad_gate_pre = (
         grad_hidden * up_wide * sigmoid_gate * (1.0 + gate_wide * (1.0 - sigmoid_gate))
     ).astype(BF16)
     grad_up_pre = (grad_hidden * activated).astype(BF16)
     grad_inner = jnp.concatenate([grad_gate_pre, grad_up_pre], axis=-1)
-    out_other, grad_inner = fence(out_other, grad_inner)
-    out_partial = combine(expert_out, core=mine, scaled=True, more=(out_other,))
-    out_partial, grad_inner, got_down = fence(out_partial, grad_inner, got_down)
-    out_partial = plain(lax.psum_scatter(out_partial, "col", scatter_dimension=0, tiled=True)[0])
 
     grad_slot_in = jnp.einsum(
         "ecf,edf->ecd", grad_inner, gate_up, preferred_element_type=F32
     ).astype(BF16)
     grad_other = combine(grad_slot_in, core=others, scaled=False)
-    grad_other, grad_inner = fence(grad_other, grad_inner)
+    near = cols // 2 + 1
+    grad_other, grad_inner, near_down, out_partial = fence(
+        grad_other, grad_inner, got_down[1:near], out_partial
+    )
+    got_down[1:near] = near_down
     grad_other = swap_cores(grad_other)
     inner_parts = []
     for mask in range(cols):
@@ -778,7 +778,7 @@
         inner_parts.append(part.astype(BF16) if mask else part)
     grad_other, inner_parts[1] = fence(grad_other, inner_parts[1])
     grad_partial = combine(grad_slot_in, core=mine, scaled=False, more=(grad_other,))
-    grad_partial, out_partial = fence(grad_partial, out_partial)
+    grad_partial, got_down = fence(grad_partial, got_down)
     grad_partial = plain(lax.psum_scatter(grad_partial, "col", scatter_dimension=0, tiled=True)[0])
     grad_partial, inner_parts, out_partial = fence(grad_partial, inner_parts, out_partial)
     grad_moe_in = plain(lax.psum_scatter(grad_partial, "chip", scatter_dimension=0, tiled=True)[0])

time: 1670 us -> 1630 us (0.976)
  blocking collectives: 60.9 us -> 20.6 us
    all_gather x1, waiting for transfers between devices: 103 us -> 160 us  [local(): lax.all_gather(moe_in, ALL, axis=0).reshape(rows, cols, per_row, col_width)]
    all_gather x1, waiting for transfers between devices: 52.1 us -> 0.01 us  [local(): lax.all_gather(cot_in, ALL, axis=0).reshape(rows, cols, per_row, col_width)]
    unnamed x10, waiting for transfers between devices: 140 us -> 99.5 us
    psum x3, blocking collectives: 60.9 us -> 20.6 us  [width_total(): return lax.psum(values, 'col')]
    ppermute x4, waiting for transfers between devices: 8.09 us -> 42.2 us  [swap_cores(): return lax.ppermute(values, 'core', [(0, 1), (1, 0)])]
    ppermute x2, waiting for transfers between devices: 27.9 us -> 0.01 us  [heads_in(): pieces.append(lax.ppermute(piece, ('core', 'col'), pairs))]
    ppermute x36 -> x33, waiting for transfers between devices: 316 us -> 334 us  [swap_cols(): return lax.ppermute(values, 'col', [(i, i ^ mask) for i in range(count)])]
  transfers between devices with their start and end apart: 61 -> 58, of which waited for: 28 -> 22; matrix products, arithmetic and copies ran while one was open for 29% -> 34% of each run, Pallas kernels for 15% -> 16%
where the time goes in v4:
time: 1630 us; the launch traced here: 1620 us
  waiting for transfers between devices  714 us (44%)
  matrix products  309 us (19%)
  Pallas kernels  254 us (16%)
  local copies, waits for them, and re-layouts  164 us (10%)
  other arithmetic  89.4 us (5%)
  starting transfers between devices  56.3 us (3%)
  blocking collectives  20.6 us (1%)
    ppermute x33, waiting for transfers between devices, swap_cols(): return lax.ppermute(values, 'col', [(i, i ^ mask) for i in range(count)])  334 us
    all_gather x1, waiting for transfers between devices, local(): lax.all_gather(moe_in, ALL, axis=0).reshape(rows, cols, per_row, col_width)  160 us
    pallas_call x4, Pallas kernels, combine_slots(): pl.pallas_call(partial(combine_kernel, scaled, each), grid_spec=pltpu.Pre...  123 us
    unnamed x10, waiting for transfers between devices  99.5 us
    pallas_call x2, Pallas kernels, gather_slots(): pl.pallas_call(partial(gather_kernel, scaled, each), grid_spec=pltpu.Pref...  83 us
    ppermute x6, waiting for transfers between devices, swap_chips(): return lax.ppermute(values, 'chip', [(i, i ^ mask) for i in range(count)])  71.6 us
    dot_general x4, matrix products, local(): jnp.einsum('ecd,ecf->edf', feature_block(slot_inputs, col ^ mask), grad_i...  67.9 us
    dot_general x1, matrix products, local(): jnp.einsum('ecf,edf->ecd', grad_inner, gate_up, preferred_element_type=F32)  42.8 us
  transfers between devices with their start and end apart: 58, of which 22 were waited for; matrix products, arithmetic and copies ran while one was open for 34% of the time, Pallas kernels for 16%

profile of v4, /device:TPU:3, one launch (start us, length us, event | category | flops | bytes accessed | tf_op | source)
XLA Modules:
  0.0 1622.7 jit_solution(17560751653670689706)
XLA Ops:
  53.0 33.1 %collective-permute-done.6 = bf16[1024,512]{1,0:T(8,128)(2,1)} collective-permute-done((bf16[1024,512]{1,0:T(8,128)(2,1)S(1)}, bf16[1024,512]{1,0:T(8,128)(2,1)}, u32[]{:S(2)}, u32[]{:S(2)}) %collective-permute-start.6) | collective-permute-done | bytes 1048608 | tf_op jit(solution)/shard_map/ppermute | solution.py:407
  108.5 16.3 %collective-permute-done.13 = bf16[256,512]{1,0:T(8,128)(2,1)S(1)} collective-permute-done((bf16[256,512]{1,0:T(8,128)(2,1)S(1)}, bf16[256,512]{1,0:T(8,128)(2,1)S(1)}, u32[]{:S(2)}, u32[]{:S(2)}) %collective-permute-start.13) | collective-permute-done | bytes 262176 | tf_op jit(solution)/shard_map/ppermute | solution.py:462
  131.7 48.5 %collective-permute-done.9 = bf16[1024,384]{0,1:T(8,128)(2,1)S(1)} collective-permute-done((bf16[1024,384]{0,1:T(8,128)(2,1)S(1)}, bf16[1024,384]{0,1:T(8,128)(2,1)S(1)}, u32[]{:S(2)}, u32[]{:S(2)}) %collective-permute-start.9) | collective-permute-done | bytes 786464 | tf_op jit(solution)/shard_map/ppermute | solution.py:462
  219.6 19.2 %attend_forward.1 = (bf16[1024,512]{1,0:T(8,128)(2,1)}, f32[1024,512]{1,0:T(8,128)}) custom-call(f32[4,1024,384]{2,1,0:T(8,128)} %add_bitcast_fusion.query_ref.key_ref.value_ref, f32[4,1024,384]{2,1,0:T(8,128)} %add_bitcast_fusion.query_ref.key_ref.value_ref, f32[4,1024,384]{2,1,0:T(8,128)} %add_bitcast_fusion.query_ref.key_ref.value_ref, ...), custom_call_target="tpu_custom_call" | custom-call | flops 2147483648 | bytes 9437184 | tf_op jit(solution)/shard_map/attend_forward/pallas_call | solution.py:108
  238.7 13.6 collective-permute-done.20
  277.3 74.7 %collective-permute-done.22 = bf16[1024,512]{1,0:T(8,128)(2,1)S(1)} collective-permute-done((bf16[1024,512]{1,0:T(8,128)(2,1)S(1)}, bf16[1024,512]{1,0:T(8,128)(2,1)S(1)}, u32[]{:S(2)}, u32[]{:S(2)}) %collective-permute-start.22) | collective-permute-done | bytes 1048608 | tf_op jit(solution)/shard_map/ppermute | solution.py:407
  416.9 159.5 %all-gather.5.cloned.1.call-done = bf16[32768,512]{1,0:T(8,128)(2,1)} async-done(((bf16[1024,512]{1,0:T(8,128)(2,1)}), bf16[32768,512]{1,0:T(8,128)(2,1)}) %all-gather.5.cloned.1.call-update) | async-done | bytes 33554448 | tf_op jit(solution)/shard_map/all_gather | solution.py:706
  580.6 41.3 %gather_slots.2 = bf16[2,2048,2048]{2,1,0:T(8,128)(2,1)} custom-call(s32[2,16]{1,0:T(2,128)} %get-tuple-element.134.low_ref, s32[2,16]{1,0:T(2,128)} %get-tuple-element.135.high_ref, bf16[8,4,1024,512]{3,2,1,0:T(8,128)(2,1)} %bitcast.305, bf16[8,4,1024,512]{3,2,1,0:T(8,128)(2,1)} %bitcast.306, s32[2,16,1,512]{3,2,1,0:T(1,128)} %reshape.129.refs_2_.refs_3_.place_ref, ...), custom_call_target="tpu_custom_call" | custom-call | flops 25769803776 | bytes 50331648 | tf_op jit(solution)/shard_map/gather_slots/pallas_call | solution.py:299
  621.9 24.6 %fusion.12 = bf16[2,2048,1024]{1,2,0:T(8,128)(2,1)} fusion(bf16[2,2048,2048]{2,1,0:T(8,128)(2,1)} %gather_slots.2, bf16[2,2048,2048]{1,2,0:T(8,128)(2,1)} %constant_dynamic-update-slice_fusion.4), kind=kOutput, calls=%fused_computation.27 | convolution fusion | flops 17184063488 | bytes 33554432 | tf_op jit(solution)/shard_map/ecd,edf->ecf/dot_general | solution.py:718
  646.5 28.3 %fusion = (bf16[2,2048,1024]{1,2,0:T(8,128)(2,1)}, bf16[2,2048,1024]{1,2,0:T(8,128)(2,1)}) fusion(bf16[2,2048,1024]{1,2,0:T(8,128)(2,1)} %fusion.12, bf16[2,2048,2048]{2,1,0:T(8,128)(2,1)} %gather_slots.2, bf16[2,2048,2048]{1,2,0:T(8,128)(2,1)} %constant_dynamic-update-slice_fusion.4), kind=kOutput, calls=%fused_computation.5 | convolution fusion | flops 17217617920 | bytes 50331648 | tf_op jit(solution)/shard_map/ecd,edf->ecf/dot_general | solution.py:721
  687.1 20.5 %collective-permute-done.30 = bf16[2,1024,512]{2,1,0:T(8,128)(2,1)S(1)} collective-permute-done((bf16[2,1024,512]{2,1,0:T(8,128)(2,1)}, bf16[2,1024,512]{2,1,0:T(8,128)(2,1)S(1)}, u32[]{:S(2)}, u32[]{:S(2)}) %collective-permute-start.30) | collective-permute-done | bytes 2097184 | tf_op jit(solution)/shard_map/ppermute | solution.py:407
  709.1 28.2 %convolution_convert_fusion.slots_ref = bf16[2,2048,2048]{2,1,0:T(8,128)(2,1)} fusion(bf16[2,2048,1024]{1,2,0:T(8,128)(2,1)} %get-tuple-element.144, bf16[2,1024,2048]{2,1,0:T(8,128)(2,1)} %constant_dynamic-update-slice_fusion), kind=kOutput, calls=%fused_computation.15 | convolution fusion | flops 17188257792 | bytes 33554432 | tf_op jit(solution)/shard_map/ecf,efd->ecd/dot_general | solution.py:739
  737.3 29.1 %combine_slots.4 = bf16[4,4,1024,512]{3,2,1,0:T(8,128)(2,1)} custom-call(s32[2,16]{1,0:T(2,128)} %get-tuple-element.134.low_ref, s32[2,16]{1,0:T(2,128)} %get-tuple-element.135.high_ref, s32[1]{0:T(128)S(6)} %sub.54.core_ref, bf16[2,2048,2048]{2,1,0:T(8,128)(2,1)} %convolution_convert_fusion.slots_ref, s32[2,16,1,512]{3,2,1,0:T(1,128)} %reshape.129.refs_2_.refs_3_.place_ref, ...), custom_call_target="tpu_custom_call" | custom-call | flops 12884901888 | bytes 33554432 | tf_op jit(solution)/shard_map/combine_slots/pallas_call | solution.py:364
  767.5 34.9 %collective-permute-done.31.refs_0_ = bf16[4,4,1024,512]{3,2,1,0:T(8,128)(2,1)} collective-permute-done((bf16[4,4,1024,512]{3,2,1,0:T(8,128)(2,1)}, bf16[4,4,1024,512]{3,2,1,0:T(8,128)(2,1)}, u32[]{:S(2)}, u32[]{:S(2)}) %collective-permute-start.31) | collective-permute-done | bytes 16777248 | tf_op jit(solution)/shard_map/ppermute | solution.py:402
  802.4 33.8 %combine_slots.5 = bf16[4,4,1024,512]{3,2,1,0:T(8,128)(2,1)} custom-call(s32[2,16]{1,0:T(2,128)} %get-tuple-element.134.low_ref, s32[2,16]{1,0:T(2,128)} %get-tuple-element.135.high_ref, s32[1]{0:T(128)} %bitcast.65.core_ref, bf16[2,2048,2048]{2,1,0:T(8,128)(2,1)} %convolution_convert_fusion.slots_ref, s32[2,16,1,512]{3,2,1,0:T(1,128)} %reshape.129.refs_2_.refs_3_.place_ref, ...), custom_call_target="tpu_custom_call" | custom-call | flops 12884901888 | bytes 33554432 | tf_op jit(solution)/shard_map/combine_slots/pallas_call | solution.py:364
  836.3 41.7 %gather_slots.3 = bf16[2,2048,2048]{2,1,0:T(8,128)(2,1)} custom-call(s32[2,16]{1,0:T(2,128)} %get-tuple-element.134.low_ref, s32[2,16]{1,0:T(2,128)} %get-tuple-element.135.high_ref, bf16[8,4,1024,512]{3,2,1,0:T(8,128)(2,1)} %bitcast.307, bf16[8,4,1024,512]{3,2,1,0:T(8,128)(2,1)} %bitcast.308, s32[2,16,1,512]{3,2,1,0:T(1,128)} %reshape.129.refs_2_.refs_3_.place_ref, ...), custom_call_target="tpu_custom_call" | custom-call | flops 25769803776 | bytes 50331648 | tf_op jit(solution)/shard_map/gather_slots/pallas_call | solution.py:299
  918.0 32.8 %fusion.3 = (bf16[2,2048,1024]{1,2,0:T(8,128)(2,1)}, bf16[2,2048,1024]{1,2,0:T(8,128)(2,1)}) fusion(bf16[2,2048,1024]{1,2,0:T(8,128)(2,1)} %get-tuple-element.264, bf16[2,2048,1024]{1,2,0:T(8,128)(2,1)} %fusion.12, bf16[2,2048,2048]{2,1,0:T(8,128)(2,1)} %gather_slots.3, bf16[2,1024,2048]{2,1,0:T(8,128)(2,1)} %constant_dynamic-update-slice_fusion), kind=kOutput, calls=%fused_computation.8 | convolution fusion | flops 17242783744 | bytes 58720256 | tf_op jit(solution)/shard_map/ecd,efd->ecf/dot_general | solution.py:755
  950.8 42.8 %convolution_convert_fusion.1.slots_ref = bf16[2,2048,2048]{2,1,0:T(8,128)(2,1)} fusion(bf16[2,2048,2048]{1,2,0:T(8,128)(2,1)} %constant_dynamic-update-slice_fusion.4, bf16[2,2048,1024]{1,2,0:T(8,128)(2,1)} %get-tuple-element.200, bf16[2,2048,1024]{1,2,0:T(8,128)(2,1)} %get-tuple-element.199), kind=kOutput, calls=%fused_computation.16 | convolution fusion | flops 34401681408 | bytes 50331648 | tf_op jit(solution)/shard_map/ecf,edf->ecd/dot_general | solution.py:762
  993.6 14.1 pad_maximum_fusion
  1007.7 27.9 %combine_slots.6 = bf16[4,4,1024,512]{3,2,1,0:T(8,128)(2,1)} custom-call(s32[2,16]{1,0:T(2,128)} %get-tuple-element.134.low_ref, s32[2,16]{1,0:T(2,128)} %get-tuple-element.135.high_ref, s32[1]{0:T(128)S(6)} %sub.54.core_ref, bf16[2,2048,2048]{2,1,0:T(8,128)(2,1)} %convolution_convert_fusion.1.slots_ref, ...), custom_call_target="tpu_custom_call" | custom-call | flops 12884901888 | bytes 33554432 | tf_op jit(solution)/shard_map/combine_slots/pallas_call | solution.py:364
  1037.4 16.5 %fusion.35 = bf16[2,512,2048]{2,1,0:T(8,128)(2,1)} fusion(bf16[2,2048,2048]{1,2,0:T(8,128)(2,1)} %pad_maximum_fusion, bf16[2,2048,2048]{2,1,0:T(8,128)(2,1)} %gather_slots.2, s32[]{:T(128)S(6)} %select_n.277), kind=kOutput, calls=%fused_computation.55 | convolution fusion | flops 8592031744 | bytes 25165828 | tf_op jit(solution)/shard_map/ecd,ecf->edf/dot_general | solution.py:774
  1061.2 32.3 %combine_slots.7 = bf16[4,4,1024,512]{3,2,1,0:T(8,128)(2,1)} custom-call(s32[2,16]{1,0:T(2,128)} %get-tuple-element.134.low_ref, s32[2,16]{1,0:T(2,128)} %get-tuple-element.135.high_ref, s32[1]{0:T(128)} %bitcast.65.core_ref, bf16[2,2048,2048]{2,1,0:T(8,128)(2,1)} %convolution_convert_fusion.1.slots_ref, ...), custom_call_target="tpu_custom_call" | custom-call | flops 12884901888 | bytes 33554432 | tf_op jit(solution)/shard_map/combine_slots/pallas_call | solution.py:364
  1093.6 17.0 %fusion.38 = bf16[2,512,2048]{2,1,0:T(8,128)(2,1)} fusion(bf16[2,2048,2048]{1,2,0:T(8,128)(2,1)} %pad_maximum_fusion, bf16[2,2048,2048]{2,1,0:T(8,128)(2,1)} %gather_slots.2, s32[]{:T(128)S(6)} %select_n.278), kind=kOutput, calls=%fused_computation.56 | convolution fusion | flops 8592031744 | bytes 25165828 | tf_op jit(solution)/shard_map/ecd,ecf->edf/dot_general | solution.py:774
  1110.6 16.8 %fusion.41 = bf16[2,512,2048]{2,1,0:T(8,128)(2,1)} fusion(bf16[2,2048,2048]{1,2,0:T(8,128)(2,1)} %pad_maximum_fusion, bf16[2,2048,2048]{2,1,0:T(8,128)(2,1)} %gather_slots.2, s32[]{:T(128)S(6)} %select_n.279), kind=kOutput, calls=%fused_computation.57 | convolution fusion | flops 8592031744 | bytes 25165828 | tf_op jit(solution)/shard_map/ecd,ecf->edf/dot_general | solution.py:774
  1127.4 17.6 %fusion.23 = f32[2,512,2048]{2,1,0:T(8,128)} fusion(bf16[2,2048,2048]{1,2,0:T(8,128)(2,1)} %pad_maximum_fusion, bf16[2,2048,2048]{2,1,0:T(8,128)(2,1)} %gather_slots.2, s32[]{:T(128)S(6)} %select_n.276), kind=kOutput, calls=%fused_computation.43 | convolution fusion | flops 8589934592 | bytes 29360132 | tf_op jit(solution)/shard_map/ecd,ecf->edf/dot_general | solution.py:774
  1145.0 99.4 %reduce-scatter.21.cloned.1.call-done = bf16[1,4,1024,512]{3,2,1,0:T(8,128)(2,1)} async-done(((bf16[4,4,1024,512]{3,2,1,0:T(8,128)(2,1)}), bf16[1,4,1024,512]{3,2,1,0:T(8,128)(2,1)}) %reduce-scatter.21.cloned.1.call-update) | async-done | bytes 4194320
  1257.0 79.2 %collective-permute-done.36 = bf16[2,512,2048]{2,1,0:T(8,128)(2,1)} collective-permute-done((bf16[2,512,2048]{2,1,0:T(8,128)(2,1)}, bf16[2,512,2048]{2,1,0:T(8,128)(2,1)}, u32[]{:S(2)}, u32[]{:S(2)}) %collective-permute-start.36) | collective-permute-done | bytes 4194336 | tf_op jit(solution)/shard_map/ppermute | solution.py:407
  1372.9 26.4 %collective-permute-done.39 = bf16[1024,512]{1,0:T(8,128)(2,1)S(1)} collective-permute-done((bf16[1024,512]{1,0:T(8,128)(2,1)S(1)}, bf16[1024,512]{1,0:T(8,128)(2,1)S(1)}, u32[]{:S(2)}, u32[]{:S(2)}) %collective-permute-start.39) | collective-permute-done | bytes 1048608 | tf_op jit(solution)/shard_map/ppermute | solution.py:407
  1441.9 28.6 %attend_backward.1 = (bf16[4,1024,384]{2,1,0:T(8,128)(2,1)}, f32[2,128]{1,0:T(2,128)}) custom-call(f32[4,1024,384]{2,1,0:T(8,128)} %add_bitcast_fusion.query_ref.key_ref.value_ref, f32[4,1024,384]{2,1,0:T(8,128)} %add_bitcast_fusion.query_ref.key_ref.value_ref, f32[4,1024,384]{2,1,0:T(8,128)} %add_bitcast_fusion.query_ref.key_ref.value_ref, ...), custom_call_target="tpu_custom_call" | custom-call | flops 5368709120 | bytes 12582912 | tf_op jit(solution)/shard_map/attend_backward/pallas_call | solution.py:194
  1470.6 23.3 %collective-permute-done.41 = bf16[2,512,2048]{2,1,0:T(8,128)(2,1)} collective-permute-done((bf16[2,512,2048]{2,1,0:T(8,128)(2,1)}, bf16[2,512,2048]{2,1,0:T(8,128)(2,1)}, u32[]{:S(2)}, u32[]{:S(2)}) %collective-permute-start.41) | collective-permute-done | bytes 4194336 | tf_op jit(solution)/shard_map/ppermute | solution.py:407
  1526.8 20.0 %collective-permute-done.44 = bf16[1024,512]{1,0:T(8,128)(2,1)} collective-permute-done((bf16[1024,512]{1,0:T(8,128)(2,1)}, bf16[1024,512]{1,0:T(8,128)(2,1)}, u32[]{:S(2)}, u32[]{:S(2)}) %collective-permute-start.44) | collective-permute-done | bytes 1048608 | tf_op jit(solution)/shard_map/ppermute | solution.py:407
  1546.8 24.3 %collective-permute-done.43 = bf16[1024,512]{1,0:T(8,128)(2,1)} collective-permute-done((bf16[1024,512]{1,0:T(8,128)(2,1)}, bf16[1024,512]{1,0:T(8,128)(2,1)}, u32[]{:S(2)}, u32[]{:S(2)}) %collective-permute-start.43) | collective-permute-done | bytes 1048608 | tf_op jit(solution)/shard_map/ppermute | solution.py:407
  (381 shorter events, 440.9 us)
Async XLA Ops:
  7.2 569.3 %all-gather.5.cloned.1.call-start = ((), (), s32[]{:S(2)}) async-start(), calls=%async_computation.10 | async-start | bytes 34603008 | tf_op jit(solution)/shard_map/all_gather | solution.py:706
  38.7 47.4 %collective-permute-start.6 = (bf16[1024,512]{1,0:T(8,128)(2,1)S(1)}, bf16[1024,512]{1,0:T(8,128)(2,1)}, u32[]{:S(2)}, u32[]{:S(2)}) collective-permute-start(bf16[1024,512]{1,0:T(8,128)(2,1)S(1)} %copy-done.4), channel_id=1, source_target_pairs={{0,2},{1,3},{2,0},{3,1},{4,6},{5,7},{6,4},{7,5},{8,10},{9,11},{10,... | collective-permute-start | bytes 3145736 | tf_op jit(solution)/shard_map/ppermute | solution.py:407
  47.9 134.2 %collective-permute-start.14 = (bf16[2,256,2048]{2,1,0:T(8,128)(2,1)}, bf16[2,256,2048]{2,1,0:T(8,128)(2,1)}, u32[]{:S(2)}, u32[]{:S(2)}) collective-permute-start(bf16[2,256,2048]{2,1,0:T(8,128)(2,1)} %get-tuple-element.213), channel_id=1, source_target_pairs={{0,1},{1,0},{2,3},{3,2},{4,5},{5,4},{6,7},{7,6},{8,9},{9,8},{10,11... | collective-permute-start | bytes 6291464 | tf_op jit(solution)/shard_map/ppermute | solution.py:407
  48.0 134.1 %collective-permute-start.15 = (bf16[2,256,2048]{2,1,0:T(8,128)(2,1)}, bf16[2,256,2048]{2,1,0:T(8,128)(2,1)}, u32[]{:S(2)}, u32[]{:S(2)}) collective-permute-start(bf16[2,256,2048]{2,1,0:T(8,128)(2,1)} %get-tuple-element.212), channel_id=1, source_target_pairs={{0,2},{1,3},{2,0},{3,1},{4,6},{5,7},{6,4},{7,5},{8,10},{9,11},{10,... | collective-permute-start | bytes 6291464 | tf_op jit(solution)/shard_map/ppermute | solution.py:407
  49.6 132.5 %collective-permute-start.16 = (bf16[2,256,2048]{2,1,0:T(8,128)(2,1)}, bf16[2,256,2048]{2,1,0:T(8,128)(2,1)}, u32[]{:S(2)}, u32[]{:S(2)}) collective-permute-start(bf16[2,256,2048]{2,1,0:T(8,128)(2,1)} %get-tuple-element.211), channel_id=1, source_target_pairs={{0,3},{1,2},{2,1},{3,0},{4,7},{5,6},{6,5},{7,4},{8,11},{9,10},{10,... | collective-permute-start | bytes 6291464 | tf_op jit(solution)/shard_map/ppermute | solution.py:407
  124.8 55.4 %collective-permute-start.9 = (bf16[1024,384]{0,1:T(8,128)(2,1)S(1)}, bf16[1024,384]{0,1:T(8,128)(2,1)S(1)}, u32[]{:S(2)}, u32[]{:S(2)}) collective-permute-start(bf16[1024,384]{0,1:T(8,128)(2,1)S(1)} %maximum_maximum_fusion), channel_id=1, source_target_pairs={{0,16},{8,24},{16,0},{24,8},{1,17},{9,25},{17,1},{25,9},{2,18},{10... | collective-permute-start | bytes 2359304 | tf_op jit(solution)/shard_map/ppermute | solution.py:462
  125.2 56.0 %collective-permute-start.10 = (bf16[1024,384]{0,1:T(8,128)(2,1)S(1)}, bf16[1024,384]{0,1:T(8,128)(2,1)S(1)}, u32[]{:S(2)}, u32[]{:S(2)}) collective-permute-start(bf16[1024,384]{0,1:T(8,128)(2,1)S(1)} %maximum_maximum_fusion), channel_id=1, source_target_pairs={{0,24},{8,16},{16,8},{24,0},{1,25},{9,17},{17,9},{25,1},{2,26},{10... | collective-permute-start | bytes 2359304 | tf_op jit(solution)/shard_map/ppermute | solution.py:462
  206.4 56.1 %collective-permute-start.24 = (bf16[4,256,512]{2,1,0:T(8,128)(2,1)S(1)}, bf16[4,256,512]{2,1,0:T(8,128)(2,1)S(1)}, u32[]{:S(2)}, u32[]{:S(2)}) collective-permute-start(bf16[4,256,512]{2,1,0:T(8,128)(2,1)S(1)} %bitcast_dynamic-update-slice_fusion.14), channel_id=1, source_target_pairs={{0,4},{4,0},{1,5},{5,1},{2,6},{6,2},{3,7},{7,3},{8,12},{12,8},{9,1... | collective-permute-start | bytes 3145736 | tf_op jit(solution)/shard_map/ppermute | solution.py:402
  259.7 102.6 %collective-permute-start.25 = (bf16[2,128,2048]{2,1,0:T(8,128)(2,1)}, bf16[2,128,2048]{2,1,0:T(8,128)(2,1)}, u32[]{:S(2)}, u32[]{:S(2)}) collective-permute-start(bf16[2,128,2048]{2,1,0:T(8,128)(2,1)} %get-tuple-element.114), channel_id=1, source_target_pairs={{0,1},{1,0},{2,3},{3,2},{4,5},{5,4},{6,7},{7,6},{8,9},{9,8},{10,11... | collective-permute-start | bytes 3145736 | tf_op jit(solution)/shard_map/ppermute | solution.py:407
  261.0 101.2 %collective-permute-start.26 = (bf16[2,128,2048]{2,1,0:T(8,128)(2,1)}, bf16[2,128,2048]{2,1,0:T(8,128)(2,1)}, u32[]{:S(2)}, u32[]{:S(2)}) collective-permute-start(bf16[2,128,2048]{2,1,0:T(8,128)(2,1)} %get-tuple-element.115), channel_id=1, source_target_pairs={{0,2},{1,3},{2,0},{3,1},{4,6},{5,7},{6,4},{7,5},{8,10},{9,11},{10,... | collective-permute-start | bytes 3145736 | tf_op jit(solution)/shard_map/ppermute | solution.py:407
  261.0 90.9 %collective-permute-start.22 = (bf16[1024,512]{1,0:T(8,128)(2,1)S(1)}, bf16[1024,512]{1,0:T(8,128)(2,1)S(1)}, u32[]{:S(2)}, u32[]{:S(2)}) collective-permute-start(bf16[1024,512]{1,0:T(8,128)(2,1)S(1)} %copy-done.33), channel_id=1, source_target_pairs={{0,2},{1,3},{2,0},{3,1},{4,6},{5,7},{6,4},{7,5},{8,10},{9,11},{10,... | collective-permute-start | bytes 3145736 | tf_op jit(solution)/shard_map/ppermute | solution.py:407
  263.5 88.6 %collective-permute-start.23 = (bf16[1024,512]{1,0:T(8,128)(2,1)S(1)}, bf16[1024,512]{1,0:T(8,128)(2,1)S(1)}, u32[]{:S(2)}, u32[]{:S(2)}) collective-permute-start(bf16[1024,512]{1,0:T(8,128)(2,1)S(1)} %copy-done.33), channel_id=1, source_target_pairs={{0,3},{1,2},{2,1},{3,0},{4,7},{5,6},{6,5},{7,4},{8,11},{9,10},{10,... | collective-permute-start | bytes 3145736 | tf_op jit(solution)/shard_map/ppermute | solution.py:407
  276.6 85.7 %collective-permute-start.27 = (bf16[2,128,2048]{2,1,0:T(8,128)(2,1)}, bf16[2,128,2048]{2,1,0:T(8,128)(2,1)}, u32[]{:S(2)}, u32[]{:S(2)}) collective-permute-start(bf16[2,128,2048]{2,1,0:T(8,128)(2,1)} %get-tuple-element.116), channel_id=1, source_target_pairs={{0,3},{1,2},{2,1},{3,0},{4,7},{5,6},{6,5},{7,4},{8,11},{9,10},{10,... | collective-permute-start | bytes 3145736 | tf_op jit(solution)/shard_map/ppermute | solution.py:407
  362.3 474.0 %all-gather.7.cloned.1.call-start = ((), (), s32[]{:S(2)}) async-start(), calls=%async_computation.11 | async-start | bytes 34603008 | tf_op jit(solution)/shard_map/all_gather | solution.py:712
  576.5 459.2 %reduce-scatter.19.cloned.1.call-start = ((), (), s32[]{:S(2)}) async-start(), calls=%async_computation.12 | async-start | bytes 20971520
  578.0 102.7 %collective-permute-start.28 = (bf16[2,1024,512]{2,1,0:T(8,128)(2,1)}, bf16[2,1024,512]{2,1,0:T(8,128)(2,1)}, u32[]{:S(2)}, u32[]{:S(2)}) collective-permute-start(bf16[2,1024,512]{2,1,0:T(8,128)(2,1)} %get-tuple-element.141), channel_id=1, source_target_pairs={{0,1},{1,0},{2,3},{3,2},{4,5},{5,4},{6,7},{7,6},{8,9},{9,8},{10,11... | collective-permute-start | bytes 6291464 | tf_op jit(solution)/shard_map/ppermute | solution.py:407
  578.3 105.6 %collective-permute-start.29 = (bf16[2,1024,512]{2,1,0:T(8,128)(2,1)}, bf16[2,1024,512]{2,1,0:T(8,128)(2,1)}, u32[]{:S(2)}, u32[]{:S(2)}) collective-permute-start(bf16[2,1024,512]{2,1,0:T(8,128)(2,1)} %get-tuple-element.142), channel_id=1, source_target_pairs={{0,2},{1,3},{2,0},{3,1},{4,6},{5,7},{6,4},{7,5},{8,10},{9,11},{10,... | collective-permute-start | bytes 6291464 | tf_op jit(solution)/shard_map/ppermute | solution.py:407
  579.5 128.1 %collective-permute-start.30 = (bf16[2,1024,512]{2,1,0:T(8,128)(2,1)}, bf16[2,1024,512]{2,1,0:T(8,128)(2,1)S(1)}, u32[]{:S(2)}, u32[]{:S(2)}) collective-permute-start(bf16[2,1024,512]{2,1,0:T(8,128)(2,1)} %get-tuple-element.143), channel_id=1, source_target_pairs={{0,3},{1,2},{2,1},{3,0},{4,7},{5,6},{6,5},{7,4},{8,11},{9,10},{10,... | collective-permute-start | bytes 6291464 | tf_op jit(solution)/shard_map/ppermute | solution.py:407
  836.2 408.2 %reduce-scatter.21.cloned.1.call-start = ((), (), s32[]{:S(2)}) async-start(), calls=%async_computation.13 | async-start | bytes 20971520
  918.0 117.6 %collective-permute-start.32 = (bf16[2,1024,512]{2,1,0:T(8,128)(2,1)}, bf16[2,1024,512]{2,1,0:T(8,128)(2,1)S(1)}, u32[]{:S(2)}, u32[]{:S(2)}) collective-permute-start(bf16[2,1024,512]{2,1,0:T(8,128)(2,1)} %fusion.77), channel_id=1, source_target_pairs={{0,1},{1,0},{2,3},{3,2},{4,5},{5,4},{6,7},{7,6},{8,9},{9,8},{10,11... | collective-permute-start | bytes 6291464 | tf_op jit(solution)/shard_map/ppermute | solution.py:407
  918.0 117.6 %collective-permute-start.33 = (bf16[2,1024,512]{2,1,0:T(8,128)(2,1)}, bf16[2,1024,512]{2,1,0:T(8,128)(2,1)}, u32[]{:S(2)}, u32[]{:S(2)}) collective-permute-start(bf16[2,1024,512]{2,1,0:T(8,128)(2,1)} %fusion.80), channel_id=1, source_target_pairs={{0,2},{1,3},{2,0},{3,1},{4,6},{5,7},{6,4},{7,5},{8,10},{9,11},{10,... | collective-permute-start | bytes 6291464 | tf_op jit(solution)/shard_map/ppermute | solution.py:407
  1035.7 57.8 %collective-permute-start.35 = (bf16[2,1024,512]{2,1,0:T(8,128)(2,1)}, bf16[2,1024,512]{2,1,0:T(8,128)(2,1)}, u32[]{:S(2)}, u32[]{:S(2)}) collective-permute-start(bf16[2,1024,512]{2,1,0:T(8,128)(2,1)} %fusion.83), channel_id=1, source_target_pairs={{0,3},{1,2},{2,1},{3,0},{4,7},{5,6},{6,5},{7,4},{8,11},{9,10},{10,... | collective-permute-start | bytes 6291464 | tf_op jit(solution)/shard_map/ppermute | solution.py:407
  1093.6 242.8 %reduce-scatter.11.cloned.1.call-start = ((), (), s32[]{:S(2)}) async-start(), calls=%async_computation.6 | async-start | bytes 5242880 | tf_op jit(solution)/shard_map/reduce_scatter | solution.py:784
  1244.4 249.5 %reduce-scatter.13.cloned.1.call-start = ((), (), s32[]{:S(2)}) async-start(), calls=%async_computation.7 | async-start | bytes 5242880 | tf_op jit(solution)/shard_map/reduce_scatter | solution.py:811
  1244.5 91.8 %collective-permute-start.36 = (bf16[2,512,2048]{2,1,0:T(8,128)(2,1)}, bf16[2,512,2048]{2,1,0:T(8,128)(2,1)}, u32[]{:S(2)}, u32[]{:S(2)}) collective-permute-start(bf16[2,512,2048]{2,1,0:T(8,128)(2,1)} %fusion.35), channel_id=1, source_target_pairs={{0,1},{1,0},{2,3},{3,2},{4,5},{5,4},{6,7},{7,6},{8,9},{9,8},{10,11... | collective-permute-start | bytes 12582920 | tf_op jit(solution)/shard_map/ppermute | solution.py:407
  1245.0 91.4 %collective-permute-start.37 = (bf16[2,512,2048]{2,1,0:T(8,128)(2,1)}, bf16[2,512,2048]{2,1,0:T(8,128)(2,1)}, u32[]{:S(2)}, u32[]{:S(2)}) collective-permute-start(bf16[2,512,2048]{2,1,0:T(8,128)(2,1)} %fusion.38), channel_id=1, source_target_pairs={{0,2},{1,3},{2,0},{3,1},{4,6},{5,7},{6,4},{7,5},{8,10},{9,11},{10,... | collective-permute-start | bytes 12582920 | tf_op jit(solution)/shard_map/ppermute | solution.py:407
  1352.0 47.4 %collective-permute-start.39 = (bf16[1024,512]{1,0:T(8,128)(2,1)S(1)}, bf16[1024,512]{1,0:T(8,128)(2,1)S(1)}, u32[]{:S(2)}, u32[]{:S(2)}) collective-permute-start(bf16[1024,512]{1,0:T(8,128)(2,1)S(1)} %get-tuple-element.220), channel_id=1, source_target_pairs={{0,2},{1,3},{2,0},{3,1},{4,6},{5,7},{6,4},{7,5},{8,10},{9,11},{10,... | collective-permute-start | bytes 3145736 | tf_op jit(solution)/shard_map/ppermute | solution.py:407
  1400.9 124.1 %reduce-scatter.17.cloned.1.call-start = ((), (), s32[]{:S(2)}) async-start(), calls=%async_computation.9 | async-start | bytes 2359296 | tf_op jit(solution)/shard_map/reduce_scatter | solution.py:812
  1401.0 92.9 %collective-permute-start.41 = (bf16[2,512,2048]{2,1,0:T(8,128)(2,1)}, bf16[2,512,2048]{2,1,0:T(8,128)(2,1)}, u32[]{:S(2)}, u32[]{:S(2)}) collective-permute-start(bf16[2,512,2048]{2,1,0:T(8,128)(2,1)} %fusion.41), channel_id=1, source_target_pairs={{0,3},{1,2},{2,1},{3,0},{4,7},{5,6},{6,5},{7,4},{8,11},{9,10},{10,... | collective-permute-start | bytes 12582920 | tf_op jit(solution)/shard_map/ppermute | solution.py:407
  1408.9 190.1 %reduce-scatter.15.cloned.1.call-start = ((), (), s32[]{:S(2)}) async-start(), calls=%async_computation.8 | async-start | bytes 7077888 | tf_op jit(solution)/shard_map/reduce_scatter | solution.py:535
  1523.4 47.8 %collective-permute-start.43 = (bf16[1024,512]{1,0:T(8,128)(2,1)}, bf16[1024,512]{1,0:T(8,128)(2,1)}, u32[]{:S(2)}, u32[]{:S(2)}) collective-permute-start(bf16[1024,512]{1,0:T(8,128)(2,1)} %get-tuple-element.217), channel_id=1, source_target_pairs={{0,2},{1,3},{2,0},{3,1},{4,6},{5,7},{6,4},{7,5},{8,10},{9,11},{10,... | collective-permute-start | bytes 3145736 | tf_op jit(solution)/shard_map/ppermute | solution.py:407
  1523.4 47.8 %collective-permute-start.42 = (bf16[1024,512]{1,0:T(8,128)(2,1)}, bf16[1024,512]{1,0:T(8,128)(2,1)}, u32[]{:S(2)}, u32[]{:S(2)}) collective-permute-start(bf16[1024,512]{1,0:T(8,128)(2,1)} %get-tuple-element.215), channel_id=1, source_target_pairs={{0,1},{1,0},{2,3},{3,2},{4,5},{5,4},{6,7},{7,6},{8,9},{9,8},{10,11... | collective-permute-start | bytes 3145736 | tf_op jit(solution)/shard_map/ppermute | solution.py:407
  (79 other events, 1620.2 us)
Sparse Core Ops, SparseCore 0:
  362.4 214.0 all-gather.4
  579.3 226.8 all-gather.6
  836.4 186.6 reduce-scatter.18
  1093.7 150.6 reduce-scatter.20
  1246.6 76.9 reduce-scatter.10
  1401.0 76.6 reduce-scatter.12
  1480.0 33.4 reduce-scatter.16
  1518.7 68.5 reduce-scatter.14

commit v5 on v4

--- a/solution.py
+++ b/solution.py
@@ -642,18 +642,18 @@
 
     tokens_all = gather_cols(tokens)
     small = gather_cols(jnp.concatenate([attn_gain, segments.astype(F32).reshape(-1)]))
-    qkv_rows, small, tokens_all, out_in = fence(
-        heads_in(qkv_weight, ratio, head_size), small, tokens_all, out_weight
-    )
-    gain_all = small[:, :col_width]
-    segs = small[:, col_width:].astype(jnp.int32)
     cuts = (0, col_width // 2, 3 * col_width // 4, col_width)
     first, second, last = (
         split_parts(gate_up_parts[:, :, cuts[i] : cuts[i + 1]]) for i in range(3)
     )
+    qkv_rows, small, tokens_all, out_in, first, second, last = fence(
+        heads_in(qkv_weight, ratio, head_size), small, tokens_all, out_weight, first, second, last
+    )
+    gain_all = small[:, :col_width]
+    segs = small[:, col_width:].astype(jnp.int32)
     gate_up_first = send_parts(first)
-    qkv_rows, out_rows, gate_up_first, second, last = fence(
-        over_chips(qkv_rows), over_chips(out_in), gate_up_first, second, last
+    qkv_rows, out_rows, gate_up_first, last = fence(
+        over_chips(qkv_rows), over_chips(out_in), gate_up_first, last
     )
     gate_up_second, gate_up_last = send_parts(second), send_parts(last)
     if groups > 1:
@@ -742,51 +742,72 @@
     out_partial, cot_all = fence(out_partial, cot_all)
     out_partial = plain(lax.psum_scatter(out_partial, "col", scatter_dimension=0, tiled=True)[0])
 
+    near = cols // 2 + 1
     grad_slot = gather_slots(cot_all, place, gate, low, high, capacity, True)
-    down_grads = []
-    for mask in range(cols):
+
+    def down_grad(mask, hidden, grad_slot):
         part = jnp.einsum(
             "ecf,ecd->efd", hidden, feature_block(grad_slot, col ^ mask),
             preferred_element_type=F32,
         )
-        down_grads.append(part.astype(BF16) if mask else part)
-    down_grads, grad_slot = fence(down_grads, grad_slot)
-    got_down = send_parts(down_grads)
+        return part.astype(BF16) if mask else part
+
+    near_down = [down_grad(mask, hidden, grad_slot) for mask in range(1, near)]
+    near_down, grad_slot = fence(near_down, grad_slot)
+    near_down = [swap_cols(part, 1 + i) for i, part in enumerate(near_down)]
     grad_hidden = jnp.einsum("ecd,efd->ecf", grad_slot, down, preferred_element_type=F32)
     grad_gate_pre = (
         grad_hidden * up_wide * sigmoid_gate * (1.0 + gate_wide * (1.0 - sigmoid_gate))
     ).astype(BF16)
     grad_up_pre = (grad_hidden * activated).astype(BF16)
-    grad_inner = jnp.concatenate([grad_gate_pre, grad_up_pre], axis=-1)
 
     grad_slot_in = jnp.einsum(
-        "ecf,edf->ecd", grad_inner, gate_up, preferred_element_type=F32
+        "ecf,edf->ecd",
+        jnp.concatenate([grad_gate_pre, grad_up_pre], axis=-1),
+        gate_up,
+        preferred_element_type=F32,
     ).astype(BF16)
     grad_other = combine(grad_slot_in, core=others, scaled=False)
-    near = cols // 2 + 1
-    grad_other, grad_inner, near_down, out_partial = fence(
-        grad_other, grad_inner, got_down[1:near], out_partial
-    )
-    got_down[1:near] = near_down
+    grad_other, grad_gate_pre, grad_up_pre, near_down, out_partial, hidden, grad_slot = fence(
+        grad_other, grad_gate_pre, grad_up_pre, near_down, out_partial, hidden, grad_slot
+    )
     grad_other = swap_cores(grad_other)
-    inner_parts = []
-    for mask in range(cols):
-        part = jnp.einsum(
-            "ecd,ecf->edf", feature_block(slot_inputs, col ^ mask), grad_inner,
-            preferred_element_type=F32,
-        )
-        inner_parts.append(part.astype(BF16) if mask else part)
-    grad_other, inner_parts[1] = fence(grad_other, inner_parts[1])
+    grad_inner = jnp.concatenate([grad_gate_pre, grad_up_pre], axis=-1)
+    far_down = [down_grad(mask, hidden, grad_slot) for mask in range(near, cols)]
+    grad_other, grad_inner, far_down, hidden, grad_slot = fence(
+        grad_other, grad_inner, far_down, hidden, grad_slot
+    )
+    far_down = [swap_cols(part, near + i) for i, part in enumerate(far_down)]
     grad_partial = combine(grad_slot_in, core=mine, scaled=False, more=(grad_other,))
-    grad_partial, got_down = fence(grad_partial, got_down)
+    grad_partial, grad_inner, hidden, grad_slot = fence(
+        grad_partial, grad_inner, hidden, grad_slot
+    )
     grad_partial = plain(lax.psum_scatter(grad_partial, "col", scatter_dimension=0, tiled=True)[0])
-    grad_partial, inner_parts, out_partial = fence(grad_partial, inner_parts, out_partial)
+    fourth = col_width // 4
+
+    def inner_grad(mask, begin=0, count=col_width):
+        features = lax.dynamic_slice_in_dim(
+            slot_inputs, (col ^ mask) * col_width + begin, count, 2
+        )
+        part = jnp.einsum("ecd,ecf->edf", features, grad_inner, preferred_element_type=F32)
+        return part.astype(BF16) if mask else part
+
+    inner_parts = [inner_grad(mask) for mask in range(near)]
+    far_first = [inner_grad(mask, 0, fourth) for mask in range(near, cols)]
+    far_rest = [inner_grad(mask, fourth, col_width - fourth) for mask in range(near, cols)]
+    own_down = down_grad(0, hidden, grad_slot)
+    grad_partial, inner_parts, far_first, far_rest, own_down, far_down = fence(
+        grad_partial, inner_parts, far_first, far_rest, own_down, far_down
+    )
     grad_moe_in = plain(lax.psum_scatter(grad_partial, "chip", scatter_dimension=0, tiled=True)[0])
-    far_parts = inner_parts[near:]
     got_inner = inner_parts[:1] + [swap_cols(inner_parts[mask], mask) for mask in range(1, near)]
-    grad_moe_in, got_inner, out_partial, far_parts = fence(
-        grad_moe_in, got_inner, out_partial, far_parts
-    )
+    grad_down = jnp.zeros((cols, mine_count, part_units, col_width), F32)
+    for mask, part in enumerate([own_down] + near_down + far_down):
+        grad_down = lax.dynamic_update_index_in_dim(grad_down, part.astype(F32), col ^ mask, 0)
+    grad_moe_in, got_inner, out_partial, far_first, far_rest, grad_down = fence(
+        grad_moe_in, got_inner, out_partial, far_first, far_rest, grad_down
+    )
+    far_first = [swap_cols(part, near + i) for i, part in enumerate(far_first)]
     grad_moe_in = grad_moe_in.astype(F32)
 
     gain_two = jnp.sum(grad_moe_in * hidden_one * rate_two, axis=0)
@@ -794,20 +815,28 @@
         grad_moe_in, hidden_one, rate_two, moe_gain, model_width
     )
     grad_branch = plain(grad_hidden_one.astype(BF16))
-    grad_heads = sum_cols(
-        split_parts(
-            jnp.einsum("td,ckd->ctk", grad_branch, out_split, preferred_element_type=F32).astype(BF16)
-        )
-    ).astype(BF16)
-    grad_down = jnp.zeros((cols, mine_count, part_units, col_width), F32)
-    for mask in range(cols):
-        grad_down = lax.dynamic_update_index_in_dim(
-            grad_down, got_down[mask].astype(F32), col ^ mask, 0
-        )
-    grad_heads, out_partial, far_parts, grad_down = fence(
-        grad_heads, out_partial, far_parts, grad_down
-    )
-    far_parts = [swap_cols(part, near + i) for i, part in enumerate(far_parts)]
+    head_parts = split_parts(
+        jnp.einsum("td,ckd->ctk", grad_branch, out_split, preferred_element_type=F32).astype(BF16)
+    )
+    head_parts, far_first, got_inner = fence(head_parts, far_first, got_inner)
+    grad_heads = sum_cols(head_parts).astype(BF16)
+    grad_gate_up = jnp.zeros((cols, mine_count, col_width, 2 * part_units), F32)
+    for mask in range(near):
+        grad_gate_up = lax.dynamic_update_index_in_dim(
+            grad_gate_up, got_inner[mask].astype(F32), col ^ mask, 0
+        )
+
+    def place_far(result, parts, begin):
+        for mask in range(near, cols):
+            part = parts[mask - near].astype(F32)[None]
+            result = lax.dynamic_update_slice(result, part, (col ^ mask, 0, begin, 0))
+        return result
+
+    grad_gate_up = place_far(grad_gate_up, far_first, 0)
+    grad_heads, out_partial, grad_gate_up, far_rest = fence(
+        grad_heads, out_partial, grad_gate_up, far_rest
+    )
+    far_rest = [swap_cols(part, near + i) for i, part in enumerate(far_rest)]
     moe_result = lax.psum_scatter(out_partial, "chip", scatter_dimension=0, tiled=True)[0]
     grad_out_weight = lax.psum_scatter(
         by_head(
@@ -820,14 +849,7 @@
     grad_projected, grad_gains = attend_backward(
         qkv, cosine, sine, seg_row, head_gains, grad_heads, logs
     )
-    grad_gate_up = jnp.zeros((cols, mine_count, col_width, 2 * part_units), F32)
-    for mask in range(near):
-        grad_gate_up = lax.dynamic_update_index_in_dim(
-            grad_gate_up, got_inner[mask].astype(F32), col ^ mask, 0
-        )
-    grad_projected, far_parts, moe_result, grad_gate_up = fence(
-        grad_projected, far_parts, moe_result, grad_gate_up
-    )
+    grad_projected, far_rest, moe_result = fence(grad_projected, far_rest, moe_result)
     output = (hidden_one + moe_result.astype(F32)).astype(BF16)
     normed_parts = [
         plain(
@@ -841,7 +863,7 @@
         normed_parts = jnp.where(core == 0, mine_first, mine_last)
     else:
         normed_parts = normed_parts[0]
-    normed_parts, grad_projected, far_parts = fence(normed_parts, grad_projected, far_parts)
+    normed_parts, grad_projected, far_rest = fence(normed_parts, grad_projected, far_rest)
     grad_normed = sum_cols(
         [
             lax.dynamic_slice_in_dim(normed_parts, (col ^ mask) * col_width, col_width, 1)
@@ -875,10 +897,7 @@
         - stream * rate_one * rate_one * rate_one * across / model_width
     ).astype(BF16)
 
-    for mask in range(near, cols):
-        grad_gate_up = lax.dynamic_update_index_in_dim(
-            grad_gate_up, far_parts[mask - near].astype(F32), col ^ mask, 0
-        )
+    grad_gate_up = place_far(grad_gate_up, far_rest, fourth)
     grad_gate_up = (
         grad_gate_up.reshape(experts_here, split, col_width, 2, part_units)
         .transpose(0, 2, 3, 1, 4)

time: 1630 us -> 1680 us (1.031)
  waiting for transfers between devices: 714 us -> 739 us
    unnamed x10, waiting for transfers between devices: 99.5 us -> 139 us
    dot_general x9 -> x10, matrix products: 151 us -> 162 us  [the longest x5 76.1 us: inner_grad(): jnp.einsum('ecd,ecf->edf', features, grad_inner, preferred_element_type=F32)]
    ppermute x33 -> x34, waiting for transfers between devices: 334 us -> 324 us  [swap_cols(): return lax.ppermute(values, 'col', [(i, i ^ mask) for i in range(count)])]
  transfers between devices with their start and end apart: 58 -> 59, of which waited for: 22 -> 26; matrix products, arithmetic and copies ran while one was open for 34% -> 33% of each run, Pallas kernels for 16% -> 13%
where the time goes in v5:
time: 1680 us; the launch traced here: 1670 us
  waiting for transfers between devices  739 us (44%)
  matrix products  321 us (19%)
  Pallas kernels  251 us (15%)
  local copies, waits for them, and re-layouts  160 us (10%)
  other arithmetic  88.4 us (5%)
  starting transfers between devices  60.2 us (4%)
  blocking collectives  32.7 us (2%)
    ppermute x34, waiting for transfers between devices, swap_cols(): return lax.ppermute(values, 'col', [(i, i ^ mask) for i in range(count)])  324 us
    all_gather x1, waiting for transfers between devices, local(): lax.all_gather(moe_in, ALL, axis=0).reshape(rows, cols, per_row, col_width)  153 us
    unnamed x10, waiting for transfers between devices  139 us
    pallas_call x4, Pallas kernels, combine_slots(): pl.pallas_call(partial(combine_kernel, scaled, each), grid_spec=pltpu.Pre...  122 us
    pallas_call x2, Pallas kernels, gather_slots(): pl.pallas_call(partial(gather_kernel, scaled, each), grid_spec=pltpu.Pref...  81.4 us
    dot_general x5, matrix products, inner_grad(): jnp.einsum('ecd,ecf->edf', features, grad_inner, preferred_element_type=F32)  76.1 us
    ppermute x6, waiting for transfers between devices, swap_chips(): return lax.ppermute(values, 'chip', [(i, i ^ mask) for i in range(count)])  68.4 us
    dot_general x4, matrix products, down_grad(): jnp.einsum('ecf,ecd->efd', hidden, feature_block(grad_slot, col ^ mask),...  43 us
  transfers between devices with their start and end apart: 59, of which 26 were waited for; matrix products, arithmetic and copies ran while one was open for 33% of the time, Pallas kernels for 13%

profile of v5, /device:TPU:3, one launch (start us, length us, event | category | flops | bytes accessed | tf_op | source)
XLA Modules:
  0.0 1667.4 jit_solution(14287069813482103237)
XLA Ops:
  52.0 38.4 %collective-permute-done.6 = bf16[1024,512]{1,0:T(8,128)(2,1)} collective-permute-done((bf16[1024,512]{1,0:T(8,128)(2,1)S(1)}, bf16[1024,512]{1,0:T(8,128)(2,1)}, u32[]{:S(2)}, u32[]{:S(2)}) %collective-permute-start.6) | collective-permute-done | bytes 1048608 | tf_op jit(solution)/shard_map/ppermute | solution.py:407
  116.2 14.4 collective-permute-done.13
  133.9 49.8 %collective-permute-done.9 = bf16[1024,384]{0,1:T(8,128)(2,1)S(1)} collective-permute-done((bf16[1024,384]{0,1:T(8,128)(2,1)S(1)}, bf16[1024,384]{0,1:T(8,128)(2,1)S(1)}, u32[]{:S(2)}, u32[]{:S(2)}) %collective-permute-start.9) | collective-permute-done | bytes 786464 | tf_op jit(solution)/shard_map/ppermute | solution.py:462
  230.6 19.1 %attend_forward.1 = (bf16[1024,512]{1,0:T(8,128)(2,1)}, f32[1024,512]{1,0:T(8,128)}) custom-call(f32[4,1024,384]{2,1,0:T(8,128)} %add_bitcast_fusion.query_ref.key_ref.value_ref, f32[4,1024,384]{2,1,0:T(8,128)} %add_bitcast_fusion.query_ref.key_ref.value_ref, f32[4,1024,384]{2,1,0:T(8,128)} %add_bitcast_fusion.query_ref.key_ref.value_ref, ...), custom_call_target="tpu_custom_call" | custom-call | flops 2147483648 | bytes 9437184 | tf_op jit(solution)/shard_map/attend_forward/pallas_call | solution.py:108
  276.0 73.5 %collective-permute-done.22 = bf16[1024,512]{1,0:T(8,128)(2,1)S(1)} collective-permute-done((bf16[1024,512]{1,0:T(8,128)(2,1)S(1)}, bf16[1024,512]{1,0:T(8,128)(2,1)S(1)}, u32[]{:S(2)}, u32[]{:S(2)}) %collective-permute-start.22) | collective-permute-done | bytes 1048608 | tf_op jit(solution)/shard_map/ppermute | solution.py:407
  352.2 18.7 %psum.21 = f32[1024]{0:T(1024)S(1)} all-reduce(f32[1024]{0:T(1024)S(1)} %get-tuple-element.306), channel_id=1, replica_groups=mesh['chip'=4,'core'=2,'col'=4] {'col'}, use_global_device_ids=true, to_apply=%region_4.5 | all-reduce | flops 1024 | bytes 8192 | tf_op jit(solution)/shard_map/psum | solution.py:39
  427.5 152.8 %all-gather.5.cloned.1.call-done = bf16[32768,512]{1,0:T(8,128)(2,1)} async-done(((bf16[1024,512]{1,0:T(8,128)(2,1)}), bf16[32768,512]{1,0:T(8,128)(2,1)}) %all-gather.5.cloned.1.call-update) | async-done | bytes 33554448 | tf_op jit(solution)/shard_map/all_gather | solution.py:706
  584.5 40.4 %gather_slots.2 = bf16[2,2048,2048]{2,1,0:T(8,128)(2,1)} custom-call(s32[2,16]{1,0:T(2,128)} %get-tuple-element.164.low_ref, s32[2,16]{1,0:T(2,128)} %get-tuple-element.165.high_ref, bf16[8,4,1024,512]{3,2,1,0:T(8,128)(2,1)} %bitcast.311, bf16[8,4,1024,512]{3,2,1,0:T(8,128)(2,1)} %bitcast.312, s32[2,16,1,512]{3,2,1,0:T(1,128)} %reshape.129.refs_2_.refs_3_.place_ref, ...), custom_call_target="tpu_custom_call" | custom-call | flops 25769803776 | bytes 50331648 | tf_op jit(solution)/shard_map/gather_slots/pallas_call | solution.py:299
  624.9 25.2 %fusion.19 = bf16[2,2048,1024]{1,2,0:T(8,128)(2,1)} fusion(bf16[2,2048,2048]{2,1,0:T(8,128)(2,1)} %gather_slots.2, bf16[2,2048,2048]{1,2,0:T(8,128)(2,1)} %constant_dynamic-update-slice_fusion.4), kind=kOutput, calls=%fused_computation.31 | convolution fusion | flops 17184063488 | bytes 33554432 | tf_op jit(solution)/shard_map/ecd,edf->ecf/dot_general | solution.py:718
  650.1 28.4 %fusion = (bf16[2,2048,1024]{1,2,0:T(8,128)(2,1)}, bf16[2,2048,1024]{1,2,0:T(8,128)(2,1)}) fusion(bf16[2,2048,1024]{1,2,0:T(8,128)(2,1)} %fusion.19, bf16[2,2048,2048]{2,1,0:T(8,128)(2,1)} %gather_slots.2, bf16[2,2048,2048]{1,2,0:T(8,128)(2,1)} %constant_dynamic-update-slice_fusion.4), kind=kOutput, calls=%fused_computation.5 | convolution fusion | flops 17217617920 | bytes 50331648 | tf_op jit(solution)/shard_map/ecd,edf->ecf/dot_general | solution.py:721
  690.8 20.7 %collective-permute-done.30 = bf16[2,1024,512]{2,1,0:T(8,128)(2,1)S(1)} collective-permute-done((bf16[2,1024,512]{2,1,0:T(8,128)(2,1)}, bf16[2,1024,512]{2,1,0:T(8,128)(2,1)S(1)}, u32[]{:S(2)}, u32[]{:S(2)}) %collective-permute-start.30) | collective-permute-done | bytes 2097184 | tf_op jit(solution)/shard_map/ppermute | solution.py:407
  713.0 28.2 %convolution_convert_fusion.slots_ref = bf16[2,2048,2048]{2,1,0:T(8,128)(2,1)} fusion(bf16[2,2048,1024]{1,2,0:T(8,128)(2,1)} %get-tuple-element.193, bf16[2,1024,2048]{2,1,0:T(8,128)(2,1)} %constant_dynamic-update-slice_fusion), kind=kOutput, calls=%fused_computation.20 | convolution fusion | flops 17188257792 | bytes 33554432 | tf_op jit(solution)/shard_map/ecf,efd->ecd/dot_general | solution.py:739
  741.2 30.7 %combine_slots.4 = bf16[4,4,1024,512]{3,2,1,0:T(8,128)(2,1)} custom-call(s32[2,16]{1,0:T(2,128)} %get-tuple-element.164.low_ref, s32[2,16]{1,0:T(2,128)} %get-tuple-element.165.high_ref, s32[1]{0:T(128)S(6)} %sub.54.core_ref, bf16[2,2048,2048]{2,1,0:T(8,128)(2,1)} %convolution_convert_fusion.slots_ref, s32[2,16,1,512]{3,2,1,0:T(1,128)} %reshape.129.refs_2_.refs_3_.place_ref, ...), custom_call_target="tpu_custom_call" | custom-call | flops 12884901888 | bytes 33554432 | tf_op jit(solution)/shard_map/combine_slots/pallas_call | solution.py:364
  771.9 30.3 %collective-permute-done.31.refs_0_ = bf16[4,4,1024,512]{3,2,1,0:T(8,128)(2,1)} collective-permute-done((bf16[4,4,1024,512]{3,2,1,0:T(8,128)(2,1)}, bf16[4,4,1024,512]{3,2,1,0:T(8,128)(2,1)}, u32[]{:S(2)}, u32[]{:S(2)}) %collective-permute-start.31) | collective-permute-done | bytes 16777248 | tf_op jit(solution)/shard_map/ppermute | solution.py:402
  802.2 32.0 %combine_slots.5 = bf16[4,4,1024,512]{3,2,1,0:T(8,128)(2,1)} custom-call(s32[2,16]{1,0:T(2,128)} %get-tuple-element.164.low_ref, s32[2,16]{1,0:T(2,128)} %get-tuple-element.165.high_ref, s32[1]{0:T(128)} %bitcast.65.core_ref, bf16[2,2048,2048]{2,1,0:T(8,128)(2,1)} %convolution_convert_fusion.slots_ref, s32[2,16,1,512]{3,2,1,0:T(1,128)} %reshape.129.refs_2_.refs_3_.place_ref, ...), custom_call_target="tpu_custom_call" | custom-call | flops 12884901888 | bytes 33554432 | tf_op jit(solution)/shard_map/combine_slots/pallas_call | solution.py:364
  834.3 41.0 %gather_slots.3 = bf16[2,2048,2048]{2,1,0:T(8,128)(2,1)} custom-call(s32[2,16]{1,0:T(2,128)} %get-tuple-element.164.low_ref, s32[2,16]{1,0:T(2,128)} %get-tuple-element.165.high_ref, bf16[8,4,1024,512]{3,2,1,0:T(8,128)(2,1)} %bitcast.313, bf16[8,4,1024,512]{3,2,1,0:T(8,128)(2,1)} %bitcast.314, s32[2,16,1,512]{3,2,1,0:T(1,128)} %reshape.129.refs_2_.refs_3_.place_ref, ...), custom_call_target="tpu_custom_call" | custom-call | flops 25769803776 | bytes 50331648 | tf_op jit(solution)/shard_map/gather_slots/pallas_call | solution.py:299
  896.7 33.1 %fusion.3 = (bf16[2,2048,1024]{1,2,0:T(8,128)(2,1)}, bf16[2,2048,1024]{1,2,0:T(8,128)(2,1)}) fusion(bf16[2,2048,1024]{1,2,0:T(8,128)(2,1)} %get-tuple-element.309, bf16[2,2048,1024]{1,2,0:T(8,128)(2,1)} %fusion.19, bf16[2,2048,2048]{2,1,0:T(8,128)(2,1)} %gather_slots.3, bf16[2,1024,2048]{2,1,0:T(8,128)(2,1)} %constant_dynamic-update-slice_fusion), kind=kOutput, calls=%fused_computation.8 | convolution fusion | flops 17242783744 | bytes 58720256 | tf_op jit(solution)/shard_map/ecd,efd->ecf/dot_general | solution.py:758
  929.8 42.6 %fusion.12.slots_ref = bf16[2,2048,2048]{2,1,0:T(8,128)(2,1)} fusion(bf16[2,2048,2048]{1,2,0:T(8,128)(2,1)} %constant_dynamic-update-slice_fusion.4, bf16[2,2048,1024]{1,2,0:T(8,128)(2,1)} %get-tuple-element.184, bf16[2,2048,1024]{1,2,0:T(8,128)(2,1)} %get-tuple-element.183), kind=kOutput, calls=%fused_computation.19 | convolution fusion | flops 34401681408 | bytes 50331648 | tf_op jit(solution)/shard_map/ecf,edf->ecd/dot_general | solution.py:764
  972.4 29.0 %combine_slots.6 = bf16[4,4,1024,512]{3,2,1,0:T(8,128)(2,1)} custom-call(s32[2,16]{1,0:T(2,128)} %get-tuple-element.164.low_ref, s32[2,16]{1,0:T(2,128)} %get-tuple-element.165.high_ref, s32[1]{0:T(128)S(6)} %sub.54.core_ref, bf16[2,2048,2048]{2,1,0:T(8,128)(2,1)} %fusion.12.slots_ref, s32[2,16,1,512]{3,2,1,0:T(1,128)} %reshape.129.refs_2_.refs_3_.place_ref, ...), custom_call_target="tpu_custom_call" | custom-call | flops 12884901888 | bytes 33554432 | tf_op jit(solution)/shard_map/combine_slots/pallas_call | solution.py:364
  1001.5 31.6 %reduce-scatter.19.cloned.1.call-done = bf16[1,4,1024,512]{3,2,1,0:T(8,128)(2,1)} async-done(((bf16[4,4,1024,512]{3,2,1,0:T(8,128)(2,1)}), bf16[1,4,1024,512]{3,2,1,0:T(8,128)(2,1)}) %reduce-scatter.19.cloned.1.call-update) | async-done | bytes 4194320
  1058.9 30.1 %combine_slots.7 = bf16[4,4,1024,512]{3,2,1,0:T(8,128)(2,1)} custom-call(s32[2,16]{1,0:T(2,128)} %get-tuple-element.164.low_ref, s32[2,16]{1,0:T(2,128)} %get-tuple-element.165.high_ref, s32[1]{0:T(128)} %bitcast.65.core_ref, bf16[2,2048,2048]{2,1,0:T(8,128)(2,1)} %fusion.12.slots_ref, s32[2,16,1,512]{3,2,1,0:T(1,128)} %reshape.129.refs_2_.refs_3_.place_ref, ...), custom_call_target="tpu_custom_call" | custom-call | flops 12884901888 | bytes 33554432 | tf_op jit(solution)/shard_map/combine_slots/pallas_call | solution.py:364
  1101.9 16.5 fusion.40
  1118.3 16.3 fusion.43
  1134.6 17.3 %fusion.32 = f32[2,512,2048]{2,1,0:T(8,128)} fusion(bf16[2,2048,2048]{1,2,0:T(8,128)(2,1)} %pad_maximum_fusion, bf16[2,2048,2048]{2,1,0:T(8,128)(2,1)} %gather_slots.2, s32[]{:T(128)S(6)} %select_n.280), kind=kOutput, calls=%fused_computation.49 | convolution fusion | flops 8589934592 | bytes 29360132 | tf_op jit(solution)/shard_map/ecd,ecf->edf/dot_general | solution.py:792
  1176.3 107.1 %reduce-scatter.21.cloned.1.call-done = bf16[1,4,1024,512]{3,2,1,0:T(8,128)(2,1)} async-done(((bf16[4,4,1024,512]{3,2,1,0:T(8,128)(2,1)}), bf16[1,4,1024,512]{3,2,1,0:T(8,128)(2,1)}) %reduce-scatter.21.cloned.1.call-update) | async-done | bytes 4194320
  1307.3 68.1 %collective-permute-done.36 = bf16[2,512,2048]{2,1,0:T(8,128)(2,1)} collective-permute-done((bf16[2,512,2048]{2,1,0:T(8,128)(2,1)}, bf16[2,512,2048]{2,1,0:T(8,128)(2,1)}, u32[]{:S(2)}, u32[]{:S(2)}) %collective-permute-start.36) | collective-permute-done | bytes 4194336 | tf_op jit(solution)/shard_map/ppermute | solution.py:407
  1390.4 16.3 collective-permute-done.38
  1439.7 16.1 collective-permute-done.40
  1465.5 28.7 %attend_backward.1 = (bf16[4,1024,384]{2,1,0:T(8,128)(2,1)}, f32[2,128]{1,0:T(2,128)}) custom-call(f32[4,1024,384]{2,1,0:T(8,128)} %add_bitcast_fusion.query_ref.key_ref.value_ref, f32[4,1024,384]{2,1,0:T(8,128)} %add_bitcast_fusion.query_ref.key_ref.value_ref, f32[4,1024,384]{2,1,0:T(8,128)} %add_bitcast_fusion.query_ref.key_ref.value_ref, ...), custom_call_target="tpu_custom_call" | custom-call | flops 5368709120 | bytes 12582912 | tf_op jit(solution)/shard_map/attend_backward/pallas_call | solution.py:194
  1494.2 33.7 %collective-permute-done.42 = bf16[2,384,2048]{2,1,0:T(8,128)(2,1)} collective-permute-done((bf16[2,384,2048]{2,1,0:T(8,128)(2,1)}, bf16[2,384,2048]{2,1,0:T(8,128)(2,1)}, u32[]{:S(2)}, u32[]{:S(2)}) %collective-permute-start.42) | collective-permute-done | bytes 3145760 | tf_op jit(solution)/shard_map/ppermute | solution.py:407
  1571.6 16.6 collective-permute-done.45
  1588.2 23.2 %collective-permute-done.44 = bf16[1024,512]{1,0:T(8,128)(2,1)} collective-permute-done((bf16[1024,512]{1,0:T(8,128)(2,1)}, bf16[1024,512]{1,0:T(8,128)(2,1)}, u32[]{:S(2)}, u32[]{:S(2)}) %collective-permute-start.44) | collective-permute-done | bytes 1048608 | tf_op jit(solution)/shard_map/ppermute | solution.py:407
  (384 shorter events, 481.9 us)
Async XLA Ops:
  7.2 573.1 %all-gather.5.cloned.1.call-start = ((), (), s32[]{:S(2)}) async-start(), calls=%async_computation.10 | async-start | bytes 34603008 | tf_op jit(solution)/shard_map/all_gather | solution.py:706
  43.0 47.4 %collective-permute-start.6 = (bf16[1024,512]{1,0:T(8,128)(2,1)S(1)}, bf16[1024,512]{1,0:T(8,128)(2,1)}, u32[]{:S(2)}, u32[]{:S(2)}) collective-permute-start(bf16[1024,512]{1,0:T(8,128)(2,1)S(1)} %copy-done.4), channel_id=1, source_target_pairs={{0,2},{1,3},{2,0},{3,1},{4,6},{5,7},{6,4},{7,5},{8,10},{9,11},{10,... | collective-permute-start | bytes 3145736 | tf_op jit(solution)/shard_map/ppermute | solution.py:407
  98.5 87.1 %collective-permute-start.14 = (bf16[2,256,2048]{2,1,0:T(8,128)(2,1)}, bf16[2,256,2048]{2,1,0:T(8,128)(2,1)}, u32[]{:S(2)}, u32[]{:S(2)}) collective-permute-start(bf16[2,256,2048]{2,1,0:T(8,128)(2,1)} %get-tuple-element.126), channel_id=1, source_target_pairs={{0,1},{1,0},{2,3},{3,2},{4,5},{5,4},{6,7},{7,6},{8,9},{9,8},{10,11... | collective-permute-start | bytes 6291464 | tf_op jit(solution)/shard_map/ppermute | solution.py:407
  98.7 87.0 %collective-permute-start.15 = (bf16[2,256,2048]{2,1,0:T(8,128)(2,1)}, bf16[2,256,2048]{2,1,0:T(8,128)(2,1)}, u32[]{:S(2)}, u32[]{:S(2)}) collective-permute-start(bf16[2,256,2048]{2,1,0:T(8,128)(2,1)} %get-tuple-element.127), channel_id=1, source_target_pairs={{0,2},{1,3},{2,0},{3,1},{4,6},{5,7},{6,4},{7,5},{8,10},{9,11},{10,... | collective-permute-start | bytes 6291464 | tf_op jit(solution)/shard_map/ppermute | solution.py:407
  105.9 85.1 %collective-permute-start.16 = (bf16[2,256,2048]{2,1,0:T(8,128)(2,1)}, bf16[2,256,2048]{2,1,0:T(8,128)(2,1)}, u32[]{:S(2)}, u32[]{:S(2)}) collective-permute-start(bf16[2,256,2048]{2,1,0:T(8,128)(2,1)} %get-tuple-element.128), channel_id=1, source_target_pairs={{0,3},{1,2},{2,1},{3,0},{4,7},{5,6},{6,5},{7,4},{8,11},{9,10},{10,... | collective-permute-start | bytes 6291464 | tf_op jit(solution)/shard_map/ppermute | solution.py:407
  130.6 53.1 %collective-permute-start.9 = (bf16[1024,384]{0,1:T(8,128)(2,1)S(1)}, bf16[1024,384]{0,1:T(8,128)(2,1)S(1)}, u32[]{:S(2)}, u32[]{:S(2)}) collective-permute-start(bf16[1024,384]{0,1:T(8,128)(2,1)S(1)} %maximum_maximum_fusion), channel_id=1, source_target_pairs={{0,16},{8,24},{16,0},{24,8},{1,17},{9,25},{17,1},{25,9},{2,18},{10... | collective-permute-start | bytes 2359304 | tf_op jit(solution)/shard_map/ppermute | solution.py:462
  130.7 54.0 %collective-permute-start.10 = (bf16[1024,384]{0,1:T(8,128)(2,1)S(1)}, bf16[1024,384]{0,1:T(8,128)(2,1)S(1)}, u32[]{:S(2)}, u32[]{:S(2)}) collective-permute-start(bf16[1024,384]{0,1:T(8,128)(2,1)S(1)} %maximum_maximum_fusion), channel_id=1, source_target_pairs={{0,24},{8,16},{16,8},{24,0},{1,25},{9,17},{17,9},{25,1},{2,26},{10... | collective-permute-start | bytes 2359304 | tf_op jit(solution)/shard_map/ppermute | solution.py:462
  201.7 48.0 %collective-permute-start.18 = (bf16[2,128,2048]{2,1,0:T(8,128)(2,1)}, bf16[2,128,2048]{2,1,0:T(8,128)(2,1)S(1)}, u32[]{:S(2)}, u32[]{:S(2)}) collective-permute-start(bf16[2,128,2048]{2,1,0:T(8,128)(2,1)} %get-tuple-element.138), channel_id=1, source_target_pairs={{0,1},{1,0},{2,3},{3,2},{4,5},{5,4},{6,7},{7,6},{8,9},{9,8},{10,11... | collective-permute-start | bytes 3145736 | tf_op jit(solution)/shard_map/ppermute | solution.py:407
  202.0 47.7 %collective-permute-start.19 = (bf16[2,128,2048]{2,1,0:T(8,128)(2,1)}, bf16[2,128,2048]{2,1,0:T(8,128)(2,1)}, u32[]{:S(2)}, u32[]{:S(2)}) collective-permute-start(bf16[2,128,2048]{2,1,0:T(8,128)(2,1)} %get-tuple-element.139), channel_id=1, source_target_pairs={{0,2},{1,3},{2,0},{3,1},{4,6},{5,7},{6,4},{7,5},{8,10},{9,11},{10,... | collective-permute-start | bytes 3145736 | tf_op jit(solution)/shard_map/ppermute | solution.py:407
  257.9 114.3 %collective-permute-start.25 = (bf16[2,128,2048]{2,1,0:T(8,128)(2,1)}, bf16[2,128,2048]{2,1,0:T(8,128)(2,1)}, u32[]{:S(2)}, u32[]{:S(2)}) collective-permute-start(bf16[2,128,2048]{2,1,0:T(8,128)(2,1)} %get-tuple-element.144), channel_id=1, source_target_pairs={{0,1},{1,0},{2,3},{3,2},{4,5},{5,4},{6,7},{7,6},{8,9},{9,8},{10,11... | collective-permute-start | bytes 3145736 | tf_op jit(solution)/shard_map/ppermute | solution.py:407
  258.4 113.8 %collective-permute-start.26 = (bf16[2,128,2048]{2,1,0:T(8,128)(2,1)}, bf16[2,128,2048]{2,1,0:T(8,128)(2,1)}, u32[]{:S(2)}, u32[]{:S(2)}) collective-permute-start(bf16[2,128,2048]{2,1,0:T(8,128)(2,1)} %get-tuple-element.145), channel_id=1, source_target_pairs={{0,2},{1,3},{2,0},{3,1},{4,6},{5,7},{6,4},{7,5},{8,10},{9,11},{10,... | collective-permute-start | bytes 3145736 | tf_op jit(solution)/shard_map/ppermute | solution.py:407
  259.6 89.9 %collective-permute-start.22 = (bf16[1024,512]{1,0:T(8,128)(2,1)S(1)}, bf16[1024,512]{1,0:T(8,128)(2,1)S(1)}, u32[]{:S(2)}, u32[]{:S(2)}) collective-permute-start(bf16[1024,512]{1,0:T(8,128)(2,1)S(1)} %copy-done.28), channel_id=1, source_target_pairs={{0,2},{1,3},{2,0},{3,1},{4,6},{5,7},{6,4},{7,5},{8,10},{9,11},{10,... | collective-permute-start | bytes 3145736 | tf_op jit(solution)/shard_map/ppermute | solution.py:407
  259.8 89.8 %collective-permute-start.23 = (bf16[1024,512]{1,0:T(8,128)(2,1)S(1)}, bf16[1024,512]{1,0:T(8,128)(2,1)S(1)}, u32[]{:S(2)}, u32[]{:S(2)}) collective-permute-start(bf16[1024,512]{1,0:T(8,128)(2,1)S(1)} %copy-done.28), channel_id=1, source_target_pairs={{0,3},{1,2},{2,1},{3,0},{4,7},{5,6},{6,5},{7,4},{8,11},{9,10},{10,... | collective-permute-start | bytes 3145736 | tf_op jit(solution)/shard_map/ppermute | solution.py:407
  274.2 98.0 %collective-permute-start.27 = (bf16[2,128,2048]{2,1,0:T(8,128)(2,1)}, bf16[2,128,2048]{2,1,0:T(8,128)(2,1)}, u32[]{:S(2)}, u32[]{:S(2)}) collective-permute-start(bf16[2,128,2048]{2,1,0:T(8,128)(2,1)} %get-tuple-element.146), channel_id=1, source_target_pairs={{0,3},{1,2},{2,1},{3,0},{4,7},{5,6},{6,5},{7,4},{8,11},{9,10},{10,... | collective-permute-start | bytes 3145736 | tf_op jit(solution)/shard_map/ppermute | solution.py:407
  372.3 462.0 %all-gather.7.cloned.1.call-start = ((), (), s32[]{:S(2)}) async-start(), calls=%async_computation.11 | async-start | bytes 34603008 | tf_op jit(solution)/shard_map/all_gather | solution.py:712
  580.3 452.7 %reduce-scatter.19.cloned.1.call-start = ((), (), s32[]{:S(2)}) async-start(), calls=%async_computation.12 | async-start | bytes 20971520
  581.8 102.6 %collective-permute-start.28 = (bf16[2,1024,512]{2,1,0:T(8,128)(2,1)}, bf16[2,1024,512]{2,1,0:T(8,128)(2,1)}, u32[]{:S(2)}, u32[]{:S(2)}) collective-permute-start(bf16[2,1024,512]{2,1,0:T(8,128)(2,1)} %get-tuple-element.171), channel_id=1, source_target_pairs={{0,1},{1,0},{2,3},{3,2},{4,5},{5,4},{6,7},{7,6},{8,9},{9,8},{10,11... | collective-permute-start | bytes 6291464 | tf_op jit(solution)/shard_map/ppermute | solution.py:407
  582.2 105.4 %collective-permute-start.29 = (bf16[2,1024,512]{2,1,0:T(8,128)(2,1)}, bf16[2,1024,512]{2,1,0:T(8,128)(2,1)}, u32[]{:S(2)}, u32[]{:S(2)}) collective-permute-start(bf16[2,1024,512]{2,1,0:T(8,128)(2,1)} %get-tuple-element.172), channel_id=1, source_target_pairs={{0,2},{1,3},{2,0},{3,1},{4,6},{5,7},{6,4},{7,5},{8,10},{9,11},{10,... | collective-permute-start | bytes 6291464 | tf_op jit(solution)/shard_map/ppermute | solution.py:407
  583.3 128.1 %collective-permute-start.30 = (bf16[2,1024,512]{2,1,0:T(8,128)(2,1)}, bf16[2,1024,512]{2,1,0:T(8,128)(2,1)S(1)}, u32[]{:S(2)}, u32[]{:S(2)}) collective-permute-start(bf16[2,1024,512]{2,1,0:T(8,128)(2,1)} %get-tuple-element.173), channel_id=1, source_target_pairs={{0,3},{1,2},{2,1},{3,0},{4,7},{5,6},{6,5},{7,4},{8,11},{9,10},{10,... | collective-permute-start | bytes 6291464 | tf_op jit(solution)/shard_map/ppermute | solution.py:407
  834.2 449.1 %reduce-scatter.21.cloned.1.call-start = ((), (), s32[]{:S(2)}) async-start(), calls=%async_computation.13 | async-start | bytes 20971520
  896.7 104.7 %collective-permute-start.32 = (bf16[2,1024,512]{2,1,0:T(8,128)(2,1)}, bf16[2,1024,512]{2,1,0:T(8,128)(2,1)S(1)}, u32[]{:S(2)}, u32[]{:S(2)}) collective-permute-start(bf16[2,1024,512]{2,1,0:T(8,128)(2,1)} %fusion.80), channel_id=1, source_target_pairs={{0,1},{1,0},{2,3},{3,2},{4,5},{5,4},{6,7},{7,6},{8,9},{9,8},{10,11... | collective-permute-start | bytes 6291464 | tf_op jit(solution)/shard_map/ppermute | solution.py:407
  896.7 104.7 %collective-permute-start.33 = (bf16[2,1024,512]{2,1,0:T(8,128)(2,1)}, bf16[2,1024,512]{2,1,0:T(8,128)(2,1)}, u32[]{:S(2)}, u32[]{:S(2)}) collective-permute-start(bf16[2,1024,512]{2,1,0:T(8,128)(2,1)} %fusion.83), channel_id=1, source_target_pairs={{0,2},{1,3},{2,0},{3,1},{4,6},{5,7},{6,4},{7,5},{8,10},{9,11},{10,... | collective-permute-start | bytes 6291464 | tf_op jit(solution)/shard_map/ppermute | solution.py:407
  1089.0 286.5 %reduce-scatter.11.cloned.1.call-start = ((), (), s32[]{:S(2)}) async-start(), calls=%async_computation.6 | async-start | bytes 5242880 | tf_op jit(solution)/shard_map/reduce_scatter | solution.py:802
  1089.0 87.3 %collective-permute-start.35 = (bf16[2,1024,512]{2,1,0:T(8,128)(2,1)}, bf16[2,1024,512]{2,1,0:T(8,128)(2,1)}, u32[]{:S(2)}, u32[]{:S(2)}) collective-permute-start(bf16[2,1024,512]{2,1,0:T(8,128)(2,1)} %fusion.86), channel_id=1, source_target_pairs={{0,3},{1,2},{2,1},{3,0},{4,7},{5,6},{6,5},{7,4},{8,11},{9,10},{10,... | collective-permute-start | bytes 6291464 | tf_op jit(solution)/shard_map/ppermute | solution.py:407
  1283.4 250.8 %reduce-scatter.13.cloned.1.call-start = ((), (), s32[]{:S(2)}) async-start(), calls=%async_computation.7 | async-start | bytes 5242880 | tf_op jit(solution)/shard_map/reduce_scatter | solution.py:840
  1283.6 91.8 %collective-permute-start.36 = (bf16[2,512,2048]{2,1,0:T(8,128)(2,1)}, bf16[2,512,2048]{2,1,0:T(8,128)(2,1)}, u32[]{:S(2)}, u32[]{:S(2)}) collective-permute-start(bf16[2,512,2048]{2,1,0:T(8,128)(2,1)} %fusion.40), channel_id=1, source_target_pairs={{0,1},{1,0},{2,3},{3,2},{4,5},{5,4},{6,7},{7,6},{8,9},{9,8},{10,11... | collective-permute-start | bytes 12582920 | tf_op jit(solution)/shard_map/ppermute | solution.py:407
  1284.1 91.4 %collective-permute-start.37 = (bf16[2,512,2048]{2,1,0:T(8,128)(2,1)}, bf16[2,512,2048]{2,1,0:T(8,128)(2,1)}, u32[]{:S(2)}, u32[]{:S(2)}) collective-permute-start(bf16[2,512,2048]{2,1,0:T(8,128)(2,1)} %fusion.43), channel_id=1, source_target_pairs={{0,2},{1,3},{2,0},{3,1},{4,6},{5,7},{6,4},{7,5},{8,10},{9,11},{10,... | collective-permute-start | bytes 12582920 | tf_op jit(solution)/shard_map/ppermute | solution.py:407
  1407.5 48.2 %collective-permute-start.40 = (bf16[1024,512]{1,0:T(8,128)(2,1)S(1)}, bf16[1024,512]{1,0:T(8,128)(2,1)S(1)}, u32[]{:S(2)}, u32[]{:S(2)}) collective-permute-start(bf16[1024,512]{1,0:T(8,128)(2,1)S(1)} %get-tuple-element.214), channel_id=1, source_target_pairs={{0,2},{1,3},{2,0},{3,1},{4,6},{5,7},{6,4},{7,5},{8,10},{9,11},{10,... | collective-permute-start | bytes 3145736 | tf_op jit(solution)/shard_map/ppermute | solution.py:407
  1457.4 112.4 %reduce-scatter.17.cloned.1.call-start = ((), (), s32[]{:S(2)}) async-start(), calls=%async_computation.9 | async-start | bytes 2359296 | tf_op jit(solution)/shard_map/reduce_scatter | solution.py:841
  1457.4 70.5 %collective-permute-start.42 = (bf16[2,384,2048]{2,1,0:T(8,128)(2,1)}, bf16[2,384,2048]{2,1,0:T(8,128)(2,1)}, u32[]{:S(2)}, u32[]{:S(2)}) collective-permute-start(bf16[2,384,2048]{2,1,0:T(8,128)(2,1)} %convolution_convert_fusion.2), channel_id=1, source_target_pairs={{0,3},{1,2},{2,1},{3,0},{4,7},{5,6},{6,5},{7,4},{8,11},{9,10},{10,... | collective-permute-start | bytes 9437192 | tf_op jit(solution)/shard_map/ppermute | solution.py:407
  1465.3 176.6 %reduce-scatter.15.cloned.1.call-start = ((), (), s32[]{:S(2)}) async-start(), calls=%async_computation.8 | async-start | bytes 7077888 | tf_op jit(solution)/shard_map/reduce_scatter | solution.py:535
  1563.9 47.6 %collective-permute-start.44 = (bf16[1024,512]{1,0:T(8,128)(2,1)}, bf16[1024,512]{1,0:T(8,128)(2,1)}, u32[]{:S(2)}, u32[]{:S(2)}) collective-permute-start(bf16[1024,512]{1,0:T(8,128)(2,1)} %get-tuple-element.261), channel_id=1, source_target_pairs={{0,2},{1,3},{2,0},{3,1},{4,6},{5,7},{6,4},{7,5},{8,10},{9,11},{10,... | collective-permute-start | bytes 3145736 | tf_op jit(solution)/shard_map/ppermute | solution.py:407
  (79 other events, 1776.0 us)
Sparse Core Ops, SparseCore 0:
  372.4 207.8 all-gather.4
  583.2 226.9 all-gather.6
  834.4 198.6 reduce-scatter.18
  1089.1 194.2 reduce-scatter.20
  1285.5 76.8 reduce-scatter.10
  1457.5 76.6 reduce-scatter.12
  1536.5 33.2 reduce-scatter.16
  1572.1 69.6 reduce-scatter.14

commit v6 on v4

--- a/solution.py
+++ b/solution.py
@@ -317,9 +317,11 @@
     )(low, high, rows, rows, places, places, gates, gates)
 
 
-def combine_kernel(scaled, each, low_ref, high_ref, core_ref, slots_ref, place_ref, gate_ref, *refs):
+def combine_kernel(
+    scaled, added, each, begin, low_ref, high_ref, core_ref, slots_ref, place_ref, gate_ref, *refs
+):
     out_ref, total_ref = refs[-2:]
-    chip, piece = pl.program_id(0), pl.program_id(1)
+    chip, piece = pl.program_id(0) + begin, pl.program_id(1)
     block = (2 * chip + core_ref[0]) * each + piece
     experts = slots_ref.shape[0]
     parts, width = out_ref.shape[0], out_ref.shape[3]
@@ -346,56 +348,72 @@
         lax.fori_loop(low_ref[e, block], high_ref[e, block], body, 0)
     for c in range(parts):
         total = total_ref[:, c * width : (c + 1) * width]
-        if len(refs) == 3:
+        if added:
             total = total + refs[0][c, 0].astype(F32)
         out_ref[c, 0] = total.astype(BF16)
 
 
-def combine_slots(slots, place, gate, low, high, core, chips, per_row, parts, scaled, more=()):
+def combine_slots(
+    slots, place, gate, low, high, core, chips, per_row, parts, scaled, begin=0, more=None, into=None
+):
     experts, capacity, model_width = slots.shape
     width = model_width // parts
     each = per_row // BLOCK
     blocks = place.shape[1] // BLOCK
+    count = chips // 2
 
     def token_block(z, j, low_ref, high_ref, core_ref):
-        return (0, (2 * z + core_ref[0]) * each + j, 0, 0)
-
-    sums = pl.BlockSpec((parts, 1, BLOCK, width), lambda z, j, *_: (0, z, j, 0))
-    return pl.pallas_call(
-        partial(combine_kernel, scaled, each),
-        grid_spec=pltpu.PrefetchScalarGridSpec(
-            num_scalar_prefetch=3,
-            grid=(chips, each),
-            in_specs=[
-                pl.BlockSpec(
-                    (experts, capacity, model_width),
-                    lambda *_: (0, 0, 0),
-                    pipeline_mode=pl.Buffered(1),
-                ),
-                pl.BlockSpec((experts, 1, 1, BLOCK), token_block),
-                pl.BlockSpec((experts, 1, 1, BLOCK), token_block),
-            ]
-            + [sums] * len(more),
-            out_specs=sums,
-            scratch_shapes=[pltpu.VMEM((BLOCK, model_width), F32)],
-        ),
-        out_shape=jax.ShapeDtypeStruct((parts, chips, per_row, width), BF16),
-        compiler_params=pltpu.CompilerParams(vmem_limit_bytes=VMEM_BYTES),
-        cost_estimate=pl.CostEstimate(
-            flops=24 * experts * TILE * BLOCK * model_width,
-            bytes_accessed=slots.size * 2 + parts * chips * per_row * width * 2,
-            transcendentals=0,
-        ),
-        name="combine_slots",
-    )(
+        return (0, (2 * (z + begin) + core_ref[0]) * each + j, 0, 0)
+
+    half = pl.BlockSpec((parts, 1, BLOCK, width), lambda z, j, *_: (0, z, j, 0))
+    whole = pl.BlockSpec((parts, 1, BLOCK, width), lambda z, j, *_: (0, z + begin, j, 0))
+    added = more is not None
+    in_specs = [
+        pl.BlockSpec(
+            (experts, capacity, model_width),
+            lambda *_: (0, 0, 0),
+            pipeline_mode=pl.Buffered(1),
+        ),
+        pl.BlockSpec((experts, 1, 1, BLOCK), token_block),
+        pl.BlockSpec((experts, 1, 1, BLOCK), token_block),
+    ]
+    inputs = [
         low,
         high,
         core,
         slots,
         place.reshape(experts, blocks, 1, BLOCK),
         gate.reshape(experts, blocks, 1, BLOCK),
-        *more,
-    )
+    ]
+    aliases = {}
+    if added:
+        in_specs.append(half)
+        inputs.append(more)
+    if into is not None:
+        aliases = {len(inputs): 0}
+        in_specs.append(pl.BlockSpec(memory_space=pl.ANY))
+        inputs.append(into)
+    return pl.pallas_call(
+        partial(combine_kernel, scaled, added, each, begin),
+        grid_spec=pltpu.PrefetchScalarGridSpec(
+            num_scalar_prefetch=3,
+            grid=(count, each),
+            in_specs=in_specs,
+            out_specs=whole if added else half,
+            scratch_shapes=[pltpu.VMEM((BLOCK, model_width), F32)],
+        ),
+        out_shape=jax.ShapeDtypeStruct(
+            (parts, chips if added else count, per_row, width), BF16
+        ),
+        input_output_aliases=aliases,
+        compiler_params=pltpu.CompilerParams(vmem_limit_bytes=VMEM_BYTES),
+        cost_estimate=pl.CostEstimate(
+            flops=12 * experts * TILE * BLOCK * model_width,
+            bytes_accessed=slots.size * 2 + parts * count * per_row * width * 2,
+            transcendentals=0,
+        ),
+        name="combine_slots",
+    )(*inputs)
 
 
 def swap_cores(values):
@@ -737,38 +755,58 @@
         return lax.dynamic_slice_in_dim(values, index * col_width, col_width, 2)
 
     expert_out = jnp.einsum("ecf,efd->ecd", hidden, down, preferred_element_type=F32).astype(BF16)
-    out_other = swap_cores(combine(expert_out, core=others, scaled=True))
-    out_partial = combine(expert_out, core=mine, scaled=True, more=(out_other,))
+    middle = chips // 2
+    out_first = combine(expert_out, core=others, scaled=True)
+    out_last = combine(expert_out, core=others, scaled=True, begin=middle)
+    out_partial = combine(expert_out, core=mine, scaled=True, more=swap_cores(out_first))
+    out_partial = combine(
+        expert_out, core=mine, scaled=True, begin=middle, more=swap_cores(out_last), into=out_partial
+    )
     out_partial, cot_all = fence(out_partial, cot_all)
     out_partial = plain(lax.psum_scatter(out_partial, "col", scatter_dimension=0, tiled=True)[0])
 
     grad_slot = gather_slots(cot_all, place, gate, low, high, capacity, True)
-    down_grads = []
-    for mask in range(cols):
+
+    def down_grad(mask, hidden, grad_slot):
         part = jnp.einsum(
             "ecf,ecd->efd", hidden, feature_block(grad_slot, col ^ mask),
             preferred_element_type=F32,
         )
-        down_grads.append(part.astype(BF16) if mask else part)
+        return part.astype(BF16) if mask else part
+
+    near = cols // 2 + 1
+    down_grads = [down_grad(mask, hidden, grad_slot) for mask in range(1, cols)]
     down_grads, grad_slot = fence(down_grads, grad_slot)
-    got_down = send_parts(down_grads)
+    near_down = [swap_cols(part, 1 + i) for i, part in enumerate(down_grads[: near - 1])]
+    far_down = [swap_cols(part, near + i) for i, part in enumerate(down_grads[near - 1 :])]
     grad_hidden = jnp.einsum("ecd,efd->ecf", grad_slot, down, preferred_element_type=F32)
     grad_gate_pre = (
         grad_hidden * up_wide * sigmoid_gate * (1.0 + gate_wide * (1.0 - sigmoid_gate))
     ).astype(BF16)
     grad_up_pre = (grad_hidden * activated).astype(BF16)
+
+    grad_slot_in = jnp.einsum(
+        "ecf,edf->ecd",
+        jnp.concatenate([grad_gate_pre, grad_up_pre], axis=-1),
+        gate_up,
+        preferred_element_type=F32,
+    ).astype(BF16)
+    grad_first = swap_cores(combine(grad_slot_in, core=others, scaled=False))
+    grad_last = combine(grad_slot_in, core=others, scaled=False, begin=middle)
+    grad_last, grad_gate_pre, grad_up_pre, near_down, out_partial = fence(
+        grad_last, grad_gate_pre, grad_up_pre, near_down, out_partial
+    )
+    grad_last = swap_cores(grad_last)
     grad_inner = jnp.concatenate([grad_gate_pre, grad_up_pre], axis=-1)
-
-    grad_slot_in = jnp.einsum(
-        "ecf,edf->ecd", grad_inner, gate_up, preferred_element_type=F32
-    ).astype(BF16)
-    grad_other = combine(grad_slot_in, core=others, scaled=False)
-    near = cols // 2 + 1
-    grad_other, grad_inner, near_down, out_partial = fence(
-        grad_other, grad_inner, got_down[1:near], out_partial
-    )
-    got_down[1:near] = near_down
-    grad_other = swap_cores(grad_other)
+    grad_first, grad_inner = fence(grad_first, grad_inner)
+    grad_partial = combine(grad_slot_in, core=mine, scaled=False, more=grad_first)
+    grad_partial = combine(
+        grad_slot_in, core=mine, scaled=False, begin=middle, more=grad_last, into=grad_partial
+    )
+    grad_partial, grad_inner, far_down, hidden, grad_slot = fence(
+        grad_partial, grad_inner, far_down, hidden, grad_slot
+    )
+    grad_partial = plain(lax.psum_scatter(grad_partial, "col", scatter_dimension=0, tiled=True)[0])
     inner_parts = []
     for mask in range(cols):
         part = jnp.einsum(
@@ -776,11 +814,9 @@
             preferred_element_type=F32,
         )
         inner_parts.append(part.astype(BF16) if mask else part)
-    grad_other, inner_parts[1] = fence(grad_other, inner_parts[1])
-    grad_partial = combine(grad_slot_in, core=mine, scaled=False, more=(grad_other,))
-    grad_partial, got_down = fence(grad_partial, got_down)
-    grad_partial = plain(lax.psum_scatter(grad_partial, "col", scatter_dimension=0, tiled=True)[0])
-    grad_partial, inner_parts, out_partial = fence(grad_partial, inner_parts, out_partial)
+    own_down = down_grad(0, hidden, grad_slot)
+    grad_partial, inner_parts, own_down = fence(grad_partial, inner_parts, own_down)
+    got_down = [own_down] + near_down + far_down
     grad_moe_in = plain(lax.psum_scatter(grad_partial, "chip", scatter_dimension=0, tiled=True)[0])
     far_parts = inner_parts[near:]
     got_inner = inner_parts[:1] + [swap_cols(inner_parts[mask], mask) for mask in range(1, near)]

time: 1630 us -> 1610 us (0.988)
  waiting for transfers between devices: 714 us -> 656 us
  Pallas kernels: 254 us -> 282 us
    ppermute x4 -> x6, waiting for transfers between devices: 42.2 us -> 0.02 us  [swap_cores(): return lax.ppermute(values, 'core', [(0, 1), (1, 0)])]
    pallas_call x4 -> x8, Pallas kernels: 123 us -> 155 us  [combine_slots(): pl.pallas_call(partial(combine_kernel, scaled, added, each, begin), grid_...]
    unnamed x10, waiting for transfers between devices: 99.5 us -> 82 us
  transfers between devices with their start and end apart: 58 -> 60, of which waited for: 22 -> 22; matrix products, arithmetic and copies ran while one was open for 34% -> 34% of each run, Pallas kernels for 16% -> 18%
where the time goes in v6:
time: 1610 us; the launch traced here: 1600 us
  waiting for transfers between devices  656 us (41%)
  matrix products  310 us (19%)
  Pallas kernels  282 us (18%)
  local copies, waits for them, and re-layouts  164 us (10%)
  other arithmetic  89.1 us (6%)
  starting transfers between devices  59.9 us (4%)
  blocking collectives  20.3 us (1%)
    ppermute x33, waiting for transfers between devices, swap_cols(): return lax.ppermute(values, 'col', [(i, i ^ mask) for i in range(count)])  335 us
    all_gather x1, waiting for transfers between devices, local(): lax.all_gather(moe_in, ALL, axis=0).reshape(rows, cols, per_row, col_width)  160 us
    pallas_call x8, Pallas kernels, combine_slots(): pl.pallas_call(partial(combine_kernel, scaled, added, each, begin), grid_...  155 us
    unnamed x10, waiting for transfers between devices  82 us
    pallas_call x2, Pallas kernels, gather_slots(): pl.pallas_call(partial(gather_kernel, scaled, each), grid_spec=pltpu.Pref...  80.1 us
    ppermute x6, waiting for transfers between devices, swap_chips(): return lax.ppermute(values, 'chip', [(i, i ^ mask) for i in range(count)])  71.4 us
    dot_general x4, matrix products, local(): jnp.einsum('ecd,ecf->edf', feature_block(slot_inputs, col ^ mask), grad_i...  67.6 us
    dot_general x1, matrix products, local(): jnp.einsum('ecf,edf->ecd', jnp.concatenate([grad_gate_pre, grad_up_pre],...  42.4 us
  transfers between devices with their start and end apart: 60, of which 22 were waited for; matrix products, arithmetic and copies ran while one was open for 34% of the time, Pallas kernels for 18%

profile of v6, /device:TPU:3, one launch (start us, length us, event | category | flops | bytes accessed | tf_op | source)
XLA Modules:
  0.0 1596.6 jit_solution(13488236953076976282)
XLA Ops:
  53.0 33.2 %collective-permute-done.6 = bf16[1024,512]{1,0:T(8,128)(2,1)} collective-permute-done((bf16[1024,512]{1,0:T(8,128)(2,1)S(1)}, bf16[1024,512]{1,0:T(8,128)(2,1)}, u32[]{:S(2)}, u32[]{:S(2)}) %collective-permute-start.6) | collective-permute-done | bytes 1048608 | tf_op jit(solution)/shard_map/ppermute | solution.py:425
  131.9 48.4 %collective-permute-done.9 = bf16[1024,384]{0,1:T(8,128)(2,1)S(1)} collective-permute-done((bf16[1024,384]{0,1:T(8,128)(2,1)S(1)}, bf16[1024,384]{0,1:T(8,128)(2,1)S(1)}, u32[]{:S(2)}, u32[]{:S(2)}) %collective-permute-start.9) | collective-permute-done | bytes 786464 | tf_op jit(solution)/shard_map/ppermute | solution.py:480
  219.9 19.2 %attend_forward.1 = (bf16[1024,512]{1,0:T(8,128)(2,1)}, f32[1024,512]{1,0:T(8,128)}) custom-call(f32[4,1024,384]{2,1,0:T(8,128)} %add_bitcast_fusion.query_ref.key_ref.value_ref, f32[4,1024,384]{2,1,0:T(8,128)} %add_bitcast_fusion.query_ref.key_ref.value_ref, f32[4,1024,384]{2,1,0:T(8,128)} %add_bitcast_fusion.query_ref.key_ref.value_ref, ...), custom_call_target="tpu_custom_call" | custom-call | flops 2147483648 | bytes 9437184 | tf_op jit(solution)/shard_map/attend_forward/pallas_call | solution.py:108
  277.6 74.6 %collective-permute-done.22 = bf16[1024,512]{1,0:T(8,128)(2,1)S(1)} collective-permute-done((bf16[1024,512]{1,0:T(8,128)(2,1)S(1)}, bf16[1024,512]{1,0:T(8,128)(2,1)S(1)}, u32[]{:S(2)}, u32[]{:S(2)}) %collective-permute-start.22) | collective-permute-done | bytes 1048608 | tf_op jit(solution)/shard_map/ppermute | solution.py:425
  417.2 159.6 %all-gather.5.cloned.1.call-done = bf16[32768,512]{1,0:T(8,128)(2,1)} async-done(((bf16[1024,512]{1,0:T(8,128)(2,1)}), bf16[32768,512]{1,0:T(8,128)(2,1)}) %all-gather.5.cloned.1.call-update) | async-done | bytes 33554448 | tf_op jit(solution)/shard_map/all_gather | solution.py:724
  580.9 39.8 %gather_slots.2 = bf16[2,2048,2048]{2,1,0:T(8,128)(2,1)} custom-call(s32[2,16]{1,0:T(2,128)} %get-tuple-element.134.low_ref, s32[2,16]{1,0:T(2,128)} %get-tuple-element.135.high_ref, bf16[8,4,1024,512]{3,2,1,0:T(8,128)(2,1)} %bitcast.305, bf16[8,4,1024,512]{3,2,1,0:T(8,128)(2,1)} %bitcast.306, s32[2,16,1,512]{3,2,1,0:T(1,128)} %reshape.137.refs_2_.refs_3_.place_ref, ...), custom_call_target="tpu_custom_call" | custom-call | flops 25769803776 | bytes 50331648 | tf_op jit(solution)/shard_map/gather_slots/pallas_call | solution.py:299
  620.8 25.2 %fusion.19 = bf16[2,2048,1024]{1,2,0:T(8,128)(2,1)} fusion(bf16[2,2048,2048]{2,1,0:T(8,128)(2,1)} %gather_slots.2, bf16[2,2048,2048]{1,2,0:T(8,128)(2,1)} %constant_dynamic-update-slice_fusion.4), kind=kOutput, calls=%fused_computation.31 | convolution fusion | flops 17184063488 | bytes 33554432 | tf_op jit(solution)/shard_map/ecd,edf->ecf/dot_general | solution.py:736
  646.0 28.2 %fusion = (bf16[2,2048,1024]{1,2,0:T(8,128)(2,1)}, bf16[2,2048,1024]{1,2,0:T(8,128)(2,1)}) fusion(bf16[2,2048,1024]{1,2,0:T(8,128)(2,1)} %fusion.19, bf16[2,2048,2048]{2,1,0:T(8,128)(2,1)} %gather_slots.2, bf16[2,2048,2048]{1,2,0:T(8,128)(2,1)} %constant_dynamic-update-slice_fusion.4), kind=kOutput, calls=%fused_computation.5 | convolution fusion | flops 17217617920 | bytes 50331648 | tf_op jit(solution)/shard_map/ecd,edf->ecf/dot_general | solution.py:739
  686.6 21.3 %collective-permute-done.30 = bf16[2,1024,512]{2,1,0:T(8,128)(2,1)S(1)} collective-permute-done((bf16[2,1024,512]{2,1,0:T(8,128)(2,1)}, bf16[2,1024,512]{2,1,0:T(8,128)(2,1)S(1)}, u32[]{:S(2)}, u32[]{:S(2)}) %collective-permute-start.30) | collective-permute-done | bytes 2097184 | tf_op jit(solution)/shard_map/ppermute | solution.py:425
  709.5 28.0 %convolution_convert_fusion.slots_ref = bf16[2,2048,2048]{2,1,0:T(8,128)(2,1)} fusion(bf16[2,2048,1024]{1,2,0:T(8,128)(2,1)} %get-tuple-element.160, bf16[2,1024,2048]{2,1,0:T(8,128)(2,1)} %constant_dynamic-update-slice_fusion), kind=kOutput, calls=%fused_computation.20 | convolution fusion | flops 17188257792 | bytes 33554432 | tf_op jit(solution)/shard_map/ecf,efd->ecd/dot_general | solution.py:757
  737.6 18.5 %combine_slots.9 = bf16[4,2,1024,512]{3,2,1,0:T(8,128)(2,1)} custom-call(s32[2,16]{1,0:T(2,128)} %get-tuple-element.134.low_ref, s32[2,16]{1,0:T(2,128)} %get-tuple-element.135.high_ref, s32[1]{0:T(128)S(6)} %sub.54.core_ref, bf16[2,2048,2048]{2,1,0:T(8,128)(2,1)} %convolution_convert_fusion.slots_ref, s32[2,16,1,512]{3,2,1,0:T(1,128)} %reshape.137.refs_2_.refs_3_.place_ref, ...), custom_call_target="tpu_custom_call" | custom-call | flops 6442450944 | bytes 25165824 | tf_op jit(solution)/shard_map/combine_slots/pallas_call | solution.py:396
  756.4 20.2 %combine_slots.8 = bf16[4,2,1024,512]{3,2,1,0:T(8,128)(2,1)} custom-call(s32[2,16]{1,0:T(2,128)} %get-tuple-element.134.low_ref, s32[2,16]{1,0:T(2,128)} %get-tuple-element.135.high_ref, s32[1]{0:T(128)S(6)} %sub.54.core_ref, bf16[2,2048,2048]{2,1,0:T(8,128)(2,1)} %convolution_convert_fusion.slots_ref, s32[2,16,1,512]{3,2,1,0:T(1,128)} %reshape.137.refs_2_.refs_3_.place_ref, ...), custom_call_target="tpu_custom_call" | custom-call | flops 6442450944 | bytes 25165824 | tf_op jit(solution)/shard_map/combine_slots/pallas_call | solution.py:396
  776.7 20.4 %combine_slots.10.refs_1_ = bf16[4,4,1024,512]{3,2,1,0:T(8,128)(2,1)} custom-call(s32[2,16]{1,0:T(2,128)} %get-tuple-element.134.low_ref, s32[2,16]{1,0:T(2,128)} %get-tuple-element.135.high_ref, s32[1]{0:T(128)} %bitcast.65.core_ref, bf16[2,2048,2048]{2,1,0:T(8,128)(2,1)} %convolution_convert_fusion.slots_ref, ...), custom_call_target="tpu_custom_call" | custom-call | flops 6442450944 | bytes 25165824 | tf_op jit(solution)/shard_map/combine_slots/pallas_call | solution.py:396
  797.1 19.8 %combine_slots.11 = bf16[4,4,1024,512]{3,2,1,0:T(8,128)(2,1)} custom-call(s32[2,16]{1,0:T(2,128)} %get-tuple-element.134.low_ref, s32[2,16]{1,0:T(2,128)} %get-tuple-element.135.high_ref, s32[1]{0:T(128)} %bitcast.65.core_ref, bf16[2,2048,2048]{2,1,0:T(8,128)(2,1)} %convolution_convert_fusion.slots_ref, ...), custom_call_target="tpu_custom_call", output_to_operand_aliasing={{}: (7, {})} | custom-call | flops 6442450944 | bytes 25165824 | tf_op jit(solution)/shard_map/combine_slots/pallas_call | solution.py:396
  817.0 40.3 %gather_slots.3 = bf16[2,2048,2048]{2,1,0:T(8,128)(2,1)} custom-call(s32[2,16]{1,0:T(2,128)} %get-tuple-element.134.low_ref, s32[2,16]{1,0:T(2,128)} %get-tuple-element.135.high_ref, bf16[8,4,1024,512]{3,2,1,0:T(8,128)(2,1)} %bitcast.307, bf16[8,4,1024,512]{3,2,1,0:T(8,128)(2,1)} %bitcast.308, s32[2,16,1,512]{3,2,1,0:T(1,128)} %reshape.137.refs_2_.refs_3_.place_ref, ...), custom_call_target="tpu_custom_call" | custom-call | flops 25769803776 | bytes 50331648 | tf_op jit(solution)/shard_map/gather_slots/pallas_call | solution.py:299
  891.7 33.0 %fusion.3 = (bf16[2,2048,1024]{1,2,0:T(8,128)(2,1)}, bf16[2,2048,1024]{1,2,0:T(8,128)(2,1)}) fusion(bf16[2,2048,1024]{1,2,0:T(8,128)(2,1)} %get-tuple-element.264, bf16[2,2048,1024]{1,2,0:T(8,128)(2,1)} %fusion.19, bf16[2,2048,2048]{2,1,0:T(8,128)(2,1)} %gather_slots.3, bf16[2,1024,2048]{2,1,0:T(8,128)(2,1)} %constant_dynamic-update-slice_fusion), kind=kOutput, calls=%fused_computation.8 | convolution fusion | flops 17242783744 | bytes 58720256 | tf_op jit(solution)/shard_map/ecd,efd->ecf/dot_general | solution.py:782
  924.6 42.4 %fusion.12.slots_ref = bf16[2,2048,2048]{2,1,0:T(8,128)(2,1)} fusion(bf16[2,2048,2048]{1,2,0:T(8,128)(2,1)} %constant_dynamic-update-slice_fusion.4, bf16[2,2048,1024]{1,2,0:T(8,128)(2,1)} %get-tuple-element.154, bf16[2,2048,1024]{1,2,0:T(8,128)(2,1)} %get-tuple-element.153), kind=kOutput, calls=%fused_computation.19 | convolution fusion | flops 34401681408 | bytes 50331648 | tf_op jit(solution)/shard_map/ecf,edf->ecd/dot_general | solution.py:788
  967.0 17.5 %combine_slots.13 = bf16[4,2,1024,512]{3,2,1,0:T(8,128)(2,1)} custom-call(s32[2,16]{1,0:T(2,128)} %get-tuple-element.134.low_ref, s32[2,16]{1,0:T(2,128)} %get-tuple-element.135.high_ref, s32[1]{0:T(128)S(6)} %sub.54.core_ref, bf16[2,2048,2048]{2,1,0:T(8,128)(2,1)} %fusion.12.slots_ref, s32[2,16,1,512]{3,2,1,0:T(1,128)} %reshape.137.refs_2_.refs_3_.place_ref, ...), custom_call_target="tpu_custom_call" | custom-call | flops 6442450944 | bytes 25165824 | tf_op jit(solution)/shard_map/combine_slots/pallas_call | solution.py:396
  984.5 20.2 %combine_slots.12 = bf16[4,2,1024,512]{3,2,1,0:T(8,128)(2,1)} custom-call(s32[2,16]{1,0:T(2,128)} %get-tuple-element.134.low_ref, s32[2,16]{1,0:T(2,128)} %get-tuple-element.135.high_ref, s32[1]{0:T(128)S(6)} %sub.54.core_ref, bf16[2,2048,2048]{2,1,0:T(8,128)(2,1)} %fusion.12.slots_ref, s32[2,16,1,512]{3,2,1,0:T(1,128)} %reshape.137.refs_2_.refs_3_.place_ref, ...), custom_call_target="tpu_custom_call" | custom-call | flops 6442450944 | bytes 25165824 | tf_op jit(solution)/shard_map/combine_slots/pallas_call | solution.py:396
  1025.7 19.3 %combine_slots.14.refs_1_ = bf16[4,4,1024,512]{3,2,1,0:T(8,128)(2,1)} custom-call(s32[2,16]{1,0:T(2,128)} %get-tuple-element.134.low_ref, s32[2,16]{1,0:T(2,128)} %get-tuple-element.135.high_ref, s32[1]{0:T(128)} %bitcast.65.core_ref, bf16[2,2048,2048]{2,1,0:T(8,128)(2,1)} %fusion.12.slots_ref, s32[2,16,1,512]{3,2,1,0:T(1,128)} %reshape.137.refs_2_.refs_3_.place_ref, ...), custom_call_target="tpu_custom_call" | custom-call | flops 6442450944 | bytes 25165824 | tf_op jit(solution)/shard_map/combine_slots/pallas_call | solution.py:396
  1045.0 18.5 %combine_slots.15 = bf16[4,4,1024,512]{3,2,1,0:T(8,128)(2,1)} custom-call(s32[2,16]{1,0:T(2,128)} %get-tuple-element.134.low_ref, s32[2,16]{1,0:T(2,128)} %get-tuple-element.135.high_ref, s32[1]{0:T(128)} %bitcast.65.core_ref, bf16[2,2048,2048]{2,1,0:T(8,128)(2,1)} %fusion.12.slots_ref, ...), custom_call_target="tpu_custom_call", output_to_operand_aliasing={{}: (7, {})} | custom-call | flops 6442450944 | bytes 25165824 | tf_op jit(solution)/shard_map/combine_slots/pallas_call | solution.py:396
  1074.7 16.7 %fusion.42 = bf16[2,512,2048]{2,1,0:T(8,128)(2,1)} fusion(bf16[2,2048,2048]{1,2,0:T(8,128)(2,1)} %pad_maximum_fusion, bf16[2,2048,2048]{2,1,0:T(8,128)(2,1)} %gather_slots.2, s32[]{:T(128)S(6)} %select_n.277), kind=kOutput, calls=%fused_computation.59 | convolution fusion | flops 8592031744 | bytes 25165828 | tf_op jit(solution)/shard_map/ecd,ecf->edf/dot_general | solution.py:812
  1091.4 16.7 %fusion.45 = bf16[2,512,2048]{2,1,0:T(8,128)(2,1)} fusion(bf16[2,2048,2048]{1,2,0:T(8,128)(2,1)} %pad_maximum_fusion, bf16[2,2048,2048]{2,1,0:T(8,128)(2,1)} %gather_slots.2, s32[]{:T(128)S(6)} %select_n.278), kind=kOutput, calls=%fused_computation.60 | convolution fusion | flops 8592031744 | bytes 25165828 | tf_op jit(solution)/shard_map/ecd,ecf->edf/dot_general | solution.py:812
  1108.1 17.0 %fusion.48 = bf16[2,512,2048]{2,1,0:T(8,128)(2,1)} fusion(bf16[2,2048,2048]{1,2,0:T(8,128)(2,1)} %pad_maximum_fusion, bf16[2,2048,2048]{2,1,0:T(8,128)(2,1)} %gather_slots.2, s32[]{:T(128)S(6)} %select_n.279), kind=kOutput, calls=%fused_computation.61 | convolution fusion | flops 8592031744 | bytes 25165828 | tf_op jit(solution)/shard_map/ecd,ecf->edf/dot_general | solution.py:812
  1125.0 17.2 %fusion.34 = f32[2,512,2048]{2,1,0:T(8,128)} fusion(bf16[2,2048,2048]{1,2,0:T(8,128)(2,1)} %pad_maximum_fusion, bf16[2,2048,2048]{2,1,0:T(8,128)(2,1)} %gather_slots.2, s32[]{:T(128)S(6)} %select_n.276), kind=kOutput, calls=%fused_computation.51 | convolution fusion | flops 8589934592 | bytes 29360132 | tf_op jit(solution)/shard_map/ecd,ecf->edf/dot_general | solution.py:812
  1142.3 76.3 %reduce-scatter.21.cloned.1.call-done = bf16[1,4,1024,512]{3,2,1,0:T(8,128)(2,1)} async-done(((bf16[4,4,1024,512]{3,2,1,0:T(8,128)(2,1)}), bf16[1,4,1024,512]{3,2,1,0:T(8,128)(2,1)}) %reduce-scatter.21.cloned.1.call-update) | async-done | bytes 4194320
  1231.3 79.2 %collective-permute-done.38 = bf16[2,512,2048]{2,1,0:T(8,128)(2,1)} collective-permute-done((bf16[2,512,2048]{2,1,0:T(8,128)(2,1)}, bf16[2,512,2048]{2,1,0:T(8,128)(2,1)}, u32[]{:S(2)}, u32[]{:S(2)}) %collective-permute-start.38) | collective-permute-done | bytes 4194336 | tf_op jit(solution)/shard_map/ppermute | solution.py:425
  1346.7 26.4 %collective-permute-done.41 = bf16[1024,512]{1,0:T(8,128)(2,1)S(1)} collective-permute-done((bf16[1024,512]{1,0:T(8,128)(2,1)S(1)}, bf16[1024,512]{1,0:T(8,128)(2,1)S(1)}, u32[]{:S(2)}, u32[]{:S(2)}) %collective-permute-start.41) | collective-permute-done | bytes 1048608 | tf_op jit(solution)/shard_map/ppermute | solution.py:425
  1415.7 28.6 %attend_backward.1 = (bf16[4,1024,384]{2,1,0:T(8,128)(2,1)}, f32[2,128]{1,0:T(2,128)}) custom-call(f32[4,1024,384]{2,1,0:T(8,128)} %add_bitcast_fusion.query_ref.key_ref.value_ref, f32[4,1024,384]{2,1,0:T(8,128)} %add_bitcast_fusion.query_ref.key_ref.value_ref, f32[4,1024,384]{2,1,0:T(8,128)} %add_bitcast_fusion.query_ref.key_ref.value_ref, ...), custom_call_target="tpu_custom_call" | custom-call | flops 5368709120 | bytes 12582912 | tf_op jit(solution)/shard_map/attend_backward/pallas_call | solution.py:194
  1444.4 23.4 %collective-permute-done.43 = bf16[2,512,2048]{2,1,0:T(8,128)(2,1)} collective-permute-done((bf16[2,512,2048]{2,1,0:T(8,128)(2,1)}, bf16[2,512,2048]{2,1,0:T(8,128)(2,1)}, u32[]{:S(2)}, u32[]{:S(2)}) %collective-permute-start.43) | collective-permute-done | bytes 4194336 | tf_op jit(solution)/shard_map/ppermute | solution.py:425
  1500.6 20.0 %collective-permute-done.46 = bf16[1024,512]{1,0:T(8,128)(2,1)} collective-permute-done((bf16[1024,512]{1,0:T(8,128)(2,1)}, bf16[1024,512]{1,0:T(8,128)(2,1)}, u32[]{:S(2)}, u32[]{:S(2)}) %collective-permute-start.46) | collective-permute-done | bytes 1048608 | tf_op jit(solution)/shard_map/ppermute | solution.py:425
  1520.6 24.3 %collective-permute-done.45 = bf16[1024,512]{1,0:T(8,128)(2,1)} collective-permute-done((bf16[1024,512]{1,0:T(8,128)(2,1)}, bf16[1024,512]{1,0:T(8,128)(2,1)}, u32[]{:S(2)}, u32[]{:S(2)}) %collective-permute-start.45) | collective-permute-done | bytes 1048608 | tf_op jit(solution)/shard_map/ppermute | solution.py:425
  (389 shorter events, 487.4 us)
Async XLA Ops:
  7.2 569.6 %all-gather.5.cloned.1.call-start = ((), (), s32[]{:S(2)}) async-start(), calls=%async_computation.10 | async-start | bytes 34603008 | tf_op jit(solution)/shard_map/all_gather | solution.py:724
  38.9 47.4 %collective-permute-start.6 = (bf16[1024,512]{1,0:T(8,128)(2,1)S(1)}, bf16[1024,512]{1,0:T(8,128)(2,1)}, u32[]{:S(2)}, u32[]{:S(2)}) collective-permute-start(bf16[1024,512]{1,0:T(8,128)(2,1)S(1)} %copy-done.4), channel_id=1, source_target_pairs={{0,2},{1,3},{2,0},{3,1},{4,6},{5,7},{6,4},{7,5},{8,10},{9,11},{10,... | collective-permute-start | bytes 3145736 | tf_op jit(solution)/shard_map/ppermute | solution.py:425
  47.9 134.4 %collective-permute-start.14 = (bf16[2,256,2048]{2,1,0:T(8,128)(2,1)}, bf16[2,256,2048]{2,1,0:T(8,128)(2,1)}, u32[]{:S(2)}, u32[]{:S(2)}) collective-permute-start(bf16[2,256,2048]{2,1,0:T(8,128)(2,1)} %get-tuple-element.213), channel_id=1, source_target_pairs={{0,1},{1,0},{2,3},{3,2},{4,5},{5,4},{6,7},{7,6},{8,9},{9,8},{10,11... | collective-permute-start | bytes 6291464 | tf_op jit(solution)/shard_map/ppermute | solution.py:425
  48.0 134.3 %collective-permute-start.15 = (bf16[2,256,2048]{2,1,0:T(8,128)(2,1)}, bf16[2,256,2048]{2,1,0:T(8,128)(2,1)}, u32[]{:S(2)}, u32[]{:S(2)}) collective-permute-start(bf16[2,256,2048]{2,1,0:T(8,128)(2,1)} %get-tuple-element.212), channel_id=1, source_target_pairs={{0,2},{1,3},{2,0},{3,1},{4,6},{5,7},{6,4},{7,5},{8,10},{9,11},{10,... | collective-permute-start | bytes 6291464 | tf_op jit(solution)/shard_map/ppermute | solution.py:425
  49.6 132.8 %collective-permute-start.16 = (bf16[2,256,2048]{2,1,0:T(8,128)(2,1)}, bf16[2,256,2048]{2,1,0:T(8,128)(2,1)}, u32[]{:S(2)}, u32[]{:S(2)}) collective-permute-start(bf16[2,256,2048]{2,1,0:T(8,128)(2,1)} %get-tuple-element.211), channel_id=1, source_target_pairs={{0,3},{1,2},{2,1},{3,0},{4,7},{5,6},{6,5},{7,4},{8,11},{9,10},{10,... | collective-permute-start | bytes 6291464 | tf_op jit(solution)/shard_map/ppermute | solution.py:425
  125.0 55.3 %collective-permute-start.9 = (bf16[1024,384]{0,1:T(8,128)(2,1)S(1)}, bf16[1024,384]{0,1:T(8,128)(2,1)S(1)}, u32[]{:S(2)}, u32[]{:S(2)}) collective-permute-start(bf16[1024,384]{0,1:T(8,128)(2,1)S(1)} %maximum_maximum_fusion), channel_id=1, source_target_pairs={{0,16},{8,24},{16,0},{24,8},{1,17},{9,25},{17,1},{25,9},{2,18},{10... | collective-permute-start | bytes 2359304 | tf_op jit(solution)/shard_map/ppermute | solution.py:480
  125.4 56.0 %collective-permute-start.10 = (bf16[1024,384]{0,1:T(8,128)(2,1)S(1)}, bf16[1024,384]{0,1:T(8,128)(2,1)S(1)}, u32[]{:S(2)}, u32[]{:S(2)}) collective-permute-start(bf16[1024,384]{0,1:T(8,128)(2,1)S(1)} %maximum_maximum_fusion), channel_id=1, source_target_pairs={{0,24},{8,16},{16,8},{24,0},{1,25},{9,17},{17,9},{25,1},{2,26},{10... | collective-permute-start | bytes 2359304 | tf_op jit(solution)/shard_map/ppermute | solution.py:480
  206.7 56.0 %collective-permute-start.24 = (bf16[4,256,512]{2,1,0:T(8,128)(2,1)S(1)}, bf16[4,256,512]{2,1,0:T(8,128)(2,1)S(1)}, u32[]{:S(2)}, u32[]{:S(2)}) collective-permute-start(bf16[4,256,512]{2,1,0:T(8,128)(2,1)S(1)} %bitcast_dynamic-update-slice_fusion.14), channel_id=1, source_target_pairs={{0,4},{4,0},{1,5},{5,1},{2,6},{6,2},{3,7},{7,3},{8,12},{12,8},{9,1... | collective-permute-start | bytes 3145736 | tf_op jit(solution)/shard_map/ppermute | solution.py:420
  259.9 102.7 %collective-permute-start.25 = (bf16[2,128,2048]{2,1,0:T(8,128)(2,1)}, bf16[2,128,2048]{2,1,0:T(8,128)(2,1)}, u32[]{:S(2)}, u32[]{:S(2)}) collective-permute-start(bf16[2,128,2048]{2,1,0:T(8,128)(2,1)} %get-tuple-element.114), channel_id=1, source_target_pairs={{0,1},{1,0},{2,3},{3,2},{4,5},{5,4},{6,7},{7,6},{8,9},{9,8},{10,11... | collective-permute-start | bytes 3145736 | tf_op jit(solution)/shard_map/ppermute | solution.py:425
  261.3 101.3 %collective-permute-start.26 = (bf16[2,128,2048]{2,1,0:T(8,128)(2,1)}, bf16[2,128,2048]{2,1,0:T(8,128)(2,1)}, u32[]{:S(2)}, u32[]{:S(2)}) collective-permute-start(bf16[2,128,2048]{2,1,0:T(8,128)(2,1)} %get-tuple-element.115), channel_id=1, source_target_pairs={{0,2},{1,3},{2,0},{3,1},{4,6},{5,7},{6,4},{7,5},{8,10},{9,11},{10,... | collective-permute-start | bytes 3145736 | tf_op jit(solution)/shard_map/ppermute | solution.py:425
  261.3 90.9 %collective-permute-start.22 = (bf16[1024,512]{1,0:T(8,128)(2,1)S(1)}, bf16[1024,512]{1,0:T(8,128)(2,1)S(1)}, u32[]{:S(2)}, u32[]{:S(2)}) collective-permute-start(bf16[1024,512]{1,0:T(8,128)(2,1)S(1)} %copy-done.33), channel_id=1, source_target_pairs={{0,2},{1,3},{2,0},{3,1},{4,6},{5,7},{6,4},{7,5},{8,10},{9,11},{10,... | collective-permute-start | bytes 3145736 | tf_op jit(solution)/shard_map/ppermute | solution.py:425
  263.7 88.6 %collective-permute-start.23 = (bf16[1024,512]{1,0:T(8,128)(2,1)S(1)}, bf16[1024,512]{1,0:T(8,128)(2,1)S(1)}, u32[]{:S(2)}, u32[]{:S(2)}) collective-permute-start(bf16[1024,512]{1,0:T(8,128)(2,1)S(1)} %copy-done.33), channel_id=1, source_target_pairs={{0,3},{1,2},{2,1},{3,0},{4,7},{5,6},{6,5},{7,4},{8,11},{9,10},{10,... | collective-permute-start | bytes 3145736 | tf_op jit(solution)/shard_map/ppermute | solution.py:425
  276.9 85.7 %collective-permute-start.27 = (bf16[2,128,2048]{2,1,0:T(8,128)(2,1)}, bf16[2,128,2048]{2,1,0:T(8,128)(2,1)}, u32[]{:S(2)}, u32[]{:S(2)}) collective-permute-start(bf16[2,128,2048]{2,1,0:T(8,128)(2,1)} %get-tuple-element.116), channel_id=1, source_target_pairs={{0,3},{1,2},{2,1},{3,0},{4,7},{5,6},{6,5},{7,4},{8,11},{9,10},{10,... | collective-permute-start | bytes 3145736 | tf_op jit(solution)/shard_map/ppermute | solution.py:425
  362.6 454.3 %all-gather.7.cloned.1.call-start = ((), (), s32[]{:S(2)}) async-start(), calls=%async_computation.11 | async-start | bytes 34603008 | tf_op jit(solution)/shard_map/all_gather | solution.py:730
  576.8 433.5 %reduce-scatter.19.cloned.1.call-start = ((), (), s32[]{:S(2)}) async-start(), calls=%async_computation.12 | async-start | bytes 20971520
  578.3 101.9 %collective-permute-start.28 = (bf16[2,1024,512]{2,1,0:T(8,128)(2,1)}, bf16[2,1024,512]{2,1,0:T(8,128)(2,1)}, u32[]{:S(2)}, u32[]{:S(2)}) collective-permute-start(bf16[2,1024,512]{2,1,0:T(8,128)(2,1)} %get-tuple-element.141), channel_id=1, source_target_pairs={{0,1},{1,0},{2,3},{3,2},{4,5},{5,4},{6,7},{7,6},{8,9},{9,8},{10,11... | collective-permute-start | bytes 6291464 | tf_op jit(solution)/shard_map/ppermute | solution.py:425
  578.6 104.7 %collective-permute-start.29 = (bf16[2,1024,512]{2,1,0:T(8,128)(2,1)}, bf16[2,1024,512]{2,1,0:T(8,128)(2,1)}, u32[]{:S(2)}, u32[]{:S(2)}) collective-permute-start(bf16[2,1024,512]{2,1,0:T(8,128)(2,1)} %get-tuple-element.142), channel_id=1, source_target_pairs={{0,2},{1,3},{2,0},{3,1},{4,6},{5,7},{6,4},{7,5},{8,10},{9,11},{10,... | collective-permute-start | bytes 6291464 | tf_op jit(solution)/shard_map/ppermute | solution.py:425
  579.8 128.1 %collective-permute-start.30 = (bf16[2,1024,512]{2,1,0:T(8,128)(2,1)}, bf16[2,1024,512]{2,1,0:T(8,128)(2,1)S(1)}, u32[]{:S(2)}, u32[]{:S(2)}) collective-permute-start(bf16[2,1024,512]{2,1,0:T(8,128)(2,1)} %get-tuple-element.143), channel_id=1, source_target_pairs={{0,3},{1,2},{2,1},{3,0},{4,7},{5,6},{6,5},{7,4},{8,11},{9,10},{10,... | collective-permute-start | bytes 6291464 | tf_op jit(solution)/shard_map/ppermute | solution.py:425
  817.0 401.6 %reduce-scatter.21.cloned.1.call-start = ((), (), s32[]{:S(2)}) async-start(), calls=%async_computation.13 | async-start | bytes 20971520
  887.0 117.7 %collective-permute-start.33 = (bf16[2,1024,512]{2,1,0:T(8,128)(2,1)}, bf16[2,1024,512]{2,1,0:T(8,128)(2,1)S(1)}, u32[]{:S(2)}, u32[]{:S(2)}) collective-permute-start(bf16[2,1024,512]{2,1,0:T(8,128)(2,1)} %fusion.84), channel_id=1, source_target_pairs={{0,1},{1,0},{2,3},{3,2},{4,5},{5,4},{6,7},{7,6},{8,9},{9,8},{10,11... | collective-permute-start | bytes 6291464 | tf_op jit(solution)/shard_map/ppermute | solution.py:425
  889.0 115.7 %collective-permute-start.34 = (bf16[2,1024,512]{2,1,0:T(8,128)(2,1)}, bf16[2,1024,512]{2,1,0:T(8,128)(2,1)}, u32[]{:S(2)}, u32[]{:S(2)}) collective-permute-start(bf16[2,1024,512]{2,1,0:T(8,128)(2,1)} %fusion.87), channel_id=1, source_target_pairs={{0,2},{1,3},{2,0},{3,1},{4,6},{5,7},{6,4},{7,5},{8,10},{9,11},{10,... | collective-permute-start | bytes 6291464 | tf_op jit(solution)/shard_map/ppermute | solution.py:425
  1010.8 52.7 %collective-permute-start.37 = (bf16[2,1024,512]{2,1,0:T(8,128)(2,1)}, bf16[2,1024,512]{2,1,0:T(8,128)(2,1)}, u32[]{:S(2)}, u32[]{:S(2)}) collective-permute-start(bf16[2,1024,512]{2,1,0:T(8,128)(2,1)} %fusion.90), channel_id=1, source_target_pairs={{0,3},{1,2},{2,1},{3,0},{4,7},{5,6},{6,5},{7,4},{8,11},{9,10},{10,... | collective-permute-start | bytes 6291464 | tf_op jit(solution)/shard_map/ppermute | solution.py:425
  1063.5 247.1 %reduce-scatter.11.cloned.1.call-start = ((), (), s32[]{:S(2)}) async-start(), calls=%async_computation.6 | async-start | bytes 5242880 | tf_op jit(solution)/shard_map/reduce_scatter | solution.py:820
  1218.6 249.2 %reduce-scatter.13.cloned.1.call-start = ((), (), s32[]{:S(2)}) async-start(), calls=%async_computation.7 | async-start | bytes 5242880 | tf_op jit(solution)/shard_map/reduce_scatter | solution.py:847
  1218.8 91.8 %collective-permute-start.38 = (bf16[2,512,2048]{2,1,0:T(8,128)(2,1)}, bf16[2,512,2048]{2,1,0:T(8,128)(2,1)}, u32[]{:S(2)}, u32[]{:S(2)}) collective-permute-start(bf16[2,512,2048]{2,1,0:T(8,128)(2,1)} %fusion.42), channel_id=1, source_target_pairs={{0,1},{1,0},{2,3},{3,2},{4,5},{5,4},{6,7},{7,6},{8,9},{9,8},{10,11... | collective-permute-start | bytes 12582920 | tf_op jit(solution)/shard_map/ppermute | solution.py:425
  1219.2 91.4 %collective-permute-start.39 = (bf16[2,512,2048]{2,1,0:T(8,128)(2,1)}, bf16[2,512,2048]{2,1,0:T(8,128)(2,1)}, u32[]{:S(2)}, u32[]{:S(2)}) collective-permute-start(bf16[2,512,2048]{2,1,0:T(8,128)(2,1)} %fusion.45), channel_id=1, source_target_pairs={{0,2},{1,3},{2,0},{3,1},{4,6},{5,7},{6,4},{7,5},{8,10},{9,11},{10,... | collective-permute-start | bytes 12582920 | tf_op jit(solution)/shard_map/ppermute | solution.py:425
  1325.8 47.4 %collective-permute-start.41 = (bf16[1024,512]{1,0:T(8,128)(2,1)S(1)}, bf16[1024,512]{1,0:T(8,128)(2,1)S(1)}, u32[]{:S(2)}, u32[]{:S(2)}) collective-permute-start(bf16[1024,512]{1,0:T(8,128)(2,1)S(1)} %get-tuple-element.220), channel_id=1, source_target_pairs={{0,2},{1,3},{2,0},{3,1},{4,6},{5,7},{6,4},{7,5},{8,10},{9,11},{10,... | collective-permute-start | bytes 3145736 | tf_op jit(solution)/shard_map/ppermute | solution.py:425
  1374.8 124.1 %reduce-scatter.17.cloned.1.call-start = ((), (), s32[]{:S(2)}) async-start(), calls=%async_computation.9 | async-start | bytes 2359296 | tf_op jit(solution)/shard_map/reduce_scatter | solution.py:848
  1374.8 92.9 %collective-permute-start.43 = (bf16[2,512,2048]{2,1,0:T(8,128)(2,1)}, bf16[2,512,2048]{2,1,0:T(8,128)(2,1)}, u32[]{:S(2)}, u32[]{:S(2)}) collective-permute-start(bf16[2,512,2048]{2,1,0:T(8,128)(2,1)} %fusion.48), channel_id=1, source_target_pairs={{0,3},{1,2},{2,1},{3,0},{4,7},{5,6},{6,5},{7,4},{8,11},{9,10},{10,... | collective-permute-start | bytes 12582920 | tf_op jit(solution)/shard_map/ppermute | solution.py:425
  1382.6 190.1 %reduce-scatter.15.cloned.1.call-start = ((), (), s32[]{:S(2)}) async-start(), calls=%async_computation.8 | async-start | bytes 7077888 | tf_op jit(solution)/shard_map/reduce_scatter | solution.py:553
  1497.2 47.7 %collective-permute-start.45 = (bf16[1024,512]{1,0:T(8,128)(2,1)}, bf16[1024,512]{1,0:T(8,128)(2,1)}, u32[]{:S(2)}, u32[]{:S(2)}) collective-permute-start(bf16[1024,512]{1,0:T(8,128)(2,1)} %get-tuple-element.217), channel_id=1, source_target_pairs={{0,2},{1,3},{2,0},{3,1},{4,6},{5,7},{6,4},{7,5},{8,10},{9,11},{10,... | collective-permute-start | bytes 3145736 | tf_op jit(solution)/shard_map/ppermute | solution.py:425
  1497.2 47.7 %collective-permute-start.44 = (bf16[1024,512]{1,0:T(8,128)(2,1)}, bf16[1024,512]{1,0:T(8,128)(2,1)}, u32[]{:S(2)}, u32[]{:S(2)}) collective-permute-start(bf16[1024,512]{1,0:T(8,128)(2,1)} %get-tuple-element.215), channel_id=1, source_target_pairs={{0,1},{1,0},{2,3},{3,2},{4,5},{5,4},{6,7},{7,6},{8,9},{9,8},{10,11... | collective-permute-start | bytes 3145736 | tf_op jit(solution)/shard_map/ppermute | solution.py:425
  (81 other events, 1679.3 us)
Sparse Core Ops, SparseCore 0:
  362.7 213.9 all-gather.4
  579.6 226.8 all-gather.6
  817.1 193.1 reduce-scatter.18
  1063.7 154.8 reduce-scatter.20
  1220.7 76.9 reduce-scatter.10
  1374.9 76.6 reduce-scatter.12
  1453.9 33.4 reduce-scatter.16
  1492.6 68.5 reduce-scatter.14

commit v7 on v6

--- a/solution.py
+++ b/solution.py
@@ -861,9 +861,7 @@
         grad_gate_up = lax.dynamic_update_index_in_dim(
             grad_gate_up, got_inner[mask].astype(F32), col ^ mask, 0
         )
-    grad_projected, far_parts, moe_result, grad_gate_up = fence(
-        grad_projected, far_parts, moe_result, grad_gate_up
-    )
+    grad_projected, moe_result, grad_gate_up = fence(grad_projected, moe_result, grad_gate_up)
     output = (hidden_one + moe_result.astype(F32)).astype(BF16)
     normed_parts = [
         plain(

time: 1610 us -> 1610 us (level)
  transfers between devices with their start and end apart: 60 -> 60, of which waited for: 22 -> 20; matrix products, arithmetic and copies ran while one was open for 34% -> 34% of each run, Pallas kernels for 18% -> 18%
where the time goes in v7:
time: 1610 us; the launch traced here: 1600 us
  waiting for transfers between devices  656 us (41%)
  matrix products  307 us (19%)
  Pallas kernels  283 us (18%)
  local copies, waits for them, and re-layouts  164 us (10%)
  other arithmetic  89.6 us (6%)
  starting transfers between devices  64.8 us (4%)
  blocking collectives  20.3 us (1%)
    ppermute x33, waiting for transfers between devices, swap_cols(): return lax.ppermute(values, 'col', [(i, i ^ mask) for i in range(count)])  332 us
    all_gather x1, waiting for transfers between devices, local(): lax.all_gather(moe_in, ALL, axis=0).reshape(rows, cols, per_row, col_width)  160 us
    pallas_call x8, Pallas kernels, combine_slots(): pl.pallas_call(partial(combine_kernel, scaled, added, each, begin), grid_...  155 us
    pallas_call x2, Pallas kernels, gather_slots(): pl.pallas_call(partial(gather_kernel, scaled, each), grid_spec=pltpu.Pref...  80.3 us
    unnamed x10, waiting for transfers between devices  75 us
    ppermute x6, waiting for transfers between devices, swap_chips(): return lax.ppermute(values, 'chip', [(i, i ^ mask) for i in range(count)])  71.4 us
    dot_general x4, matrix products, local(): jnp.einsum('ecd,ecf->edf', feature_block(slot_inputs, col ^ mask), grad_i...  67.9 us
    dot_general x1, matrix products, local(): jnp.einsum('ecf,edf->ecd', jnp.concatenate([grad_gate_pre, grad_up_pre],...  42.4 us
  transfers between devices with their start and end apart: 60, of which 20 were waited for; matrix products, arithmetic and copies ran while one was open for 34% of the time, Pallas kernels for 18%

profile of v7, /device:TPU:3, one launch (start us, length us, event | category | flops | bytes accessed | tf_op | source)
XLA Modules:
  0.0 1599.9 jit_solution(10810594825103492194)
XLA Ops:
  53.0 33.2 %collective-permute-done.6 = bf16[1024,512]{1,0:T(8,128)(2,1)} collective-permute-done((bf16[1024,512]{1,0:T(8,128)(2,1)S(1)}, bf16[1024,512]{1,0:T(8,128)(2,1)}, u32[]{:S(2)}, u32[]{:S(2)}) %collective-permute-start.6) | collective-permute-done | bytes 1048608 | tf_op jit(solution)/shard_map/ppermute | solution.py:425
  131.9 48.5 %collective-permute-done.9 = bf16[1024,384]{0,1:T(8,128)(2,1)S(1)} collective-permute-done((bf16[1024,384]{0,1:T(8,128)(2,1)S(1)}, bf16[1024,384]{0,1:T(8,128)(2,1)S(1)}, u32[]{:S(2)}, u32[]{:S(2)}) %collective-permute-start.9) | collective-permute-done | bytes 786464 | tf_op jit(solution)/shard_map/ppermute | solution.py:480
  219.9 19.2 %attend_forward.1 = (bf16[1024,512]{1,0:T(8,128)(2,1)}, f32[1024,512]{1,0:T(8,128)}) custom-call(f32[4,1024,384]{2,1,0:T(8,128)} %add_bitcast_fusion.query_ref.key_ref.value_ref, f32[4,1024,384]{2,1,0:T(8,128)} %add_bitcast_fusion.query_ref.key_ref.value_ref, f32[4,1024,384]{2,1,0:T(8,128)} %add_bitcast_fusion.query_ref.key_ref.value_ref, ...), custom_call_target="tpu_custom_call" | custom-call | flops 2147483648 | bytes 9437184 | tf_op jit(solution)/shard_map/attend_forward/pallas_call | solution.py:108
  277.6 74.5 %collective-permute-done.22 = bf16[1024,512]{1,0:T(8,128)(2,1)S(1)} collective-permute-done((bf16[1024,512]{1,0:T(8,128)(2,1)S(1)}, bf16[1024,512]{1,0:T(8,128)(2,1)S(1)}, u32[]{:S(2)}, u32[]{:S(2)}) %collective-permute-start.22) | collective-permute-done | bytes 1048608 | tf_op jit(solution)/shard_map/ppermute | solution.py:425
  417.2 159.5 %all-gather.5.cloned.1.call-done = bf16[32768,512]{1,0:T(8,128)(2,1)} async-done(((bf16[1024,512]{1,0:T(8,128)(2,1)}), bf16[32768,512]{1,0:T(8,128)(2,1)}) %all-gather.5.cloned.1.call-update) | async-done | bytes 33554448 | tf_op jit(solution)/shard_map/all_gather | solution.py:724
  580.9 39.8 %gather_slots.2 = bf16[2,2048,2048]{2,1,0:T(8,128)(2,1)} custom-call(s32[2,16]{1,0:T(2,128)} %get-tuple-element.133.low_ref, s32[2,16]{1,0:T(2,128)} %get-tuple-element.134.high_ref, bf16[8,4,1024,512]{3,2,1,0:T(8,128)(2,1)} %bitcast.305, bf16[8,4,1024,512]{3,2,1,0:T(8,128)(2,1)} %bitcast.306, s32[2,16,1,512]{3,2,1,0:T(1,128)} %reshape.137.refs_2_.refs_3_.place_ref, ...), custom_call_target="tpu_custom_call" | custom-call | flops 25769803776 | bytes 50331648 | tf_op jit(solution)/shard_map/gather_slots/pallas_call | solution.py:299
  620.7 25.2 %fusion.19 = bf16[2,2048,1024]{1,2,0:T(8,128)(2,1)} fusion(bf16[2,2048,2048]{2,1,0:T(8,128)(2,1)} %gather_slots.2, bf16[2,2048,2048]{1,2,0:T(8,128)(2,1)} %constant_dynamic-update-slice_fusion.4), kind=kOutput, calls=%fused_computation.31 | convolution fusion | flops 17184063488 | bytes 33554432 | tf_op jit(solution)/shard_map/ecd,edf->ecf/dot_general | solution.py:736
  645.9 28.2 %fusion = (bf16[2,2048,1024]{1,2,0:T(8,128)(2,1)}, bf16[2,2048,1024]{1,2,0:T(8,128)(2,1)}) fusion(bf16[2,2048,1024]{1,2,0:T(8,128)(2,1)} %fusion.19, bf16[2,2048,2048]{2,1,0:T(8,128)(2,1)} %gather_slots.2, bf16[2,2048,2048]{1,2,0:T(8,128)(2,1)} %constant_dynamic-update-slice_fusion.4), kind=kOutput, calls=%fused_computation.5 | convolution fusion | flops 17217617920 | bytes 50331648 | tf_op jit(solution)/shard_map/ecd,edf->ecf/dot_general | solution.py:739
  686.5 21.4 %collective-permute-done.30 = bf16[2,1024,512]{2,1,0:T(8,128)(2,1)S(1)} collective-permute-done((bf16[2,1024,512]{2,1,0:T(8,128)(2,1)}, bf16[2,1024,512]{2,1,0:T(8,128)(2,1)S(1)}, u32[]{:S(2)}, u32[]{:S(2)}) %collective-permute-start.30) | collective-permute-done | bytes 2097184 | tf_op jit(solution)/shard_map/ppermute | solution.py:425
  709.5 28.0 %convolution_convert_fusion.slots_ref = bf16[2,2048,2048]{2,1,0:T(8,128)(2,1)} fusion(bf16[2,2048,1024]{1,2,0:T(8,128)(2,1)} %get-tuple-element.159, bf16[2,1024,2048]{2,1,0:T(8,128)(2,1)} %constant_dynamic-update-slice_fusion), kind=kOutput, calls=%fused_computation.20 | convolution fusion | flops 17188257792 | bytes 33554432 | tf_op jit(solution)/shard_map/ecf,efd->ecd/dot_general | solution.py:757
  737.5 18.6 %combine_slots.9 = bf16[4,2,1024,512]{3,2,1,0:T(8,128)(2,1)} custom-call(s32[2,16]{1,0:T(2,128)} %get-tuple-element.133.low_ref, s32[2,16]{1,0:T(2,128)} %get-tuple-element.134.high_ref, s32[1]{0:T(128)S(6)} %sub.54.core_ref, bf16[2,2048,2048]{2,1,0:T(8,128)(2,1)} %convolution_convert_fusion.slots_ref, s32[2,16,1,512]{3,2,1,0:T(1,128)} %reshape.137.refs_2_.refs_3_.place_ref, ...), custom_call_target="tpu_custom_call" | custom-call | flops 6442450944 | bytes 25165824 | tf_op jit(solution)/shard_map/combine_slots/pallas_call | solution.py:396
  758.7 20.2 %combine_slots.8 = bf16[4,2,1024,512]{3,2,1,0:T(8,128)(2,1)} custom-call(s32[2,16]{1,0:T(2,128)} %get-tuple-element.133.low_ref, s32[2,16]{1,0:T(2,128)} %get-tuple-element.134.high_ref, s32[1]{0:T(128)S(6)} %sub.54.core_ref, bf16[2,2048,2048]{2,1,0:T(8,128)(2,1)} %convolution_convert_fusion.slots_ref, s32[2,16,1,512]{3,2,1,0:T(1,128)} %reshape.137.refs_2_.refs_3_.place_ref, ...), custom_call_target="tpu_custom_call" | custom-call | flops 6442450944 | bytes 25165824 | tf_op jit(solution)/shard_map/combine_slots/pallas_call | solution.py:396
  779.0 20.5 %combine_slots.10.refs_1_ = bf16[4,4,1024,512]{3,2,1,0:T(8,128)(2,1)} custom-call(s32[2,16]{1,0:T(2,128)} %get-tuple-element.133.low_ref, s32[2,16]{1,0:T(2,128)} %get-tuple-element.134.high_ref, s32[1]{0:T(128)} %bitcast.65.core_ref, bf16[2,2048,2048]{2,1,0:T(8,128)(2,1)} %convolution_convert_fusion.slots_ref, ...), custom_call_target="tpu_custom_call" | custom-call | flops 6442450944 | bytes 25165824 | tf_op jit(solution)/shard_map/combine_slots/pallas_call | solution.py:396
  799.5 19.7 %combine_slots.11 = bf16[4,4,1024,512]{3,2,1,0:T(8,128)(2,1)} custom-call(s32[2,16]{1,0:T(2,128)} %get-tuple-element.133.low_ref, s32[2,16]{1,0:T(2,128)} %get-tuple-element.134.high_ref, s32[1]{0:T(128)} %bitcast.65.core_ref, bf16[2,2048,2048]{2,1,0:T(8,128)(2,1)} %convolution_convert_fusion.slots_ref, ...), custom_call_target="tpu_custom_call", output_to_operand_aliasing={{}: (7, {})} | custom-call | flops 6442450944 | bytes 25165824 | tf_op jit(solution)/shard_map/combine_slots/pallas_call | solution.py:396
  819.3 40.5 %gather_slots.3 = bf16[2,2048,2048]{2,1,0:T(8,128)(2,1)} custom-call(s32[2,16]{1,0:T(2,128)} %get-tuple-element.133.low_ref, s32[2,16]{1,0:T(2,128)} %get-tuple-element.134.high_ref, bf16[8,4,1024,512]{3,2,1,0:T(8,128)(2,1)} %bitcast.307, bf16[8,4,1024,512]{3,2,1,0:T(8,128)(2,1)} %bitcast.308, s32[2,16,1,512]{3,2,1,0:T(1,128)} %reshape.137.refs_2_.refs_3_.place_ref, ...), custom_call_target="tpu_custom_call" | custom-call | flops 25769803776 | bytes 50331648 | tf_op jit(solution)/shard_map/gather_slots/pallas_call | solution.py:299
  890.5 33.0 %fusion.3 = (bf16[2,2048,1024]{1,2,0:T(8,128)(2,1)}, bf16[2,2048,1024]{1,2,0:T(8,128)(2,1)}) fusion(bf16[2,2048,1024]{1,2,0:T(8,128)(2,1)} %get-tuple-element.262, bf16[2,2048,1024]{1,2,0:T(8,128)(2,1)} %fusion.19, bf16[2,2048,2048]{2,1,0:T(8,128)(2,1)} %gather_slots.3, bf16[2,1024,2048]{2,1,0:T(8,128)(2,1)} %constant_dynamic-update-slice_fusion), kind=kOutput, calls=%fused_computation.8 | convolution fusion | flops 17242783744 | bytes 58720256 | tf_op jit(solution)/shard_map/ecd,efd->ecf/dot_general | solution.py:782
  923.5 42.4 %fusion.12.slots_ref = bf16[2,2048,2048]{2,1,0:T(8,128)(2,1)} fusion(bf16[2,2048,2048]{1,2,0:T(8,128)(2,1)} %constant_dynamic-update-slice_fusion.4, bf16[2,2048,1024]{1,2,0:T(8,128)(2,1)} %get-tuple-element.153, bf16[2,2048,1024]{1,2,0:T(8,128)(2,1)} %get-tuple-element.152), kind=kOutput, calls=%fused_computation.19 | convolution fusion | flops 34401681408 | bytes 50331648 | tf_op jit(solution)/shard_map/ecf,edf->ecd/dot_general | solution.py:788
  965.9 17.6 %combine_slots.13 = bf16[4,2,1024,512]{3,2,1,0:T(8,128)(2,1)} custom-call(s32[2,16]{1,0:T(2,128)} %get-tuple-element.133.low_ref, s32[2,16]{1,0:T(2,128)} %get-tuple-element.134.high_ref, s32[1]{0:T(128)S(6)} %sub.54.core_ref, bf16[2,2048,2048]{2,1,0:T(8,128)(2,1)} %fusion.12.slots_ref, s32[2,16,1,512]{3,2,1,0:T(1,128)} %reshape.137.refs_2_.refs_3_.place_ref, ...), custom_call_target="tpu_custom_call" | custom-call | flops 6442450944 | bytes 25165824 | tf_op jit(solution)/shard_map/combine_slots/pallas_call | solution.py:396
  991.1 20.1 %combine_slots.12 = bf16[4,2,1024,512]{3,2,1,0:T(8,128)(2,1)} custom-call(s32[2,16]{1,0:T(2,128)} %get-tuple-element.133.low_ref, s32[2,16]{1,0:T(2,128)} %get-tuple-element.134.high_ref, s32[1]{0:T(128)S(6)} %sub.54.core_ref, bf16[2,2048,2048]{2,1,0:T(8,128)(2,1)} %fusion.12.slots_ref, s32[2,16,1,512]{3,2,1,0:T(1,128)} %reshape.137.refs_2_.refs_3_.place_ref, ...), custom_call_target="tpu_custom_call" | custom-call | flops 6442450944 | bytes 25165824 | tf_op jit(solution)/shard_map/combine_slots/pallas_call | solution.py:396
  1025.7 19.3 %combine_slots.14.refs_1_ = bf16[4,4,1024,512]{3,2,1,0:T(8,128)(2,1)} custom-call(s32[2,16]{1,0:T(2,128)} %get-tuple-element.133.low_ref, s32[2,16]{1,0:T(2,128)} %get-tuple-element.134.high_ref, s32[1]{0:T(128)} %bitcast.65.core_ref, bf16[2,2048,2048]{2,1,0:T(8,128)(2,1)} %fusion.12.slots_ref, s32[2,16,1,512]{3,2,1,0:T(1,128)} %reshape.137.refs_2_.refs_3_.place_ref, ...), custom_call_target="tpu_custom_call" | custom-call | flops 6442450944 | bytes 25165824 | tf_op jit(solution)/shard_map/combine_slots/pallas_call | solution.py:396
  1045.0 18.5 %combine_slots.15 = bf16[4,4,1024,512]{3,2,1,0:T(8,128)(2,1)} custom-call(s32[2,16]{1,0:T(2,128)} %get-tuple-element.133.low_ref, s32[2,16]{1,0:T(2,128)} %get-tuple-element.134.high_ref, s32[1]{0:T(128)} %bitcast.65.core_ref, bf16[2,2048,2048]{2,1,0:T(8,128)(2,1)} %fusion.12.slots_ref, ...), custom_call_target="tpu_custom_call", output_to_operand_aliasing={{}: (7, {})} | custom-call | flops 6442450944 | bytes 25165824 | tf_op jit(solution)/shard_map/combine_slots/pallas_call | solution.py:396
  1074.8 16.9 %fusion.42 = bf16[2,512,2048]{2,1,0:T(8,128)(2,1)} fusion(bf16[2,2048,2048]{1,2,0:T(8,128)(2,1)} %pad_maximum_fusion, bf16[2,2048,2048]{2,1,0:T(8,128)(2,1)} %gather_slots.2, s32[]{:T(128)S(6)} %select_n.277), kind=kOutput, calls=%fused_computation.59 | convolution fusion | flops 8592031744 | bytes 25165828 | tf_op jit(solution)/shard_map/ecd,ecf->edf/dot_general | solution.py:812
  1091.7 16.6 %fusion.45 = bf16[2,512,2048]{2,1,0:T(8,128)(2,1)} fusion(bf16[2,2048,2048]{1,2,0:T(8,128)(2,1)} %pad_maximum_fusion, bf16[2,2048,2048]{2,1,0:T(8,128)(2,1)} %gather_slots.2, s32[]{:T(128)S(6)} %select_n.278), kind=kOutput, calls=%fused_computation.60 | convolution fusion | flops 8592031744 | bytes 25165828 | tf_op jit(solution)/shard_map/ecd,ecf->edf/dot_general | solution.py:812
  1108.3 17.1 %fusion.48 = bf16[2,512,2048]{2,1,0:T(8,128)(2,1)} fusion(bf16[2,2048,2048]{1,2,0:T(8,128)(2,1)} %pad_maximum_fusion, bf16[2,2048,2048]{2,1,0:T(8,128)(2,1)} %gather_slots.2, s32[]{:T(128)S(6)} %select_n.279), kind=kOutput, calls=%fused_computation.61 | convolution fusion | flops 8592031744 | bytes 25165828 | tf_op jit(solution)/shard_map/ecd,ecf->edf/dot_general | solution.py:812
  1125.4 17.3 %fusion.34 = f32[2,512,2048]{2,1,0:T(8,128)} fusion(bf16[2,2048,2048]{1,2,0:T(8,128)(2,1)} %pad_maximum_fusion, bf16[2,2048,2048]{2,1,0:T(8,128)(2,1)} %gather_slots.2, s32[]{:T(128)S(6)} %select_n.276), kind=kOutput, calls=%fused_computation.51 | convolution fusion | flops 8589934592 | bytes 29360132 | tf_op jit(solution)/shard_map/ecd,ecf->edf/dot_general | solution.py:812
  1142.7 74.8 %reduce-scatter.21.cloned.1.call-done = bf16[1,4,1024,512]{3,2,1,0:T(8,128)(2,1)} async-done(((bf16[4,4,1024,512]{3,2,1,0:T(8,128)(2,1)}), bf16[1,4,1024,512]{3,2,1,0:T(8,128)(2,1)}) %reduce-scatter.21.cloned.1.call-update) | async-done | bytes 4194320
  1230.4 79.3 %collective-permute-done.38 = bf16[2,512,2048]{2,1,0:T(8,128)(2,1)} collective-permute-done((bf16[2,512,2048]{2,1,0:T(8,128)(2,1)}, bf16[2,512,2048]{2,1,0:T(8,128)(2,1)}, u32[]{:S(2)}, u32[]{:S(2)}) %collective-permute-start.38) | collective-permute-done | bytes 4194336 | tf_op jit(solution)/shard_map/ppermute | solution.py:425
  1345.8 26.4 %collective-permute-done.41 = bf16[1024,512]{1,0:T(8,128)(2,1)S(1)} collective-permute-done((bf16[1024,512]{1,0:T(8,128)(2,1)S(1)}, bf16[1024,512]{1,0:T(8,128)(2,1)S(1)}, u32[]{:S(2)}, u32[]{:S(2)}) %collective-permute-start.41) | collective-permute-done | bytes 1048608 | tf_op jit(solution)/shard_map/ppermute | solution.py:425
  1412.0 28.7 %attend_backward.1 = (bf16[4,1024,384]{2,1,0:T(8,128)(2,1)}, f32[2,128]{1,0:T(2,128)}) custom-call(f32[4,1024,384]{2,1,0:T(8,128)} %add_bitcast_fusion.query_ref.key_ref.value_ref, f32[4,1024,384]{2,1,0:T(8,128)} %add_bitcast_fusion.query_ref.key_ref.value_ref, f32[4,1024,384]{2,1,0:T(8,128)} %add_bitcast_fusion.query_ref.key_ref.value_ref, ...), custom_call_target="tpu_custom_call" | custom-call | flops 5368709120 | bytes 12582912 | tf_op jit(solution)/shard_map/attend_backward/pallas_call | solution.py:194
  1465.7 20.6 %collective-permute-done.43 = bf16[2,512,2048]{2,1,0:T(8,128)(2,1)} collective-permute-done((bf16[2,512,2048]{2,1,0:T(8,128)(2,1)}, bf16[2,512,2048]{2,1,0:T(8,128)(2,1)}, u32[]{:S(2)}, u32[]{:S(2)}) %collective-permute-start.43) | collective-permute-done | bytes 4194336 | tf_op jit(solution)/shard_map/ppermute | solution.py:425
  1504.0 20.1 %collective-permute-done.46 = bf16[1024,512]{1,0:T(8,128)(2,1)} collective-permute-done((bf16[1024,512]{1,0:T(8,128)(2,1)}, bf16[1024,512]{1,0:T(8,128)(2,1)}, u32[]{:S(2)}, u32[]{:S(2)}) %collective-permute-start.46) | collective-permute-done | bytes 1048608 | tf_op jit(solution)/shard_map/ppermute | solution.py:425
  1524.1 24.2 %collective-permute-done.45 = bf16[1024,512]{1,0:T(8,128)(2,1)} collective-permute-done((bf16[1024,512]{1,0:T(8,128)(2,1)}, bf16[1024,512]{1,0:T(8,128)(2,1)}, u32[]{:S(2)}, u32[]{:S(2)}) %collective-permute-start.45) | collective-permute-done | bytes 1048608 | tf_op jit(solution)/shard_map/ppermute | solution.py:425
  (393 shorter events, 494.1 us)
Async XLA Ops:
  7.2 569.5 %all-gather.5.cloned.1.call-start = ((), (), s32[]{:S(2)}) async-start(), calls=%async_computation.10 | async-start | bytes 34603008 | tf_op jit(solution)/shard_map/all_gather | solution.py:724
  38.8 47.4 %collective-permute-start.6 = (bf16[1024,512]{1,0:T(8,128)(2,1)S(1)}, bf16[1024,512]{1,0:T(8,128)(2,1)}, u32[]{:S(2)}, u32[]{:S(2)}) collective-permute-start(bf16[1024,512]{1,0:T(8,128)(2,1)S(1)} %copy-done.4), channel_id=1, source_target_pairs={{0,2},{1,3},{2,0},{3,1},{4,6},{5,7},{6,4},{7,5},{8,10},{9,11},{10,... | collective-permute-start | bytes 3145736 | tf_op jit(solution)/shard_map/ppermute | solution.py:425
  47.9 134.4 %collective-permute-start.14 = (bf16[2,256,2048]{2,1,0:T(8,128)(2,1)}, bf16[2,256,2048]{2,1,0:T(8,128)(2,1)}, u32[]{:S(2)}, u32[]{:S(2)}) collective-permute-start(bf16[2,256,2048]{2,1,0:T(8,128)(2,1)} %get-tuple-element.211), channel_id=1, source_target_pairs={{0,1},{1,0},{2,3},{3,2},{4,5},{5,4},{6,7},{7,6},{8,9},{9,8},{10,11... | collective-permute-start | bytes 6291464 | tf_op jit(solution)/shard_map/ppermute | solution.py:425
  48.0 134.3 %collective-permute-start.15 = (bf16[2,256,2048]{2,1,0:T(8,128)(2,1)}, bf16[2,256,2048]{2,1,0:T(8,128)(2,1)}, u32[]{:S(2)}, u32[]{:S(2)}) collective-permute-start(bf16[2,256,2048]{2,1,0:T(8,128)(2,1)} %get-tuple-element.210), channel_id=1, source_target_pairs={{0,2},{1,3},{2,0},{3,1},{4,6},{5,7},{6,4},{7,5},{8,10},{9,11},{10,... | collective-permute-start | bytes 6291464 | tf_op jit(solution)/shard_map/ppermute | solution.py:425
  49.6 132.7 %collective-permute-start.16 = (bf16[2,256,2048]{2,1,0:T(8,128)(2,1)}, bf16[2,256,2048]{2,1,0:T(8,128)(2,1)}, u32[]{:S(2)}, u32[]{:S(2)}) collective-permute-start(bf16[2,256,2048]{2,1,0:T(8,128)(2,1)} %get-tuple-element.209), channel_id=1, source_target_pairs={{0,3},{1,2},{2,1},{3,0},{4,7},{5,6},{6,5},{7,4},{8,11},{9,10},{10,... | collective-permute-start | bytes 6291464 | tf_op jit(solution)/shard_map/ppermute | solution.py:425
  125.0 55.4 %collective-permute-start.9 = (bf16[1024,384]{0,1:T(8,128)(2,1)S(1)}, bf16[1024,384]{0,1:T(8,128)(2,1)S(1)}, u32[]{:S(2)}, u32[]{:S(2)}) collective-permute-start(bf16[1024,384]{0,1:T(8,128)(2,1)S(1)} %maximum_maximum_fusion), channel_id=1, source_target_pairs={{0,16},{8,24},{16,0},{24,8},{1,17},{9,25},{17,1},{25,9},{2,18},{10... | collective-permute-start | bytes 2359304 | tf_op jit(solution)/shard_map/ppermute | solution.py:480
  125.3 56.0 %collective-permute-start.10 = (bf16[1024,384]{0,1:T(8,128)(2,1)S(1)}, bf16[1024,384]{0,1:T(8,128)(2,1)S(1)}, u32[]{:S(2)}, u32[]{:S(2)}) collective-permute-start(bf16[1024,384]{0,1:T(8,128)(2,1)S(1)} %maximum_maximum_fusion), channel_id=1, source_target_pairs={{0,24},{8,16},{16,8},{24,0},{1,25},{9,17},{17,9},{25,1},{2,26},{10... | collective-permute-start | bytes 2359304 | tf_op jit(solution)/shard_map/ppermute | solution.py:480
  206.7 56.0 %collective-permute-start.24 = (bf16[4,256,512]{2,1,0:T(8,128)(2,1)S(1)}, bf16[4,256,512]{2,1,0:T(8,128)(2,1)S(1)}, u32[]{:S(2)}, u32[]{:S(2)}) collective-permute-start(bf16[4,256,512]{2,1,0:T(8,128)(2,1)S(1)} %bitcast_dynamic-update-slice_fusion.14), channel_id=1, source_target_pairs={{0,4},{4,0},{1,5},{5,1},{2,6},{6,2},{3,7},{7,3},{8,12},{12,8},{9,1... | collective-permute-start | bytes 3145736 | tf_op jit(solution)/shard_map/ppermute | solution.py:420
  259.9 102.7 %collective-permute-start.25 = (bf16[2,128,2048]{2,1,0:T(8,128)(2,1)}, bf16[2,128,2048]{2,1,0:T(8,128)(2,1)}, u32[]{:S(2)}, u32[]{:S(2)}) collective-permute-start(bf16[2,128,2048]{2,1,0:T(8,128)(2,1)} %get-tuple-element.113), channel_id=1, source_target_pairs={{0,1},{1,0},{2,3},{3,2},{4,5},{5,4},{6,7},{7,6},{8,9},{9,8},{10,11... | collective-permute-start | bytes 3145736 | tf_op jit(solution)/shard_map/ppermute | solution.py:425
  261.2 101.3 %collective-permute-start.26 = (bf16[2,128,2048]{2,1,0:T(8,128)(2,1)}, bf16[2,128,2048]{2,1,0:T(8,128)(2,1)}, u32[]{:S(2)}, u32[]{:S(2)}) collective-permute-start(bf16[2,128,2048]{2,1,0:T(8,128)(2,1)} %get-tuple-element.114), channel_id=1, source_target_pairs={{0,2},{1,3},{2,0},{3,1},{4,6},{5,7},{6,4},{7,5},{8,10},{9,11},{10,... | collective-permute-start | bytes 3145736 | tf_op jit(solution)/shard_map/ppermute | solution.py:425
  261.2 90.9 %collective-permute-start.22 = (bf16[1024,512]{1,0:T(8,128)(2,1)S(1)}, bf16[1024,512]{1,0:T(8,128)(2,1)S(1)}, u32[]{:S(2)}, u32[]{:S(2)}) collective-permute-start(bf16[1024,512]{1,0:T(8,128)(2,1)S(1)} %copy-done.35), channel_id=1, source_target_pairs={{0,2},{1,3},{2,0},{3,1},{4,6},{5,7},{6,4},{7,5},{8,10},{9,11},{10,... | collective-permute-start | bytes 3145736 | tf_op jit(solution)/shard_map/ppermute | solution.py:425
  263.7 88.6 %collective-permute-start.23 = (bf16[1024,512]{1,0:T(8,128)(2,1)S(1)}, bf16[1024,512]{1,0:T(8,128)(2,1)S(1)}, u32[]{:S(2)}, u32[]{:S(2)}) collective-permute-start(bf16[1024,512]{1,0:T(8,128)(2,1)S(1)} %copy-done.35), channel_id=1, source_target_pairs={{0,3},{1,2},{2,1},{3,0},{4,7},{5,6},{6,5},{7,4},{8,11},{9,10},{10,... | collective-permute-start | bytes 3145736 | tf_op jit(solution)/shard_map/ppermute | solution.py:425
  276.9 85.7 %collective-permute-start.27 = (bf16[2,128,2048]{2,1,0:T(8,128)(2,1)}, bf16[2,128,2048]{2,1,0:T(8,128)(2,1)}, u32[]{:S(2)}, u32[]{:S(2)}) collective-permute-start(bf16[2,128,2048]{2,1,0:T(8,128)(2,1)} %get-tuple-element.115), channel_id=1, source_target_pairs={{0,3},{1,2},{2,1},{3,0},{4,7},{5,6},{6,5},{7,4},{8,11},{9,10},{10,... | collective-permute-start | bytes 3145736 | tf_op jit(solution)/shard_map/ppermute | solution.py:425
  362.6 456.6 %all-gather.7.cloned.1.call-start = ((), (), s32[]{:S(2)}) async-start(), calls=%async_computation.11 | async-start | bytes 34603008 | tf_op jit(solution)/shard_map/all_gather | solution.py:730
  576.7 434.5 %reduce-scatter.19.cloned.1.call-start = ((), (), s32[]{:S(2)}) async-start(), calls=%async_computation.12 | async-start | bytes 20971520
  578.2 101.8 %collective-permute-start.28 = (bf16[2,1024,512]{2,1,0:T(8,128)(2,1)}, bf16[2,1024,512]{2,1,0:T(8,128)(2,1)}, u32[]{:S(2)}, u32[]{:S(2)}) collective-permute-start(bf16[2,1024,512]{2,1,0:T(8,128)(2,1)} %get-tuple-element.140), channel_id=1, source_target_pairs={{0,1},{1,0},{2,3},{3,2},{4,5},{5,4},{6,7},{7,6},{8,9},{9,8},{10,11... | collective-permute-start | bytes 6291464 | tf_op jit(solution)/shard_map/ppermute | solution.py:425
  578.6 104.6 %collective-permute-start.29 = (bf16[2,1024,512]{2,1,0:T(8,128)(2,1)}, bf16[2,1024,512]{2,1,0:T(8,128)(2,1)}, u32[]{:S(2)}, u32[]{:S(2)}) collective-permute-start(bf16[2,1024,512]{2,1,0:T(8,128)(2,1)} %get-tuple-element.141), channel_id=1, source_target_pairs={{0,2},{1,3},{2,0},{3,1},{4,6},{5,7},{6,4},{7,5},{8,10},{9,11},{10,... | collective-permute-start | bytes 6291464 | tf_op jit(solution)/shard_map/ppermute | solution.py:425
  579.8 128.1 %collective-permute-start.30 = (bf16[2,1024,512]{2,1,0:T(8,128)(2,1)}, bf16[2,1024,512]{2,1,0:T(8,128)(2,1)S(1)}, u32[]{:S(2)}, u32[]{:S(2)}) collective-permute-start(bf16[2,1024,512]{2,1,0:T(8,128)(2,1)} %get-tuple-element.142), channel_id=1, source_target_pairs={{0,3},{1,2},{2,1},{3,0},{4,7},{5,6},{6,5},{7,4},{8,11},{9,10},{10,... | collective-permute-start | bytes 6291464 | tf_op jit(solution)/shard_map/ppermute | solution.py:425
  819.2 398.3 %reduce-scatter.21.cloned.1.call-start = ((), (), s32[]{:S(2)}) async-start(), calls=%async_computation.13 | async-start | bytes 20971520
  889.3 121.9 %collective-permute-start.33 = (bf16[2,1024,512]{2,1,0:T(8,128)(2,1)}, bf16[2,1024,512]{2,1,0:T(8,128)(2,1)S(1)}, u32[]{:S(2)}, u32[]{:S(2)}) collective-permute-start(bf16[2,1024,512]{2,1,0:T(8,128)(2,1)} %fusion.84), channel_id=1, source_target_pairs={{0,1},{1,0},{2,3},{3,2},{4,5},{5,4},{6,7},{7,6},{8,9},{9,8},{10,11... | collective-permute-start | bytes 6291464 | tf_op jit(solution)/shard_map/ppermute | solution.py:425
  890.5 120.7 %collective-permute-start.34 = (bf16[2,1024,512]{2,1,0:T(8,128)(2,1)}, bf16[2,1024,512]{2,1,0:T(8,128)(2,1)}, u32[]{:S(2)}, u32[]{:S(2)}) collective-permute-start(bf16[2,1024,512]{2,1,0:T(8,128)(2,1)} %fusion.87), channel_id=1, source_target_pairs={{0,2},{1,3},{2,0},{3,1},{4,6},{5,7},{6,4},{7,5},{8,10},{9,11},{10,... | collective-permute-start | bytes 6291464 | tf_op jit(solution)/shard_map/ppermute | solution.py:425
  1011.4 52.1 %collective-permute-start.37 = (bf16[2,1024,512]{2,1,0:T(8,128)(2,1)}, bf16[2,1024,512]{2,1,0:T(8,128)(2,1)}, u32[]{:S(2)}, u32[]{:S(2)}) collective-permute-start(bf16[2,1024,512]{2,1,0:T(8,128)(2,1)} %fusion.90), channel_id=1, source_target_pairs={{0,3},{1,2},{2,1},{3,0},{4,7},{5,6},{6,5},{7,4},{8,11},{9,10},{10,... | collective-permute-start | bytes 6291464 | tf_op jit(solution)/shard_map/ppermute | solution.py:425
  1063.5 246.1 %reduce-scatter.11.cloned.1.call-start = ((), (), s32[]{:S(2)}) async-start(), calls=%async_computation.6 | async-start | bytes 5242880 | tf_op jit(solution)/shard_map/reduce_scatter | solution.py:820
  1217.6 233.0 %reduce-scatter.13.cloned.1.call-start = ((), (), s32[]{:S(2)}) async-start(), calls=%async_computation.7 | async-start | bytes 5242880 | tf_op jit(solution)/shard_map/reduce_scatter | solution.py:847
  1217.8 91.8 %collective-permute-start.38 = (bf16[2,512,2048]{2,1,0:T(8,128)(2,1)}, bf16[2,512,2048]{2,1,0:T(8,128)(2,1)}, u32[]{:S(2)}, u32[]{:S(2)}) collective-permute-start(bf16[2,512,2048]{2,1,0:T(8,128)(2,1)} %fusion.42), channel_id=1, source_target_pairs={{0,1},{1,0},{2,3},{3,2},{4,5},{5,4},{6,7},{7,6},{8,9},{9,8},{10,11... | collective-permute-start | bytes 12582920 | tf_op jit(solution)/shard_map/ppermute | solution.py:425
  1218.2 91.4 %collective-permute-start.39 = (bf16[2,512,2048]{2,1,0:T(8,128)(2,1)}, bf16[2,512,2048]{2,1,0:T(8,128)(2,1)}, u32[]{:S(2)}, u32[]{:S(2)}) collective-permute-start(bf16[2,512,2048]{2,1,0:T(8,128)(2,1)} %fusion.45), channel_id=1, source_target_pairs={{0,2},{1,3},{2,0},{3,1},{4,6},{5,7},{6,4},{7,5},{8,10},{9,11},{10,... | collective-permute-start | bytes 12582920 | tf_op jit(solution)/shard_map/ppermute | solution.py:425
  1324.8 47.5 %collective-permute-start.41 = (bf16[1024,512]{1,0:T(8,128)(2,1)S(1)}, bf16[1024,512]{1,0:T(8,128)(2,1)S(1)}, u32[]{:S(2)}, u32[]{:S(2)}) collective-permute-start(bf16[1024,512]{1,0:T(8,128)(2,1)S(1)} %get-tuple-element.218), channel_id=1, source_target_pairs={{0,2},{1,3},{2,0},{3,1},{4,6},{5,7},{6,4},{7,5},{8,10},{9,11},{10,... | collective-permute-start | bytes 3145736 | tf_op jit(solution)/shard_map/ppermute | solution.py:425
  1373.8 128.4 %reduce-scatter.17.cloned.1.call-start = ((), (), s32[]{:S(2)}) async-start(), calls=%async_computation.9 | async-start | bytes 2359296 | tf_op jit(solution)/shard_map/reduce_scatter | solution.py:848
  1393.4 92.9 %collective-permute-start.43 = (bf16[2,512,2048]{2,1,0:T(8,128)(2,1)}, bf16[2,512,2048]{2,1,0:T(8,128)(2,1)}, u32[]{:S(2)}, u32[]{:S(2)}) collective-permute-start(bf16[2,512,2048]{2,1,0:T(8,128)(2,1)} %fusion.48), channel_id=1, source_target_pairs={{0,3},{1,2},{2,1},{3,0},{4,7},{5,6},{6,5},{7,4},{8,11},{9,10},{10,... | collective-permute-start | bytes 12582920 | tf_op jit(solution)/shard_map/ppermute | solution.py:425
  1398.4 177.6 %reduce-scatter.15.cloned.1.call-start = ((), (), s32[]{:S(2)}) async-start(), calls=%async_computation.8 | async-start | bytes 7077888 | tf_op jit(solution)/shard_map/reduce_scatter | solution.py:553
  1500.5 47.8 %collective-permute-start.45 = (bf16[1024,512]{1,0:T(8,128)(2,1)}, bf16[1024,512]{1,0:T(8,128)(2,1)}, u32[]{:S(2)}, u32[]{:S(2)}) collective-permute-start(bf16[1024,512]{1,0:T(8,128)(2,1)} %get-tuple-element.215), channel_id=1, source_target_pairs={{0,2},{1,3},{2,0},{3,1},{4,6},{5,7},{6,4},{7,5},{8,10},{9,11},{10,... | collective-permute-start | bytes 3145736 | tf_op jit(solution)/shard_map/ppermute | solution.py:425
  1500.5 47.8 %collective-permute-start.44 = (bf16[1024,512]{1,0:T(8,128)(2,1)}, bf16[1024,512]{1,0:T(8,128)(2,1)}, u32[]{:S(2)}, u32[]{:S(2)}) collective-permute-start(bf16[1024,512]{1,0:T(8,128)(2,1)} %get-tuple-element.213), channel_id=1, source_target_pairs={{0,1},{1,0},{2,3},{3,2},{4,5},{5,4},{6,7},{7,6},{8,9},{9,8},{10,11... | collective-permute-start | bytes 3145736 | tf_op jit(solution)/shard_map/ppermute | solution.py:425
  (83 other events, 1775.4 us)
Sparse Core Ops, SparseCore 0:
  362.7 213.9 all-gather.4
  579.6 226.8 all-gather.6
  819.4 189.4 reduce-scatter.18
  1063.7 153.8 reduce-scatter.20
  1219.7 76.9 reduce-scatter.10
  1373.9 76.6 reduce-scatter.12
  1452.9 33.4 reduce-scatter.16
  1495.9 68.5 reduce-scatter.14
